TPU v7x, 256 devices: a whole 4x4x8 slice. The times are simulated.
256 devices in a mesh: dp: 16 (over z, core), tensor: 16 (over y, x).
Axes of the slice: x: 4, y: 4, z: 8, core: 2. Of those that a mesh axis runs over, the one named last changes fastest.
Arguments:
- hidden_in: bfloat16 [16384, 896], P('dp', 'tensor'), may hold values from -6 to 6
- out_grad: bfloat16 [16384, 896], P('dp', 'tensor'), may hold values from -6 to 6
- w_gate: bfloat16 [4096, 896], P('tensor'), may hold values from -0.1875 to 0.1875
- w_up: bfloat16 [4096, 896], P('tensor'), may hold values from -0.1875 to 0.1875
- w_down: bfloat16 [4096, 896], P('tensor'), may hold values from -0.1875 to 0.1875
- error_in: bfloat16 [16, 3, 4096, 896], P('dp', None, 'tensor'), may hold values from -96 to 96
- q_init: float32 [3, 32, 896], P(None, None, 'tensor'), may hold values from -6 to 6
Outputs:
- input_grad: bfloat16 [16384, 896], P('dp', 'tensor')
- error_out: bfloat16 [16, 3, 4096, 896], P('dp', None, 'tensor')
- q_out: float32 [3, 32, 896], P(None, None, 'tensor')
All inputs are finite; a program needn't handle non-finite values.
Results may differ from a plain program's by a relative error of at most 0.017.
Values may be sent and summed in bfloat16 or wider, within the bound.
No kernel may reach another device: no remote copies, remote signals or barrier semaphores. Data moves between devices by JAX's collectives and lax.ppermute only.
A program may use at most 128 MiB of HBM per device.

v0:
```python
import jax
import jax.numpy as jnp
from jax import lax
from jax.sharding import PartitionSpec as P


def rows_dot(left, right):
    return lax.dot_general(
        left, right, (((1,), (1,)), ((), ())), preferred_element_type=jnp.float32
    )


def inner_dot(left, right):
    return lax.dot_general(
        left, right, (((0,), (0,)), ((), ())), preferred_element_type=jnp.float32
    )


def ortho_one(chol_factor, p_trans):
    return lax.linalg.triangular_solve(chol_factor, p_trans, left_side=True, lower=True)


def per_device(hidden_in, out_grad, w_gate, w_up, w_down, error_in, q_init):
    n_workers = lax.axis_size("dp")
    n_tensor = lax.axis_size("tensor")
    shard = hidden_in.shape[1]
    highest = lax.Precision.HIGHEST
    x_full, dy_full = (
        lax.all_gather(hidden_in, "tensor", axis=1, tiled=True),
        lax.all_gather(out_grad, "tensor", axis=1, tiled=True),
    )
    gate_pre = rows_dot(x_full, w_gate)
    up_pre = rows_dot(x_full, w_up)
    gate_sig = jax.nn.sigmoid(gate_pre)
    gate_act = gate_pre * gate_sig
    hidden = (gate_act * up_pre).astype(jnp.bfloat16)
    hidden_grad = rows_dot(dy_full, w_down)
    gate_grad = (hidden_grad * up_pre * gate_sig * (1.0 + gate_pre * (1.0 - gate_sig))).astype(
        jnp.bfloat16
    )
    up_grad = (hidden_grad * gate_act).astype(jnp.bfloat16)
    partial_value = jnp.dot(gate_grad, w_gate, preferred_element_type=jnp.float32)
    partial_value = partial_value + jnp.dot(up_grad, w_up, preferred_element_type=jnp.float32)
    partial_value = partial_value.astype(jnp.bfloat16)
    input_grad = (
        lax.psum_scatter(partial_value, "tensor", scatter_dimension=1, tiled=True)
        .astype(jnp.float32)
        .astype(jnp.bfloat16)
    )
    matrices = jnp.stack(
        [inner_dot(gate_grad, x_full), inner_dot(up_grad, x_full), inner_dot(hidden, dy_full)]
    )
    matrices = matrices + error_in[0].astype(jnp.float32)
    q_full = lax.all_gather(q_init, "tensor", axis=2, tiled=True)
    p_local = jnp.einsum("khd,krd->khr", matrices, q_full, precision=highest)
    p_factor = lax.psum(p_local.astype(jnp.bfloat16), "dp").astype(jnp.float32) / n_workers
    gram_part = jnp.einsum("khr,khs->krs", p_factor, p_factor, precision=highest)
    gram_matrix = lax.psum(gram_part, "tensor")
    chol_factor = jnp.linalg.cholesky(gram_matrix)
    p_ortho = jax.vmap(ortho_one)(chol_factor, jnp.swapaxes(p_factor, 1, 2))
    q_part = jnp.einsum("krh,khd->krd", p_ortho, matrices, precision=highest)
    rank = q_part.shape[1]
    received = lax.all_to_all(
        q_part.astype(jnp.bfloat16), "tensor", split_axis=2, concat_axis=0, tiled=True
    ).astype(q_part.dtype)
    owned = jnp.sum(received.reshape(n_tensor, 3, rank, shard), axis=0)
    q_out = lax.psum(owned, "dp") / n_workers
    q_new = lax.all_gather(q_out, "tensor", axis=2, tiled=True)
    approx = jnp.einsum("krh,krd->khd", p_ortho, q_new, precision=highest)
    error_out = (matrices - approx)[None].astype(jnp.bfloat16)
    return (input_grad, error_out, q_out)


def solution(mesh):
    in_specs = (
        P("dp", "tensor"),
        P("dp", "tensor"),
        P("tensor", None),
        P("tensor", None),
        P("tensor", None),
        P("dp", None, "tensor", None),
        P(None, None, "tensor"),
    )
    out_specs = (P("dp", "tensor"), P("dp", None, "tensor", None), P(None, None, "tensor"))
    return jax.shard_map(
        per_device, mesh=mesh, in_specs=in_specs, out_specs=out_specs, check_vma=False
    )
```

profile of v0, /device:TPU:1, one launch (start us, length us, event | category | flops | bytes accessed | tf_op | source)
XLA Modules:
  0.0 359.6 jit_solution(10535488992322038769)
XLA Ops:
  7.2 0.0 copy-start
  7.2 0.0 all-gather.5.cloned.1.call-start
  7.2 0.7 all-gather.5.cloned.1.call-update
  7.9 0.0 all-gather.3.cloned.1.call-start
  8.0 0.7 all-gather.3.cloned.1.call-update
  8.7 0.0 reduce-scatter.4.cloned.1.call-start
  8.7 0.9 copy.21
  9.6 26.4 %all_gather.14 = f32[3,32,896]{1,0,2:T(4,128)} all-gather(f32[3,32,56]{1,0,2:T(4,128)S(1)} %copy.21), channel_id=1, replica_groups=mesh['dp'=16,'tensor'=16] {'tensor'}, dimensions={2}, use_global_device_ids=true | all-gather | bytes 365568 | tf_op jit(solution)/shard_map/all_gather | solution.py:54
  36.1 0.0 copy-start.13
  36.1 26.7 %all-gather.5.cloned.1.call-done = bf16[1024,896]{0,1:T(8,128)(2,1)} async-done(((bf16[1024,56]{0,1:T(8,128)(2,1)}), bf16[1024,896]{0,1:T(8,128)(2,1)}) %all-gather.5.cloned.1.call-update) | async-done | bytes 1835024 | tf_op jit(solution)/shard_map/all_gather | solution.py:29
  62.8 0.0 copy-done
  62.8 0.0 copy-start.1
  62.8 3.4 fusion.19
  66.1 0.0 copy-done.13
  66.1 0.0 copy-done.1
  66.1 1.7 fusion.18
  67.9 46.1 %all-gather.3.cloned.1.call-done = bf16[1024,896]{0,1:T(8,128)(2,1)} async-done(((bf16[1024,56]{0,1:T(8,128)(2,1)}), bf16[1024,896]{0,1:T(8,128)(2,1)}) %all-gather.3.cloned.1.call-update) | async-done | bytes 1835024 | tf_op jit(solution)/shard_map/all_gather | solution.py:30
  114.0 0.0 copy-done.15
  114.0 3.0 multiply_convert_fusion.1
  117.0 0.0 copy-start.10
  117.1 0.0 copy-start.12
  117.1 0.7 fusion.20
  117.8 0.1 copy-done.10
  117.8 0.2 copy-done.12
  118.0 2.0 add_convert_fusion
  120.0 0.0 reduce-scatter.4.cloned.1.call-update
  120.0 0.0 copy-start.11
  120.0 0.0 copy-start.14
  120.0 1.9 convolution_bitcast_fusion.1
  122.0 0.0 copy-done.11
  122.0 0.0 copy-start.8
  122.0 0.0 copy-start.9
  122.0 0.8 convolution_bitcast_fusion.2
  122.8 0.0 copy-done.14
  122.8 0.4 copy-done.8
  123.2 0.3 copy-done.9
  123.5 0.8 convolution_bitcast_fusion
  124.4 0.1 copy-done.2
  124.5 0.9 copy-done.7
  125.4 0.0 copy-done.4
  125.4 0.7 copy-done.5
  126.1 2.7 fusion.4
  128.8 46.5 %psum.21 = bf16[3,256,32]{1,2,0:T(8,128)(2,1)S(1)} all-reduce(bf16[3,256,32]{1,2,0:T(8,128)(2,1)S(1)} %fusion.4), channel_id=1, replica_groups=mesh['dp'=16,'tensor'=16] {'dp'}, use_global_device_ids=true, to_apply=%region_1.0 | all-reduce | flops 24576 | bytes 98304 | tf_op jit(solution)/shard_map/psum | solution.py:56
  175.3 0.2 fusion.10
  175.5 58.1 %psum.22 = f32[3,32,32]{1,2,0:T(8,128)S(1)} all-reduce(f32[3,32,32]{1,2,0:T(8,128)S(1)} %fusion.10), channel_id=1, replica_groups=mesh['dp'=16,'tensor'=16] {'tensor'}, use_global_device_ids=true, to_apply=%region_2.0 | all-reduce | flops 3072 | bytes 24576 | tf_op jit(solution)/shard_map/psum | solution.py:58
  233.6 0.1 copy.24
  233.7 8.8 %custom-call.7 = f32[3,32,32]{2,1,0:T(8,128)S(1)} custom-call(f32[3,32,32]{2,1,0:T(8,128)S(1)} %fusion.12), custom_call_target="Cholesky" | custom-call | tf_op jit(solution)/shard_map/jit(cholesky)/cholesky | solution.py:59
  242.6 0.1 compare_reduce_fusion
  242.7 0.1 select_bitcast_fusion
  242.8 7.4 %custom-call.8 = f32[3,1,32,32]{2,3,1,0:T(8,128)S(1)} custom-call(f32[3,1,32,32]{3,2,1,0:T(8,128)S(1)} %select_bitcast_fusion), custom_call_target="InvertDiagBlocksLowerTriangular" | custom-call | tf_op jit(solution)/shard_map/vmap()/triangular_solve | solution.py:20
  250.1 0.3 fusion.9
  250.5 3.1 convolution_convert_fusion
  253.6 1.1 copy.26
  254.6 0.6 reshape.25
  255.3 9.6 %all_to_all.4 = bf16[16,2,2688]{2,1,0:T(2,128)(2,1)S(1)} all-to-all(bf16[16,2,2688]{2,1,0:T(2,128)(2,1)S(1)} %reshape.25), channel_id=1, replica_groups=mesh['dp'=16,'tensor'=16] {'tensor'}, dimensions={0} | all-to-all | bytes 344064 | tf_op jit(solution)/shard_map/all_to_all | solution.py:63
  264.9 0.6 reshape.26
  265.5 0.0 copy-start.3
  265.5 0.5 convert_reduce_fusion
  266.0 61.5 %psum.23 = f32[3,32,56]{1,0,2:T(4,128)S(1)} all-reduce(f32[3,32,56]{1,0,2:T(4,128)S(1)} %convert_reduce_fusion), channel_id=1, replica_groups=mesh['dp'=16,'tensor'=16] {'dp'}, use_global_device_ids=true, to_apply=%region_6.7 | all-reduce | flops 5376 | bytes 43008 | tf_op jit(solution)/shard_map/psum | solution.py:67
  327.6 0.7 copy.28
  328.3 19.6 %all_gather.15 = f32[3,32,896]{1,0,2:T(4,128)S(1)} all-gather(f32[3,32,56]{1,0,2:T(4,128)S(1)} %broadcast_multiply_fusion), channel_id=1, replica_groups=mesh['dp'=16,'tensor'=16] {'tensor'}, dimensions={2}, use_global_device_ids=true | all-gather | bytes 365568 | tf_op jit(solution)/shard_map/all_gather | solution.py:68
  348.0 0.0 copy-done.3
  348.0 0.0 copy-done.6
  348.0 5.1 %fusion = bf16[1,3,256,896]{3,2,1,0:T(8,128)(2,1)} fusion(f32[3,32,256]{2,1,0:T(8,128)S(1)} %fusion.9, f32[3,32,896]{1,0,2:T(4,128)S(1)} %all_gather.15, bf16[1,3,256,896]{3,2,1,0:T(8,128)(2,1)S(1)} %copy-done.6, f32[1,256,896]{2,1,0:T(8,128)} %copy-done.7, f32[1,256,896]{2,1,0:T(8,128)S(1)} %convolution_bitcast_fusion.1, f32[1,256,896]{2,1,0:T(8,128)S(1)} %copy-done.3), kind=kOutput, calls=%fused_computation.4 | convolution fusion | flops 268369920 | bytes 5947392 | tf_op jit(solution)/shard_map/krh,krd->khd/dot_general | solution.py:69
  (12 shorter events, 0.1 us)
Async XLA Ops:
  7.2 55.6 %copy-start = (bf16[256,896]{1,0:T(8,128)(2,1)S(1)}, bf16[256,896]{1,0:T(8,128)(2,1)}, u32[]{:S(2)}) copy-start(bf16[256,896]{1,0:T(8,128)(2,1)} %param.9) | copy-start | bytes 1376260
  7.2 55.6 %all-gather.5.cloned.1.call-start = ((), (), s32[]{:S(2)}) async-start(), calls=%async_computation.3 | async-start | bytes 1949696 | tf_op jit(solution)/shard_map/all_gather | solution.py:29
  7.9 106.1 %all-gather.3.cloned.1.call-start = ((), (), s32[]{:S(2)}) async-start(), calls=%async_computation.2 | async-start | bytes 1949696 | tf_op jit(solution)/shard_map/all_gather | solution.py:30
  8.7 344.4 %reduce-scatter.4.cloned.1.call-start = ((), (), s32[]{:S(2)}) async-start(), calls=%async_computation.4 | async-start | bytes 1949696
  36.1 30.0 %copy-start.13 = (bf16[256,896]{1,0:T(8,128)(2,1)S(1)}, bf16[256,896]{1,0:T(8,128)(2,1)}, u32[]{:S(2)}) copy-start(bf16[256,896]{1,0:T(8,128)(2,1)} %param.10) | copy-start | bytes 1376260
  62.8 3.4 copy-start.1
  66.1 47.9 %copy-start.15 = (bf16[256,896]{1,0:T(8,128)(2,1)S(1)}, bf16[256,896]{1,0:T(8,128)(2,1)}, u32[]{:S(2)}) copy-start(bf16[256,896]{1,0:T(8,128)(2,1)} %param.11) | copy-start | bytes 1376260
  117.0 0.8 copy-start.10
  117.1 1.0 copy-start.12
  120.0 2.0 copy-start.11
  120.0 2.8 copy-start.14
  122.0 1.2 copy-start.8
  122.0 1.5 copy-start.9
  123.5 0.9 copy-start.2
  123.5 1.9 copy-start.4
  123.5 2.6 copy-start.5
  124.5 0.9 copy-start.7
  265.5 82.4 %copy-start.3 = (f32[1,256,896]{2,1,0:T(8,128)S(1)}, f32[1,256,896]{2,1,0:T(8,128)}, u32[]{:S(2)}) copy-start(f32[1,256,896]{2,1,0:T(8,128)} %copy-done.2) | copy-start | bytes 2752516
  328.3 19.6 %copy-start.6 = (bf16[1,3,256,896]{3,2,1,0:T(8,128)(2,1)S(1)}, bf16[1,3,256,896]{3,2,1,0:T(8,128)(2,1)}, u32[]{:S(2)}) copy-start(bf16[1,3,256,896]{3,2,1,0:T(8,128)(2,1)} %param.12) | copy-start | bytes 4128772
Sparse Core Ops, SparseCore 0:
  10.4 52.2 all-gather.4
  65.2 48.7 all-gather.2
  120.1 77.9 reduce-scatter.3
where the time goes:
time: 366 us; the launch traced here: 360 us
  blocking collectives  222 us (61%)
  waiting for transfers between devices  74.2 us (20%)
  matrix products  25.8 us (7%)
  other arithmetic  17 us (5%)
  between operations  14 us (4%)
  local copies, waits for them, and re-layouts  6.74 us (2%)
    psum x1, blocking collectives, per_device(): q_out = lax.psum(owned, 'dp') / n_workers  61.5 us
    psum x1, blocking collectives, per_device(): gram_matrix = lax.psum(gram_part, 'tensor')  58.1 us
    psum x1, blocking collectives, per_device(): lax.psum(p_local.astype(jnp.bfloat16), 'dp').astype(jnp.float32) / n_workers  46.5 us
    all_gather x1, waiting for transfers between devices, per_device(): lax.all_gather(out_grad, 'tensor', axis=1, tiled=True)  46.1 us
    all_gather x1, waiting for transfers between devices, per_device(): lax.all_gather(hidden_in, 'tensor', axis=1, tiled=True)  26.7 us
    all_gather x1, blocking collectives, per_device(): q_full = lax.all_gather(q_init, 'tensor', axis=2, tiled=True)  26.4 us
    all_gather x1, blocking collectives, per_device(): q_new = lax.all_gather(q_out, 'tensor', axis=2, tiled=True)  19.6 us
    all_to_all x1, blocking collectives, per_device(): lax.all_to_all(q_part.astype(jnp.bfloat16), 'tensor', split_axis=2, conca...  9.65 us
  transfers between devices with their start and end apart: 3, of which 2 were waited for; matrix products, arithmetic and copies ran while one was open for 11% of the time, Pallas kernels for 0%

commit v1 on v0

v1 whole, which is shorter than its diff:
```python
import jax
import jax.numpy as jnp
from jax import lax
from jax.experimental import pallas as pl
from jax.experimental.pallas import tpu as pltpu
from jax.sharding import PartitionSpec as P

BF = jnp.bfloat16
F32 = jnp.float32
HIGHEST = lax.Precision.HIGHEST
SIDE = 4
DEPTH = 8


def x_ring(k):
    return [(y * SIDE + x, y * SIDE + (x + k) % SIDE) for y in range(SIDE) for x in range(SIDE)]


def y_ring(k):
    return [(y * SIDE + x, ((y + k) % SIDE) * SIDE + x) for y in range(SIDE) for x in range(SIDE)]


CORE_PAIR = [(i, i ^ 1) for i in range(2 * DEPTH)]
Z_GROUPS = [[z * 2 + c for z in range(DEPTH)] for c in range(2)]


def gather_pair(a, b, x, y):
    a_near = [a] + [None] * 3
    b_near = [b] + [None] * 3
    for k in (1, 3, 2):
        a_near[k] = lax.ppermute(a, "tensor", x_ring(k))
        b_near[k] = lax.ppermute(b, "tensor", y_ring(k))
    a_row = jnp.stack([lax.dynamic_index_in_dim(jnp.stack(a_near), (x - i) % SIDE, 0, False) for i in range(SIDE)])
    b_row = jnp.stack([lax.dynamic_index_in_dim(jnp.stack(b_near), (y - i) % SIDE, 0, False) for i in range(SIDE)])
    a_far = [a_row] + [None] * 3
    b_far = [b_row] + [None] * 3
    for k in (1, 3, 2):
        a_far[k] = lax.ppermute(a_row, "tensor", y_ring(k))
        b_far[k] = lax.ppermute(b_row, "tensor", x_ring(k))
    a_all = jnp.stack([lax.dynamic_index_in_dim(jnp.stack(a_far), (y - i) % SIDE, 0, False) for i in range(SIDE)])
    b_all = jnp.stack(
        [lax.dynamic_index_in_dim(jnp.stack(b_far), (x - i) % SIDE, 0, False) for i in range(SIDE)], axis=1
    )
    rows = a.shape[0] * SIDE * SIDE
    return a_all.reshape(rows, -1), b_all.reshape(rows, -1)


def chol_inverse_kernel(gram_ref, out_ref):
    n = gram_ref.shape[-1]
    gram = gram_ref[...]
    rows = lax.broadcasted_iota(jnp.int32, (1, n, n), 1)
    cols = lax.broadcasted_iota(jnp.int32, (1, n, n), 2)
    eye = jnp.broadcast_to(jnp.where(rows == cols, 1.0, 0.0), gram.shape)
    work = jnp.concatenate([gram, eye], axis=2)
    below = lax.broadcasted_iota(jnp.int32, (1, n, 1), 1)
    for k in range(n):
        pivot = work[:, k : k + 1, :]
        scale = 1.0 / pivot[:, :, k : k + 1]
        factor = jnp.where(below > k, work[:, :, k : k + 1] * scale, 0.0)
        work = work - factor * pivot
    diag = jnp.sum(jnp.where(rows == cols, work[:, :, :n], 0.0), axis=2, keepdims=True)
    out_ref[...] = work[:, :, n:] * lax.rsqrt(diag)


def chol_inverse(gram):
    return pl.pallas_call(
        chol_inverse_kernel,
        out_shape=jax.ShapeDtypeStruct(gram.shape, F32),
        in_specs=[pl.BlockSpec(memory_space=pltpu.VMEM)],
        out_specs=pl.BlockSpec(memory_space=pltpu.VMEM),
    )(gram)


def dot(a, b, ca, cb, precision=None):
    return lax.dot_general(a, b, (((ca,), (cb,)), ((), ())), precision=precision, preferred_element_type=F32)


def sum_pair(value):
    return value + lax.ppermute(value, "dp", CORE_PAIR)


def join_halves(half, core):
    other = lax.ppermute(half, "dp", CORE_PAIR)
    return jnp.where(core == 0, jnp.concatenate([half, other]), jnp.concatenate([other, half]))


def sum_z(value):
    spread = jnp.broadcast_to(value[None], (DEPTH,) + value.shape)
    return jnp.sum(
        lax.all_to_all(spread, "dp", 0, 0, tiled=True, axis_index_groups=Z_GROUPS).astype(F32), axis=0
    )


def per_device(hidden_in, out_grad, w_gate, w_up, w_down, error_in, q_init):
    n_workers = lax.axis_size("dp")
    n_tensor = lax.axis_size("tensor")
    me = lax.axis_index("tensor")
    y, x = me // SIDE, me % SIDE
    core = lax.axis_index("dp") % 2
    rank = q_init.shape[1]
    shard = hidden_in.shape[1]
    width = shard * n_tensor
    n_rows = 3 * rank
    half_rows = n_rows // 2

    x_all, dy_all = gather_pair(hidden_in.T, out_grad.T, x, y)
    q_cols = q_init.reshape(n_rows, shard).T
    q_all = lax.all_to_all(
        jnp.broadcast_to(q_cols[None], (n_tensor,) + q_cols.shape), "tensor", 0, 0, tiled=True
    ).reshape(width, n_rows)

    gate_pre = dot(w_gate, x_all, 1, 0)
    up_pre = dot(w_up, x_all, 1, 0)
    gate_sig = jax.nn.sigmoid(gate_pre)
    gate_act = gate_pre * gate_sig
    hidden = (gate_act * up_pre).astype(BF)
    hidden_grad = dot(w_down, dy_all, 1, 0)
    gate_grad = (hidden_grad * up_pre * gate_sig * (1.0 + gate_pre * (1.0 - gate_sig))).astype(BF)
    up_grad = (hidden_grad * gate_act).astype(BF)
    term = (dot(w_gate, gate_grad, 0, 0) + dot(w_up, up_grad, 0, 0)).astype(BF)
    input_grad = lax.psum_scatter(term, "tensor", scatter_dimension=0, tiled=True).T

    matrices = [dot(gate_grad, x_all, 1, 1), dot(up_grad, x_all, 1, 1), dot(hidden, dy_all, 1, 1)]
    matrices = [m + error_in[0, k].astype(F32) for k, m in enumerate(matrices)]

    p_local = jnp.concatenate(
        [dot(q_all[:, k * rank : (k + 1) * rank], m, 0, 1, HIGHEST) for k, m in enumerate(matrices)]
    )
    p_pair = sum_pair(p_local.astype(BF).astype(F32))
    p_half = lax.dynamic_slice_in_dim(p_pair, core * half_rows, half_rows, 0)
    p_trans = join_halves(sum_z(p_half.astype(BF)), core) / n_workers

    s_rows = []
    for k, m in enumerate(matrices):
        p_k = p_trans[k * rank : (k + 1) * rank]
        s_rows.append(
            jnp.concatenate(
                [dot(p_k, m, 1, 0, HIGHEST), dot(p_k, p_k, 1, 1, HIGHEST), jnp.zeros((rank, 96), F32)], axis=1
            )
        )
    s_local = jnp.concatenate(s_rows)
    s_pair = lax.dynamic_slice_in_dim(s_local, core * half_rows, half_rows, 0) + lax.ppermute(
        lax.dynamic_slice_in_dim(s_local, (1 - core) * half_rows, half_rows, 0), "dp", CORE_PAIR
    )
    s_split = s_pair.reshape(n_tensor, -1, 128)
    s_mine = jnp.sum(lax.all_to_all(s_split, "tensor", 0, 0, tiled=True), axis=0)
    s_mine = sum_z(s_mine)
    s_half = lax.all_to_all(
        jnp.broadcast_to(s_mine[None], (n_tensor,) + s_mine.shape), "tensor", 0, 0, tiled=True
    ).reshape(s_pair.shape)
    s_all = join_halves(s_half, core).reshape(3, rank, -1) / n_workers

    inverse = chol_inverse(s_all[:, :, width : width + rank])
    q_new = jnp.einsum("krs,ksd->krd", inverse, s_all[:, :, :width], precision=HIGHEST)
    p_ortho = jnp.einsum("krs,ksh->krh", inverse, p_trans.reshape(3, rank, -1), precision=HIGHEST)
    error_out = jnp.stack([m - dot(p_ortho[k], q_new[k], 0, 0, HIGHEST) for k, m in enumerate(matrices)])
    q_out = lax.dynamic_slice_in_dim(q_new, me * shard, shard, 2)
    return (input_grad, error_out[None].astype(BF), q_out)


def solution(mesh):
    in_specs = (
        P("dp", "tensor"),
        P("dp", "tensor"),
        P("tensor", None),
        P("tensor", None),
        P("tensor", None),
        P("dp", None, "tensor", None),
        P(None, None, "tensor"),
    )
    out_specs = (P("dp", "tensor"), P("dp", None, "tensor", None), P(None, None, "tensor"))
    return jax.shard_map(
        per_device, mesh=mesh, in_specs=in_specs, out_specs=out_specs, check_vma=False
    )
```

time: 366 us -> 222 us (0.61); the launches traced: 360 us -> 221 us
  blocking collectives: 222 us -> 27.6 us
  starting transfers between devices: 0.11 us -> 49.4 us
  other arithmetic: 17 us -> 7.33 us
  waiting for transfers between devices: 74.2 us -> 81.3 us
  Pallas kernels: 0 us -> 4.2 us
    psum x3 -> x0, blocking collectives: 166 us -> none  [the longest x1 61.5 us: per_device(): q_out = lax.psum(owned, 'dp') / n_workers]
    all_gather x2 -> x0, waiting for transfers between devices: 72.8 us -> none  [the longest x1 46.1 us: per_device(): lax.all_gather(out_grad, 'tensor', axis=1, tiled=True)]
    unnamed x4 -> x2, waiting for transfers between devices: 1.39 us -> 62.1 us
    all_gather x2 -> x0, blocking collectives: 46.1 us -> none  [the longest x1 26.4 us: per_device(): q_full = lax.all_gather(q_init, 'tensor', axis=2, tiled=True)]
    ppermute x0 -> x16, starting transfers between devices: none -> 33.4 us  [the longest x2 7.95 us: join_halves(): other = lax.ppermute(half, 'dp', CORE_PAIR)]
    all_to_all x1 -> x2, blocking collectives: 9.65 us -> 27.6 us  [the longest x1 17.4 us: sum_z(): lax.all_to_all(spread, 'dp', 0, 0, tiled=True, axis_index_groups=Z_GROUPS)]
    all_to_all x0 -> x3, starting transfers between devices: none -> 16 us  [the longest x1 7.13 us: per_device(): lax.all_to_all(jnp.broadcast_to(q_cols[None], (n_tensor,) + q_cols.shape)...]
    ppermute x0 -> x16, waiting for transfers between devices: none -> 12.3 us  [the longest x3 9.02 us: gather_pair(): a_far[k] = lax.ppermute(a_row, 'tensor', y_ring(k))]
  transfers between devices with their start and end apart: 3 -> 20, of which waited for: 2 -> 9; matrix products, arithmetic and copies ran while one was open for 11% -> 13% of each run, Pallas kernels for 0% -> 2%
where the time goes in v1:
time: 222 us; the launch traced here: 221 us
  waiting for transfers between devices  81.3 us (37%)
  starting transfers between devices  49.4 us (22%)
  blocking collectives  27.6 us (12%)
  matrix products  26.3 us (12%)
  between operations  15.1 us (7%)
  local copies, waits for them, and re-layouts  9.9 us (4%)
  other arithmetic  7.33 us (3%)
  Pallas kernels  4.2 us (2%)
    unnamed x2, waiting for transfers between devices  62.1 us
    dot_general x20, matrix products, dot(): lax.dot_general(a, b, (((ca,), (cb,)), ((), ())), precision=precision, pr...  23.9 us
    all_to_all x1, blocking collectives, sum_z(): lax.all_to_all(spread, 'dp', 0, 0, tiled=True, axis_index_groups=Z_GROUPS)  17.4 us
    all_to_all x1, blocking collectives, per_device(): lax.all_to_all(jnp.broadcast_to(s_mine[None], (n_tensor,) + s_mine.shape)...  10.1 us
    ppermute x3, waiting for transfers between devices, gather_pair(): a_far[k] = lax.ppermute(a_row, 'tensor', y_ring(k))  9.02 us
    ppermute x2, starting transfers between devices, join_halves(): other = lax.ppermute(half, 'dp', CORE_PAIR)  7.95 us
    all_to_all x1, starting transfers between devices, per_device(): lax.all_to_all(jnp.broadcast_to(q_cols[None], (n_tensor,) + q_cols.shape)...  7.13 us
    ppermute x1, starting transfers between devices, sum_pair(): return value + lax.ppermute(value, 'dp', CORE_PAIR)  6.82 us
  transfers between devices with their start and end apart: 20, of which 9 were waited for; matrix products, arithmetic and copies ran while one was open for 13% of the time, Pallas kernels for 2%

profile of v1, /device:TPU:1, one launch (start us, length us, event | category | flops | bytes accessed | tf_op | source)
XLA Modules:
  0.0 221.1 jit_solution(10267213336781235098)
XLA Ops:
  7.2 3.7 %collective-permute-start.7 = (bf16[56,1024]{1,0:T(8,128)(2,1)}, bf16[56,1024]{1,0:T(8,128)(2,1)S(1)}, u32[]{:S(2)}, u32[]{:S(2)}) collective-permute-start(bf16[56,1024]{1,0:T(8,128)(2,1)} %bitcast.127), channel_id=1, source_target_pairs={{0,2},{1,3},{2,0},{3,1},{4,6},{5,7},{6,4},{7,5},{8,10},{9,11},{10,... | collective-permute-start | bytes 344072 | tf_op jit(solution)/shard_map/ppermute | solution.py:31
  11.2 2.4 %collective-permute-start.8 = (bf16[56,1024]{1,0:T(8,128)(2,1)}, bf16[56,1024]{1,0:T(8,128)(2,1)S(1)}, u32[]{:S(2)}, u32[]{:S(2)}) collective-permute-start(bf16[56,1024]{1,0:T(8,128)(2,1)} %bitcast.129), channel_id=1, source_target_pairs={{0,3},{1,0},{2,1},{3,2},{4,7},{5,4},{6,5},{7,6},{8,11},{9,8},{10,9... | collective-permute-start | bytes 344072 | tf_op jit(solution)/shard_map/ppermute | solution.py:31
  13.5 2.9 %collective-permute-start.1 = (bf16[56,1024]{1,0:T(8,128)(2,1)}, bf16[56,1024]{1,0:T(8,128)(2,1)S(1)}, u32[]{:S(2)}, u32[]{:S(2)}) collective-permute-start(bf16[56,1024]{1,0:T(8,128)(2,1)} %bitcast.131), channel_id=1, source_target_pairs={{0,8},{1,9},{2,10},{3,11},{4,12},{5,13},{6,14},{7,15},{8,0},{9,1},... | collective-permute-start | bytes 344072 | tf_op jit(solution)/shard_map/ppermute | solution.py:32
  16.4 0.4 collective-permute-start
  16.8 2.3 %collective-permute-start.2 = (bf16[56,1024]{1,0:T(8,128)(2,1)}, bf16[56,1024]{1,0:T(8,128)(2,1)S(1)}, u32[]{:S(2)}, u32[]{:S(2)}) collective-permute-start(bf16[56,1024]{1,0:T(8,128)(2,1)} %bitcast.133), channel_id=1, source_target_pairs={{0,12},{1,13},{2,14},{3,15},{4,0},{5,1},{6,2},{7,3},{8,4},{9,5},{1... | collective-permute-start | bytes 344072 | tf_op jit(solution)/shard_map/ppermute | solution.py:32
  19.1 1.0 pad_maximum_fusion.7
  20.1 0.8 fusion.33
  21.0 0.4 collective-permute-start.10
  21.4 0.4 collective-permute-start.9
  21.8 2.3 %collective-permute-start.11 = (bf16[4,56,1024]{2,1,0:T(8,128)(2,1)}, bf16[4,56,1024]{2,1,0:T(8,128)(2,1)S(1)}, u32[]{:S(2)}, u32[]{:S(2)}) collective-permute-start(bf16[4,56,1024]{2,1,0:T(8,128)(2,1)} %get-tuple-element.32), channel_id=1, source_target_pairs={{0,12},{1,13},{2,14},{3,15},{4,0},{5,1},{6,2},{7,3},{8,4},{9,5},{1... | collective-permute-start | bytes 1376264 | tf_op jit(solution)/shard_map/ppermute | solution.py:38
  24.3 0.9 fusion.34
  25.1 1.7 collective-permute-start.4
  26.9 1.2 collective-permute-start.3
  28.0 4.4 %collective-permute-done.10 = bf16[4,56,1024]{2,1,0:T(8,128)(2,1)S(1)} collective-permute-done((bf16[4,56,1024]{2,1,0:T(8,128)(2,1)}, bf16[4,56,1024]{2,1,0:T(8,128)(2,1)S(1)}, u32[]{:S(2)}, u32[]{:S(2)}) %collective-permute-start.10) | collective-permute-done | bytes 458784 | tf_op jit(solution)/shard_map/ppermute | solution.py:38
  32.5 0.8 broadcast_in_dim.8
  33.3 7.1 %all-to-all-start = ((f32[16,56,96]{2,1,0:T(8,128)}), f32[16,56,96]{2,1,0:T(8,128)}, u32[]{:S(2)}, u32[]{:S(2)}) async-start(f32[16,56,96]{2,1,0:T(8,128)} %broadcast_in_dim.8), calls=%async_computation | async-start | bytes 917504 | tf_op jit(solution)/shard_map/all_to_all | solution.py:108
  40.5 4.6 %collective-permute-done.9 = bf16[4,56,1024]{2,1,0:T(8,128)(2,1)S(1)} collective-permute-done((bf16[4,56,1024]{2,1,0:T(8,128)(2,1)}, bf16[4,56,1024]{2,1,0:T(8,128)(2,1)S(1)}, u32[]{:S(2)}, u32[]{:S(2)}) %collective-permute-start.9) | collective-permute-done | bytes 458784 | tf_op jit(solution)/shard_map/ppermute | solution.py:38
  45.9 1.4 pad_maximum_fusion
  47.8 0.8 convolution_bitcast_fusion
  48.8 0.8 convolution_bitcast_fusion.1
  49.9 1.1 copy-done.5
  50.9 0.8 convolution_add_fusion
  52.0 1.0 multiply_convert_fusion.1
  53.0 0.8 convolution_add_fusion.1
  53.9 0.8 convolution_add_fusion.2
  54.7 2.1 fusion.9
  56.9 1.9 fusion.7
  58.8 2.1 fusion.8
  61.0 6.8 %collective-permute-start.12 = (f32[96,256]{1,0:T(8,128)S(1)}, f32[96,256]{1,0:T(8,128)S(1)}, u32[]{:S(2)}, u32[]{:S(2)}) collective-permute-start(f32[96,256]{1,0:T(8,128)S(1)} %maximum_convert_fusion), channel_id=1, source_target_pairs={{0,16},{16,0},{32,48},{48,32},{64,80},{80,64},{96,112},{112,96},{1... | collective-permute-start | bytes 294920 | tf_op jit(solution)/shard_map/ppermute | solution.py:79
  67.8 0.9 collective-permute-done.12
  68.8 17.4 %all_to_all.25 = bf16[8,48,256]{2,1,0:T(8,128)(2,1)S(1)} all-to-all(bf16[8,48,256]{2,1,0:T(8,128)(2,1)S(1)} %broadcast_in_dim.9), channel_id=1, replica_groups={{0,32,64,96,128,160,192,224},{16,48,80,112,144,176,208,240},{1,33,65,97..., dimensions={0} | all-to-all | bytes 393216 | tf_op jit(solution)/shard_map/all_to_all | solution.py:90
  86.2 2.1 collective-permute-start.13
  88.3 0.9 collective-permute-done.13
  89.7 0.6 fusion.22
  90.3 0.6 fusion.26
  90.8 0.6 fusion.30
  91.5 0.7 collective-permute-start.14
  92.2 1.1 collective-permute-done.14
  93.3 0.7 reshape.105
  94.0 5.5 %all-to-all-start.2 = ((f32[16,24,128]{2,1,0:T(8,128)}), f32[16,24,128]{2,1,0:T(8,128)S(1)}, u32[]{:S(2)}, u32[]{:S(2)}) async-start(f32[16,24,128]{2,1,0:T(8,128)} %reshape.105), calls=%async_computation.2 | async-start | bytes 393216 | tf_op jit(solution)/shard_map/all_to_all | solution.py:146
  99.5 3.5 %fusion.35 = f32[1024,896]{1,0:T(8,128)} fusion(bf16[256,1024]{0,1:T(8,128)(2,1)} %copy-done.2, bf16[256,896]{1,0:T(8,128)(2,1)S(1)} %copy-done), kind=kOutput, calls=%fused_computation.92 | convolution fusion | flops 469762048 | bytes 4653056 | tf_op jit(solution)/shard_map/dot_general | solution.py:75
  103.1 3.7 %all-to-all-done.2 = f32[16,24,128]{2,1,0:T(8,128)S(1)} async-done(((f32[16,24,128]{2,1,0:T(8,128)}), f32[16,24,128]{2,1,0:T(8,128)S(1)}, u32[]{:S(2)}, u32[]{:S(2)}) %all-to-all-start.2) | async-done | bytes 196640 | tf_op jit(solution)/shard_map/all_to_all | solution.py:146
  106.8 0.6 broadcast_in_dim.10
  107.4 3.4 %all-to-all-start.3 = ((f32[8,24,128]{2,1,0:T(8,128)}), f32[8,24,128]{2,1,0:T(8,128)S(1)}, u32[]{:S(2)}, u32[]{:S(2)}) async-start(f32[8,24,128]{2,1,0:T(8,128)} %broadcast_in_dim.10), calls=%async_computation.3 | async-start | bytes 196608 | tf_op jit(solution)/shard_map/all_to_all | solution.py:90
  110.8 4.3 %fusion = bf16[896,1024]{0,1:T(8,128)(2,1)} fusion(f32[1024,896]{1,0:T(8,128)} %fusion.35, bf16[256,1024]{0,1:T(8,128)(2,1)} %copy-done.1, bf16[256,896]{1,0:T(8,128)(2,1)} %param.10), kind=kOutput, calls=%fused_computation.5 | convolution fusion | flops 471597056 | bytes 6488064 | tf_op jit(solution)/shard_map/dot_general | solution.py:75
  115.2 3.2 %all-to-all-done.3 = f32[8,24,128]{2,1,0:T(8,128)S(1)} async-done(((f32[8,24,128]{2,1,0:T(8,128)}), f32[8,24,128]{2,1,0:T(8,128)S(1)}, u32[]{:S(2)}, u32[]{:S(2)}) %all-to-all-start.3) | async-done | bytes 98336 | tf_op jit(solution)/shard_map/all_to_all | solution.py:90
  118.4 10.1 %all_to_all.26 = f32[16,24,128]{2,1,0:T(8,128)S(1)} all-to-all(f32[16,24,128]{2,1,0:T(8,128)S(1)} %broadcast_in_dim.11), channel_id=1, replica_groups=mesh['dp'=16,'tensor'=16] {'tensor'}, dimensions={0} | all-to-all | bytes 393216 | tf_op jit(solution)/shard_map/all_to_all | solution.py:148
  128.5 0.7 reshape.106
  129.2 5.9 %collective-permute-start.15 = (f32[48,1024]{1,0:T(8,128)}, f32[48,1024]{1,0:T(8,128)S(1)}, u32[]{:S(2)}, u32[]{:S(2)}) collective-permute-start(f32[48,1024]{1,0:T(8,128)} %reshape.106), channel_id=1, source_target_pairs={{0,16},{16,0},{32,48},{48,32},{64,80},{80,64},{96,112},{112,96},{1... | collective-permute-start | bytes 589832 | tf_op jit(solution)/shard_map/ppermute | solution.py:83
  135.1 0.6 dynamic-slice
  136.4 1.1 fusion.14
  137.5 0.7 copy-done.4
  138.2 0.6 slice.74.gram_ref
  138.8 4.2 %shard_map.94 = f32[3,32,32]{2,1,0:T(8,128)} custom-call(f32[3,32,32]{2,1,0:T(8,128)} %slice.74.gram_ref), custom_call_target="tpu_custom_call" | custom-call | tf_op jit(solution)/shard_map/pallas_call | solution.py:66
  143.0 1.4 fusion.15
  144.4 0.7 constant_dynamic-slice_fusion
  145.2 1.0 fusion.36
  146.2 0.9 fusion.4
  147.1 0.9 fusion.5
  148.1 0.9 fusion.6
  149.0 1.3 pad_maximum_fusion.4
  150.3 62.1 %all-reduce.3.cloned.1.call-done = bf16[896,1024]{0,1:T(8,128)(2,1)} async-done(((bf16[896,1024]{0,1:T(8,128)(2,1)}), bf16[896,1024]{0,1:T(8,128)(2,1)}) %all-reduce.3.cloned.1.call-update) | async-done | bytes 1835024
  212.3 1.2 dynamic-slice_bitcast_fusion.4
  213.5 0.8 copy.17
  (58 shorter events, 3.5 us)
Async XLA Ops:
  7.2 40.6 %copy-start = (bf16[256,896]{1,0:T(8,128)(2,1)S(1)}, bf16[256,896]{1,0:T(8,128)(2,1)}, u32[]{:S(2)}) copy-start(bf16[256,896]{1,0:T(8,128)(2,1)} %param.9) | copy-start | bytes 1376260
  7.2 16.9 %copy-start.6 = (bf16[1024,56]{0,1:T(8,128)(2,1)S(1)}, bf16[1024,56]{0,1:T(8,128)(2,1)}, u32[]{:S(2)}) copy-start(bf16[1024,56]{0,1:T(8,128)(2,1)} %param.8) | copy-start | bytes 344068
  7.2 9.7 %collective-permute-start.7 = (bf16[56,1024]{1,0:T(8,128)(2,1)}, bf16[56,1024]{1,0:T(8,128)(2,1)S(1)}, u32[]{:S(2)}, u32[]{:S(2)}) collective-permute-start(bf16[56,1024]{1,0:T(8,128)(2,1)} %bitcast.127), channel_id=1, source_target_pairs={{0,2},{1,3},{2,0},{3,1},{4,6},{5,7},{6,4},{7,5},{8,10},{9,11},{10,... | collective-permute-start | bytes 344072 | tf_op jit(solution)/shard_map/ppermute | solution.py:31
  10.8 8.3 %collective-permute-start.6 = (bf16[56,1024]{1,0:T(8,128)(2,1)}, bf16[56,1024]{1,0:T(8,128)(2,1)S(1)}, u32[]{:S(2)}, u32[]{:S(2)}) collective-permute-start(bf16[56,1024]{1,0:T(8,128)(2,1)} %bitcast.128), channel_id=1, source_target_pairs={{0,1},{1,2},{2,3},{3,0},{4,5},{5,6},{6,7},{7,4},{8,9},{9,10},{10,1... | collective-permute-start | bytes 344072 | tf_op jit(solution)/shard_map/ppermute | solution.py:31
  11.2 8.0 %collective-permute-start.8 = (bf16[56,1024]{1,0:T(8,128)(2,1)}, bf16[56,1024]{1,0:T(8,128)(2,1)S(1)}, u32[]{:S(2)}, u32[]{:S(2)}) collective-permute-start(bf16[56,1024]{1,0:T(8,128)(2,1)} %bitcast.129), channel_id=1, source_target_pairs={{0,3},{1,0},{2,1},{3,2},{4,7},{5,4},{6,5},{7,6},{8,11},{9,8},{10,9... | collective-permute-start | bytes 344072 | tf_op jit(solution)/shard_map/ppermute | solution.py:31
  13.5 8.3 %collective-permute-start.1 = (bf16[56,1024]{1,0:T(8,128)(2,1)}, bf16[56,1024]{1,0:T(8,128)(2,1)S(1)}, u32[]{:S(2)}, u32[]{:S(2)}) collective-permute-start(bf16[56,1024]{1,0:T(8,128)(2,1)} %bitcast.131), channel_id=1, source_target_pairs={{0,8},{1,9},{2,10},{3,11},{4,12},{5,13},{6,14},{7,15},{8,0},{9,1},... | collective-permute-start | bytes 344072 | tf_op jit(solution)/shard_map/ppermute | solution.py:32
  16.4 7.7 %collective-permute-start = (bf16[56,1024]{1,0:T(8,128)(2,1)}, bf16[56,1024]{1,0:T(8,128)(2,1)S(1)}, u32[]{:S(2)}, u32[]{:S(2)}) collective-permute-start(bf16[56,1024]{1,0:T(8,128)(2,1)} %bitcast.132), channel_id=1, source_target_pairs={{0,4},{1,5},{2,6},{3,7},{4,8},{5,9},{6,10},{7,11},{8,12},{9,13},{1... | collective-permute-start | bytes 344072 | tf_op jit(solution)/shard_map/ppermute | solution.py:32
  16.8 7.3 %collective-permute-start.2 = (bf16[56,1024]{1,0:T(8,128)(2,1)}, bf16[56,1024]{1,0:T(8,128)(2,1)S(1)}, u32[]{:S(2)}, u32[]{:S(2)}) collective-permute-start(bf16[56,1024]{1,0:T(8,128)(2,1)} %bitcast.133), channel_id=1, source_target_pairs={{0,12},{1,13},{2,14},{3,15},{4,0},{5,1},{6,2},{7,3},{8,4},{9,5},{1... | collective-permute-start | bytes 344072 | tf_op jit(solution)/shard_map/ppermute | solution.py:32
  21.0 11.5 %copy-start.7 = (f32[3,32,56]{2,1,0:T(8,128)S(1)}, f32[3,32,56]{2,1,0:T(8,128)}, u32[]{:S(2)}) copy-start(f32[3,32,56]{2,1,0:T(8,128)} %param.13) | copy-start | bytes 64516
  21.0 11.5 %collective-permute-start.10 = (bf16[4,56,1024]{2,1,0:T(8,128)(2,1)}, bf16[4,56,1024]{2,1,0:T(8,128)(2,1)S(1)}, u32[]{:S(2)}, u32[]{:S(2)}) collective-permute-start(bf16[4,56,1024]{2,1,0:T(8,128)(2,1)} %get-tuple-element.32), channel_id=1, source_target_pairs={{0,8},{1,9},{2,10},{3,11},{4,12},{5,13},{6,14},{7,15},{8,0},{9,1},... | collective-permute-start | bytes 1376264 | tf_op jit(solution)/shard_map/ppermute | solution.py:38
  21.4 23.6 %collective-permute-start.9 = (bf16[4,56,1024]{2,1,0:T(8,128)(2,1)}, bf16[4,56,1024]{2,1,0:T(8,128)(2,1)S(1)}, u32[]{:S(2)}, u32[]{:S(2)}) collective-permute-start(bf16[4,56,1024]{2,1,0:T(8,128)(2,1)} %get-tuple-element.32), channel_id=1, source_target_pairs={{0,4},{1,5},{2,6},{3,7},{4,8},{5,9},{6,10},{7,11},{8,12},{9,13},{1... | collective-permute-start | bytes 1376264 | tf_op jit(solution)/shard_map/ppermute | solution.py:38
  21.8 23.2 %collective-permute-start.11 = (bf16[4,56,1024]{2,1,0:T(8,128)(2,1)}, bf16[4,56,1024]{2,1,0:T(8,128)(2,1)S(1)}, u32[]{:S(2)}, u32[]{:S(2)}) collective-permute-start(bf16[4,56,1024]{2,1,0:T(8,128)(2,1)} %get-tuple-element.32), channel_id=1, source_target_pairs={{0,12},{1,13},{2,14},{3,15},{4,0},{5,1},{6,2},{7,3},{8,4},{9,5},{1... | collective-permute-start | bytes 1376264 | tf_op jit(solution)/shard_map/ppermute | solution.py:38
  25.1 20.4 %collective-permute-start.4 = (bf16[4,56,1024]{2,1,0:T(8,128)(2,1)}, bf16[4,56,1024]{2,1,0:T(8,128)(2,1)S(1)}, u32[]{:S(2)}, u32[]{:S(2)}) collective-permute-start(bf16[4,56,1024]{2,1,0:T(8,128)(2,1)} %get-tuple-element.26), channel_id=1, source_target_pairs={{0,2},{1,3},{2,0},{3,1},{4,6},{5,7},{6,4},{7,5},{8,10},{9,11},{10,... | collective-permute-start | bytes 1376264 | tf_op jit(solution)/shard_map/ppermute | solution.py:39
  26.9 18.7 %collective-permute-start.3 = (bf16[4,56,1024]{2,1,0:T(8,128)(2,1)}, bf16[4,56,1024]{2,1,0:T(8,128)(2,1)}, u32[]{:S(2)}, u32[]{:S(2)}) collective-permute-start(bf16[4,56,1024]{2,1,0:T(8,128)(2,1)} %get-tuple-element.26), channel_id=1, source_target_pairs={{0,1},{1,2},{2,3},{3,0},{4,5},{5,6},{6,7},{7,4},{8,9},{9,10},{10,1... | collective-permute-start | bytes 1376264 | tf_op jit(solution)/shard_map/ppermute | solution.py:39
  32.4 13.5 %collective-permute-start.5 = (bf16[4,56,1024]{2,1,0:T(8,128)(2,1)}, bf16[4,56,1024]{2,1,0:T(8,128)(2,1)}, u32[]{:S(2)}, u32[]{:S(2)}) collective-permute-start(bf16[4,56,1024]{2,1,0:T(8,128)(2,1)} %get-tuple-element.26), channel_id=1, source_target_pairs={{0,3},{1,0},{2,1},{3,2},{4,7},{5,4},{6,5},{7,6},{8,11},{9,8},{10,9... | collective-permute-start | bytes 1376264 | tf_op jit(solution)/shard_map/ppermute | solution.py:39
  33.3 21.4 %all-to-all-start = ((f32[16,56,96]{2,1,0:T(8,128)}), f32[16,56,96]{2,1,0:T(8,128)}, u32[]{:S(2)}, u32[]{:S(2)}) async-start(f32[16,56,96]{2,1,0:T(8,128)} %broadcast_in_dim.8), calls=%async_computation | async-start | bytes 917504 | tf_op jit(solution)/shard_map/all_to_all | solution.py:108
  47.8 1.0 copy-start.3
  49.6 1.3 copy-start.5
  50.9 1.0 copy-start.8
  53.0 0.8 copy-start.1
  53.0 1.0 copy-start.2
  61.0 7.8 %collective-permute-start.12 = (f32[96,256]{1,0:T(8,128)S(1)}, f32[96,256]{1,0:T(8,128)S(1)}, u32[]{:S(2)}, u32[]{:S(2)}) collective-permute-start(f32[96,256]{1,0:T(8,128)S(1)} %maximum_convert_fusion), channel_id=1, source_target_pairs={{0,16},{16,0},{32,48},{48,32},{64,80},{80,64},{96,112},{112,96},{1... | collective-permute-start | bytes 294920 | tf_op jit(solution)/shard_map/ppermute | solution.py:79
  86.2 2.9 %collective-permute-start.13 = (f32[48,256]{1,0:T(8,128)S(1)}, f32[48,256]{1,0:T(8,128)S(1)}, u32[]{:S(2)}, u32[]{:S(2)}) collective-permute-start(f32[48,256]{1,0:T(8,128)S(1)} %convert_reduce_fusion), channel_id=1, source_target_pairs={{0,16},{16,0},{32,48},{48,32},{64,80},{80,64},{96,112},{112,96},{1... | collective-permute-start | bytes 147464 | tf_op jit(solution)/shard_map/ppermute | solution.py:83
  91.5 1.7 collective-permute-start.14
  94.0 12.7 %all-to-all-start.2 = ((f32[16,24,128]{2,1,0:T(8,128)}), f32[16,24,128]{2,1,0:T(8,128)S(1)}, u32[]{:S(2)}, u32[]{:S(2)}) async-start(f32[16,24,128]{2,1,0:T(8,128)} %reshape.105), calls=%async_computation.2 | async-start | bytes 393216 | tf_op jit(solution)/shard_map/all_to_all | solution.py:146
  107.4 10.9 %all-to-all-start.3 = ((f32[8,24,128]{2,1,0:T(8,128)}), f32[8,24,128]{2,1,0:T(8,128)S(1)}, u32[]{:S(2)}, u32[]{:S(2)}) async-start(f32[8,24,128]{2,1,0:T(8,128)} %broadcast_in_dim.10), calls=%async_computation.3 | async-start | bytes 196608 | tf_op jit(solution)/shard_map/all_to_all | solution.py:90
  110.8 101.5 %all-reduce.3.cloned.1.call-start = ((), (), s32[]{:S(2)}) async-start(), calls=%async_computation.5 | async-start | bytes 3670016
  115.1 20.0 %copy-start.9 = (u32[256]{0:T(256)S(1)}, u32[256]{0:T(256)}, u32[]{:S(2)}) copy-start(u32[256]{0:T(256)} %constant.160) | copy-start | bytes 3076
  129.2 7.2 %collective-permute-start.15 = (f32[48,1024]{1,0:T(8,128)}, f32[48,1024]{1,0:T(8,128)S(1)}, u32[]{:S(2)}, u32[]{:S(2)}) collective-permute-start(f32[48,1024]{1,0:T(8,128)} %reshape.106), channel_id=1, source_target_pairs={{0,16},{16,0},{32,48},{48,32},{64,80},{80,64},{96,112},{112,96},{1... | collective-permute-start | bytes 589832 | tf_op jit(solution)/shard_map/ppermute | solution.py:83
  137.4 0.7 copy-start.4
Sparse Core Ops, SparseCore 0:
  115.3 96.9 all-reduce.2

commit v2 on v0

v2 whole, which is shorter than its diff:
```python
import jax
import jax.numpy as jnp
from jax import lax
from jax.experimental import pallas as pl
from jax.experimental.pallas import tpu as pltpu
from jax.sharding import PartitionSpec as P

BF = jnp.bfloat16
F32 = jnp.float32
SIDE = 4
DEPTH = 8
RANK = 32
ROWS = 3 * RANK
HALF = ROWS // 2
LANES = 128
TILES = HALF * 1024 // (8 * LANES)
MIB = 1 << 20

X_GROUPS = [[y * SIDE + x for x in range(SIDE)] for y in range(SIDE)]
Y_GROUPS = [[y * SIDE + x for y in range(SIDE)] for x in range(SIDE)]
CORE_PAIR = [(i, i ^ 1) for i in range(2 * DEPTH)]
Z_GROUPS = [[z * 2 + c for z in range(DEPTH)] for c in range(2)]


def x_ring(k):
    return [(y * SIDE + x, y * SIDE + (x + k) % SIDE) for y in range(SIDE) for x in range(SIDE)]


def y_ring(k):
    return [(y * SIDE + x, ((y + k) % SIDE) * SIDE + x) for y in range(SIDE) for x in range(SIDE)]


def spread(value, axis, groups, size):
    return lax.all_to_all(
        jnp.broadcast_to(value[None], (size,) + value.shape), axis, 0, 0, tiled=True, axis_index_groups=groups
    )


def ring_pieces(value, ring):
    near = [value] + [None] * 3
    for k in (1, 3, 2):
        near[k] = lax.ppermute(value, "tensor", ring(k))
    return near


def order_kernel(place_ref, *refs):
    for pieces, out_ref in ((refs[:SIDE], refs[-2]), (refs[SIDE:-2], refs[-1])):
        for i, ref in enumerate(pieces):
            out_ref[lax.rem(place_ref[0] - i + SIDE, SIDE)] = ref[...]


def order(position, a_pieces, b_pieces):
    vmem = pl.BlockSpec(memory_space=pltpu.VMEM)
    out_shape = tuple(jax.ShapeDtypeStruct((SIDE,) + p[0].shape, p[0].dtype) for p in (a_pieces, b_pieces))
    return pl.pallas_call(
        order_kernel,
        out_shape=out_shape,
        in_specs=[pl.BlockSpec(memory_space=pltpu.SMEM)] + [vmem] * (2 * SIDE),
        out_specs=(vmem, vmem),
    )(position.reshape(1), *a_pieces, *b_pieces)


def gather_all(x_part, dy_part, q_part, me):
    rows = SIDE * x_part.shape[0]
    dy_col = spread(dy_part, "tensor", Y_GROUPS, SIDE)
    near, q_near, dy_col = lax.optimization_barrier(
        (ring_pieces(x_part, x_ring), ring_pieces(q_part, x_ring), dy_col)
    )
    x_row, q_row = order(me % SIDE, near, q_near)
    x_row, q_row, dy_col = lax.optimization_barrier((x_row, q_row, dy_col))
    dy_all = spread(dy_col, "tensor", X_GROUPS, SIDE)
    far, q_far = lax.optimization_barrier((ring_pieces(x_row, y_ring), ring_pieces(q_row, y_ring)))
    return [p.reshape(rows, -1) for p in far], [p.reshape(rows, -1) for p in q_far], dy_all


def swap_order(value):
    blocks = value.reshape((SIDE, SIDE, -1) + value.shape[1:])
    return jnp.swapaxes(blocks, 0, 1).reshape(value.shape)


def scatter_sum(blocks, x):
    got = [blocks[0]] + [lax.ppermute(blocks[k], "tensor", y_ring(k)) for k in (1, 3, 2)]
    got = lax.optimization_barrier(got)
    total = sum(v.astype(F32) for v in got).astype(blocks[0].dtype)
    total = lax.optimization_barrier(total).reshape(SIDE, -1, total.shape[1])

    def part(k):
        return lax.dynamic_index_in_dim(total, (x + k) % SIDE, 0, False)

    got = [part(0)] + [lax.ppermute(part(k), "tensor", x_ring(k)) for k in (1, 3, 2)]
    return sum(v.astype(F32) for v in got).astype(total.dtype)


def split(value):
    high = value.astype(BF)
    return high, (value - high.astype(F32)).astype(BF)


def dot(a, b, ca, cb):
    return lax.dot_general(a, b, (((ca,), (cb,)), ((), ())), preferred_element_type=F32)


def dot3(a, b, ca, cb):
    a_high, a_low = split(a)
    b_high, b_low = split(b)
    return dot(
        jnp.concatenate([a_high, a_high, a_low], axis=ca), jnp.concatenate([b_high, b_low, b_high], axis=cb), ca, cb
    )


def own_half(core, value):
    low, high = value[:HALF], value[HALF:]
    first = core == 0
    return jnp.where(first, low, high), jnp.where(first, high, low)


def whole(core, mine, other):
    first = core == 0
    return jnp.concatenate([jnp.where(first, mine, other), jnp.where(first, other, mine)])


def factors_kernel(place_ref, q0_ref, q1_ref, q2_ref, q3_ref, err_ref, q_both_ref, p_ref, q_ref):
    rows = q0_ref.shape[0]
    for i, ref in enumerate((q0_ref, q1_ref, q2_ref, q3_ref)):
        at = pl.multiple_of(lax.rem(place_ref[0] - i + SIDE, SIDE) * rows, 8)
        q_ref[pl.ds(at, rows), :] = ref[...]
    block = rows // SIDE
    swapped = [
        q_ref[(y * SIDE + x) * block : (y * SIDE + x + 1) * block, 2 * RANK :]
        for x in range(SIDE)
        for y in range(SIDE)
    ]
    q_rows = q_ref[...].T
    for k in range(3):
        q_both = jnp.concatenate(split(q_rows[k * RANK : (k + 1) * RANK]))
        both = dot(q_both, err_ref[0, k], 1, 1)
        p_ref[pl.ds(k * RANK, RANK), :] = both[:RANK] + both[RANK:]
        q_both_ref[k] = q_both if k < 2 else jnp.concatenate(split(jnp.concatenate(swapped).T))


def factors(place, pieces, error_in):
    vmem = pl.BlockSpec(memory_space=pltpu.VMEM)
    hid, width = error_in.shape[2:]
    return pl.pallas_call(
        factors_kernel,
        out_shape=(jax.ShapeDtypeStruct((3, 2 * RANK, width), BF), jax.ShapeDtypeStruct((ROWS, hid), F32)),
        in_specs=[pl.BlockSpec(memory_space=pltpu.SMEM)] + [vmem] * 5,
        out_specs=(vmem, vmem),
        scratch_shapes=[pltpu.VMEM((width, ROWS), F32)],
    )(place, *pieces, error_in)


def backward_kernel(place_ref, p0_ref, p1_ref, p2_ref, p3_ref, dy_hbm, gate_hbm, up_hbm, down_hbm, q_ref, p_err_ref,
                    gate_grad_ref, up_grad_ref, hidden_ref, mine_ref, theirs_ref, x_ref,
                    dy_ref, gate_ref, up_ref, down_ref, sems):
    rows = p0_ref.shape[0]
    copies = [pltpu.make_async_copy(gate_hbm, gate_ref, sems.at[0])]
    for i, ref in enumerate((p0_ref, p1_ref, p2_ref, p3_ref)):
        at = pl.multiple_of(lax.rem(place_ref[0] - i + SIDE, SIDE) * rows, 16)
        copies.append(pltpu.make_async_copy(ref, x_ref.at[pl.ds(at, rows), :], sems.at[1 + i]))
    late = [
        pltpu.make_async_copy(up_hbm, up_ref, sems.at[5]),
        pltpu.make_async_copy(down_hbm, down_ref, sems.at[6]),
        pltpu.make_async_copy(dy_hbm, dy_ref, sems.at[7]),
    ]
    for copy in copies + late:
        copy.start()
    for copy in copies:
        copy.wait()
    tokens = x_ref.shape[1]
    chunk = 256
    spans = [slice(i, i + chunk) for i in range(0, tokens, chunk)]
    gate_pres = [dot(gate_ref[...], x_ref[:, spans[0]], 1, 0)]
    for copy in late:
        copy.wait()
    sums = [jnp.zeros((2 * RANK, mine_ref.shape[1]), F32)] * 3
    for i, span in enumerate(spans):
        x, dy = x_ref[:, span], dy_ref[:, span]
        gate_pre = gate_pres[0] if i == 0 else dot(gate_ref[...], x, 1, 0)
        up_pre = dot(up_ref[...], x, 1, 0)
        hidden_grad = dot(down_ref[...], dy, 1, 0)
        gate_sig = jax.nn.sigmoid(gate_pre)
        gate_act = gate_pre * gate_sig
        hidden = (gate_act * up_pre).astype(BF)
        gate_grad = (hidden_grad * up_pre * gate_sig * (1.0 + gate_pre * (1.0 - gate_sig))).astype(BF)
        up_grad = (hidden_grad * gate_act).astype(BF)
        gate_grad_ref[:, span] = gate_grad
        up_grad_ref[:, span] = up_grad
        hidden_ref[:, span] = hidden
        for k, (left, right) in enumerate(((gate_grad, x), (up_grad, x), (hidden, dy))):
            both = dot(q_ref[k], right, 1, 0)
            halves = jnp.concatenate(split(both[:RANK] + both[RANK:]))
            sums[k] = sums[k] + dot(halves, left, 1, 1)
    p = jnp.concatenate([both[:RANK] + both[RANK:] for both in sums]) + p_err_ref[...]
    mine, theirs = own_half(place_ref[1], p)
    mine_ref[...] = mine
    theirs_ref[...] = theirs.astype(BF)


def backward(place, pieces, dy_all, q_both, p_err, w_gate, w_up, w_down):
    hid, width = w_gate.shape
    tokens = dy_all.shape[1]
    vmem = pl.BlockSpec(memory_space=pltpu.VMEM)
    anywhere = pl.BlockSpec(memory_space=pl.ANY)
    grads = jax.ShapeDtypeStruct((hid, tokens), BF)
    weights = pltpu.VMEM((hid, width), BF)
    return pl.pallas_call(
        backward_kernel,
        out_shape=(
            grads,
            grads,
            grads,
            jax.ShapeDtypeStruct((HALF, hid), F32),
            jax.ShapeDtypeStruct((HALF, hid), BF),
            jax.ShapeDtypeStruct((width, tokens), BF),
        ),
        in_specs=[pl.BlockSpec(memory_space=pltpu.SMEM)] + [anywhere] * 8 + [vmem] * 2,
        out_specs=(vmem,) * 6,
        scratch_shapes=[
            pltpu.VMEM((width, tokens), BF),
            weights,
            weights,
            weights,
            pltpu.SemaphoreType.DMA((8,)),
        ],
        compiler_params=pltpu.CompilerParams(vmem_limit_bytes=58 * MIB),
        cost_estimate=pl.CostEstimate(flops=6 * hid * width * tokens, bytes_accessed=8 * MIB, transcendentals=0),
    )(place, *pieces, dy_all, w_gate, w_up, w_down, q_both, p_err)


def term_kernel(place_ref, w_ref, gate_grad_ref, up_grad_ref, t0_ref, t1_ref, t2_ref, t3_ref):
    grads = jnp.concatenate([gate_grad_ref[...], up_grad_ref[...]])
    rows = t0_ref.shape[0]
    for i, ref in enumerate((t0_ref, t1_ref, t2_ref, t3_ref)):
        at = pl.multiple_of(lax.rem(place_ref[0] + i, SIDE) * rows, 16)
        ref[...] = dot(w_ref[pl.ds(at, rows), :], grads, 1, 0).astype(BF)


def terms(place, w_both, gate_grad, up_grad):
    vmem = pl.BlockSpec(memory_space=pltpu.VMEM)
    width, both = w_both.shape
    tokens = gate_grad.shape[1]
    out = jax.ShapeDtypeStruct((width // SIDE, tokens), BF)
    return pl.pallas_call(
        term_kernel,
        out_shape=(out,) * SIDE,
        in_specs=[pl.BlockSpec(memory_space=pltpu.SMEM)] + [vmem] * 3,
        out_specs=(vmem,) * SIDE,
        compiler_params=pltpu.CompilerParams(vmem_limit_bytes=24 * MIB),
        cost_estimate=pl.CostEstimate(flops=2 * width * both * tokens, bytes_accessed=4 * MIB, transcendentals=0),
    )(place, w_both, gate_grad, up_grad)


def matrices_kernel(gate_grad_ref, up_grad_ref, hidden_ref, x_ref, dy_ref, err_ref, m0_ref, m1_ref, m2_ref):
    m0_ref[...] = dot(gate_grad_ref[...], x_ref[...], 1, 1) + err_ref[0, 0].astype(F32)
    m1_ref[...] = dot(up_grad_ref[...], x_ref[...], 1, 1) + err_ref[0, 1].astype(F32)
    swapped = dot(hidden_ref[...], dy_ref[...], 1, 1)
    block = swapped.shape[1] // (SIDE * SIDE)
    parts = [
        swapped[:, (x * SIDE + y) * block : (x * SIDE + y + 1) * block] for y in range(SIDE) for x in range(SIDE)
    ]
    m2_ref[...] = jnp.concatenate(parts, axis=1) + err_ref[0, 2].astype(F32)


def grad_matrices(gate_grad, up_grad, hidden, x_all, dy_all, error_in):
    vmem = pl.BlockSpec(memory_space=pltpu.VMEM)
    hid, tokens = hidden.shape
    width = x_all.shape[0]
    return pl.pallas_call(
        matrices_kernel,
        out_shape=(jax.ShapeDtypeStruct((hid, width), F32),) * 3,
        in_specs=[vmem] * 6,
        out_specs=(vmem,) * 3,
        compiler_params=pltpu.CompilerParams(vmem_limit_bytes=32 * MIB),
        cost_estimate=pl.CostEstimate(flops=6 * hid * width * tokens, bytes_accessed=9 * MIB, transcendentals=0),
    )(gate_grad, up_grad, hidden, x_all, dy_all, error_in)


def sketch_kernel(core_ref, p_mine_ref, p_other_ref, m0_ref, m1_ref, m2_ref, mine_ref, theirs_ref):
    core = core_ref[0]
    p = whole(core, p_mine_ref[...], p_other_ref[...])
    rows = []
    for k, m_ref in enumerate((m0_ref, m1_ref, m2_ref)):
        p_k = p[k * RANK : (k + 1) * RANK]
        p_high, p_low = split(p_k)
        m_high, m_low = split(m_ref[...])
        both = dot(jnp.concatenate([p_high, p_low]), m_high, 1, 0)
        term = both[:RANK] + both[RANK:] + dot(p_high, m_low, 1, 0)
        gram = dot3(p_k, p_k, 1, 1)
        rows.append(jnp.concatenate([term, gram, jnp.zeros((RANK, LANES - RANK), F32)], axis=1))
    mine, theirs = own_half(core, jnp.concatenate(rows))
    for i in range(HALF // 8):
        for j in range(8):
            tile = (i * 8 + j) * 8
            rows, cols = slice(i * 8, i * 8 + 8), slice(j * LANES, (j + 1) * LANES)
            mine_ref[tile : tile + 8, :] = mine[rows, cols]
            theirs_ref[tile : tile + 8, :] = theirs[rows, cols]


def sketch(core, p_mine, p_other, matrices):
    vmem = pl.BlockSpec(memory_space=pltpu.VMEM)
    out = jax.ShapeDtypeStruct((TILES * 8, LANES), F32)
    return pl.pallas_call(
        sketch_kernel,
        out_shape=(out, out),
        in_specs=[pl.BlockSpec(memory_space=pltpu.SMEM)] + [vmem] * 5,
        out_specs=(vmem, vmem),
        compiler_params=pltpu.CompilerParams(vmem_limit_bytes=40 * MIB),
    )(core, p_mine, p_other, *matrices)


def finish_kernel(core_ref, s_mine_ref, s_other_ref, p_mine_ref, p_other_ref, m0_ref, m1_ref, m2_ref,
                  error_ref, q_ref):
    core = core_ref[0]

    def rows_of(ref):
        return jnp.concatenate(
            [
                jnp.concatenate([ref[(i * 8 + j) * 8 : (i * 8 + j) * 8 + 8, :] for j in range(8)], axis=1)
                for i in range(HALF // 8)
            ]
        )

    s = whole(core, rows_of(s_mine_ref), rows_of(s_other_ref))
    p = whole(core, p_mine_ref[...], p_other_ref[...])
    width = m0_ref.shape[1]
    gram = jnp.stack([s[k * RANK : (k + 1) * RANK, width : width + RANK] for k in range(3)])
    rows = lax.broadcasted_iota(jnp.int32, (1, RANK, RANK), 1)
    cols = lax.broadcasted_iota(jnp.int32, (1, RANK, RANK), 2)
    eye = jnp.broadcast_to(jnp.where(rows == cols, 1.0, 0.0), gram.shape)
    work = jnp.concatenate([gram, eye], axis=2)
    below = lax.broadcasted_iota(jnp.int32, (1, RANK, 1), 1)
    for k in range(RANK):
        pivot = work[:, k : k + 1, :]
        scale = 1.0 / pivot[:, :, k : k + 1]
        factor = jnp.where(below > k, work[:, :, k : k + 1] * scale, 0.0)
        work = work - factor * pivot
    diag = jnp.sum(jnp.where(rows == cols, work[:, :, :RANK], 0.0), axis=2, keepdims=True)
    inverse = work[:, :, RANK:] * lax.rsqrt(diag)
    for k, m_ref in enumerate((m0_ref, m1_ref, m2_ref)):
        part = slice(k * RANK, (k + 1) * RANK)
        q_new = dot3(inverse[k], s[part, :width], 1, 0)
        p_ortho = dot3(inverse[k], p[part], 1, 0)
        q_ref[part, :] = q_new
        error_ref[0, k] = (m_ref[...] - dot3(p_ortho, q_new, 0, 0)).astype(BF)


def finish(core, s_mine, s_other, p_mine, p_other, matrices):
    vmem = pl.BlockSpec(memory_space=pltpu.VMEM)
    hid, width = matrices[0].shape
    return pl.pallas_call(
        finish_kernel,
        out_shape=(jax.ShapeDtypeStruct((1, 3, hid, width), BF), jax.ShapeDtypeStruct((ROWS, width), F32)),
        in_specs=[pl.BlockSpec(memory_space=pltpu.SMEM)] + [vmem] * 7,
        out_specs=(vmem, vmem),
        compiler_params=pltpu.CompilerParams(vmem_limit_bytes=40 * MIB),
    )(core, s_mine, s_other, p_mine, p_other, *matrices)


def swap_core(value):
    return lax.ppermute(value, "dp", CORE_PAIR)


def per_device(hidden_in, out_grad, w_gate, w_up, w_down, error_in, q_init):
    n_workers = lax.axis_size("dp")
    n_tensor = lax.axis_size("tensor")
    me = lax.axis_index("tensor")
    y, x = me // SIDE, me % SIDE
    core = lax.axis_index("dp") % 2
    shard = hidden_in.shape[1]

    q_cols = q_init.reshape(ROWS, shard).T
    pieces, q_pieces, dy_all = gather_all(hidden_in.T, out_grad.T, q_cols, me)
    dy_all = dy_all.reshape(shard * n_tensor, -1)
    spot = jnp.stack([y, core])
    q_both, p_err = factors(spot, q_pieces, error_in)
    w_down_swapped = swap_order(w_down.T).T
    w_both = jnp.concatenate([w_gate, w_up]).T
    gate_grad, up_grad, hidden, p_mine, p_theirs, x_all = backward(
        spot, pieces, dy_all, q_both, p_err, w_gate, w_up, w_down_swapped
    )
    core = core.reshape(1)
    input_grad = scatter_sum(terms(spot, w_both, gate_grad, up_grad), x).T
    p_pair = (p_mine + swap_core(p_theirs).astype(F32)).astype(BF)
    p_half = jnp.sum(spread(p_pair, "dp", Z_GROUPS, DEPTH).astype(F32), axis=0) / n_workers

    matrices = grad_matrices(gate_grad, up_grad, hidden, x_all, dy_all, error_in)

    p_other = swap_core(p_half)
    s_mine, s_theirs = sketch(core, p_half, p_other, matrices)
    s_pair = (s_mine + swap_core(s_theirs)).reshape(n_tensor, -1, LANES)
    s_part = jnp.sum(lax.all_to_all(s_pair, "tensor", 0, 0, tiled=True), axis=0)
    s_part = jnp.sum(spread(s_part, "dp", Z_GROUPS, DEPTH), axis=0) / n_workers
    s_half = spread(s_part, "tensor", None, n_tensor).reshape(-1, LANES)
    error_out, q_new = finish(core, s_half, swap_core(s_half), p_half, p_other, matrices)
    q_out = lax.dynamic_slice_in_dim(q_new, me * shard, shard, 1).reshape(q_init.shape)
    return (input_grad, error_out, q_out)


def solution(mesh):
    in_specs = (
        P("dp", "tensor"),
        P("dp", "tensor"),
        P("tensor", None),
        P("tensor", None),
        P("tensor", None),
        P("dp", None, "tensor", None),
        P(None, None, "tensor"),
    )
    out_specs = (P("dp", "tensor"), P("dp", None, "tensor", None), P(None, None, "tensor"))
    return jax.shard_map(
        per_device, mesh=mesh, in_specs=in_specs, out_specs=out_specs, check_vma=False
    )
```

time: 366 us -> 163 us (0.45); the launches traced: 360 us -> 161 us
  blocking collectives: 222 us -> 0 us
  starting transfers between devices: 0.11 us -> 68.6 us
  waiting for transfers between devices: 74.2 us -> 40 us
  matrix products: 25.8 us -> 0 us
  Pallas kernels: 0 us -> 23.4 us
  local copies, waits for them, and re-layouts: 6.74 us -> 21.7 us
  between operations: 14 us -> 1.05 us
  other arithmetic: 17 us -> 6.62 us
    psum x3 -> x0, blocking collectives: 166 us -> none  [the longest x1 61.5 us: per_device(): q_out = lax.psum(owned, 'dp') / n_workers]
    all_gather x2 -> x0, waiting for transfers between devices: 72.8 us -> none  [the longest x1 46.1 us: per_device(): lax.all_gather(out_grad, 'tensor', axis=1, tiled=True)]
    all_gather x2 -> x0, blocking collectives: 46.1 us -> none  [the longest x1 26.4 us: per_device(): q_full = lax.all_gather(q_init, 'tensor', axis=2, tiled=True)]
    ppermute x0 -> x22, starting transfers between devices: none -> 35.7 us  [the longest x12 15.4 us: ring_pieces(): near[k] = lax.ppermute(value, 'tensor', ring(k))]
    all_to_all x0 -> x6, starting transfers between devices: none -> 32.9 us  [the longest x5 27.3 us: spread(): lax.all_to_all(jnp.broadcast_to(value[None], (size,) + value.shape), axis...]
    ppermute x0 -> x22, waiting for transfers between devices: none -> 27 us  [the longest x12 23.6 us: ring_pieces(): near[k] = lax.ppermute(value, 'tensor', ring(k))]
    dot_general x12 -> x0, matrix products: 25.5 us -> none  [the longest x3 8.15 us: rows_dot(): lax.dot_general(left, right, (((1,), (1,)), ((), ())), preferred_element_...]
    pallas_call x0 -> x7, Pallas kernels: none -> 23.4 us  [the longest x1 7.63 us: backward(): pl.pallas_call(backward_kernel, out_shape=(grads, grads, grads, jax.Shape...]
  transfers between devices with their start and end apart: 3 -> 28, of which waited for: 2 -> 12; matrix products, arithmetic and copies ran while one was open for 11% -> 6% of each run, Pallas kernels for 0% -> 5%
where the time goes in v2:
time: 163 us; the launch traced here: 161 us
  starting transfers between devices  68.6 us (42%)
  waiting for transfers between devices  40 us (25%)
  Pallas kernels  23.4 us (14%)
  local copies, waits for them, and re-layouts  21.7 us (13%)
  other arithmetic  6.62 us (4%)
    all_to_all x5, starting transfers between devices, spread(): lax.all_to_all(jnp.broadcast_to(value[None], (size,) + value.shape), axis...  27.3 us
    ppermute x12, waiting for transfers between devices, ring_pieces(): near[k] = lax.ppermute(value, 'tensor', ring(k))  23.6 us
    ppermute x12, starting transfers between devices, ring_pieces(): near[k] = lax.ppermute(value, 'tensor', ring(k))  15.4 us
    ppermute x4, starting transfers between devices, swap_core(): return lax.ppermute(value, 'dp', CORE_PAIR)  12.7 us
    unnamed x69, local copies, waits for them, and re-layouts  12.1 us
    pallas_call x1, Pallas kernels, backward(): pl.pallas_call(backward_kernel, out_shape=(grads, grads, grads, jax.Shape...  7.63 us
    all_to_all x1, waiting for transfers between devices, per_device(): s_part = jnp.sum(lax.all_to_all(s_pair, 'tensor', 0, 0, tiled=True), axis=0)  6.66 us
    all_to_all x5, waiting for transfers between devices, spread(): lax.all_to_all(jnp.broadcast_to(value[None], (size,) + value.shape), axis...  6.32 us
  transfers between devices with their start and end apart: 28, of which 12 were waited for; matrix products, arithmetic and copies ran while one was open for 6% of the time, Pallas kernels for 5%

profile of v2, /device:TPU:1, one launch (start us, length us, event | category | flops | bytes accessed | tf_op | source)
XLA Modules:
  0.0 161.3 jit_solution(13039909478301784633)
XLA Ops:
  0.6 1.7 %broadcast_in_dim.10 = bf16[4,56,1024]{2,1,0:T(8,128)(2,1)} broadcast(bf16[56,1024]{1,0:T(8,128)(2,1)} %bitcast.50), dimensions={1,2} | broadcast | bytes 573440 | tf_op jit(solution)/shard_map/broadcast_in_dim | solution.py:35
  2.3 5.0 %all-to-all-start = ((bf16[4,56,1024]{2,1,0:T(8,128)(2,1)}), bf16[4,56,1024]{2,1,0:T(8,128)(2,1)S(1)}, u32[]{:S(2)}, u32[]{:S(2)}) async-start(bf16[4,56,1024]{2,1,0:T(8,128)(2,1)} %broadcast_in_dim.10), calls=%async_computation | async-start | bytes 917504 | tf_op jit(solution)/shard_map/all_to_all | solution.py:34
  7.4 1.2 collective-permute-start
  8.6 2.5 %collective-permute-start.1 = (bf16[56,1024]{1,0:T(8,128)(2,1)}, bf16[56,1024]{1,0:T(8,128)(2,1)S(1)}, u32[]{:S(2)}, u32[]{:S(2)}) collective-permute-start(bf16[56,1024]{1,0:T(8,128)(2,1)} %bitcast.52), channel_id=1, source_target_pairs={{0,2},{1,3},{2,0},{3,1},{4,6},{5,7},{6,4},{7,5},{8,10},{9,11},{10,... | collective-permute-start | bytes 344072 | tf_op jit(solution)/shard_map/ppermute | solution.py:42
  11.0 1.2 collective-permute-start.2
  12.2 0.9 copy.22
  13.4 0.9 collective-permute-start.4
  14.3 3.7 %collective-permute-done.3.refs_5_ = f32[56,96]{1,0:T(8,128)S(1)} collective-permute-done((f32[56,96]{1,0:T(8,128)S(1)}, f32[56,96]{1,0:T(8,128)S(1)}, u32[]{:S(2)}, u32[]{:S(2)}) %collective-permute-start.3) | collective-permute-done | bytes 21536 | tf_op jit(solution)/shard_map/ppermute | solution.py:42
  18.0 2.7 %collective-permute-done.5.refs_7_ = f32[56,96]{1,0:T(8,128)S(1)} collective-permute-done((f32[56,96]{1,0:T(8,128)S(1)}, f32[56,96]{1,0:T(8,128)S(1)}, u32[]{:S(2)}, u32[]{:S(2)}) %collective-permute-start.5) | collective-permute-done | bytes 21536 | tf_op jit(solution)/shard_map/ppermute | solution.py:42
  21.5 1.9 %shard_map.94 = (bf16[4,56,1024]{2,1,0:T(8,128)(2,1)}, f32[4,56,96]{2,1,0:T(8,128)}) custom-call(s32[1]{0:T(128)} %bitcast.3.place_ref, bf16[56,1024]{1,0:T(8,128)(2,1)} %bitcast.54, bf16[56,1024]{1,0:T(8,128)(2,1)} %copy-done.24, bf16[56,1024]{1,0:T(8,128)(2,1)} %copy-done.25, bf16[56,1024]{1,0:T(8,128)(2,1)} %copy-done.26, f32[56,96]{1,0:T(8,128)} %bitcast.62, ...), custom_call_target="tpu_custom_call" | custom-call | tf_op jit(solution)/shard_map/pallas_call | solution.py:55
  23.4 1.5 broadcast_in_dim.11
  24.9 3.7 %all-to-all-start.1 = ((bf16[4,4,56,1024]{3,2,1,0:T(8,128)(2,1)}), bf16[4,4,56,1024]{3,2,1,0:T(8,128)(2,1)S(1)}, u32[]{:S(2)}, u32[]{:S(2)}) async-start(bf16[4,4,56,1024]{3,2,1,0:T(8,128)(2,1)} %broadcast_in_dim.11), calls=%async_computation.1 | async-start | bytes 3670016 | tf_op jit(solution)/shard_map/all_to_all | solution.py:34
  28.6 1.6 collective-permute-start.6
  30.2 2.4 %collective-permute-start.7 = (bf16[4,56,1024]{2,1,0:T(8,128)(2,1)S(1)}, bf16[4,56,1024]{2,1,0:T(8,128)(2,1)}, u32[]{:S(2)}, u32[]{:S(2)}) collective-permute-start(bf16[4,56,1024]{2,1,0:T(8,128)(2,1)S(1)} %copy-done.20), channel_id=1, source_target_pairs={{0,8},{1,9},{2,10},{3,11},{4,12},{5,13},{6,14},{7,15},{8,0},{9,1},... | collective-permute-start | bytes 1376264 | tf_op jit(solution)/shard_map/ppermute | solution.py:42
  32.6 1.2 collective-permute-start.8
  34.1 1.0 copy.25
  35.1 2.6 %collective-permute-start.11 = (f32[4,56,96]{2,1,0:T(8,128)S(1)}, f32[4,56,96]{2,1,0:T(8,128)S(1)}, u32[]{:S(2)}, u32[]{:S(2)}) collective-permute-start(f32[4,56,96]{2,1,0:T(8,128)S(1)} %copy-done.22), channel_id=1, source_target_pairs={{0,12},{1,13},{2,14},{3,15},{4,0},{5,1},{6,2},{7,3},{8,4},{9,5},{1... | collective-permute-start | bytes 258056 | tf_op jit(solution)/shard_map/ppermute | solution.py:42
  37.7 14.4 %collective-permute-done.10 = f32[4,56,96]{2,1,0:T(8,128)S(1)} collective-permute-done((f32[4,56,96]{2,1,0:T(8,128)S(1)}, f32[4,56,96]{2,1,0:T(8,128)S(1)}, u32[]{:S(2)}, u32[]{:S(2)}) %collective-permute-start.10) | collective-permute-done | bytes 86048 | tf_op jit(solution)/shard_map/ppermute | solution.py:42
  52.2 1.5 collective-permute-start.9
  53.6 0.7 pad_add_fusion.place_ref
  54.3 2.2 %collective-permute-done.11 = f32[4,56,96]{2,1,0:T(8,128)S(1)} collective-permute-done((f32[4,56,96]{2,1,0:T(8,128)S(1)}, f32[4,56,96]{2,1,0:T(8,128)S(1)}, u32[]{:S(2)}, u32[]{:S(2)}) %collective-permute-start.11) | collective-permute-done | bytes 86048 | tf_op jit(solution)/shard_map/ppermute | solution.py:42
  57.7 2.9 %shard_map.95 = (bf16[3,64,896]{2,1,0:T(8,128)(2,1)}, f32[96,256]{1,0:T(8,128)}) custom-call(s32[2]{0:T(128)} %pad_add_fusion.place_ref, f32[224,96]{1,0:T(8,128)} %bitcast.55, f32[224,96]{1,0:T(8,128)} %bitcast.58, f32[224,96]{1,0:T(8,128)} %bitcast.56, f32[224,96]{1,0:T(8,128)} %bitcast.57, bf16[1,3,256,896]{3,2,1,0:T(8,128)(2,1)} %err_ref.3), custom_call_target="tpu_custom_call" | custom-call | tf_op jit(solution)/shard_map/pallas_call | solution.py:144
  60.6 1.3 copy-done
  61.9 7.6 %shard_map.96 = (bf16[256,1024]{1,0:T(8,128)(2,1)}, bf16[256,1024]{1,0:T(8,128)(2,1)}, bf16[256,1024]{1,0:T(8,128)(2,1)}, f32[48,256]{1,0:T(8,128)}, bf16[48,256]{1,0:T(8,128)(2,1)}, /*index=5*/bf16[896,1024]{1,0:T(8,128)(2,1)}) custom-call(s32[2]{0:T(128)} %pad_add_fusion.place_ref, bf16[224,1024]{1,0:T(8,128)(2,1)} %bitcast.49, ...), custom_call_target="tpu_custom_call" | custom-call | flops 1409286144 | bytes 8388608 | tf_op jit(solution)/shard_map/pallas_call | solution.py:207
  69.5 5.7 %collective-permute-start.18 = (bf16[48,256]{1,0:T(8,128)(2,1)}, bf16[48,256]{1,0:T(8,128)(2,1)S(1)}, u32[]{:S(2)}, u32[]{:S(2)}) collective-permute-start(bf16[48,256]{1,0:T(8,128)(2,1)} %get-tuple-element.83), channel_id=1, source_target_pairs={{0,16},{16,0},{32,48},{48,32},{64,80},{80,64},{96,112},{112,96},{1... | collective-permute-start | bytes 73736 | tf_op jit(solution)/shard_map/ppermute | solution.py:361
  75.3 1.1 collective-permute-done.18
  76.3 0.8 add_convert_fusion.1
  77.1 0.7 broadcast_in_dim.12
  77.8 8.2 %all-to-all-start.2 = ((bf16[8,48,256]{2,1,0:T(8,128)(2,1)}), bf16[8,48,256]{2,1,0:T(8,128)(2,1)S(1)}, u32[]{:S(2)}, u32[]{:S(2)}) async-start(bf16[8,48,256]{2,1,0:T(8,128)(2,1)} %broadcast_in_dim.12), calls=%async_computation.2 | async-start | bytes 393216 | tf_op jit(solution)/shard_map/all_to_all | solution.py:34
  86.7 1.0 copy-done.10
  87.8 1.0 copy-done.12
  88.8 2.5 %shard_map.97 = (bf16[224,1024]{1,0:T(8,128)(2,1)S(1)}, bf16[224,1024]{1,0:T(8,128)(2,1)}, bf16[224,1024]{1,0:T(8,128)(2,1)}, bf16[224,1024]{1,0:T(8,128)(2,1)}) custom-call(s32[2]{0:T(128)S(1)} %copy-done.17, bf16[896,512]{1,0:T(8,128)(2,1)S(1)} %maximum_bitcast_fusion.w_ref, bf16[256,1024]{1,0:T(8,128)(2,1)S(1)} %copy-done.10, bf16[256,1024]{1,0:T(8,128)(2,1)S(1)} %copy-done.12), custom_call_target="tpu_custom_call" | custom-call | flops 939524096 | bytes 4194304 | tf_op jit(solution)/shard_map/pallas_call | solution.py:244
  91.3 0.8 copy-done.15
  92.0 1.6 %collective-permute-start.12 = (bf16[224,1024]{1,0:T(8,128)(2,1)}, bf16[224,1024]{1,0:T(8,128)(2,1)}, u32[]{:S(2)}, u32[]{:S(2)}) collective-permute-start(bf16[224,1024]{1,0:T(8,128)(2,1)} %get-tuple-element.75), channel_id=1, source_target_pairs={{0,4},{1,5},{2,6},{3,7},{4,8},{5,9},{6,10},{7,11},{8,12},{9,13},{1... | collective-permute-start | bytes 1376264 | tf_op jit(solution)/shard_map/ppermute | solution.py:82
  93.7 1.1 collective-permute-start.13
  94.7 0.7 collective-permute-start.14
  95.6 2.0 %collective-permute-start.19 = (f32[48,256]{1,0:T(8,128)S(1)}, f32[48,256]{1,0:T(8,128)S(1)}, u32[]{:S(2)}, u32[]{:S(2)}) collective-permute-start(f32[48,256]{1,0:T(8,128)S(1)} %broadcast_multiply_fusion.p_mine_ref), channel_id=1, source_target_pairs={{0,16},{16,0},{32,48},{48,32},{64,80},{80,64},{96,112},{112,96},{1... | collective-permute-start | bytes 147464 | tf_op jit(solution)/shard_map/ppermute | solution.py:361
  97.6 1.5 copy-done.9
  99.1 1.0 copy-done.11
  100.2 1.0 copy-done.13
  101.2 1.0 copy-done.14
  102.2 2.2 %shard_map.98 = (f32[256,896]{1,0:T(8,128)S(1)}, f32[256,896]{1,0:T(8,128)S(1)}, f32[256,896]{1,0:T(8,128)S(1)}) custom-call(bf16[256,1024]{1,0:T(8,128)(2,1)S(1)} %copy-done.11, bf16[256,1024]{1,0:T(8,128)(2,1)S(1)} %copy-done.13, bf16[256,1024]{1,0:T(8,128)(2,1)S(1)} %copy-done.14, bf16[896,1024]{1,0:T(8,128)(2,1)S(1)} %copy-done.9, ...), custom_call_target="tpu_custom_call" | custom-call | flops 1409286144 | bytes 9437184 | tf_op jit(solution)/shard_map/pallas_call | solution.py:269
  104.4 0.6 shard_map.99
  105.4 0.9 copy-done.3
  106.3 1.4 collective-permute-done.20
  107.8 0.7 add.90
  108.5 5.6 %all-to-all-start.3 = ((f32[16,24,128]{2,1,0:T(8,128)}), f32[16,24,128]{2,1,0:T(8,128)S(1)}, u32[]{:S(2)}, u32[]{:S(2)}) async-start(f32[16,24,128]{2,1,0:T(8,128)} %bitcast.28), calls=%async_computation.3 | async-start | bytes 393216 | tf_op jit(solution)/shard_map/all_to_all | solution.py:392
  114.2 0.9 collective-permute-done.14
  115.1 6.7 %all-to-all-done.3 = f32[16,24,128]{2,1,0:T(8,128)S(1)} async-done(((f32[16,24,128]{2,1,0:T(8,128)}), f32[16,24,128]{2,1,0:T(8,128)S(1)}, u32[]{:S(2)}, u32[]{:S(2)}) %all-to-all-start.3) | async-done | bytes 196640 | tf_op jit(solution)/shard_map/all_to_all | solution.py:392
  121.8 0.6 broadcast_in_dim.13
  122.4 6.8 %all-to-all-start.4 = ((f32[8,24,128]{2,1,0:T(8,128)}), f32[8,24,128]{2,1,0:T(8,128)S(1)}, u32[]{:S(2)}, u32[]{:S(2)}) async-start(f32[8,24,128]{2,1,0:T(8,128)} %broadcast_in_dim.13), calls=%async_computation.4 | async-start | bytes 196608 | tf_op jit(solution)/shard_map/all_to_all | solution.py:34
  129.3 2.5 %add_convert_fusion = bf16[224,1024]{1,0:T(8,128)(2,1)} fusion(bf16[224,1024]{1,0:T(8,128)(2,1)} %collective-permute-done.14, bf16[224,1024]{1,0:T(8,128)(2,1)} %collective-permute-done.13, bf16[224,1024]{1,0:T(8,128)(2,1)} %collective-permute-done.12, bf16[224,1024]{1,0:T(8,128)(2,1)S(1)} %copy-done.16), kind=kLoop, calls=%fused_computation.1 | loop fusion | flops 1835008 | bytes 2293760 | tf_op jit(solution)/shard_map/convert_element_type | solution.py:84
  131.8 5.0 %all-to-all-done.4 = f32[8,24,128]{2,1,0:T(8,128)S(1)} async-done(((f32[8,24,128]{2,1,0:T(8,128)}), f32[8,24,128]{2,1,0:T(8,128)S(1)}, u32[]{:S(2)}, u32[]{:S(2)}) %all-to-all-start.4) | async-done | bytes 98336 | tf_op jit(solution)/shard_map/all_to_all | solution.py:34
  136.9 0.7 broadcast_in_dim.14
  137.6 3.5 %all-to-all-start.5 = ((f32[16,24,128]{2,1,0:T(8,128)}), f32[16,24,128]{2,1,0:T(8,128)S(1)}, u32[]{:S(2)}, u32[]{:S(2)}) async-start(f32[16,24,128]{2,1,0:T(8,128)} %broadcast_in_dim.14), calls=%async_computation.5 | async-start | bytes 393216 | tf_op jit(solution)/shard_map/all_to_all | solution.py:34
  141.1 1.7 %dynamic-slice_bitcast_fusion.2 = (bf16[56,1024]{1,0:T(8,128)(2,1)}, bf16[56,1024]{1,0:T(8,128)(2,1)S(1)}, bf16[56,1024]{1,0:T(8,128)(2,1)S(1)}) fusion(bf16[4,56,1024]{2,1,0:T(8,128)(2,1)} %bitcast.47, s32[]{:T(128)S(6)} %select_n.55, s32[]{:T(128)S(6)} %select_n.59, s32[]{:T(128)S(6)} %select_n.57), kind=kLoop, calls=%fused_computation.10 | loop fusion | bytes 688140 | tf_op jit(solution)/shard_map/jit(dynamic_index_in_dim)/squeeze | solution.py:88
  142.8 1.2 collective-permute-start.15
  144.0 1.4 collective-permute-start.16
  145.5 1.5 collective-permute-start.17
  147.0 1.3 all-to-all-done.5
  148.2 4.9 %collective-permute-start.21 = (f32[384,128]{1,0:T(8,128)S(1)}, f32[384,128]{1,0:T(8,128)S(1)}, u32[]{:S(2)}, u32[]{:S(2)}) collective-permute-start(f32[384,128]{1,0:T(8,128)S(1)} %bitcast.42), channel_id=1, source_target_pairs={{0,16},{16,0},{32,48},{48,32},{64,80},{80,64},{96,112},{112,96},{1... | collective-permute-start | bytes 589832 | tf_op jit(solution)/shard_map/ppermute | solution.py:361
  153.1 1.8 %fusion.3 = bf16[1024,56]{0,1:T(8,128)(2,1)} fusion(bf16[56,1024]{1,0:T(8,128)(2,1)} %collective-permute-done.17, bf16[56,1024]{1,0:T(8,128)(2,1)} %collective-permute-done.16, bf16[56,1024]{1,0:T(8,128)(2,1)} %collective-permute-done.15, bf16[4,56,1024]{2,1,0:T(8,128)(2,1)} %bitcast.48, s32[]{:T(128)S(6)} %select_n.53), kind=kLoop, calls=%fused_computation.7 | loop fusion | flops 458752 | bytes 573444 | tf_op jit(solution)/shard_map/transpose | solution.py:383
  154.9 5.7 %shard_map.100 = (bf16[1,3,256,896]{3,2,1,0:T(8,128)(2,1)}, f32[96,896]{1,0:T(8,128)S(1)}) custom-call(s32[1]{0:T(128)} %bitcast.1.core_ref, f32[384,128]{1,0:T(8,128)S(1)} %bitcast.43, f32[384,128]{1,0:T(8,128)S(1)} %collective-permute-done.21.s_other_ref, f32[48,256]{1,0:T(8,128)S(1)} %broadcast_multiply_fusion.p_mine_ref, ...), custom_call_target="tpu_custom_call" | custom-call | tf_op jit(solution)/shard_map/pallas_call | solution.py:351
  160.6 0.7 constant_dynamic-slice_fusion
  (89 shorter events, 3.8 us)
Async XLA Ops:
  2.3 18.4 %all-to-all-start = ((bf16[4,56,1024]{2,1,0:T(8,128)(2,1)}), bf16[4,56,1024]{2,1,0:T(8,128)(2,1)S(1)}, u32[]{:S(2)}, u32[]{:S(2)}) async-start(bf16[4,56,1024]{2,1,0:T(8,128)(2,1)} %broadcast_in_dim.10), calls=%async_computation | async-start | bytes 917504 | tf_op jit(solution)/shard_map/all_to_all | solution.py:34
  7.4 13.4 %collective-permute-start = (bf16[56,1024]{1,0:T(8,128)(2,1)}, bf16[56,1024]{1,0:T(8,128)(2,1)S(1)}, u32[]{:S(2)}, u32[]{:S(2)}) collective-permute-start(bf16[56,1024]{1,0:T(8,128)(2,1)} %bitcast.51), channel_id=1, source_target_pairs={{0,1},{1,2},{2,3},{3,0},{4,5},{5,6},{6,7},{7,4},{8,9},{9,10},{10,1... | collective-permute-start | bytes 344072 | tf_op jit(solution)/shard_map/ppermute | solution.py:42
  8.6 12.2 %collective-permute-start.1 = (bf16[56,1024]{1,0:T(8,128)(2,1)}, bf16[56,1024]{1,0:T(8,128)(2,1)S(1)}, u32[]{:S(2)}, u32[]{:S(2)}) collective-permute-start(bf16[56,1024]{1,0:T(8,128)(2,1)} %bitcast.52), channel_id=1, source_target_pairs={{0,2},{1,3},{2,0},{3,1},{4,6},{5,7},{6,4},{7,5},{8,10},{9,11},{10,... | collective-permute-start | bytes 344072 | tf_op jit(solution)/shard_map/ppermute | solution.py:42
  11.0 9.7 %collective-permute-start.2 = (bf16[56,1024]{1,0:T(8,128)(2,1)}, bf16[56,1024]{1,0:T(8,128)(2,1)S(1)}, u32[]{:S(2)}, u32[]{:S(2)}) collective-permute-start(bf16[56,1024]{1,0:T(8,128)(2,1)} %bitcast.53), channel_id=1, source_target_pairs={{0,3},{1,0},{2,1},{3,2},{4,7},{5,4},{6,5},{7,6},{8,11},{9,8},{10,9... | collective-permute-start | bytes 344072 | tf_op jit(solution)/shard_map/ppermute | solution.py:42
  13.0 7.7 %copy-start.29 = (f32[96,56]{0,1:T(8,128)}, f32[96,56]{0,1:T(8,128)S(1)}, u32[]{:S(2)}) copy-start(f32[96,56]{0,1:T(8,128)S(1)} %copy.22) | copy-start | bytes 64516
  13.1 4.9 %collective-permute-start.3 = (f32[56,96]{1,0:T(8,128)S(1)}, f32[56,96]{1,0:T(8,128)S(1)}, u32[]{:S(2)}, u32[]{:S(2)}) collective-permute-start(f32[56,96]{1,0:T(8,128)S(1)} %bitcast.59), channel_id=1, source_target_pairs={{0,1},{1,2},{2,3},{3,0},{4,5},{5,6},{6,7},{7,4},{8,9},{9,10},{10,1... | collective-permute-start | bytes 64520 | tf_op jit(solution)/shard_map/ppermute | solution.py:42
  13.4 4.6 %collective-permute-start.4 = (f32[56,96]{1,0:T(8,128)S(1)}, f32[56,96]{1,0:T(8,128)S(1)}, u32[]{:S(2)}, u32[]{:S(2)}) collective-permute-start(f32[56,96]{1,0:T(8,128)S(1)} %bitcast.60), channel_id=1, source_target_pairs={{0,2},{1,3},{2,0},{3,1},{4,6},{5,7},{6,4},{7,5},{8,10},{9,11},{10,... | collective-permute-start | bytes 64520 | tf_op jit(solution)/shard_map/ppermute | solution.py:42
  18.0 2.8 %copy-start.30 = (f32[56,96]{1,0:T(8,128)}, f32[56,96]{1,0:T(8,128)S(1)}, u32[]{:S(2)}) copy-start(f32[56,96]{1,0:T(8,128)S(1)} %collective-permute-done.3.refs_5_) | copy-start | bytes 64516
  18.0 2.7 %collective-permute-start.5 = (f32[56,96]{1,0:T(8,128)S(1)}, f32[56,96]{1,0:T(8,128)S(1)}, u32[]{:S(2)}, u32[]{:S(2)}) collective-permute-start(f32[56,96]{1,0:T(8,128)S(1)} %bitcast.61), channel_id=1, source_target_pairs={{0,3},{1,0},{2,1},{3,2},{4,7},{5,4},{6,5},{7,6},{8,11},{9,8},{10,9... | collective-permute-start | bytes 64520 | tf_op jit(solution)/shard_map/ppermute | solution.py:42
  18.0 2.8 %copy-start.31 = (f32[56,96]{1,0:T(8,128)}, f32[56,96]{1,0:T(8,128)S(1)}, u32[]{:S(2)}) copy-start(f32[56,96]{1,0:T(8,128)S(1)} %collective-permute-done.4.refs_6_) | copy-start | bytes 64516
  20.7 0.6 copy-start.32
  20.7 0.6 copy-start.24
  20.7 0.7 copy-start.25
  20.7 0.7 copy-start.26
  24.9 3.7 %copy-start.20 = (bf16[4,56,1024]{2,1,0:T(8,128)(2,1)S(1)}, bf16[4,56,1024]{2,1,0:T(8,128)(2,1)}, u32[]{:S(2)}) copy-start(bf16[4,56,1024]{2,1,0:T(8,128)(2,1)} %get-tuple-element.61) | copy-start | bytes 1376260
  24.9 8.9 %copy-start.22 = (f32[4,56,96]{2,1,0:T(8,128)S(1)}, f32[4,56,96]{2,1,0:T(8,128)}, u32[]{:S(2)}) copy-start(f32[4,56,96]{2,1,0:T(8,128)} %get-tuple-element.66) | copy-start | bytes 258052
  24.9 9.0 %copy-start.21 = (bf16[256,896]{1,0:T(8,128)(2,1)S(1)}, bf16[256,896]{1,0:T(8,128)(2,1)}, u32[]{:S(2)}) copy-start(bf16[256,896]{1,0:T(8,128)(2,1)} %param.11) | copy-start | bytes 1376260
  24.9 35.7 %all-to-all-start.1 = ((bf16[4,4,56,1024]{3,2,1,0:T(8,128)(2,1)}), bf16[4,4,56,1024]{3,2,1,0:T(8,128)(2,1)S(1)}, u32[]{:S(2)}, u32[]{:S(2)}) async-start(bf16[4,4,56,1024]{3,2,1,0:T(8,128)(2,1)} %broadcast_in_dim.11), calls=%async_computation.1 | async-start | bytes 3670016 | tf_op jit(solution)/shard_map/all_to_all | solution.py:34
  28.6 28.4 %collective-permute-start.6 = (bf16[4,56,1024]{2,1,0:T(8,128)(2,1)S(1)}, bf16[4,56,1024]{2,1,0:T(8,128)(2,1)}, u32[]{:S(2)}, u32[]{:S(2)}) collective-permute-start(bf16[4,56,1024]{2,1,0:T(8,128)(2,1)S(1)} %copy-done.20), channel_id=1, source_target_pairs={{0,4},{1,5},{2,6},{3,7},{4,8},{5,9},{6,10},{7,11},{8,12},{9,13},{1... | collective-permute-start | bytes 1376264 | tf_op jit(solution)/shard_map/ppermute | solution.py:42
  30.2 26.8 %collective-permute-start.7 = (bf16[4,56,1024]{2,1,0:T(8,128)(2,1)S(1)}, bf16[4,56,1024]{2,1,0:T(8,128)(2,1)}, u32[]{:S(2)}, u32[]{:S(2)}) collective-permute-start(bf16[4,56,1024]{2,1,0:T(8,128)(2,1)S(1)} %copy-done.20), channel_id=1, source_target_pairs={{0,8},{1,9},{2,10},{3,11},{4,12},{5,13},{6,14},{7,15},{8,0},{9,1},... | collective-permute-start | bytes 1376264 | tf_op jit(solution)/shard_map/ppermute | solution.py:42
  32.6 24.4 %collective-permute-start.8 = (bf16[4,56,1024]{2,1,0:T(8,128)(2,1)S(1)}, bf16[4,56,1024]{2,1,0:T(8,128)(2,1)}, u32[]{:S(2)}, u32[]{:S(2)}) collective-permute-start(bf16[4,56,1024]{2,1,0:T(8,128)(2,1)S(1)} %copy-done.20), channel_id=1, source_target_pairs={{0,12},{1,13},{2,14},{3,15},{4,0},{5,1},{6,2},{7,3},{8,4},{9,5},{1... | collective-permute-start | bytes 1376264 | tf_op jit(solution)/shard_map/ppermute | solution.py:42
  33.8 18.4 %collective-permute-start.10 = (f32[4,56,96]{2,1,0:T(8,128)S(1)}, f32[4,56,96]{2,1,0:T(8,128)S(1)}, u32[]{:S(2)}, u32[]{:S(2)}) collective-permute-start(f32[4,56,96]{2,1,0:T(8,128)S(1)} %copy-done.22), channel_id=1, source_target_pairs={{0,8},{1,9},{2,10},{3,11},{4,12},{5,13},{6,14},{7,15},{8,0},{9,1},... | collective-permute-start | bytes 258056 | tf_op jit(solution)/shard_map/ppermute | solution.py:42
  35.1 21.4 %collective-permute-start.11 = (f32[4,56,96]{2,1,0:T(8,128)S(1)}, f32[4,56,96]{2,1,0:T(8,128)S(1)}, u32[]{:S(2)}, u32[]{:S(2)}) collective-permute-start(f32[4,56,96]{2,1,0:T(8,128)S(1)} %copy-done.22), channel_id=1, source_target_pairs={{0,12},{1,13},{2,14},{3,15},{4,0},{5,1},{6,2},{7,3},{8,4},{9,5},{1... | collective-permute-start | bytes 258056 | tf_op jit(solution)/shard_map/ppermute | solution.py:42
  52.2 4.9 %copy-start.23 = (f32[4,56,96]{2,1,0:T(8,128)}, f32[4,56,96]{2,1,0:T(8,128)S(1)}, u32[]{:S(2)}) copy-start(f32[4,56,96]{2,1,0:T(8,128)S(1)} %collective-permute-done.10) | copy-start | bytes 258052
  52.2 4.9 %collective-permute-start.9 = (f32[4,56,96]{2,1,0:T(8,128)S(1)}, f32[4,56,96]{2,1,0:T(8,128)S(1)}, u32[]{:S(2)}, u32[]{:S(2)}) collective-permute-start(f32[4,56,96]{2,1,0:T(8,128)S(1)} %copy-done.22), channel_id=1, source_target_pairs={{0,4},{1,5},{2,6},{3,7},{4,8},{5,9},{6,10},{7,11},{8,12},{9,13},{1... | collective-permute-start | bytes 258056 | tf_op jit(solution)/shard_map/ppermute | solution.py:42
  56.5 0.7 copy-start.27
  57.0 0.6 copy-start.28
  60.6 1.3 copy-start
  61.9 24.2 %copy-start.18 = (bf16[256,896]{1,0:T(8,128)(2,1)S(1)}, bf16[256,896]{1,0:T(8,128)(2,1)}, u32[]{:S(2)}) copy-start(bf16[256,896]{1,0:T(8,128)(2,1)} %gate_hbm.1) | copy-start | bytes 1376260
  69.5 16.8 %copy-start.19 = (bf16[256,896]{1,0:T(8,128)(2,1)S(1)}, bf16[256,896]{1,0:T(8,128)(2,1)}, u32[]{:S(2)}) copy-start(bf16[256,896]{1,0:T(8,128)(2,1)} %up_hbm.1) | copy-start | bytes 1376260
  69.5 6.8 %collective-permute-start.18 = (bf16[48,256]{1,0:T(8,128)(2,1)}, bf16[48,256]{1,0:T(8,128)(2,1)S(1)}, u32[]{:S(2)}, u32[]{:S(2)}) collective-permute-start(bf16[48,256]{1,0:T(8,128)(2,1)} %get-tuple-element.83), channel_id=1, source_target_pairs={{0,16},{16,0},{32,48},{48,32},{64,80},{80,64},{96,112},{112,96},{1... | collective-permute-start | bytes 73736 | tf_op jit(solution)/shard_map/ppermute | solution.py:361
  77.8 17.7 %all-to-all-start.2 = ((bf16[8,48,256]{2,1,0:T(8,128)(2,1)}), bf16[8,48,256]{2,1,0:T(8,128)(2,1)S(1)}, u32[]{:S(2)}, u32[]{:S(2)}) async-start(bf16[8,48,256]{2,1,0:T(8,128)(2,1)} %broadcast_in_dim.12), calls=%async_computation.2 | async-start | bytes 393216 | tf_op jit(solution)/shard_map/all_to_all | solution.py:34
  86.0 0.7 copy-start.17
  86.7 1.0 copy-start.10
  87.8 1.0 copy-start.12
  88.8 8.8 %copy-start.1 = (bf16[4,4,56,1024]{3,2,1,0:T(8,128)(2,1)S(1)}, bf16[4,4,56,1024]{3,2,1,0:T(8,128)(2,1)}, u32[]{:S(2)}) copy-start(bf16[4,4,56,1024]{3,2,1,0:T(8,128)(2,1)} %copy-done) | copy-start | bytes 5505028
  88.8 8.8 %copy-start.2 = (bf16[1,3,256,896]{3,2,1,0:T(8,128)(2,1)S(1)}, bf16[1,3,256,896]{3,2,1,0:T(8,128)(2,1)}, u32[]{:S(2)}) copy-start(bf16[1,3,256,896]{3,2,1,0:T(8,128)(2,1)} %err_ref.3) | copy-start | bytes 4128772
  91.3 0.8 copy-start.15
  92.0 22.1 %collective-permute-start.12 = (bf16[224,1024]{1,0:T(8,128)(2,1)}, bf16[224,1024]{1,0:T(8,128)(2,1)}, u32[]{:S(2)}, u32[]{:S(2)}) collective-permute-start(bf16[224,1024]{1,0:T(8,128)(2,1)} %get-tuple-element.75), channel_id=1, source_target_pairs={{0,4},{1,5},{2,6},{3,7},{4,8},{5,9},{6,10},{7,11},{8,12},{9,13},{1... | collective-permute-start | bytes 1376264 | tf_op jit(solution)/shard_map/ppermute | solution.py:82
  93.7 20.5 %collective-permute-start.13 = (bf16[224,1024]{1,0:T(8,128)(2,1)}, bf16[224,1024]{1,0:T(8,128)(2,1)}, u32[]{:S(2)}, u32[]{:S(2)}) collective-permute-start(bf16[224,1024]{1,0:T(8,128)(2,1)} %get-tuple-element.76), channel_id=1, source_target_pairs={{0,12},{1,13},{2,14},{3,15},{4,0},{5,1},{6,2},{7,3},{8,4},{9,5},{1... | collective-permute-start | bytes 1376264 | tf_op jit(solution)/shard_map/ppermute | solution.py:82
  94.7 20.4 %collective-permute-start.14 = (bf16[224,1024]{1,0:T(8,128)(2,1)}, bf16[224,1024]{1,0:T(8,128)(2,1)}, u32[]{:S(2)}, u32[]{:S(2)}) collective-permute-start(bf16[224,1024]{1,0:T(8,128)(2,1)} %get-tuple-element.77), channel_id=1, source_target_pairs={{0,8},{1,9},{2,10},{3,11},{4,12},{5,13},{6,14},{7,15},{8,0},{9,1},... | collective-permute-start | bytes 1376264 | tf_op jit(solution)/shard_map/ppermute | solution.py:82
  95.6 8.9 %collective-permute-start.19 = (f32[48,256]{1,0:T(8,128)S(1)}, f32[48,256]{1,0:T(8,128)S(1)}, u32[]{:S(2)}, u32[]{:S(2)}) collective-permute-start(f32[48,256]{1,0:T(8,128)S(1)} %broadcast_multiply_fusion.p_mine_ref), channel_id=1, source_target_pairs={{0,16},{16,0},{32,48},{48,32},{64,80},{80,64},{96,112},{112,96},{1... | collective-permute-start | bytes 147464 | tf_op jit(solution)/shard_map/ppermute | solution.py:361
  97.6 1.5 copy-start.9
  99.1 1.0 copy-start.11
  100.2 1.0 copy-start.13
  101.2 1.0 copy-start.14
  104.4 1.0 copy-start.5
  104.4 1.9 %copy-start.7 = (f32[256,896]{1,0:T(8,128)}, f32[256,896]{1,0:T(8,128)S(1)}, u32[]{:S(2)}) copy-start(f32[256,896]{1,0:T(8,128)S(1)} %get-tuple-element.88.m2_ref) | copy-start | bytes 2752516
  104.4 24.8 %copy-start.16 = (bf16[224,1024]{1,0:T(8,128)(2,1)S(1)}, bf16[224,1024]{1,0:T(8,128)(2,1)}, u32[]{:S(2)}) copy-start(bf16[224,1024]{1,0:T(8,128)(2,1)} %copy-done.15) | copy-start | bytes 1376260
  105.4 0.9 copy-start.3
  106.3 1.4 collective-permute-start.20
  108.5 13.3 %all-to-all-start.3 = ((f32[16,24,128]{2,1,0:T(8,128)}), f32[16,24,128]{2,1,0:T(8,128)S(1)}, u32[]{:S(2)}, u32[]{:S(2)}) async-start(f32[16,24,128]{2,1,0:T(8,128)} %bitcast.28), calls=%async_computation.3 | async-start | bytes 393216 | tf_op jit(solution)/shard_map/all_to_all | solution.py:392
  122.4 14.4 %all-to-all-start.4 = ((f32[8,24,128]{2,1,0:T(8,128)}), f32[8,24,128]{2,1,0:T(8,128)S(1)}, u32[]{:S(2)}, u32[]{:S(2)}) async-start(f32[8,24,128]{2,1,0:T(8,128)} %broadcast_in_dim.13), calls=%async_computation.4 | async-start | bytes 196608 | tf_op jit(solution)/shard_map/all_to_all | solution.py:34
  129.3 25.6 %copy-start.4 = (f32[256,896]{1,0:T(8,128)S(1)}, f32[256,896]{1,0:T(8,128)}, u32[]{:S(2)}) copy-start(f32[256,896]{1,0:T(8,128)} %copy-done.3) | copy-start | bytes 2752516
  129.3 25.6 %copy-start.6 = (f32[256,896]{1,0:T(8,128)S(1)}, f32[256,896]{1,0:T(8,128)}, u32[]{:S(2)}) copy-start(f32[256,896]{1,0:T(8,128)} %copy-done.5) | copy-start | bytes 2752516
  129.3 25.6 %copy-start.8 = (f32[256,896]{1,0:T(8,128)S(1)}, f32[256,896]{1,0:T(8,128)}, u32[]{:S(2)}) copy-start(f32[256,896]{1,0:T(8,128)} %copy-done.7) | copy-start | bytes 2752516
  137.6 10.7 %all-to-all-start.5 = ((f32[16,24,128]{2,1,0:T(8,128)}), f32[16,24,128]{2,1,0:T(8,128)S(1)}, u32[]{:S(2)}, u32[]{:S(2)}) async-start(f32[16,24,128]{2,1,0:T(8,128)} %broadcast_in_dim.14), calls=%async_computation.5 | async-start | bytes 393216 | tf_op jit(solution)/shard_map/all_to_all | solution.py:34
  142.8 10.3 %collective-permute-start.15 = (bf16[56,1024]{1,0:T(8,128)(2,1)}, bf16[56,1024]{1,0:T(8,128)(2,1)}, u32[]{:S(2)}, u32[]{:S(2)}) collective-permute-start(bf16[56,1024]{1,0:T(8,128)(2,1)} %get-tuple-element.93), channel_id=1, source_target_pairs={{0,1},{1,2},{2,3},{3,0},{4,5},{5,6},{6,7},{7,4},{8,9},{9,10},{10,1... | collective-permute-start | bytes 344072 | tf_op jit(solution)/shard_map/ppermute | solution.py:90
  144.0 9.1 %collective-permute-start.16 = (bf16[56,1024]{1,0:T(8,128)(2,1)S(1)}, bf16[56,1024]{1,0:T(8,128)(2,1)}, u32[]{:S(2)}, u32[]{:S(2)}) collective-permute-start(bf16[56,1024]{1,0:T(8,128)(2,1)S(1)} %get-tuple-element.95), channel_id=1, source_target_pairs={{0,3},{1,0},{2,1},{3,2},{4,7},{5,4},{6,5},{7,6},{8,11},{9,8},{10,9... | collective-permute-start | bytes 344072 | tf_op jit(solution)/shard_map/ppermute | solution.py:90
  145.5 7.7 %collective-permute-start.17 = (bf16[56,1024]{1,0:T(8,128)(2,1)S(1)}, bf16[56,1024]{1,0:T(8,128)(2,1)}, u32[]{:S(2)}, u32[]{:S(2)}) collective-permute-start(bf16[56,1024]{1,0:T(8,128)(2,1)S(1)} %get-tuple-element.94), channel_id=1, source_target_pairs={{0,2},{1,3},{2,0},{3,1},{4,6},{5,7},{6,4},{7,5},{8,10},{9,11},{10,... | collective-permute-start | bytes 344072 | tf_op jit(solution)/shard_map/ppermute | solution.py:90
  148.2 6.6 %collective-permute-start.21 = (f32[384,128]{1,0:T(8,128)S(1)}, f32[384,128]{1,0:T(8,128)S(1)}, u32[]{:S(2)}, u32[]{:S(2)}) collective-permute-start(f32[384,128]{1,0:T(8,128)S(1)} %bitcast.42), channel_id=1, source_target_pairs={{0,16},{16,0},{32,48},{48,32},{64,80},{80,64},{96,112},{112,96},{1... | collective-permute-start | bytes 589832 | tf_op jit(solution)/shard_map/ppermute | solution.py:361

commit v3 on v2

v3 whole, which is shorter than its diff:
```python
import jax
import jax.numpy as jnp
from jax import lax
from jax.experimental import pallas as pl
from jax.experimental.pallas import tpu as pltpu
from jax.sharding import PartitionSpec as P

BF = jnp.bfloat16
F32 = jnp.float32
SIDE = 4
DEPTH = 8
RANK = 32
ROWS = 3 * RANK
HALF = ROWS // 2
LANES = 128
TILES = HALF * 1024 // (8 * LANES)
MIB = 1 << 20

X_GROUPS = [[y * SIDE + x for x in range(SIDE)] for y in range(SIDE)]
Y_GROUPS = [[y * SIDE + x for y in range(SIDE)] for x in range(SIDE)]
CORE_PAIR = [(i, i ^ 1) for i in range(2 * DEPTH)]
Z_GROUPS = [[z * 2 + c for z in range(DEPTH)] for c in range(2)]


def x_ring(k):
    return [(y * SIDE + x, y * SIDE + (x + k) % SIDE) for y in range(SIDE) for x in range(SIDE)]


def y_ring(k):
    return [(y * SIDE + x, ((y + k) % SIDE) * SIDE + x) for y in range(SIDE) for x in range(SIDE)]


def spread(value, axis, groups, size):
    return lax.all_to_all(
        jnp.broadcast_to(value[None], (size,) + value.shape), axis, 0, 0, tiled=True, axis_index_groups=groups
    )


def ring_pieces(value, ring):
    near = [value] + [None] * 3
    for k in (1, 3, 2):
        near[k] = lax.ppermute(value, "tensor", ring(SIDE - k))
    return near


def pack_kernel(x_hbm, dy_hbm, q_ref, x_ref, dy_ref, sems):
    tokens = x_hbm.shape[1]
    copies = [pltpu.make_async_copy(x_hbm, x_ref.at[:, pl.ds(0, tokens)], sems.at[0])]
    for i in range(SIDE):
        copies.append(pltpu.make_async_copy(dy_hbm, dy_ref.at[i, :, pl.ds(0, tokens)], sems.at[1 + i]))
    for copy in copies:
        copy.start()
    high, low = split(q_ref[...].T)
    both = [[half[:, k * RANK : (k + 1) * RANK] for half in (high, low)] for k in range(3)]
    x_ref[:, tokens:] = jnp.concatenate(both[0] + both[1], axis=1)
    tail = jnp.concatenate(both[2] + [jnp.zeros((high.shape[0], LANES - 2 * RANK), BF)], axis=1)
    for i in range(SIDE):
        dy_ref[i, :, tokens:] = tail
    for copy in copies:
        copy.wait()


def pack(x_part, dy_part, q_rows):
    vmem = pl.BlockSpec(memory_space=pltpu.VMEM)
    anywhere = pl.BlockSpec(memory_space=pl.ANY)
    rows, tokens = x_part.shape
    return pl.pallas_call(
        pack_kernel,
        out_shape=(
            jax.ShapeDtypeStruct((rows, tokens + LANES), BF),
            jax.ShapeDtypeStruct((SIDE, rows, tokens + LANES), BF),
        ),
        in_specs=[anywhere, anywhere, vmem],
        out_specs=(vmem, vmem),
        scratch_shapes=[pltpu.SemaphoreType.DMA((1 + SIDE,))],
        compiler_params=pltpu.CompilerParams(vmem_limit_bytes=58 * MIB),
    )(x_part, dy_part, q_rows)


def order_kernel(place_ref, p0_ref, p1_ref, p2_ref, p3_ref, out_ref, sems):
    copies = [
        pltpu.make_async_copy(ref, out_ref.at[lax.rem(place_ref[0] + i, SIDE)], sems.at[i])
        for i, ref in enumerate((p0_ref, p1_ref, p2_ref, p3_ref))
    ]
    for copy in copies:
        copy.start()
    for copy in copies:
        copy.wait()


def order(position, pieces):
    anywhere = pl.BlockSpec(memory_space=pl.ANY)
    return pl.pallas_call(
        order_kernel,
        out_shape=jax.ShapeDtypeStruct((SIDE,) + pieces[0].shape, pieces[0].dtype),
        in_specs=[pl.BlockSpec(memory_space=pltpu.SMEM)] + [anywhere] * SIDE,
        out_specs=pl.BlockSpec(memory_space=pltpu.VMEM),
        scratch_shapes=[pltpu.SemaphoreType.DMA((SIDE,))],
        compiler_params=pltpu.CompilerParams(vmem_limit_bytes=20 * MIB),
    )(position.reshape(1), *pieces)


def gather_all(x_part, dy_parts, me):
    rows = SIDE * x_part.shape[0]
    dy_col = lax.all_to_all(dy_parts, "tensor", 0, 0, tiled=True, axis_index_groups=Y_GROUPS)
    near, dy_col = lax.optimization_barrier((ring_pieces(x_part, x_ring), dy_col))
    x_row, dy_col = lax.optimization_barrier((order(me % SIDE, near), dy_col))
    dy_all = spread(dy_col, "tensor", X_GROUPS, SIDE)
    far, dy_all = lax.optimization_barrier((ring_pieces(x_row, y_ring), dy_all))
    return [p.reshape(rows, -1) for p in far], dy_all.reshape(SIDE * rows, -1)


def swap_order(value):
    blocks = value.reshape((SIDE, SIDE, -1) + value.shape[1:])
    return jnp.swapaxes(blocks, 0, 1).reshape(value.shape)


def send_blocks(blocks):
    return [blocks[0]] + [lax.ppermute(blocks[k], "tensor", y_ring(k)) for k in (1, 3, 2)]


def parts_kernel(place_ref, g0_ref, g1_ref, g2_ref, g3_ref, _, o0_ref, o1_ref, o2_ref, o3_ref):
    for k, out_ref in enumerate((o0_ref, o1_ref, o2_ref, o3_ref)):
        at = lax.rem(place_ref[0] + k, SIDE)
        total = sum(ref[at].astype(F32) for ref in (g0_ref, g1_ref, g2_ref, g3_ref))
        out_ref[...] = total.astype(out_ref.dtype)


def send_parts(got, position, token):
    vmem = pl.BlockSpec(memory_space=pltpu.VMEM)
    rows, tokens = got[0].shape
    parts = pl.pallas_call(
        parts_kernel,
        out_shape=(jax.ShapeDtypeStruct((rows // SIDE, tokens), BF),) * SIDE,
        in_specs=[pl.BlockSpec(memory_space=pltpu.SMEM)] + [vmem] * (SIDE + 1),
        out_specs=(vmem,) * SIDE,
        compiler_params=pltpu.CompilerParams(vmem_limit_bytes=20 * MIB),
    )(position.reshape(1), *[v.reshape(SIDE, -1, tokens) for v in got], token)
    return [parts[0]] + [lax.ppermute(parts[k], "tensor", x_ring(k)) for k in (1, 3, 2)]


def split(value):
    high = value.astype(BF)
    return high, (value - high.astype(F32)).astype(BF)


def dot(a, b, ca, cb):
    return lax.dot_general(a, b, (((ca,), (cb,)), ((), ())), preferred_element_type=F32)


def dot3(a, b, ca, cb):
    a_high, a_low = split(a)
    b_high, b_low = split(b)
    return dot(
        jnp.concatenate([a_high, a_high, a_low], axis=ca), jnp.concatenate([b_high, b_low, b_high], axis=cb), ca, cb
    )


def own_half(core, value):
    low, high = value[:HALF], value[HALF:]
    first = core == 0
    return jnp.where(first, low, high), jnp.where(first, high, low)


def whole(core, mine, other):
    first = core == 0
    return jnp.concatenate([jnp.where(first, mine, other), jnp.where(first, other, mine)])


def prepare_kernel(gate_ref, up_ref, down_ref, err_ref, left_ref, both_ref, token_ref):
    hid, width = gate_ref.shape
    gate, up, down = gate_ref[...], up_ref[...], down_ref[...].astype(F32)
    block = width // (SIDE * SIDE)
    left_ref[0] = gate
    left_ref[1] = up
    left_ref[2] = jnp.concatenate(
        [down[:, (y * SIDE + x) * block : (y * SIDE + x + 1) * block] for x in range(SIDE) for y in range(SIDE)],
        axis=1,
    ).astype(BF)
    for k in range(3):
        left_ref[3 + k] = err_ref[0, k]
    both_ref[:, :hid] = gate.astype(F32).T.astype(BF)
    both_ref[:, hid:] = up.astype(F32).T.astype(BF)
    token_ref[...] = jnp.zeros_like(token_ref)


def prepare(w_gate, w_up, w_down, error_in):
    vmem = pl.BlockSpec(memory_space=pltpu.VMEM)
    hid, width = w_gate.shape
    return pl.pallas_call(
        prepare_kernel,
        out_shape=(
            jax.ShapeDtypeStruct((6, hid, width), BF),
            jax.ShapeDtypeStruct((width, 2 * hid), BF),
            jax.ShapeDtypeStruct((8, LANES), F32),
        ),
        in_specs=[vmem] * 4,
        out_specs=(vmem,) * 3,
        compiler_params=pltpu.CompilerParams(vmem_limit_bytes=20 * MIB),
    )(w_gate, w_up, w_down, error_in)


def backward_kernel(place_ref, p0_ref, p1_ref, p2_ref, p3_ref, dy_ref, w_ref,
                    gate_grad_ref, up_grad_ref, hidden_ref, mine_ref, theirs_ref, x_ref):
    rows = p0_ref.shape[0]
    hid, tokens = hidden_ref.shape
    for i, ref in enumerate((p0_ref, p1_ref, p2_ref, p3_ref)):
        at = pl.multiple_of(lax.rem(place_ref[0] + i, SIDE) * rows, 16)
        x_ref[pl.ds(at, rows), :] = ref[...]
    q_x = x_ref[:, tokens:]
    q_dy = dy_ref[:, tokens : tokens + 2 * RANK]
    q_rows = q_x.astype(F32).T.astype(BF)
    q_both = [q_rows[: 2 * RANK], q_rows[2 * RANK :], q_dy.astype(F32).T.astype(BF)]
    sums = [jnp.zeros((2 * RANK, hid), F32)] * 3
    chunk = 256
    for start in range(0, tokens, chunk):
        span = slice(start, start + chunk)
        x, dy = x_ref[:, span], dy_ref[:, span]
        gate_pre = dot(w_ref[0], x, 1, 0)
        up_pre = dot(w_ref[1], x, 1, 0)
        hidden_grad = dot(w_ref[2], dy, 1, 0)
        gate_sig = jax.nn.sigmoid(gate_pre)
        gate_act = gate_pre * gate_sig
        hidden = (gate_act * up_pre).astype(BF)
        gate_grad = (hidden_grad * up_pre * gate_sig * (1.0 + gate_pre * (1.0 - gate_sig))).astype(BF)
        up_grad = (hidden_grad * gate_act).astype(BF)
        gate_grad_ref[:, span] = gate_grad
        up_grad_ref[:, span] = up_grad
        hidden_ref[:, span] = hidden
        for k, (left, right) in enumerate(((gate_grad, x), (up_grad, x), (hidden, dy))):
            both = dot(q_both[k], right, 1, 0)
            halves = jnp.concatenate(split(both[:RANK] + both[RANK:]))
            sums[k] = sums[k] + dot(halves, left, 1, 1)
    block = rows // SIDE
    q_plain = q_dy.astype(F32)
    q_plain = jnp.concatenate(
        [q_plain[(x * SIDE + y) * block : (x * SIDE + y + 1) * block] for y in range(SIDE) for x in range(SIDE)]
    ).astype(BF)
    errors = [
        dot(w_ref[3 + k], q, 1, 0) for k, q in enumerate((q_x[:, : 2 * RANK], q_x[:, 2 * RANK :], q_plain))
    ]
    error_p = jnp.concatenate([both[:, :RANK] + both[:, RANK:] for both in errors], axis=1).T
    p = jnp.concatenate([both[:RANK] + both[RANK:] for both in sums]) + error_p
    mine, theirs = own_half(place_ref[1], p)
    mine_ref[...] = mine
    theirs_ref[...] = theirs.astype(BF)


def backward(place, pieces, dy_all, weights):
    hid, width = weights.shape[1:]
    wide = dy_all.shape[1]
    tokens = wide - LANES
    vmem = pl.BlockSpec(memory_space=pltpu.VMEM)
    grads = jax.ShapeDtypeStruct((hid, tokens), BF)
    return pl.pallas_call(
        backward_kernel,
        out_shape=(
            grads,
            grads,
            grads,
            jax.ShapeDtypeStruct((HALF, hid), F32),
            jax.ShapeDtypeStruct((HALF, hid), BF),
            jax.ShapeDtypeStruct((width, wide), BF),
        ),
        in_specs=[pl.BlockSpec(memory_space=pltpu.SMEM)] + [vmem] * 6,
        out_specs=(vmem,) * 6,
        compiler_params=pltpu.CompilerParams(vmem_limit_bytes=20 * MIB),
        cost_estimate=pl.CostEstimate(flops=6 * hid * width * tokens, bytes_accessed=8 * MIB, transcendentals=0),
    )(place, *pieces, dy_all, weights)


def products_kernel(place_ref, w_ref, gate_grad_ref, up_grad_ref, hidden_ref, x_ref, dy_ref, left_ref, _,
                    t0_ref, t1_ref, t2_ref, t3_ref, m0_ref, m1_ref, m2_ref, token_ref):
    tokens = hidden_ref.shape[1]
    gate_grad, up_grad = gate_grad_ref[...], up_grad_ref[...]
    grads = jnp.concatenate([gate_grad, up_grad])
    rows = t0_ref.shape[0]
    for i, ref in enumerate((t0_ref, t1_ref, t2_ref, t3_ref)):
        at = pl.multiple_of(lax.rem(place_ref[0] + i, SIDE) * rows, 16)
        ref[...] = dot(w_ref[pl.ds(at, rows), :], grads, 1, 0).astype(BF)
    x = x_ref[:, :tokens]
    m0_ref[...] = dot(gate_grad, x, 1, 1) + left_ref[3].astype(F32)
    m1_ref[...] = dot(up_grad, x, 1, 1) + left_ref[4].astype(F32)
    swapped = dot(hidden_ref[...], dy_ref[:, :tokens], 1, 1)
    block = rows // SIDE
    parts = [
        swapped[:, (x * SIDE + y) * block : (x * SIDE + y + 1) * block] for y in range(SIDE) for x in range(SIDE)
    ]
    m2_ref[...] = jnp.concatenate(parts, axis=1) + left_ref[5].astype(F32)
    token_ref[...] = jnp.zeros_like(token_ref)


def products(place, w_both, grads, x_all, dy_all, weights, other):
    vmem = pl.BlockSpec(memory_space=pltpu.VMEM)
    hid, tokens = grads[0].shape
    width = w_both.shape[0]
    out = pl.pallas_call(
        products_kernel,
        out_shape=(jax.ShapeDtypeStruct((width // SIDE, tokens), BF),) * SIDE
        + (jax.ShapeDtypeStruct((hid, width), F32),) * 3
        + (jax.ShapeDtypeStruct((8, LANES), F32),),
        in_specs=[pl.BlockSpec(memory_space=pltpu.SMEM)] + [vmem] * 8,
        out_specs=(vmem,) * (SIDE + 4),
        compiler_params=pltpu.CompilerParams(vmem_limit_bytes=20 * MIB),
        cost_estimate=pl.CostEstimate(flops=10 * hid * width * tokens, bytes_accessed=12 * MIB, transcendentals=0),
    )(place, w_both, *grads, x_all, dy_all, weights, other)
    return out[:SIDE], out[SIDE : SIDE + 3], out[-1]


def mean_kernel(value_ref, _, out_ref):
    total = value_ref[0].astype(F32)
    for i in range(1, value_ref.shape[0]):
        total = total + value_ref[i].astype(F32)
    out_ref[...] = total * (0.5 / value_ref.shape[0])


def mean(value, token):
    vmem = pl.BlockSpec(memory_space=pltpu.VMEM)
    return pl.pallas_call(
        mean_kernel,
        out_shape=jax.ShapeDtypeStruct(value.shape[1:], F32),
        in_specs=[vmem, vmem],
        out_specs=vmem,
        compiler_params=pltpu.CompilerParams(vmem_limit_bytes=20 * MIB),
    )(value, token)


def sketch_kernel(core_ref, p_mine_ref, p_other_ref, m0_ref, m1_ref, m2_ref, mine_ref, theirs_ref, gram_ref):
    core = core_ref[0]
    p = whole(core, p_mine_ref[...], p_other_ref[...])
    rows, grams = [], []
    for k, m_ref in enumerate((m0_ref, m1_ref, m2_ref)):
        p_k = p[k * RANK : (k + 1) * RANK]
        p_high, p_low = split(p_k)
        m_high, m_low = split(m_ref[...])
        both = dot(jnp.concatenate([p_high, p_low]), m_high, 1, 0)
        term = both[:RANK] + both[RANK:] + dot(p_high, m_low, 1, 0)
        grams.append(dot3(p_k, p_k, 1, 1))
        rows.append(jnp.concatenate([term, jnp.zeros((RANK, LANES), F32)], axis=1))
    gram = jnp.concatenate(grams)
    gram_ref[...] = jnp.concatenate([gram[i * 24 : (i + 1) * 24] for i in range(4)], axis=1)
    mine, theirs = own_half(core, jnp.concatenate(rows))
    for i in range(HALF // 8):
        for j in range(8):
            tile = (i * 8 + j) * 8
            rows, cols = slice(i * 8, i * 8 + 8), slice(j * LANES, (j + 1) * LANES)
            mine_ref[tile : tile + 8, :] = mine[rows, cols]
            theirs_ref[tile : tile + 8, :] = theirs[rows, cols]


def sketch(core, p_mine, p_other, matrices):
    vmem = pl.BlockSpec(memory_space=pltpu.VMEM)
    out = jax.ShapeDtypeStruct((TILES * 8, LANES), F32)
    return pl.pallas_call(
        sketch_kernel,
        out_shape=(out, out, jax.ShapeDtypeStruct((24, LANES), F32)),
        in_specs=[pl.BlockSpec(memory_space=pltpu.SMEM)] + [vmem] * 5,
        out_specs=(vmem,) * 3,
        compiler_params=pltpu.CompilerParams(vmem_limit_bytes=20 * MIB),
    )(core, p_mine, p_other, *matrices)


def ortho_kernel(core_ref, gram_ref, p_mine_ref, p_other_ref, _, inverse_ref, p_ortho_ref):
    gram = gram_ref[...]
    gram = jnp.concatenate([gram[:, i * RANK : (i + 1) * RANK] for i in range(4)])
    gram = jnp.stack([gram[k * RANK : (k + 1) * RANK] for k in range(3)])
    rows = lax.broadcasted_iota(jnp.int32, (1, RANK, RANK), 1)
    cols = lax.broadcasted_iota(jnp.int32, (1, RANK, RANK), 2)
    eye = jnp.broadcast_to(jnp.where(rows == cols, 1.0, 0.0), gram.shape)
    work = jnp.concatenate([gram, eye], axis=2)
    below = lax.broadcasted_iota(jnp.int32, (1, RANK, 1), 1)
    for k in range(RANK):
        pivot = work[:, k : k + 1, :]
        scale = 1.0 / pivot[:, :, k : k + 1]
        factor = jnp.where(below > k, work[:, :, k : k + 1] * scale, 0.0)
        work = work - factor * pivot
    diag = jnp.sum(jnp.where(rows == cols, work[:, :, :RANK], 0.0), axis=2, keepdims=True)
    inverse = work[:, :, RANK:] * lax.rsqrt(diag)
    inverse_ref[...] = inverse
    p = whole(core_ref[0], p_mine_ref[...], p_other_ref[...])
    for k in range(3):
        part = slice(k * RANK, (k + 1) * RANK)
        p_ortho_ref[part, :] = dot3(inverse[k], p[part], 1, 0)


def ortho(core, gram, p_mine, p_other, token):
    vmem = pl.BlockSpec(memory_space=pltpu.VMEM)
    return pl.pallas_call(
        ortho_kernel,
        out_shape=(
            jax.ShapeDtypeStruct((3, RANK, RANK), F32),
            jax.ShapeDtypeStruct((ROWS, p_mine.shape[1]), F32),
        ),
        in_specs=[pl.BlockSpec(memory_space=pltpu.SMEM)] + [vmem] * 4,
        out_specs=(vmem, vmem),
        cost_estimate=pl.CostEstimate(flops=MIB * 4096, bytes_accessed=MIB, transcendentals=0),
    )(core, gram, p_mine, p_other, token)


def finish_kernel(place_ref, s_mine_ref, s_other_ref, inverse_ref, p_ortho_ref, m0_hbm, m1_hbm, m2_hbm,
                  error_hbm, q_ref, m_ref, error_ref, sems):
    copies = [pltpu.make_async_copy(m, m_ref.at[k], sems.at[k]) for k, m in enumerate((m0_hbm, m1_hbm, m2_hbm))]
    for copy in copies:
        copy.start()
    width = m_ref.shape[2]

    def rows_of(ref):
        return jnp.concatenate(
            [
                jnp.concatenate([ref[(i * 8 + j) * 8 : (i * 8 + j) * 8 + 8, :] for j in range(7)], axis=1)
                for i in range(HALF // 8)
            ]
        )

    s = whole(place_ref[0], rows_of(s_mine_ref), rows_of(s_other_ref))
    stores, q_rows = [], []
    for k in range(3):
        part = slice(k * RANK, (k + 1) * RANK)
        q_new = dot3(inverse_ref[k], s[part], 1, 0)
        q_rows.append(q_new)
        copies[k].wait()
        error_ref[k] = (m_ref[k] - dot3(p_ortho_ref[part, :], q_new, 0, 0)).astype(BF)
        stores.append(pltpu.make_async_copy(error_ref.at[k], error_hbm.at[0, k], sems.at[3 + k]))
        stores[k].start()
    shard = q_ref.shape[1]
    at = place_ref[1] * shard
    q_ref[...] = pltpu.roll(jnp.concatenate(q_rows), lax.rem(width - at, width), 1)[:, :shard]
    for copy in stores:
        copy.wait()


def finish(place, s_mine, s_other, inverse, p_ortho, matrices, shard):
    vmem = pl.BlockSpec(memory_space=pltpu.VMEM)
    hbm = pl.BlockSpec(memory_space=pltpu.HBM)
    hid, width = matrices[0].shape
    return pl.pallas_call(
        finish_kernel,
        out_shape=(jax.ShapeDtypeStruct((1, 3, hid, width), BF), jax.ShapeDtypeStruct((ROWS, shard), F32)),
        in_specs=[pl.BlockSpec(memory_space=pltpu.SMEM)] + [vmem] * 4 + [hbm] * 3,
        out_specs=(hbm, vmem),
        scratch_shapes=[
            pltpu.VMEM((3, hid, width), F32),
            pltpu.VMEM((3, hid, width), BF),
            pltpu.SemaphoreType.DMA((6,)),
        ],
        compiler_params=pltpu.CompilerParams(vmem_limit_bytes=20 * MIB),
    )(place, s_mine, s_other, inverse, p_ortho, *matrices)


def after(values, other):
    return lax.optimization_barrier((values, other))[0]


def swap_core(value):
    return lax.ppermute(value, "dp", CORE_PAIR)


def z_ring(k):
    return [(z * 2 + c, (z + k) % DEPTH * 2 + c) for z in range(DEPTH) for c in range(2)]


def z_ring_swap():
    return [(z * 2 + c, (z ^ 1) * 2 + c) for z in range(DEPTH) for c in range(2)]


def take_kernel(value_ref, _, out_ref):
    out_ref[...] = value_ref[...]


def take(value, token):
    vmem = pl.BlockSpec(memory_space=pltpu.VMEM)
    return pl.pallas_call(
        take_kernel,
        out_shape=jax.ShapeDtypeStruct(value.shape, value.dtype),
        in_specs=[vmem, vmem],
        out_specs=vmem,
        compiler_params=pltpu.CompilerParams(vmem_limit_bytes=20 * MIB),
    )(value, token)


def add(values, token, scale, kind=F32):
    vmem = pl.BlockSpec(memory_space=pltpu.VMEM)

    def kernel(*refs):
        refs[-1][...] = (sum(ref[...].astype(F32) for ref in refs[:-2]) * scale).astype(kind)

    return pl.pallas_call(
        kernel,
        out_shape=jax.ShapeDtypeStruct(values[0].shape, kind),
        in_specs=[vmem] * (len(values) + 1),
        out_specs=vmem,
        compiler_params=pltpu.CompilerParams(vmem_limit_bytes=20 * MIB),
    )(*values, token)


def close_kernel(*refs):
    refs[-2][...] = sum(ref[...].astype(F32) for ref in refs[:-2]).astype(BF)
    refs[-1][...] = jnp.zeros_like(refs[-1])


def close(values):
    vmem = pl.BlockSpec(memory_space=pltpu.VMEM)
    return pl.pallas_call(
        close_kernel,
        out_shape=(jax.ShapeDtypeStruct(values[0].shape, BF), jax.ShapeDtypeStruct((8, LANES), F32)),
        in_specs=[vmem] * len(values),
        out_specs=(vmem, vmem),
        compiler_params=pltpu.CompilerParams(vmem_limit_bytes=20 * MIB),
    )(*values)


def per_device(hidden_in, out_grad, w_gate, w_up, w_down, error_in, q_init):
    n_workers = lax.axis_size("dp")
    n_tensor = lax.axis_size("tensor")
    me = lax.axis_index("tensor")
    y, x = me // SIDE, me % SIDE
    core = lax.axis_index("dp") % 2
    shard = hidden_in.shape[1]

    weights, w_both, _ = prepare(w_gate, w_up, w_down, error_in)
    x_part, dy_parts = pack(hidden_in.T, out_grad.T, q_init.reshape(ROWS, shard))
    pieces, dy_all = gather_all(x_part, dy_parts, me)
    spot = jnp.stack([y, core])
    gate_grad, up_grad, hidden, p_mine, p_theirs, x_all = backward(spot, pieces, dy_all, weights)
    core = core.reshape(1)
    p_pair = (p_mine + swap_core(p_theirs).astype(F32)).astype(BF)
    p_next = lax.ppermute(p_pair, "dp", z_ring_swap())
    blocks, matrices, token = products(
        spot, w_both, (gate_grad, up_grad, hidden), x_all, dy_all, weights, p_pair
    )
    p_two = add((p_pair, p_next), token, 1.0)
    p_half = add([p_two] + [lax.ppermute(p_two, "dp", z_ring(k)) for k in (4, 2, 6)], token, 1.0 / n_workers)
    p_other = swap_core(p_half)
    got = send_blocks(blocks)
    s_mine, s_theirs, gram = sketch(core, p_half, p_other, matrices)
    s_pair = (s_mine + swap_core(s_theirs)).reshape(n_tensor, -1, LANES)
    gram = jnp.broadcast_to(gram[None], (n_tensor,) + gram.shape)
    sums = jnp.sum(lax.all_to_all(jnp.concatenate([s_pair, gram], axis=1), "tensor", 0, 0, tiled=True), axis=0)
    s_part, gram = sums[: s_pair.shape[1]], sums[s_pair.shape[1] :]
    s_all = spread(s_part, "dp", Z_GROUPS, DEPTH)
    inverse, p_ortho = ortho(core, gram, p_half, p_other, gram)
    s_part = mean(s_all, inverse)
    got = send_parts(got, x, gram)
    input_grad, token = close(got)
    input_grad = input_grad.T
    s_half = take(spread(s_part, "tensor", None, n_tensor).reshape(-1, LANES), token)
    error_out, q_out = finish(
        jnp.stack([core[0], me]), s_half, swap_core(s_half), inverse, p_ortho, matrices, shard
    )
    return (input_grad, error_out, q_out.reshape(q_init.shape))


def solution(mesh):
    in_specs = (
        P("dp", "tensor"),
        P("dp", "tensor"),
        P("tensor", None),
        P("tensor", None),
        P("tensor", None),
        P("dp", None, "tensor", None),
        P(None, None, "tensor"),
    )
    out_specs = (P("dp", "tensor"), P("dp", None, "tensor", None), P(None, None, "tensor"))
    return jax.shard_map(
        per_device, mesh=mesh, in_specs=in_specs, out_specs=out_specs, check_vma=False
    )
```

time: 163 us -> 143 us (0.88)
  starting transfers between devices: 68.6 us -> 61.3 us
  local copies, waits for them, and re-layouts: 21.7 us -> 14.6 us
  other arithmetic: 6.62 us -> 0.99 us
  Pallas kernels: 23.4 us -> 25.4 us
    all_to_all x5 -> x3, starting transfers between devices: 27.3 us -> 12.6 us  [spread(): lax.all_to_all(jnp.broadcast_to(value[None], (size,) + value.shape), axis...]
    ppermute x18 -> x16, starting transfers between devices: 23 us -> 29 us  [the longest x6 9.36 us: ring_pieces(): near[k] = lax.ppermute(value, 'tensor', ring(SIDE - k))]
    all_to_all x1 -> x2, starting transfers between devices: 5.61 us -> 11.5 us  [the longest x1 6.49 us: per_device(): lax.all_to_all(jnp.concatenate([s_pair, gram], axis=1), 'tensor', 0, 0, t...]
    pallas_call x5 -> x12, Pallas kernels: 10.1 us -> 15.9 us  [the longest x1 4.41 us: ortho(): pl.pallas_call(ortho_kernel, out_shape=(jax.ShapeDtypeStruct((3, RANK, RA...]
    ppermute x4, starting transfers between devices: 12.7 us -> 8.13 us  [swap_core(): return lax.ppermute(value, 'dp', CORE_PAIR)]
    all_to_all x5 -> x3, waiting for transfers between devices: 6.32 us -> 3.24 us  [spread(): lax.all_to_all(jnp.broadcast_to(value[None], (size,) + value.shape), axis...]
    convert_element_type x1 -> x0, other arithmetic: 2.54 us -> none  [scatter_sum(): total = sum((v.astype(F32) for v in got)).astype(blocks[0].dtype)]
    broadcast_in_dim x5 -> x3, local copies, waits for them, and re-layouts: 5.26 us -> 2.83 us  [spread(): jnp.broadcast_to(value[None], (size,) + value.shape)]
  transfers between devices with their start and end apart: 28 -> 25, of which waited for: 12 -> 16; matrix products, arithmetic and copies ran while one was open for 6% -> 1% of each run, Pallas kernels for 5% -> 8%
where the time goes in v3:
time: 143 us; the launch traced here: 142 us
  starting transfers between devices  61.3 us (43%)
  waiting for transfers between devices  38.7 us (27%)
  Pallas kernels  25.4 us (18%)
  local copies, waits for them, and re-layouts  14.6 us (10%)
    ppermute x6, waiting for transfers between devices, ring_pieces(): near[k] = lax.ppermute(value, 'tensor', ring(SIDE - k))  18.3 us
    all_to_all x3, starting transfers between devices, spread(): lax.all_to_all(jnp.broadcast_to(value[None], (size,) + value.shape), axis...  12.6 us
    unnamed x44, local copies, waits for them, and re-layouts  11.1 us
    ppermute x6, starting transfers between devices, ring_pieces(): near[k] = lax.ppermute(value, 'tensor', ring(SIDE - k))  9.36 us
    ppermute x3, starting transfers between devices, per_device(): lax.ppermute(p_two, 'dp', z_ring(k))  8.45 us
    ppermute x4, starting transfers between devices, swap_core(): return lax.ppermute(value, 'dp', CORE_PAIR)  8.13 us
    all_to_all x1, starting transfers between devices, per_device(): lax.all_to_all(jnp.concatenate([s_pair, gram], axis=1), 'tensor', 0, 0, t...  6.49 us
    pallas_call x1, Pallas kernels, backward(): pl.pallas_call(backward_kernel, out_shape=(grads, grads, grads, jax.Shape...  5.61 us
  transfers between devices with their start and end apart: 25, of which 16 were waited for; matrix products, arithmetic and copies ran while one was open for 1% of the time, Pallas kernels for 8%

profile of v3, /device:TPU:1, one launch (start us, length us, event | category | flops | bytes accessed | tf_op | source)
XLA Modules:
  0.0 142.0 jit_solution(8984262667023781454)
XLA Ops:
  0.6 3.0 %shard_map.95 = (bf16[56,1152]{1,0:T(8,128)(2,1)}, bf16[4,56,1152]{2,1,0:T(8,128)(2,1)}) custom-call(bf16[56,1024]{1,0:T(8,128)(2,1)} %bitcast.27, bf16[56,1024]{1,0:T(8,128)(2,1)} %bitcast.28, f32[96,56]{1,0:T(8,128)} %bitcast.29), custom_call_target="tpu_custom_call" | custom-call | tf_op jit(solution)/shard_map/pallas_call | solution.py:67
  3.6 5.0 %all-to-all-start = ((bf16[4,56,1152]{2,1,0:T(8,128)(2,1)}), bf16[4,56,1152]{2,1,0:T(8,128)(2,1)S(1)}, u32[]{:S(2)}, u32[]{:S(2)}) async-start(bf16[4,56,1152]{2,1,0:T(8,128)(2,1)} %get-tuple-element.48), calls=%async_computation | async-start | bytes 1032192 | tf_op jit(solution)/shard_map/all_to_all | solution.py:105
  8.6 1.2 collective-permute-start.2
  9.8 2.5 %collective-permute-start.1 = (bf16[56,1152]{1,0:T(8,128)(2,1)}, bf16[56,1152]{1,0:T(8,128)(2,1)S(1)}, u32[]{:S(2)}, u32[]{:S(2)}) collective-permute-start(bf16[56,1152]{1,0:T(8,128)(2,1)} %get-tuple-element.49.p0_ref), channel_id=1, source_target_pairs={{0,2},{1,3},{2,0},{3,1},{4,6},{5,7},{6,4},{7,5},{8,10},{9,11},{10,... | collective-permute-start | bytes 387080 | tf_op jit(solution)/shard_map/ppermute | solution.py:42
  12.3 1.2 collective-permute-start
  13.4 0.4 collective-permute-done.2.p3_ref
  13.8 4.0 %collective-permute-done.1.p2_ref = bf16[56,1152]{1,0:T(8,128)(2,1)S(1)} collective-permute-done((bf16[56,1152]{1,0:T(8,128)(2,1)}, bf16[56,1152]{1,0:T(8,128)(2,1)S(1)}, u32[]{:S(2)}, u32[]{:S(2)}) %collective-permute-start.1) | collective-permute-done | bytes 129056 | tf_op jit(solution)/shard_map/ppermute | solution.py:42
  17.8 0.9 copy-done.15
  18.7 0.7 shard_map.96
  19.4 1.5 %broadcast_in_dim.8 = bf16[4,4,56,1152]{3,2,1,0:T(8,128)(2,1)} broadcast(bf16[4,56,1152]{2,1,0:T(8,128)(2,1)S(1)} %all-to-all-done), dimensions={1,2,3} | broadcast | bytes 2580480 | tf_op jit(solution)/shard_map/broadcast_in_dim | solution.py:35
  20.9 3.7 %all-to-all-start.1 = ((bf16[4,4,56,1152]{3,2,1,0:T(8,128)(2,1)}), bf16[4,4,56,1152]{3,2,1,0:T(8,128)(2,1)S(1)}, u32[]{:S(2)}, u32[]{:S(2)}) async-start(bf16[4,4,56,1152]{3,2,1,0:T(8,128)(2,1)} %broadcast_in_dim.8), calls=%async_computation.1 | async-start | bytes 4128768 | tf_op jit(solution)/shard_map/all_to_all | solution.py:34
  24.6 1.0 collective-permute-start.5
  25.6 2.4 %collective-permute-start.4 = (bf16[4,56,1152]{2,1,0:T(8,128)(2,1)S(1)}, bf16[4,56,1152]{2,1,0:T(8,128)(2,1)}, u32[]{:S(2)}, u32[]{:S(2)}) collective-permute-start(bf16[4,56,1152]{2,1,0:T(8,128)(2,1)S(1)} %shard_map.96), channel_id=1, source_target_pairs={{0,8},{1,9},{2,10},{3,11},{4,12},{5,13},{6,14},{7,15},{8,0},{9,1},... | collective-permute-start | bytes 1548296 | tf_op jit(solution)/shard_map/ppermute | solution.py:42
  28.0 1.2 collective-permute-start.3
  29.2 1.3 copy-done.6
  30.5 1.0 copy-done.10
  31.5 1.0 copy-done.11
  32.5 1.2 shard_map.94
  33.7 1.5 %copy-done = bf16[6,256,896]{2,1,0:T(8,128)(2,1)} copy-done((bf16[6,256,896]{2,1,0:T(8,128)(2,1)}, bf16[6,256,896]{2,1,0:T(8,128)(2,1)S(1)}, u32[]{:S(2)}) %copy-start) | copy-done | bytes 2752536
  35.3 0.9 copy-done.7
  36.2 0.7 collective-permute-done.5
  37.0 11.2 %collective-permute-done.4 = bf16[4,56,1152]{2,1,0:T(8,128)(2,1)} collective-permute-done((bf16[4,56,1152]{2,1,0:T(8,128)(2,1)S(1)}, bf16[4,56,1152]{2,1,0:T(8,128)(2,1)}, u32[]{:S(2)}, u32[]{:S(2)}) %collective-permute-start.4) | collective-permute-done | bytes 516128 | tf_op jit(solution)/shard_map/ppermute | solution.py:42
  48.1 2.0 %collective-permute-done.3 = bf16[4,56,1152]{2,1,0:T(8,128)(2,1)} collective-permute-done((bf16[4,56,1152]{2,1,0:T(8,128)(2,1)S(1)}, bf16[4,56,1152]{2,1,0:T(8,128)(2,1)}, u32[]{:S(2)}, u32[]{:S(2)}) %collective-permute-start.3) | collective-permute-done | bytes 516128 | tf_op jit(solution)/shard_map/ppermute | solution.py:42
  50.2 1.8 %copy-done.1 = bf16[6,256,896]{2,1,0:T(8,128)(2,1)S(1)} copy-done((bf16[6,256,896]{2,1,0:T(8,128)(2,1)S(1)}, bf16[6,256,896]{2,1,0:T(8,128)(2,1)}, u32[]{:S(2)}) %copy-start.1) | copy-done | bytes 2752536
  52.0 5.6 %shard_map.97 = (bf16[256,1024]{1,0:T(8,128)(2,1)S(1)}, bf16[256,1024]{1,0:T(8,128)(2,1)S(1)}, bf16[256,1024]{1,0:T(8,128)(2,1)S(1)}, f32[48,256]{1,0:T(8,128)S(...) custom-call(s32[2]{0:T(128)S(1)} %pad_add_fusion.place_ref, bf16[224,1152]{1,0:T(8,128)(2,1)S(1)} %bitcast.22, ...), custom_call_target="tpu_custom_call" | custom-call | flops 1409286144 | bytes 8388608 | tf_op jit(solution)/shard_map/pallas_call | solution.py:255
  57.6 1.8 %collective-permute-start.6 = (bf16[48,256]{1,0:T(8,128)(2,1)S(1)}, bf16[48,256]{1,0:T(8,128)(2,1)S(1)}, u32[]{:S(2)}, u32[]{:S(2)}) collective-permute-start(bf16[48,256]{1,0:T(8,128)(2,1)S(1)} %get-tuple-element.67), channel_id=1, source_target_pairs={{0,16},{16,0},{32,48},{48,32},{64,80},{80,64},{96,112},{112,96},{1... | collective-permute-start | bytes 73736 | tf_op jit(solution)/shard_map/ppermute | solution.py:455
  59.3 0.8 collective-permute-done.6
  60.2 2.5 %collective-permute-start.10 = (bf16[48,256]{1,0:T(8,128)(2,1)S(1)}, bf16[48,256]{1,0:T(8,128)(2,1)S(1)}, u32[]{:S(2)}, u32[]{:S(2)}) collective-permute-start(bf16[48,256]{1,0:T(8,128)(2,1)S(1)} %add_convert_fusion._.refs_0_), channel_id=1, source_target_pairs={{0,32},{16,48},{32,0},{48,16},{64,96},{80,112},{96,64},{112,80},{1... | collective-permute-start | bytes 73736 | tf_op jit(solution)/shard_map/ppermute | solution.py:527
  62.7 3.7 %shard_map.98 = (bf16[224,1024]{1,0:T(8,128)(2,1)S(1)}, bf16[224,1024]{1,0:T(8,128)(2,1)S(1)}, bf16[224,1024]{1,0:T(8,128)(2,1)S(1)}, bf16[224,1024]{1,0:T(8,128...) custom-call(s32[2]{0:T(128)S(1)} %pad_add_fusion.place_ref, ...), custom_call_target="tpu_custom_call" | custom-call | flops 2348810240 | bytes 12582912 | tf_op jit(solution)/shard_map/pallas_call | solution.py:297
  66.5 5.2 %collective-permute-start.13 = (f32[48,256]{1,0:T(8,128)S(1)}, f32[48,256]{1,0:T(8,128)S(1)}, u32[]{:S(2)}, u32[]{:S(2)}) collective-permute-start(f32[48,256]{1,0:T(8,128)S(1)} %shard_map.99.refs_0_), channel_id=1, source_target_pairs={{0,192},{16,208},{32,224},{48,240},{64,0},{80,16},{96,32},{112,48}... | collective-permute-start | bytes 147464 | tf_op jit(solution)/shard_map/ppermute | solution.py:532
  71.7 3.3 %collective-permute-start.11 = (f32[48,256]{1,0:T(8,128)S(1)}, f32[48,256]{1,0:T(8,128)S(1)}, u32[]{:S(2)}, u32[]{:S(2)}) collective-permute-start(f32[48,256]{1,0:T(8,128)S(1)} %shard_map.99.refs_0_), channel_id=1, source_target_pairs={{0,128},{16,144},{32,160},{48,176},{64,192},{80,208},{96,224},{112... | collective-permute-start | bytes 147464 | tf_op jit(solution)/shard_map/ppermute | solution.py:532
  74.9 1.9 %collective-permute-done.12.refs_2_ = f32[48,256]{1,0:T(8,128)S(1)} collective-permute-done((f32[48,256]{1,0:T(8,128)S(1)}, f32[48,256]{1,0:T(8,128)S(1)}, u32[]{:S(2)}, u32[]{:S(2)}) %collective-permute-start.12) | collective-permute-done | bytes 49184 | tf_op jit(solution)/shard_map/ppermute | solution.py:532
  76.8 2.1 %collective-permute-done.11.refs_1_ = f32[48,256]{1,0:T(8,128)S(1)} collective-permute-done((f32[48,256]{1,0:T(8,128)S(1)}, f32[48,256]{1,0:T(8,128)S(1)}, u32[]{:S(2)}, u32[]{:S(2)}) %collective-permute-start.11) | collective-permute-done | bytes 49184 | tf_op jit(solution)/shard_map/ppermute | solution.py:532
  78.9 1.9 %collective-permute-start.14 = (f32[48,256]{1,0:T(8,128)S(1)}, f32[48,256]{1,0:T(8,128)S(1)}, u32[]{:S(2)}, u32[]{:S(2)}) collective-permute-start(f32[48,256]{1,0:T(8,128)S(1)} %shard_map.100.p_mine_ref), channel_id=1, source_target_pairs={{0,16},{16,0},{32,48},{48,32},{64,80},{80,64},{96,112},{112,96},{1... | collective-permute-start | bytes 147464 | tf_op jit(solution)/shard_map/ppermute | solution.py:455
  80.9 0.9 collective-permute-done.14.p_other_ref
  81.7 0.7 shard_map.101
  82.4 0.9 copy-done.2
  83.7 1.1 collective-permute-done.15
  84.9 0.8 pad_maximum_fusion
  85.7 6.5 %all-to-all-start.2 = ((f32[16,48,128]{2,1,0:T(8,128)}), f32[16,48,128]{2,1,0:T(8,128)S(1)}, u32[]{:S(2)}, u32[]{:S(2)}) async-start(f32[16,48,128]{2,1,0:T(8,128)} %pad_maximum_fusion), calls=%async_computation.2 | async-start | bytes 786432 | tf_op jit(solution)/shard_map/all_to_all | solution.py:538
  92.2 1.4 collective-permute-start.7
  93.5 1.4 collective-permute-start.8
  94.9 1.6 %collective-permute-start.9 = (bf16[224,1024]{1,0:T(8,128)(2,1)}, bf16[224,1024]{1,0:T(8,128)(2,1)}, u32[]{:S(2)}, u32[]{:S(2)}) collective-permute-start(bf16[224,1024]{1,0:T(8,128)(2,1)} %copy-done.19), channel_id=1, source_target_pairs={{0,8},{1,9},{2,10},{3,11},{4,12},{5,13},{6,14},{7,15},{8,0},{9,1},... | collective-permute-start | bytes 1376264 | tf_op jit(solution)/shard_map/ppermute | solution.py:119
  96.5 5.2 %all-to-all-done.2 = f32[16,48,128]{2,1,0:T(8,128)S(1)} async-done(((f32[16,48,128]{2,1,0:T(8,128)}), f32[16,48,128]{2,1,0:T(8,128)S(1)}, u32[]{:S(2)}, u32[]{:S(2)}) %all-to-all-start.2) | async-done | bytes 393248 | tf_op jit(solution)/shard_map/all_to_all | solution.py:538
  101.7 0.6 fusion
  102.3 0.6 broadcast_in_dim.10
  103.0 5.4 %all-to-all-start.3 = ((f32[8,24,128]{2,1,0:T(8,128)}), f32[8,24,128]{2,1,0:T(8,128)S(1)}, u32[]{:S(2)}, u32[]{:S(2)}) async-start(f32[8,24,128]{2,1,0:T(8,128)} %broadcast_in_dim.10), calls=%async_computation.3 | async-start | bytes 196608 | tf_op jit(solution)/shard_map/all_to_all | solution.py:34
  108.4 4.4 %shard_map.104 = (f32[3,32,32]{2,1,0:T(8,128)}, f32[96,256]{1,0:T(8,128)}) custom-call(s32[1]{0:T(128)} %bitcast.2.core_ref, f32[24,128]{1,0:T(8,128)} %get-tuple-element.90._.gram_ref, f32[48,256]{1,0:T(8,128)} %copy-done.14, f32[48,256]{1,0:T(8,128)} %copy-done.18, f32[24,128]{1,0:T(8,128)} %get-tuple-element.90._.gram_ref), custom_call_target="tpu_custom_call" | custom-call | flops 4294967296 | bytes 1048576 | tf_op jit(solution)/shard_map/pallas_call | solution.py:388
  112.8 3.2 %all-to-all-done.3.value_ref = f32[8,24,128]{2,1,0:T(8,128)S(1)} async-done(((f32[8,24,128]{2,1,0:T(8,128)}), f32[8,24,128]{2,1,0:T(8,128)S(1)}, u32[]{:S(2)}, u32[]{:S(2)}) %all-to-all-start.3) | async-done | bytes 98336 | tf_op jit(solution)/shard_map/all_to_all | solution.py:34
  116.0 0.8 copy-done.12
  116.8 0.7 broadcast_in_dim.11
  117.5 3.5 %all-to-all-start.4 = ((f32[16,24,128]{2,1,0:T(8,128)}), f32[16,24,128]{2,1,0:T(8,128)S(1)}, u32[]{:S(2)}, u32[]{:S(2)}) async-start(f32[16,24,128]{2,1,0:T(8,128)} %broadcast_in_dim.11), calls=%async_computation.4 | async-start | bytes 393216 | tf_op jit(solution)/shard_map/all_to_all | solution.py:34
  121.1 1.5 %shard_map.102 = (bf16[56,1024]{1,0:T(8,128)(2,1)S(1)}, bf16[56,1024]{1,0:T(8,128)(2,1)S(1)}, bf16[56,1024]{1,0:T(8,128)(2,1)S(1)}, bf16[56,1024]{1,0:T(8,128)(2,1)S(1)}) custom-call(s32[1]{0:T(128)} %bitcast.place_ref, bf16[4,56,1024]{2,1,0:T(8,128)(2,1)S(1)} %bitcast.25, bf16[4,56,1024]{2,1,0:T(8,128)(2,1)} %bitcast.12.g1_ref, ...), custom_call_target="tpu_custom_call" | custom-call | tf_op jit(solution)/shard_map/pallas_call | solution.py:132
  122.6 1.3 collective-permute-start.16
  124.0 1.4 %collective-permute-start.17 = (bf16[56,1024]{1,0:T(8,128)(2,1)S(1)}, bf16[56,1024]{1,0:T(8,128)(2,1)S(1)}, u32[]{:S(2)}, u32[]{:S(2)}) collective-permute-start(bf16[56,1024]{1,0:T(8,128)(2,1)S(1)} %get-tuple-element.81), channel_id=1, source_target_pairs={{0,3},{1,0},{2,1},{3,2},{4,7},{5,4},{6,5},{7,6},{8,11},{9,8},{10,9... | collective-permute-start | bytes 344072 | tf_op jit(solution)/shard_map/ppermute | solution.py:139
  125.4 1.5 %collective-permute-start.18 = (bf16[56,1024]{1,0:T(8,128)(2,1)S(1)}, bf16[56,1024]{1,0:T(8,128)(2,1)S(1)}, u32[]{:S(2)}, u32[]{:S(2)}) collective-permute-start(bf16[56,1024]{1,0:T(8,128)(2,1)S(1)} %get-tuple-element.82), channel_id=1, source_target_pairs={{0,2},{1,3},{2,0},{3,1},{4,6},{5,7},{6,4},{7,5},{8,10},{9,11},{10,... | collective-permute-start | bytes 344072 | tf_op jit(solution)/shard_map/ppermute | solution.py:139
  126.9 0.6 collective-permute-done.16.refs_1_
  127.6 1.2 collective-permute-done.17.refs_2_
  128.8 2.4 %collective-permute-done.18.refs_3_ = bf16[56,1024]{1,0:T(8,128)(2,1)S(1)} collective-permute-done((bf16[56,1024]{1,0:T(8,128)(2,1)S(1)}, bf16[56,1024]{1,0:T(8,128)(2,1)S(1)}, u32[]{:S(2)}, u32[]{:S(2)}) %collective-permute-start.18) | collective-permute-done | bytes 114720 | tf_op jit(solution)/shard_map/ppermute | solution.py:139
  131.1 0.7 shard_map.103
  131.9 4.1 %collective-permute-start.19 = (f32[384,128]{1,0:T(8,128)S(1)}, f32[384,128]{1,0:T(8,128)S(1)}, u32[]{:S(2)}, u32[]{:S(2)}) collective-permute-start(f32[384,128]{1,0:T(8,128)S(1)} %shard_map.106.s_mine_ref), channel_id=1, source_target_pairs={{0,16},{16,0},{32,48},{48,32},{64,80},{80,64},{96,112},{112,96},{1... | collective-permute-start | bytes 589832 | tf_op jit(solution)/shard_map/ppermute | solution.py:455
  136.0 1.0 collective-permute-done.19.s_other_ref
  137.0 0.9 copy-done.16
  137.9 3.9 %shard_map.107 = (bf16[1,3,256,896]{3,2,1,0:T(8,128)(2,1)}, f32[96,56]{1,0:T(8,128)}) custom-call(s32[2]{0:T(128)S(1)} %pad_add_fusion.1.place_ref, f32[384,128]{1,0:T(8,128)S(1)} %shard_map.106.s_mine_ref, f32[384,128]{1,0:T(8,128)S(1)} %collective-permute-done.19.s_other_ref, f32[3,32,32]{2,1,0:T(8,128)S(1)} %copy-done.13, f32[96,256]{1,0:T(8,128)S(1)} %copy-done.16, ...), custom_call_target="tpu_custom_call" | custom-call | tf_op jit(solution)/shard_map/pallas_call | solution.py:436
  (55 shorter events, 0.7 us)
Async XLA Ops:
  3.6 14.2 %all-to-all-start = ((bf16[4,56,1152]{2,1,0:T(8,128)(2,1)}), bf16[4,56,1152]{2,1,0:T(8,128)(2,1)S(1)}, u32[]{:S(2)}, u32[]{:S(2)}) async-start(bf16[4,56,1152]{2,1,0:T(8,128)(2,1)} %get-tuple-element.48), calls=%async_computation | async-start | bytes 1032192 | tf_op jit(solution)/shard_map/all_to_all | solution.py:105
  8.6 5.2 %collective-permute-start.2 = (bf16[56,1152]{1,0:T(8,128)(2,1)}, bf16[56,1152]{1,0:T(8,128)(2,1)S(1)}, u32[]{:S(2)}, u32[]{:S(2)}) collective-permute-start(bf16[56,1152]{1,0:T(8,128)(2,1)} %get-tuple-element.49.p0_ref), channel_id=1, source_target_pairs={{0,1},{1,2},{2,3},{3,0},{4,5},{5,6},{6,7},{7,4},{8,9},{9,10},{10,1... | collective-permute-start | bytes 387080 | tf_op jit(solution)/shard_map/ppermute | solution.py:42
  9.8 8.0 %collective-permute-start.1 = (bf16[56,1152]{1,0:T(8,128)(2,1)}, bf16[56,1152]{1,0:T(8,128)(2,1)S(1)}, u32[]{:S(2)}, u32[]{:S(2)}) collective-permute-start(bf16[56,1152]{1,0:T(8,128)(2,1)} %get-tuple-element.49.p0_ref), channel_id=1, source_target_pairs={{0,2},{1,3},{2,0},{3,1},{4,6},{5,7},{6,4},{7,5},{8,10},{9,11},{10,... | collective-permute-start | bytes 387080 | tf_op jit(solution)/shard_map/ppermute | solution.py:42
  12.3 5.5 %collective-permute-start = (bf16[56,1152]{1,0:T(8,128)(2,1)}, bf16[56,1152]{1,0:T(8,128)(2,1)S(1)}, u32[]{:S(2)}, u32[]{:S(2)}) collective-permute-start(bf16[56,1152]{1,0:T(8,128)(2,1)} %get-tuple-element.49.p0_ref), channel_id=1, source_target_pairs={{0,3},{1,0},{2,1},{3,2},{4,7},{5,4},{6,5},{7,6},{8,11},{9,8},{10,9... | collective-permute-start | bytes 387080 | tf_op jit(solution)/shard_map/ppermute | solution.py:42
  17.8 0.9 copy-start.15
  20.9 8.3 %copy-start.9 = (bf16[256,896]{1,0:T(8,128)(2,1)S(1)}, bf16[256,896]{1,0:T(8,128)(2,1)}, u32[]{:S(2)}) copy-start(bf16[256,896]{1,0:T(8,128)(2,1)} %gate_ref.1) | copy-start | bytes 1376260
  20.9 29.3 %all-to-all-start.1 = ((bf16[4,4,56,1152]{3,2,1,0:T(8,128)(2,1)}), bf16[4,4,56,1152]{3,2,1,0:T(8,128)(2,1)S(1)}, u32[]{:S(2)}, u32[]{:S(2)}) async-start(bf16[4,4,56,1152]{3,2,1,0:T(8,128)(2,1)} %broadcast_in_dim.8), calls=%async_computation.1 | async-start | bytes 4128768 | tf_op jit(solution)/shard_map/all_to_all | solution.py:34
  24.6 12.4 %collective-permute-start.5 = (bf16[4,56,1152]{2,1,0:T(8,128)(2,1)S(1)}, bf16[4,56,1152]{2,1,0:T(8,128)(2,1)S(1)}, u32[]{:S(2)}, u32[]{:S(2)}) collective-permute-start(bf16[4,56,1152]{2,1,0:T(8,128)(2,1)S(1)} %shard_map.96), channel_id=1, source_target_pairs={{0,4},{1,5},{2,6},{3,7},{4,8},{5,9},{6,10},{7,11},{8,12},{9,13},{1... | collective-permute-start | bytes 1548296 | tf_op jit(solution)/shard_map/ppermute | solution.py:42
  25.6 22.6 %collective-permute-start.4 = (bf16[4,56,1152]{2,1,0:T(8,128)(2,1)S(1)}, bf16[4,56,1152]{2,1,0:T(8,128)(2,1)}, u32[]{:S(2)}, u32[]{:S(2)}) collective-permute-start(bf16[4,56,1152]{2,1,0:T(8,128)(2,1)S(1)} %shard_map.96), channel_id=1, source_target_pairs={{0,8},{1,9},{2,10},{3,11},{4,12},{5,13},{6,14},{7,15},{8,0},{9,1},... | collective-permute-start | bytes 1548296 | tf_op jit(solution)/shard_map/ppermute | solution.py:42
  28.0 22.2 %collective-permute-start.3 = (bf16[4,56,1152]{2,1,0:T(8,128)(2,1)S(1)}, bf16[4,56,1152]{2,1,0:T(8,128)(2,1)}, u32[]{:S(2)}, u32[]{:S(2)}) collective-permute-start(bf16[4,56,1152]{2,1,0:T(8,128)(2,1)S(1)} %shard_map.96), channel_id=1, source_target_pairs={{0,12},{1,13},{2,14},{3,15},{4,0},{5,1},{6,2},{7,3},{8,4},{9,5},{1... | collective-permute-start | bytes 1548296 | tf_op jit(solution)/shard_map/ppermute | solution.py:42
  29.2 1.3 copy-start.6
  30.5 1.0 copy-start.10
  31.5 1.0 copy-start.11
  33.7 1.5 %copy-start = (bf16[6,256,896]{2,1,0:T(8,128)(2,1)}, bf16[6,256,896]{2,1,0:T(8,128)(2,1)S(1)}, u32[]{:S(2)}) copy-start(bf16[6,256,896]{2,1,0:T(8,128)(2,1)S(1)} %get-tuple-element.61.w_ref.left_ref) | copy-start | bytes 8257540
  35.2 0.9 copy-start.7
  50.2 1.8 %copy-start.1 = (bf16[6,256,896]{2,1,0:T(8,128)(2,1)S(1)}, bf16[6,256,896]{2,1,0:T(8,128)(2,1)}, u32[]{:S(2)}) copy-start(bf16[6,256,896]{2,1,0:T(8,128)(2,1)} %copy-done) | copy-start | bytes 8257540
  52.0 10.8 %copy-start.8 = (bf16[896,512]{1,0:T(8,128)(2,1)S(1)}, bf16[896,512]{1,0:T(8,128)(2,1)}, u32[]{:S(2)}) copy-start(bf16[896,512]{1,0:T(8,128)(2,1)} %copy-done.7) | copy-start | bytes 2752516
  57.6 2.6 %collective-permute-start.6 = (bf16[48,256]{1,0:T(8,128)(2,1)S(1)}, bf16[48,256]{1,0:T(8,128)(2,1)S(1)}, u32[]{:S(2)}, u32[]{:S(2)}) collective-permute-start(bf16[48,256]{1,0:T(8,128)(2,1)S(1)} %get-tuple-element.67), channel_id=1, source_target_pairs={{0,16},{16,0},{32,48},{48,32},{64,80},{80,64},{96,112},{112,96},{1... | collective-permute-start | bytes 73736 | tf_op jit(solution)/shard_map/ppermute | solution.py:455
  60.2 6.2 %collective-permute-start.10 = (bf16[48,256]{1,0:T(8,128)(2,1)S(1)}, bf16[48,256]{1,0:T(8,128)(2,1)S(1)}, u32[]{:S(2)}, u32[]{:S(2)}) collective-permute-start(bf16[48,256]{1,0:T(8,128)(2,1)S(1)} %add_convert_fusion._.refs_0_), channel_id=1, source_target_pairs={{0,32},{16,48},{32,0},{48,16},{64,96},{80,112},{96,64},{112,80},{1... | collective-permute-start | bytes 73736 | tf_op jit(solution)/shard_map/ppermute | solution.py:527
  66.4 16.0 %copy-start.4 = (f32[256,896]{1,0:T(8,128)}, f32[256,896]{1,0:T(8,128)S(1)}, u32[]{:S(2)}) copy-start(f32[256,896]{1,0:T(8,128)S(1)} %get-tuple-element.75.m2_ref.m2_hbm) | copy-start | bytes 2752516
  66.4 18.5 %copy-start.19 = (bf16[224,1024]{1,0:T(8,128)(2,1)}, bf16[224,1024]{1,0:T(8,128)(2,1)S(1)}, u32[]{:S(2)}) copy-start(bf16[224,1024]{1,0:T(8,128)(2,1)S(1)} %get-tuple-element.71) | copy-start | bytes 1376260
  66.4 18.5 %copy-start.20 = (bf16[224,1024]{1,0:T(8,128)(2,1)}, bf16[224,1024]{1,0:T(8,128)(2,1)S(1)}, u32[]{:S(2)}) copy-start(bf16[224,1024]{1,0:T(8,128)(2,1)S(1)} %get-tuple-element.70) | copy-start | bytes 1376260
  66.4 18.5 %copy-start.21 = (bf16[224,1024]{1,0:T(8,128)(2,1)}, bf16[224,1024]{1,0:T(8,128)(2,1)S(1)}, u32[]{:S(2)}) copy-start(bf16[224,1024]{1,0:T(8,128)(2,1)S(1)} %get-tuple-element.69) | copy-start | bytes 1376260
  66.5 8.5 %collective-permute-start.13 = (f32[48,256]{1,0:T(8,128)S(1)}, f32[48,256]{1,0:T(8,128)S(1)}, u32[]{:S(2)}, u32[]{:S(2)}) collective-permute-start(f32[48,256]{1,0:T(8,128)S(1)} %shard_map.99.refs_0_), channel_id=1, source_target_pairs={{0,192},{16,208},{32,224},{48,240},{64,0},{80,16},{96,32},{112,48}... | collective-permute-start | bytes 147464 | tf_op jit(solution)/shard_map/ppermute | solution.py:532
  71.7 5.1 %collective-permute-start.12 = (f32[48,256]{1,0:T(8,128)S(1)}, f32[48,256]{1,0:T(8,128)S(1)}, u32[]{:S(2)}, u32[]{:S(2)}) collective-permute-start(f32[48,256]{1,0:T(8,128)S(1)} %shard_map.99.refs_0_), channel_id=1, source_target_pairs={{0,64},{16,80},{32,96},{48,112},{64,128},{80,144},{96,160},{112,17... | collective-permute-start | bytes 147464 | tf_op jit(solution)/shard_map/ppermute | solution.py:532
  71.7 7.2 %collective-permute-start.11 = (f32[48,256]{1,0:T(8,128)S(1)}, f32[48,256]{1,0:T(8,128)S(1)}, u32[]{:S(2)}, u32[]{:S(2)}) collective-permute-start(f32[48,256]{1,0:T(8,128)S(1)} %shard_map.99.refs_0_), channel_id=1, source_target_pairs={{0,128},{16,144},{32,160},{48,176},{64,192},{80,208},{96,224},{112... | collective-permute-start | bytes 147464 | tf_op jit(solution)/shard_map/ppermute | solution.py:532
  78.9 6.7 %copy-start.14 = (f32[48,256]{1,0:T(8,128)}, f32[48,256]{1,0:T(8,128)S(1)}, u32[]{:S(2)}) copy-start(f32[48,256]{1,0:T(8,128)S(1)} %shard_map.100.p_mine_ref) | copy-start | bytes 147460
  78.9 2.8 %collective-permute-start.14 = (f32[48,256]{1,0:T(8,128)S(1)}, f32[48,256]{1,0:T(8,128)S(1)}, u32[]{:S(2)}, u32[]{:S(2)}) collective-permute-start(f32[48,256]{1,0:T(8,128)S(1)} %shard_map.100.p_mine_ref), channel_id=1, source_target_pairs={{0,16},{16,0},{32,48},{48,32},{64,80},{80,64},{96,112},{112,96},{1... | collective-permute-start | bytes 147464 | tf_op jit(solution)/shard_map/ppermute | solution.py:455
  81.7 3.9 %copy-start.18 = (f32[48,256]{1,0:T(8,128)}, f32[48,256]{1,0:T(8,128)S(1)}, u32[]{:S(2)}) copy-start(f32[48,256]{1,0:T(8,128)S(1)} %collective-permute-done.14.p_other_ref) | copy-start | bytes 147460
  82.4 0.9 copy-start.2
  83.4 1.4 %collective-permute-start.15 = (f32[384,128]{1,0:T(8,128)S(1)}, f32[384,128]{1,0:T(8,128)S(1)}, u32[]{:S(2)}, u32[]{:S(2)}) collective-permute-start(f32[384,128]{1,0:T(8,128)S(1)} %get-tuple-element.77), channel_id=1, source_target_pairs={{0,16},{16,0},{32,48},{48,32},{64,80},{80,64},{96,112},{112,96},{1... | collective-permute-start | bytes 589832 | tf_op jit(solution)/shard_map/ppermute | solution.py:455
  85.7 16.0 %all-to-all-start.2 = ((f32[16,48,128]{2,1,0:T(8,128)}), f32[16,48,128]{2,1,0:T(8,128)S(1)}, u32[]{:S(2)}, u32[]{:S(2)}) async-start(f32[16,48,128]{2,1,0:T(8,128)} %pad_maximum_fusion), calls=%async_computation.2 | async-start | bytes 786432 | tf_op jit(solution)/shard_map/all_to_all | solution.py:538
  92.2 28.9 %collective-permute-start.7 = (bf16[224,1024]{1,0:T(8,128)(2,1)}, bf16[224,1024]{1,0:T(8,128)(2,1)}, u32[]{:S(2)}, u32[]{:S(2)}) collective-permute-start(bf16[224,1024]{1,0:T(8,128)(2,1)} %copy-done.21), channel_id=1, source_target_pairs={{0,4},{1,5},{2,6},{3,7},{4,8},{5,9},{6,10},{7,11},{8,12},{9,13},{1... | collective-permute-start | bytes 1376264 | tf_op jit(solution)/shard_map/ppermute | solution.py:119
  93.5 27.6 %collective-permute-start.8 = (bf16[224,1024]{1,0:T(8,128)(2,1)}, bf16[224,1024]{1,0:T(8,128)(2,1)}, u32[]{:S(2)}, u32[]{:S(2)}) collective-permute-start(bf16[224,1024]{1,0:T(8,128)(2,1)} %copy-done.20), channel_id=1, source_target_pairs={{0,12},{1,13},{2,14},{3,15},{4,0},{5,1},{6,2},{7,3},{8,4},{9,5},{1... | collective-permute-start | bytes 1376264 | tf_op jit(solution)/shard_map/ppermute | solution.py:119
  94.9 26.2 %collective-permute-start.9 = (bf16[224,1024]{1,0:T(8,128)(2,1)}, bf16[224,1024]{1,0:T(8,128)(2,1)}, u32[]{:S(2)}, u32[]{:S(2)}) collective-permute-start(bf16[224,1024]{1,0:T(8,128)(2,1)} %copy-done.19), channel_id=1, source_target_pairs={{0,8},{1,9},{2,10},{3,11},{4,12},{5,13},{6,14},{7,15},{8,0},{9,1},... | collective-permute-start | bytes 1376264 | tf_op jit(solution)/shard_map/ppermute | solution.py:119
  103.0 13.0 %all-to-all-start.3 = ((f32[8,24,128]{2,1,0:T(8,128)}), f32[8,24,128]{2,1,0:T(8,128)S(1)}, u32[]{:S(2)}, u32[]{:S(2)}) async-start(f32[8,24,128]{2,1,0:T(8,128)} %broadcast_in_dim.10), calls=%async_computation.3 | async-start | bytes 196608 | tf_op jit(solution)/shard_map/all_to_all | solution.py:34
  108.4 12.7 %copy-start.17 = (f32[24,128]{1,0:T(8,128)S(1)}, f32[24,128]{1,0:T(8,128)}, u32[]{:S(2)}) copy-start(f32[24,128]{1,0:T(8,128)} %get-tuple-element.90._.gram_ref) | copy-start | bytes 36868
  112.8 24.2 %copy-start.3 = (f32[256,896]{1,0:T(8,128)S(1)}, f32[256,896]{1,0:T(8,128)}, u32[]{:S(2)}) copy-start(f32[256,896]{1,0:T(8,128)} %copy-done.2) | copy-start | bytes 2752516
  112.8 24.2 %copy-start.5 = (f32[256,896]{1,0:T(8,128)S(1)}, f32[256,896]{1,0:T(8,128)}, u32[]{:S(2)}) copy-start(f32[256,896]{1,0:T(8,128)} %copy-done.4) | copy-start | bytes 2752516
  116.0 0.8 copy-start.12
  116.8 20.2 %copy-start.13 = (f32[3,32,32]{2,1,0:T(8,128)S(1)}, f32[3,32,32]{2,1,0:T(8,128)}, u32[]{:S(2)}) copy-start(f32[3,32,32]{2,1,0:T(8,128)} %get-tuple-element.84._.inverse_ref) | copy-start | bytes 36868
  117.5 14.3 %all-to-all-start.4 = ((f32[16,24,128]{2,1,0:T(8,128)}), f32[16,24,128]{2,1,0:T(8,128)S(1)}, u32[]{:S(2)}, u32[]{:S(2)}) async-start(f32[16,24,128]{2,1,0:T(8,128)} %broadcast_in_dim.11), calls=%async_computation.4 | async-start | bytes 393216 | tf_op jit(solution)/shard_map/all_to_all | solution.py:34
  122.6 4.9 %collective-permute-start.16 = (bf16[56,1024]{1,0:T(8,128)(2,1)S(1)}, bf16[56,1024]{1,0:T(8,128)(2,1)S(1)}, u32[]{:S(2)}, u32[]{:S(2)}) collective-permute-start(bf16[56,1024]{1,0:T(8,128)(2,1)S(1)} %get-tuple-element.80), channel_id=1, source_target_pairs={{0,1},{1,2},{2,3},{3,0},{4,5},{5,6},{6,7},{7,4},{8,9},{9,10},{10,1... | collective-permute-start | bytes 344072 | tf_op jit(solution)/shard_map/ppermute | solution.py:139
  124.0 4.8 %collective-permute-start.17 = (bf16[56,1024]{1,0:T(8,128)(2,1)S(1)}, bf16[56,1024]{1,0:T(8,128)(2,1)S(1)}, u32[]{:S(2)}, u32[]{:S(2)}) collective-permute-start(bf16[56,1024]{1,0:T(8,128)(2,1)S(1)} %get-tuple-element.81), channel_id=1, source_target_pairs={{0,3},{1,0},{2,1},{3,2},{4,7},{5,4},{6,5},{7,6},{8,11},{9,8},{10,9... | collective-permute-start | bytes 344072 | tf_op jit(solution)/shard_map/ppermute | solution.py:139
  125.4 5.7 %collective-permute-start.18 = (bf16[56,1024]{1,0:T(8,128)(2,1)S(1)}, bf16[56,1024]{1,0:T(8,128)(2,1)S(1)}, u32[]{:S(2)}, u32[]{:S(2)}) collective-permute-start(bf16[56,1024]{1,0:T(8,128)(2,1)S(1)} %get-tuple-element.82), channel_id=1, source_target_pairs={{0,2},{1,3},{2,0},{3,1},{4,6},{5,7},{6,4},{7,5},{8,10},{9,11},{10,... | collective-permute-start | bytes 344072 | tf_op jit(solution)/shard_map/ppermute | solution.py:139
  131.9 5.2 %collective-permute-start.19 = (f32[384,128]{1,0:T(8,128)S(1)}, f32[384,128]{1,0:T(8,128)S(1)}, u32[]{:S(2)}, u32[]{:S(2)}) collective-permute-start(f32[384,128]{1,0:T(8,128)S(1)} %shard_map.106.s_mine_ref), channel_id=1, source_target_pairs={{0,16},{16,0},{32,48},{48,32},{64,80},{80,64},{96,112},{112,96},{1... | collective-permute-start | bytes 589832 | tf_op jit(solution)/shard_map/ppermute | solution.py:455
  137.0 0.9 copy-start.16

commit v4 on v3

--- a/solution.py
+++ b/solution.py
@@ -15,6 +15,7 @@
 LANES = 128
 TILES = HALF * 1024 // (8 * LANES)
 MIB = 1 << 20
+STORE = 112
 
 X_GROUPS = [[y * SIDE + x for x in range(SIDE)] for y in range(SIDE)]
 Y_GROUPS = [[y * SIDE + x for y in range(SIDE)] for x in range(SIDE)]
@@ -167,7 +168,7 @@
     return jnp.concatenate([jnp.where(first, mine, other), jnp.where(first, other, mine)])
 
 
-def prepare_kernel(gate_ref, up_ref, down_ref, err_ref, left_ref, both_ref, token_ref):
+def prepare_kernel(gate_ref, up_ref, down_ref, err_ref, left_hbm, both_ref, token_ref, left_ref, sem):
     hid, width = gate_ref.shape
     gate, up, down = gate_ref[...], up_ref[...], down_ref[...].astype(F32)
     block = width // (SIDE * SIDE)
@@ -179,9 +180,12 @@
     ).astype(BF)
     for k in range(3):
         left_ref[3 + k] = err_ref[0, k]
+    copy = pltpu.make_async_copy(left_ref, left_hbm.at[pl.ds(0, 6)], sem)
+    copy.start()
     both_ref[:, :hid] = gate.astype(F32).T.astype(BF)
     both_ref[:, hid:] = up.astype(F32).T.astype(BF)
     token_ref[...] = jnp.zeros_like(token_ref)
+    copy.wait()
 
 
 def prepare(w_gate, w_up, w_down, error_in):
@@ -190,35 +194,47 @@
     return pl.pallas_call(
         prepare_kernel,
         out_shape=(
-            jax.ShapeDtypeStruct((6, hid, width), BF),
+            jax.ShapeDtypeStruct((STORE, hid, width), BF),
             jax.ShapeDtypeStruct((width, 2 * hid), BF),
             jax.ShapeDtypeStruct((8, LANES), F32),
         ),
         in_specs=[vmem] * 4,
-        out_specs=(vmem,) * 3,
+        out_specs=(pl.BlockSpec(memory_space=pltpu.HBM), vmem, vmem),
+        scratch_shapes=[pltpu.VMEM((6, hid, width), BF), pltpu.SemaphoreType.DMA],
         compiler_params=pltpu.CompilerParams(vmem_limit_bytes=20 * MIB),
     )(w_gate, w_up, w_down, error_in)
 
 
-def backward_kernel(place_ref, p0_ref, p1_ref, p2_ref, p3_ref, dy_ref, w_ref,
-                    gate_grad_ref, up_grad_ref, hidden_ref, mine_ref, theirs_ref, x_ref):
+def backward_kernel(place_ref, p0_ref, p1_ref, p2_ref, p3_ref, dy_ref, w_hbm,
+                    gate_grad_ref, up_grad_ref, hidden_ref, p_out_ref, x_ref, w_ref, hidden_grad_ref, sems):
     rows = p0_ref.shape[0]
     hid, tokens = hidden_ref.shape
+    chunk = 256
+    loads = [pltpu.make_async_copy(w_hbm.at[k], w_ref.at[k], sems.at[k]) for k in range(6)]
+    pieces = []
     for i, ref in enumerate((p0_ref, p1_ref, p2_ref, p3_ref)):
         at = pl.multiple_of(lax.rem(place_ref[0] + i, SIDE) * rows, 16)
-        x_ref[pl.ds(at, rows), :] = ref[...]
+        pieces.append(pltpu.make_async_copy(ref, x_ref.at[pl.ds(at, rows), :], sems.at[6 + i]))
+    for copy in [loads[2]] + pieces + loads[:2] + loads[3:]:
+        copy.start()
+    q_dy = dy_ref[:, tokens : tokens + 2 * RANK]
+    q_dy_rows = q_dy.astype(F32).T.astype(BF)
+    loads[2].wait()
+    for start in range(0, tokens, chunk):
+        span = slice(start, start + chunk)
+        hidden_grad_ref[:, span] = dot(w_ref[2], dy_ref[:, span], 1, 0)
+    for copy in pieces + loads[:2]:
+        copy.wait()
     q_x = x_ref[:, tokens:]
-    q_dy = dy_ref[:, tokens : tokens + 2 * RANK]
     q_rows = q_x.astype(F32).T.astype(BF)
-    q_both = [q_rows[: 2 * RANK], q_rows[2 * RANK :], q_dy.astype(F32).T.astype(BF)]
+    q_both = [q_rows[: 2 * RANK], q_rows[2 * RANK :], q_dy_rows]
     sums = [jnp.zeros((2 * RANK, hid), F32)] * 3
-    chunk = 256
     for start in range(0, tokens, chunk):
         span = slice(start, start + chunk)
         x, dy = x_ref[:, span], dy_ref[:, span]
         gate_pre = dot(w_ref[0], x, 1, 0)
         up_pre = dot(w_ref[1], x, 1, 0)
-        hidden_grad = dot(w_ref[2], dy, 1, 0)
+        hidden_grad = hidden_grad_ref[:, span]
         gate_sig = jax.nn.sigmoid(gate_pre)
         gate_act = gate_pre * gate_sig
         hidden = (gate_act * up_pre).astype(BF)
@@ -236,14 +252,14 @@
     q_plain = jnp.concatenate(
         [q_plain[(x * SIDE + y) * block : (x * SIDE + y + 1) * block] for y in range(SIDE) for x in range(SIDE)]
     ).astype(BF)
+    for copy in loads[3:]:
+        copy.wait()
     errors = [
         dot(w_ref[3 + k], q, 1, 0) for k, q in enumerate((q_x[:, : 2 * RANK], q_x[:, 2 * RANK :], q_plain))
     ]
     error_p = jnp.concatenate([both[:, :RANK] + both[:, RANK:] for both in errors], axis=1).T
     p = jnp.concatenate([both[:RANK] + both[RANK:] for both in sums]) + error_p
-    mine, theirs = own_half(place_ref[1], p)
-    mine_ref[...] = mine
-    theirs_ref[...] = theirs.astype(BF)
+    p_out_ref[...] = p.astype(BF)
 
 
 def backward(place, pieces, dy_all, weights):
@@ -251,6 +267,7 @@
     wide = dy_all.shape[1]
     tokens = wide - LANES
     vmem = pl.BlockSpec(memory_space=pltpu.VMEM)
+    hbm = pl.BlockSpec(memory_space=pltpu.HBM)
     grads = jax.ShapeDtypeStruct((hid, tokens), BF)
     return pl.pallas_call(
         backward_kernel,
@@ -258,53 +275,81 @@
             grads,
             grads,
             grads,
-            jax.ShapeDtypeStruct((HALF, hid), F32),
-            jax.ShapeDtypeStruct((HALF, hid), BF),
+            jax.ShapeDtypeStruct((ROWS, hid), BF),
             jax.ShapeDtypeStruct((width, wide), BF),
         ),
-        in_specs=[pl.BlockSpec(memory_space=pltpu.SMEM)] + [vmem] * 6,
-        out_specs=(vmem,) * 6,
+        in_specs=[pl.BlockSpec(memory_space=pltpu.SMEM)] + [hbm] * SIDE + [vmem, hbm],
+        out_specs=(vmem,) * 5,
+        scratch_shapes=[
+            pltpu.VMEM((6, hid, width), BF),
+            pltpu.VMEM((hid, tokens), F32),
+            pltpu.SemaphoreType.DMA((6 + SIDE,)),
+        ],
         compiler_params=pltpu.CompilerParams(vmem_limit_bytes=20 * MIB),
         cost_estimate=pl.CostEstimate(flops=6 * hid * width * tokens, bytes_accessed=8 * MIB, transcendentals=0),
     )(place, *pieces, dy_all, weights)
 
 
-def products_kernel(place_ref, w_ref, gate_grad_ref, up_grad_ref, hidden_ref, x_ref, dy_ref, left_ref, _,
-                    t0_ref, t1_ref, t2_ref, t3_ref, m0_ref, m1_ref, m2_ref, token_ref):
-    tokens = hidden_ref.shape[1]
-    gate_grad, up_grad = gate_grad_ref[...], up_grad_ref[...]
-    grads = jnp.concatenate([gate_grad, up_grad])
+def term_kernel(place_ref, w_ref, gate_grad_ref, up_grad_ref, _, t0_ref, t1_ref, t2_ref, t3_ref, token_ref):
+    grads = jnp.concatenate([gate_grad_ref[...], up_grad_ref[...]])
     rows = t0_ref.shape[0]
     for i, ref in enumerate((t0_ref, t1_ref, t2_ref, t3_ref)):
         at = pl.multiple_of(lax.rem(place_ref[0] + i, SIDE) * rows, 16)
         ref[...] = dot(w_ref[pl.ds(at, rows), :], grads, 1, 0).astype(BF)
+    token_ref[...] = jnp.zeros_like(token_ref)
+
+
+def terms(place, w_both, gate_grad, up_grad, other):
+    vmem = pl.BlockSpec(memory_space=pltpu.VMEM)
+    tokens = gate_grad.shape[1]
+    width, both = w_both.shape
+    out = pl.pallas_call(
+        term_kernel,
+        out_shape=(jax.ShapeDtypeStruct((width // SIDE, tokens), BF),) * SIDE
+        + (jax.ShapeDtypeStruct((8, LANES), F32),),
+        in_specs=[pl.BlockSpec(memory_space=pltpu.SMEM)] + [vmem] * 4,
+        out_specs=(vmem,) * (SIDE + 1),
+        compiler_params=pltpu.CompilerParams(vmem_limit_bytes=20 * MIB),
+        cost_estimate=pl.CostEstimate(flops=2 * width * both * tokens, bytes_accessed=4 * MIB, transcendentals=0),
+    )(place, w_both, gate_grad, up_grad, other)
+    return out[:SIDE], out[SIDE]
+
+
+def matrices_kernel(gate_grad_ref, up_grad_ref, hidden_ref, x_ref, dy_ref, left_hbm, _,
+                    m0_ref, m1_ref, m2_ref, token_ref, left_ref, sems):
+    loads = [pltpu.make_async_copy(left_hbm.at[3 + k], left_ref.at[k], sems.at[k]) for k in range(3)]
+    for copy in loads:
+        copy.start()
+    tokens = hidden_ref.shape[1]
     x = x_ref[:, :tokens]
-    m0_ref[...] = dot(gate_grad, x, 1, 1) + left_ref[3].astype(F32)
-    m1_ref[...] = dot(up_grad, x, 1, 1) + left_ref[4].astype(F32)
+    m0_ref[...] = dot(gate_grad_ref[...], x, 1, 1)
+    m1_ref[...] = dot(up_grad_ref[...], x, 1, 1)
     swapped = dot(hidden_ref[...], dy_ref[:, :tokens], 1, 1)
-    block = rows // SIDE
+    block = swapped.shape[1] // (SIDE * SIDE)
     parts = [
         swapped[:, (x * SIDE + y) * block : (x * SIDE + y + 1) * block] for y in range(SIDE) for x in range(SIDE)
     ]
-    m2_ref[...] = jnp.concatenate(parts, axis=1) + left_ref[5].astype(F32)
+    m2_ref[...] = jnp.concatenate(parts, axis=1)
+    for k, m_ref in enumerate((m0_ref, m1_ref, m2_ref)):
+        loads[k].wait()
+        m_ref[...] += left_ref[k].astype(F32)
     token_ref[...] = jnp.zeros_like(token_ref)
 
 
-def products(place, w_both, grads, x_all, dy_all, weights, other):
+def grad_matrices(grads, x_all, dy_all, weights, other):
     vmem = pl.BlockSpec(memory_space=pltpu.VMEM)
     hid, tokens = grads[0].shape
-    width = w_both.shape[0]
+    width = dy_all.shape[0]
     out = pl.pallas_call(
-        products_kernel,
-        out_shape=(jax.ShapeDtypeStruct((width // SIDE, tokens), BF),) * SIDE
-        + (jax.ShapeDtypeStruct((hid, width), F32),) * 3
-        + (jax.ShapeDtypeStruct((8, LANES), F32),),
-        in_specs=[pl.BlockSpec(memory_space=pltpu.SMEM)] + [vmem] * 8,
-        out_specs=(vmem,) * (SIDE + 4),
-        compiler_params=pltpu.CompilerParams(vmem_limit_bytes=20 * MIB),
-        cost_estimate=pl.CostEstimate(flops=10 * hid * width * tokens, bytes_accessed=12 * MIB, transcendentals=0),
-    )(place, w_both, *grads, x_all, dy_all, weights, other)
-    return out[:SIDE], out[SIDE : SIDE + 3], out[-1]
+        matrices_kernel,
+        out_shape=(jax.ShapeDtypeStruct((hid, width), F32),) * 3 + (jax.ShapeDtypeStruct((8, LANES), F32),),
+        in_specs=[vmem] * 5 + [pl.BlockSpec(memory_space=pltpu.HBM), vmem],
+        out_specs=(vmem,) * 4,
+        scratch_shapes=[pltpu.VMEM((3, hid, width), BF), pltpu.SemaphoreType.DMA((3,))],
+        compiler_params=pltpu.CompilerParams(vmem_limit_bytes=20 * MIB),
+        cost_estimate=pl.CostEstimate(flops=6 * hid * width * tokens, bytes_accessed=9 * MIB, transcendentals=0),
+    )(*grads, x_all, dy_all, weights, other)
+    return out[:3], out[3]
 
 
 def mean_kernel(value_ref, _, out_ref):
@@ -319,15 +364,15 @@
     return pl.pallas_call(
         mean_kernel,
         out_shape=jax.ShapeDtypeStruct(value.shape[1:], F32),
-        in_specs=[vmem, vmem],
+        in_specs=[vmem, pl.BlockSpec(memory_space=pl.ANY)],
         out_specs=vmem,
         compiler_params=pltpu.CompilerParams(vmem_limit_bytes=20 * MIB),
     )(value, token)
 
 
-def sketch_kernel(core_ref, p_mine_ref, p_other_ref, m0_ref, m1_ref, m2_ref, mine_ref, theirs_ref, gram_ref):
+def sketch_kernel(core_ref, p_ref, m0_ref, m1_ref, m2_ref, mine_ref, theirs_ref, gram_ref):
     core = core_ref[0]
-    p = whole(core, p_mine_ref[...], p_other_ref[...])
+    p = p_ref[...]
     rows, grams = [], []
     for k, m_ref in enumerate((m0_ref, m1_ref, m2_ref)):
         p_k = p[k * RANK : (k + 1) * RANK]
@@ -348,19 +393,19 @@
             theirs_ref[tile : tile + 8, :] = theirs[rows, cols]
 
 
-def sketch(core, p_mine, p_other, matrices):
+def sketch(core, p_trans, matrices):
     vmem = pl.BlockSpec(memory_space=pltpu.VMEM)
     out = jax.ShapeDtypeStruct((TILES * 8, LANES), F32)
     return pl.pallas_call(
         sketch_kernel,
         out_shape=(out, out, jax.ShapeDtypeStruct((24, LANES), F32)),
-        in_specs=[pl.BlockSpec(memory_space=pltpu.SMEM)] + [vmem] * 5,
+        in_specs=[pl.BlockSpec(memory_space=pltpu.SMEM)] + [vmem] * 4,
         out_specs=(vmem,) * 3,
         compiler_params=pltpu.CompilerParams(vmem_limit_bytes=20 * MIB),
-    )(core, p_mine, p_other, *matrices)
-
-
-def ortho_kernel(core_ref, gram_ref, p_mine_ref, p_other_ref, _, inverse_ref, p_ortho_ref):
+    )(core, p_trans, *matrices)
+
+
+def ortho_kernel(gram_ref, inverse_ref, token_ref):
     gram = gram_ref[...]
     gram = jnp.concatenate([gram[:, i * RANK : (i + 1) * RANK] for i in range(4)])
     gram = jnp.stack([gram[k * RANK : (k + 1) * RANK] for k in range(3)])
@@ -377,27 +422,24 @@
     diag = jnp.sum(jnp.where(rows == cols, work[:, :, :RANK], 0.0), axis=2, keepdims=True)
     inverse = work[:, :, RANK:] * lax.rsqrt(diag)
     inverse_ref[...] = inverse
-    p = whole(core_ref[0], p_mine_ref[...], p_other_ref[...])
-    for k in range(3):
-        part = slice(k * RANK, (k + 1) * RANK)
-        p_ortho_ref[part, :] = dot3(inverse[k], p[part], 1, 0)
-
-
-def ortho(core, gram, p_mine, p_other, token):
+    token_ref[...] = jnp.zeros_like(token_ref)
+
+
+def ortho(gram):
     vmem = pl.BlockSpec(memory_space=pltpu.VMEM)
     return pl.pallas_call(
         ortho_kernel,
         out_shape=(
             jax.ShapeDtypeStruct((3, RANK, RANK), F32),
-            jax.ShapeDtypeStruct((ROWS, p_mine.shape[1]), F32),
+            jax.ShapeDtypeStruct((8, LANES), F32),
         ),
-        in_specs=[pl.BlockSpec(memory_space=pltpu.SMEM)] + [vmem] * 4,
+        in_specs=[vmem],
         out_specs=(vmem, vmem),
         cost_estimate=pl.CostEstimate(flops=MIB * 4096, bytes_accessed=MIB, transcendentals=0),
-    )(core, gram, p_mine, p_other, token)
-
-
-def finish_kernel(place_ref, s_mine_ref, s_other_ref, inverse_ref, p_ortho_ref, m0_hbm, m1_hbm, m2_hbm,
+    )(gram)
+
+
+def finish_kernel(place_ref, s_mine_ref, s_other_ref, inverse_ref, p_ref, m0_hbm, m1_hbm, m2_hbm,
                   error_hbm, q_ref, m_ref, error_ref, sems):
     copies = [pltpu.make_async_copy(m, m_ref.at[k], sems.at[k]) for k, m in enumerate((m0_hbm, m1_hbm, m2_hbm))]
     for copy in copies:
@@ -418,8 +460,9 @@
         part = slice(k * RANK, (k + 1) * RANK)
         q_new = dot3(inverse_ref[k], s[part], 1, 0)
         q_rows.append(q_new)
+        p_ortho = dot3(inverse_ref[k], p_ref[part, :], 1, 0)
         copies[k].wait()
-        error_ref[k] = (m_ref[k] - dot3(p_ortho_ref[part, :], q_new, 0, 0)).astype(BF)
+        error_ref[k] = (m_ref[k] - dot3(p_ortho, q_new, 0, 0)).astype(BF)
         stores.append(pltpu.make_async_copy(error_ref.at[k], error_hbm.at[0, k], sems.at[3 + k]))
         stores[k].start()
     shard = q_ref.shape[1]
@@ -429,7 +472,7 @@
         copy.wait()
 
 
-def finish(place, s_mine, s_other, inverse, p_ortho, matrices, shard):
+def finish(place, s_mine, s_other, inverse, p_trans, matrices, shard):
     vmem = pl.BlockSpec(memory_space=pltpu.VMEM)
     hbm = pl.BlockSpec(memory_space=pltpu.HBM)
     hid, width = matrices[0].shape
@@ -444,7 +487,7 @@
             pltpu.SemaphoreType.DMA((6,)),
         ],
         compiler_params=pltpu.CompilerParams(vmem_limit_bytes=20 * MIB),
-    )(place, s_mine, s_other, inverse, p_ortho, *matrices)
+    )(place, s_mine, s_other, inverse, p_trans, *matrices)
 
 
 def after(values, other):
@@ -455,12 +498,8 @@
     return lax.ppermute(value, "dp", CORE_PAIR)
 
 
-def z_ring(k):
-    return [(z * 2 + c, (z + k) % DEPTH * 2 + c) for z in range(DEPTH) for c in range(2)]
-
-
-def z_ring_swap():
-    return [(z * 2 + c, (z ^ 1) * 2 + c) for z in range(DEPTH) for c in range(2)]
+def z_swap(bit):
+    return [(z * 2 + c, (z ^ bit) * 2 + c) for z in range(DEPTH) for c in range(2)]
 
 
 def take_kernel(value_ref, _, out_ref):
@@ -521,31 +560,30 @@
     x_part, dy_parts = pack(hidden_in.T, out_grad.T, q_init.reshape(ROWS, shard))
     pieces, dy_all = gather_all(x_part, dy_parts, me)
     spot = jnp.stack([y, core])
-    gate_grad, up_grad, hidden, p_mine, p_theirs, x_all = backward(spot, pieces, dy_all, weights)
+    gate_grad, up_grad, hidden, p_part, x_all = backward(spot, pieces, dy_all, weights)
     core = core.reshape(1)
-    p_pair = (p_mine + swap_core(p_theirs).astype(F32)).astype(BF)
-    p_next = lax.ppermute(p_pair, "dp", z_ring_swap())
-    blocks, matrices, token = products(
-        spot, w_both, (gate_grad, up_grad, hidden), x_all, dy_all, weights, p_pair
-    )
-    p_two = add((p_pair, p_next), token, 1.0)
-    p_half = add([p_two] + [lax.ppermute(p_two, "dp", z_ring(k)) for k in (4, 2, 6)], token, 1.0 / n_workers)
-    p_other = swap_core(p_half)
+    p_pair = add((p_part, swap_core(p_part)), p_part, 1.0, BF)
+    p_next = lax.ppermute(p_pair, "dp", z_swap(1))
+    matrices, token = grad_matrices((gate_grad, up_grad, hidden), x_all, dy_all, weights, p_pair)
+    p_pair = add((p_pair, p_next), token, 1.0, BF)
+    p_pair = add((p_pair, lax.ppermute(p_pair, "dp", z_swap(2))), token, 1.0, BF)
+    blocks, token = terms(spot, w_both, gate_grad, up_grad, p_pair)
+    p_trans = add((p_pair, lax.ppermute(p_pair, "dp", z_swap(4))), token, 1.0 / n_workers)
     got = send_blocks(blocks)
-    s_mine, s_theirs, gram = sketch(core, p_half, p_other, matrices)
+    s_mine, s_theirs, gram = sketch(core, p_trans, matrices)
     s_pair = (s_mine + swap_core(s_theirs)).reshape(n_tensor, -1, LANES)
     gram = jnp.broadcast_to(gram[None], (n_tensor,) + gram.shape)
     sums = jnp.sum(lax.all_to_all(jnp.concatenate([s_pair, gram], axis=1), "tensor", 0, 0, tiled=True), axis=0)
     s_part, gram = sums[: s_pair.shape[1]], sums[s_pair.shape[1] :]
     s_all = spread(s_part, "dp", Z_GROUPS, DEPTH)
-    inverse, p_ortho = ortho(core, gram, p_half, p_other, gram)
-    s_part = mean(s_all, inverse)
+    inverse, token = ortho(gram)
+    s_part = mean(s_all, token)
     got = send_parts(got, x, gram)
     input_grad, token = close(got)
     input_grad = input_grad.T
     s_half = take(spread(s_part, "tensor", None, n_tensor).reshape(-1, LANES), token)
     error_out, q_out = finish(
-        jnp.stack([core[0], me]), s_half, swap_core(s_half), inverse, p_ortho, matrices, shard
+        jnp.stack([core[0], me]), s_half, swap_core(s_half), inverse, p_trans, matrices, shard
     )
     return (input_grad, error_out, q_out.reshape(q_init.shape))
 

time: 143 us -> 141 us (0.986)
  Pallas kernels: 25.4 us -> 29.8 us
  local copies, waits for them, and re-layouts: 14.6 us -> 10.5 us
  waiting for transfers between devices: 38.7 us -> 35.7 us
    unnamed x44 -> x32, local copies, waits for them, and re-layouts: 11.1 us -> 7.03 us
    pallas_call x2 -> x3, Pallas kernels: 4.88 us -> 8.79 us  [the longest x1 3.51 us: grad_matrices(): pl.pallas_call(matrices_kernel, out_shape=(jax.ShapeDtypeStruct((hid, wid...]
    ppermute x4 -> x3, waiting for transfers between devices: 3.99 us -> 1.77 us  [the longest x1 1.76 us: per_device(): lax.ppermute(p_pair, 'dp', z_swap(2))]
    ppermute x4 -> x3, waiting for transfers between devices: 3.82 us -> 2.95 us  [swap_core(): return lax.ppermute(value, 'dp', CORE_PAIR)]
    ppermute x4 -> x3, starting transfers between devices: 11 us -> 10.9 us  [the longest x1 5.2 us: per_device(): lax.ppermute(p_pair, 'dp', z_swap(4))]
    ppermute x4 -> x3, starting transfers between devices: 8.13 us -> 8.07 us  [swap_core(): return lax.ppermute(value, 'dp', CORE_PAIR)]
  transfers between devices with their start and end apart: 25 -> 23, of which waited for: 16 -> 13; matrix products, arithmetic and copies ran while one was open for 1% -> 2% of each run, Pallas kernels for 8% -> 11%
where the time goes in v4:
time: 141 us; the launch traced here: 140 us
  starting transfers between devices  62.2 us (44%)
  waiting for transfers between devices  35.7 us (25%)
  Pallas kernels  29.8 us (21%)
  local copies, waits for them, and re-layouts  10.5 us (7%)
    ppermute x6, waiting for transfers between devices, ring_pieces(): near[k] = lax.ppermute(value, 'tensor', ring(SIDE - k))  18.2 us
    all_to_all x3, starting transfers between devices, spread(): lax.all_to_all(jnp.broadcast_to(value[None], (size,) + value.shape), axis...  13.7 us
    ppermute x6, starting transfers between devices, ring_pieces(): near[k] = lax.ppermute(value, 'tensor', ring(SIDE - k))  9.36 us
    ppermute x3, starting transfers between devices, swap_core(): return lax.ppermute(value, 'dp', CORE_PAIR)  8.07 us
    unnamed x32, local copies, waits for them, and re-layouts  7.03 us
    pallas_call x1, Pallas kernels, backward(): pl.pallas_call(backward_kernel, out_shape=(grads, grads, grads, jax.Shape...  6.49 us
    all_to_all x1, starting transfers between devices, per_device(): lax.all_to_all(jnp.concatenate([s_pair, gram], axis=1), 'tensor', 0, 0, t...  6.47 us
    ppermute x1, starting transfers between devices, per_device(): lax.ppermute(p_pair, 'dp', z_swap(4))  5.2 us
  transfers between devices with their start and end apart: 23, of which 13 were waited for; matrix products, arithmetic and copies ran while one was open for 2% of the time, Pallas kernels for 11%

profile of v4, /device:TPU:1, one launch (start us, length us, event | category | flops | bytes accessed | tf_op | source)
XLA Modules:
  0.0 140.1 jit_solution(2741463084923637967)
XLA Ops:
  0.6 2.8 %shard_map.95 = (bf16[56,1152]{1,0:T(8,128)(2,1)}, bf16[4,56,1152]{2,1,0:T(8,128)(2,1)}) custom-call(bf16[56,1024]{1,0:T(8,128)(2,1)} %bitcast.27, bf16[56,1024]{1,0:T(8,128)(2,1)} %bitcast.28, f32[96,56]{1,0:T(8,128)} %bitcast.29), custom_call_target="tpu_custom_call" | custom-call | tf_op jit(solution)/shard_map/pallas_call | solution.py:68
  3.4 5.0 %all-to-all-start = ((bf16[4,56,1152]{2,1,0:T(8,128)(2,1)}), bf16[4,56,1152]{2,1,0:T(8,128)(2,1)S(1)}, u32[]{:S(2)}, u32[]{:S(2)}) async-start(bf16[4,56,1152]{2,1,0:T(8,128)(2,1)} %get-tuple-element.48), calls=%async_computation | async-start | bytes 1032192 | tf_op jit(solution)/shard_map/all_to_all | solution.py:106
  8.5 1.2 collective-permute-start.2
  9.7 2.5 %collective-permute-start.1 = (bf16[56,1152]{1,0:T(8,128)(2,1)}, bf16[56,1152]{1,0:T(8,128)(2,1)S(1)}, u32[]{:S(2)}, u32[]{:S(2)}) collective-permute-start(bf16[56,1152]{1,0:T(8,128)(2,1)} %get-tuple-element.49.p0_ref), channel_id=1, source_target_pairs={{0,2},{1,3},{2,0},{3,1},{4,6},{5,7},{6,4},{7,5},{8,10},{9,11},{10,... | collective-permute-start | bytes 387080 | tf_op jit(solution)/shard_map/ppermute | solution.py:43
  12.1 1.2 collective-permute-start
  13.3 0.4 collective-permute-done.2.p3_ref
  13.7 4.0 %collective-permute-done.1.p2_ref = bf16[56,1152]{1,0:T(8,128)(2,1)S(1)} collective-permute-done((bf16[56,1152]{1,0:T(8,128)(2,1)}, bf16[56,1152]{1,0:T(8,128)(2,1)S(1)}, u32[]{:S(2)}, u32[]{:S(2)}) %collective-permute-start.1) | collective-permute-done | bytes 129056 | tf_op jit(solution)/shard_map/ppermute | solution.py:43
  17.6 0.0 all-to-all-done
  17.6 0.9 copy-done.10
  18.5 0.7 shard_map.96
  19.2 1.5 %broadcast_in_dim.8 = bf16[4,4,56,1152]{3,2,1,0:T(8,128)(2,1)} broadcast(bf16[4,56,1152]{2,1,0:T(8,128)(2,1)S(1)} %all-to-all-done), dimensions={1,2,3} | broadcast | bytes 2580480 | tf_op jit(solution)/shard_map/broadcast_in_dim | solution.py:36
  20.7 3.7 %all-to-all-start.1 = ((bf16[4,4,56,1152]{3,2,1,0:T(8,128)(2,1)}), bf16[4,4,56,1152]{3,2,1,0:T(8,128)(2,1)S(1)}, u32[]{:S(2)}, u32[]{:S(2)}) async-start(bf16[4,4,56,1152]{3,2,1,0:T(8,128)(2,1)} %broadcast_in_dim.8), calls=%async_computation.1 | async-start | bytes 4128768 | tf_op jit(solution)/shard_map/all_to_all | solution.py:35
  24.4 1.0 collective-permute-start.5
  25.4 2.4 %collective-permute-start.4 = (bf16[4,56,1152]{2,1,0:T(8,128)(2,1)S(1)}, bf16[4,56,1152]{2,1,0:T(8,128)(2,1)}, u32[]{:S(2)}, u32[]{:S(2)}) collective-permute-start(bf16[4,56,1152]{2,1,0:T(8,128)(2,1)S(1)} %shard_map.96), channel_id=1, source_target_pairs={{0,8},{1,9},{2,10},{3,11},{4,12},{5,13},{6,14},{7,15},{8,0},{9,1},... | collective-permute-start | bytes 1548296 | tf_op jit(solution)/shard_map/ppermute | solution.py:43
  27.8 1.2 collective-permute-start.3
  29.0 1.3 copy-done.4
  30.3 1.0 copy-done.6
  31.4 1.0 copy-done.7
  32.4 2.8 %shard_map.94 = (bf16[112,256,896]{2,1,0:T(8,128)(2,1)}, bf16[896,512]{1,0:T(8,128)(2,1)S(1)}, f32[8,128]{1,0:T(8,128)}) custom-call(bf16[256,896]{1,0:T(8,128)(2,1)S(1)} %copy-done.5, bf16[256,896]{1,0:T(8,128)(2,1)S(1)} %copy-done.6, bf16[256,896]{1,0:T(8,128)(2,1)S(1)} %copy-done.7, bf16[1,3,256,896]{3,2,1,0:T(8,128)(2,1)S(1)} %copy-done.4), custom_call_target="tpu_custom_call" | custom-call | tf_op jit(solution)/shard_map/pallas_call | solution.py:194
  35.2 0.0 copy-start.14
  35.2 0.9 copy-done.14
  36.1 0.1 pad_add_fusion.place_ref
  36.2 0.6 collective-permute-done.5
  36.8 11.2 %collective-permute-done.4 = bf16[4,56,1152]{2,1,0:T(8,128)(2,1)} collective-permute-done((bf16[4,56,1152]{2,1,0:T(8,128)(2,1)S(1)}, bf16[4,56,1152]{2,1,0:T(8,128)(2,1)}, u32[]{:S(2)}, u32[]{:S(2)}) %collective-permute-start.4) | collective-permute-done | bytes 516128 | tf_op jit(solution)/shard_map/ppermute | solution.py:43
  48.0 2.0 %collective-permute-done.3 = bf16[4,56,1152]{2,1,0:T(8,128)(2,1)} collective-permute-done((bf16[4,56,1152]{2,1,0:T(8,128)(2,1)S(1)}, bf16[4,56,1152]{2,1,0:T(8,128)(2,1)}, u32[]{:S(2)}, u32[]{:S(2)}) %collective-permute-start.3) | collective-permute-done | bytes 516128 | tf_op jit(solution)/shard_map/ppermute | solution.py:43
  50.0 6.5 %shard_map.97 = (bf16[256,1024]{1,0:T(8,128)(2,1)S(1)}, bf16[256,1024]{1,0:T(8,128)(2,1)S(1)}, bf16[256,1024]{1,0:T(8,128)(2,1)S(1)}, bf16[96,256]{1,0:T(8,128)(2,1)S(1)}, bf16[896,1152]{1,0:T(8,128)(2,1)S(1)}) custom-call(s32[2]{0:T(128)S(1)} %pad_add_fusion.place_ref, bf16[224,1152]{1,0:T(8,128)(2,1)S(1)} %bitcast.22, bf16[224,1152]{1,0:T(8,128)(2,1)} %bitcast.7.p1_ref, ...), custom_call_target="tpu_custom_call" | custom-call | flops 1409286144 | bytes 8388608 | tf_op jit(solution)/shard_map/pallas_call | solution.py:272
  56.5 1.7 %collective-permute-start.6 = (bf16[96,256]{1,0:T(8,128)(2,1)S(1)}, bf16[96,256]{1,0:T(8,128)(2,1)S(1)}, u32[]{:S(2)}, u32[]{:S(2)}) collective-permute-start(bf16[96,256]{1,0:T(8,128)(2,1)S(1)} %get-tuple-element.64.refs_0_.refs_2_), channel_id=1, source_target_pairs={{0,16},{16,0},{32,48},{48,32},{64,80},{80,64},{96,112},{112,96},{1... | collective-permute-start | bytes 147464 | tf_op jit(solution)/shard_map/ppermute | solution.py:498
  58.3 0.9 collective-permute-done.6.refs_1_
  59.2 2.6 %collective-permute-start.7 = (bf16[96,256]{1,0:T(8,128)(2,1)S(1)}, bf16[96,256]{1,0:T(8,128)(2,1)S(1)}, u32[]{:S(2)}, u32[]{:S(2)}) collective-permute-start(bf16[96,256]{1,0:T(8,128)(2,1)S(1)} %shard_map.98._.refs_0_), channel_id=1, source_target_pairs={{0,32},{16,48},{32,0},{48,16},{64,96},{80,112},{96,64},{112,80},{1... | collective-permute-start | bytes 147464 | tf_op jit(solution)/shard_map/ppermute | solution.py:566
  61.8 3.5 %shard_map.99 = (f32[256,896]{1,0:T(8,128)S(1)}, f32[256,896]{1,0:T(8,128)S(1)}, f32[256,896]{1,0:T(8,128)S(1)}, f32[8,128]{1,0:T(8,128)S(1)}) custom-call(bf16[256,1024]{1,0:T(8,128)(2,1)S(1)} %get-tuple-element.62.gate_grad_ref, bf16[256,1024]{1,0:T(8,128)(2,1)S(1)} %get-tuple-element.63.up_grad_ref, bf16[256,1024]{1,0:T(8,128)(2,1)S(1)} %get-tuple-element.65.hidden_ref, ...), custom_call_target="tpu_custom_call" | custom-call | flops 1409286144 | bytes 9437184 | tf_op jit(solution)/shard_map/pallas_call | solution.py:343
  65.3 3.1 %collective-permute-start.8 = (bf16[96,256]{1,0:T(8,128)(2,1)S(1)}, bf16[96,256]{1,0:T(8,128)(2,1)S(1)}, u32[]{:S(2)}, u32[]{:S(2)}) collective-permute-start(bf16[96,256]{1,0:T(8,128)(2,1)S(1)} %shard_map.100.refs_0_), channel_id=1, source_target_pairs={{0,64},{16,80},{32,96},{48,112},{64,0},{80,16},{96,32},{112,48},{1... | collective-permute-start | bytes 147464 | tf_op jit(solution)/shard_map/ppermute | solution.py:569
  68.4 1.8 %collective-permute-done.8.refs_1_ = bf16[96,256]{1,0:T(8,128)(2,1)S(1)} collective-permute-done((bf16[96,256]{1,0:T(8,128)(2,1)S(1)}, bf16[96,256]{1,0:T(8,128)(2,1)S(1)}, u32[]{:S(2)}, u32[]{:S(2)}) %collective-permute-start.8) | collective-permute-done | bytes 49184 | tf_op jit(solution)/shard_map/ppermute | solution.py:569
  70.2 5.2 %collective-permute-start.12 = (bf16[96,256]{1,0:T(8,128)(2,1)S(1)}, bf16[96,256]{1,0:T(8,128)(2,1)S(1)}, u32[]{:S(2)}, u32[]{:S(2)}) collective-permute-start(bf16[96,256]{1,0:T(8,128)(2,1)S(1)} %shard_map.101._.refs_0_), channel_id=1, source_target_pairs={{0,128},{16,144},{32,160},{48,176},{64,192},{80,208},{96,224},{112... | collective-permute-start | bytes 147464 | tf_op jit(solution)/shard_map/ppermute | solution.py:571
  75.4 2.4 %shard_map.102 = (bf16[224,1024]{1,0:T(8,128)(2,1)S(1)}, bf16[224,1024]{1,0:T(8,128)(2,1)}, bf16[224,1024]{1,0:T(8,128)(2,1)}, bf16[224,1024]{1,0:T(8,128)(2,1)}, f32[8,128]{1,0:T(8,128)S(1)}) custom-call(s32[2]{0:T(128)S(1)} %pad_add_fusion.place_ref, bf16[896,512]{1,0:T(8,128)(2,1)S(1)} %copy-done.15, ...), custom_call_target="tpu_custom_call" | custom-call | flops 939524096 | bytes 4194304 | tf_op jit(solution)/shard_map/pallas_call | solution.py:306
  77.9 0.6 shard_map.104
  78.5 0.1 copy-done.8
  78.6 2.2 %collective-permute-start.13 = (f32[384,128]{1,0:T(8,128)S(1)}, f32[384,128]{1,0:T(8,128)S(1)}, u32[]{:S(2)}, u32[]{:S(2)}) collective-permute-start(f32[384,128]{1,0:T(8,128)S(1)} %get-tuple-element.77), channel_id=1, source_target_pairs={{0,16},{16,0},{32,48},{48,32},{64,80},{80,64},{96,112},{112,96},{1... | collective-permute-start | bytes 589832 | tf_op jit(solution)/shard_map/ppermute | solution.py:498
  80.8 1.1 collective-permute-done.13
  82.0 0.8 pad_maximum_fusion
  82.8 6.5 %all-to-all-start.2 = ((f32[16,48,128]{2,1,0:T(8,128)}), f32[16,48,128]{2,1,0:T(8,128)S(1)}, u32[]{:S(2)}, u32[]{:S(2)}) async-start(f32[16,48,128]{2,1,0:T(8,128)} %pad_maximum_fusion), calls=%async_computation.2 | async-start | bytes 786432 | tf_op jit(solution)/shard_map/all_to_all | solution.py:576
  89.2 1.4 collective-permute-start.9
  90.6 1.4 collective-permute-start.10
  92.0 1.6 %collective-permute-start.11 = (bf16[224,1024]{1,0:T(8,128)(2,1)}, bf16[224,1024]{1,0:T(8,128)(2,1)}, u32[]{:S(2)}, u32[]{:S(2)}) collective-permute-start(bf16[224,1024]{1,0:T(8,128)(2,1)} %get-tuple-element.71), channel_id=1, source_target_pairs={{0,8},{1,9},{2,10},{3,11},{4,12},{5,13},{6,14},{7,15},{8,0},{9,1},... | collective-permute-start | bytes 1376264 | tf_op jit(solution)/shard_map/ppermute | solution.py:120
  93.6 5.2 %all-to-all-done.2 = f32[16,48,128]{2,1,0:T(8,128)S(1)} async-done(((f32[16,48,128]{2,1,0:T(8,128)}), f32[16,48,128]{2,1,0:T(8,128)S(1)}, u32[]{:S(2)}, u32[]{:S(2)}) %all-to-all-start.2) | async-done | bytes 393248 | tf_op jit(solution)/shard_map/all_to_all | solution.py:576
  98.8 0.6 fusion
  99.4 0.6 broadcast_in_dim.10
  100.0 6.4 %all-to-all-start.3 = ((f32[8,24,128]{2,1,0:T(8,128)}), f32[8,24,128]{2,1,0:T(8,128)S(1)}, u32[]{:S(2)}, u32[]{:S(2)}) async-start(f32[8,24,128]{2,1,0:T(8,128)} %broadcast_in_dim.10), calls=%async_computation.3 | async-start | bytes 196608 | tf_op jit(solution)/shard_map/all_to_all | solution.py:35
  106.5 4.2 %shard_map.107 = (f32[3,32,32]{2,1,0:T(8,128)}, f32[8,128]{1,0:T(8,128)}) custom-call(f32[24,128]{1,0:T(8,128)} %get-tuple-element.90._.gram_ref), custom_call_target="tpu_custom_call" | custom-call | flops 4294967296 | bytes 1048576 | tf_op jit(solution)/shard_map/pallas_call | solution.py:430
  110.7 3.5 %all-to-all-done.3.value_ref = f32[8,24,128]{2,1,0:T(8,128)S(1)} async-done(((f32[8,24,128]{2,1,0:T(8,128)}), f32[8,24,128]{2,1,0:T(8,128)S(1)}, u32[]{:S(2)}, u32[]{:S(2)}) %all-to-all-start.3) | async-done | bytes 98336 | tf_op jit(solution)/shard_map/all_to_all | solution.py:35
  114.2 0.7 copy-done.13
  114.9 0.7 broadcast_in_dim.11
  115.6 3.5 %all-to-all-start.4 = ((f32[16,24,128]{2,1,0:T(8,128)}), f32[16,24,128]{2,1,0:T(8,128)S(1)}, u32[]{:S(2)}, u32[]{:S(2)}) async-start(f32[16,24,128]{2,1,0:T(8,128)} %broadcast_in_dim.11), calls=%async_computation.4 | async-start | bytes 393216 | tf_op jit(solution)/shard_map/all_to_all | solution.py:35
  119.2 1.0 copy-done.9
  120.2 1.5 %shard_map.105 = (bf16[56,1024]{1,0:T(8,128)(2,1)S(1)}, bf16[56,1024]{1,0:T(8,128)(2,1)S(1)}, bf16[56,1024]{1,0:T(8,128)(2,1)S(1)}, bf16[56,1024]{1,0:T(8,128)(2,1)S(1)}) custom-call(s32[1]{0:T(128)} %bitcast.place_ref, bf16[4,56,1024]{2,1,0:T(8,128)(2,1)S(1)} %bitcast.25, bf16[4,56,1024]{2,1,0:T(8,128)(2,1)} %bitcast.12.g1_ref, ...), custom_call_target="tpu_custom_call" | custom-call | tf_op jit(solution)/shard_map/pallas_call | solution.py:133
  121.7 1.3 collective-permute-start.14
  123.0 1.4 %collective-permute-start.15 = (bf16[56,1024]{1,0:T(8,128)(2,1)S(1)}, bf16[56,1024]{1,0:T(8,128)(2,1)S(1)}, u32[]{:S(2)}, u32[]{:S(2)}) collective-permute-start(bf16[56,1024]{1,0:T(8,128)(2,1)S(1)} %get-tuple-element.81), channel_id=1, source_target_pairs={{0,3},{1,0},{2,1},{3,2},{4,7},{5,4},{6,5},{7,6},{8,11},{9,8},{10,9... | collective-permute-start | bytes 344072 | tf_op jit(solution)/shard_map/ppermute | solution.py:140
  124.4 1.5 %collective-permute-start.16 = (bf16[56,1024]{1,0:T(8,128)(2,1)S(1)}, bf16[56,1024]{1,0:T(8,128)(2,1)S(1)}, u32[]{:S(2)}, u32[]{:S(2)}) collective-permute-start(bf16[56,1024]{1,0:T(8,128)(2,1)S(1)} %get-tuple-element.82), channel_id=1, source_target_pairs={{0,2},{1,3},{2,0},{3,1},{4,6},{5,7},{6,4},{7,5},{8,10},{9,11},{10,... | collective-permute-start | bytes 344072 | tf_op jit(solution)/shard_map/ppermute | solution.py:140
  126.0 1.8 %collective-permute-done.14.refs_1_ = bf16[56,1024]{1,0:T(8,128)(2,1)S(1)} collective-permute-done((bf16[56,1024]{1,0:T(8,128)(2,1)S(1)}, bf16[56,1024]{1,0:T(8,128)(2,1)S(1)}, u32[]{:S(2)}, u32[]{:S(2)}) %collective-permute-start.14) | collective-permute-done | bytes 114720 | tf_op jit(solution)/shard_map/ppermute | solution.py:140
  127.8 2.3 %collective-permute-done.16.refs_3_ = bf16[56,1024]{1,0:T(8,128)(2,1)S(1)} collective-permute-done((bf16[56,1024]{1,0:T(8,128)(2,1)S(1)}, bf16[56,1024]{1,0:T(8,128)(2,1)S(1)}, u32[]{:S(2)}, u32[]{:S(2)}) %collective-permute-start.16) | collective-permute-done | bytes 114720 | tf_op jit(solution)/shard_map/ppermute | solution.py:140
  130.2 0.7 shard_map.106
  130.9 4.1 %collective-permute-start.17 = (f32[384,128]{1,0:T(8,128)S(1)}, f32[384,128]{1,0:T(8,128)S(1)}, u32[]{:S(2)}, u32[]{:S(2)}) collective-permute-start(f32[384,128]{1,0:T(8,128)S(1)} %shard_map.109.s_mine_ref), channel_id=1, source_target_pairs={{0,16},{16,0},{32,48},{48,32},{64,80},{80,64},{96,112},{112,96},{1... | collective-permute-start | bytes 589832 | tf_op jit(solution)/shard_map/ppermute | solution.py:498
  135.0 0.1 pad_add_fusion.1.place_ref
  135.1 1.0 collective-permute-done.17.s_other_ref
  136.1 3.9 %shard_map.110 = (bf16[1,3,256,896]{3,2,1,0:T(8,128)(2,1)}, f32[96,56]{1,0:T(8,128)}) custom-call(s32[2]{0:T(128)S(1)} %pad_add_fusion.1.place_ref, f32[384,128]{1,0:T(8,128)S(1)} %shard_map.109.s_mine_ref, f32[384,128]{1,0:T(8,128)S(1)} %collective-permute-done.17.s_other_ref, f32[3,32,32]{2,1,0:T(8,128)S(1)} %copy-done.12, ...), custom_call_target="tpu_custom_call" | custom-call | tf_op jit(solution)/shard_map/pallas_call | solution.py:479
  (41 shorter events, 0.2 us)
Async XLA Ops:
  3.4 14.2 %all-to-all-start = ((bf16[4,56,1152]{2,1,0:T(8,128)(2,1)}), bf16[4,56,1152]{2,1,0:T(8,128)(2,1)S(1)}, u32[]{:S(2)}, u32[]{:S(2)}) async-start(bf16[4,56,1152]{2,1,0:T(8,128)(2,1)} %get-tuple-element.48), calls=%async_computation | async-start | bytes 1032192 | tf_op jit(solution)/shard_map/all_to_all | solution.py:106
  8.5 5.2 %collective-permute-start.2 = (bf16[56,1152]{1,0:T(8,128)(2,1)}, bf16[56,1152]{1,0:T(8,128)(2,1)S(1)}, u32[]{:S(2)}, u32[]{:S(2)}) collective-permute-start(bf16[56,1152]{1,0:T(8,128)(2,1)} %get-tuple-element.49.p0_ref), channel_id=1, source_target_pairs={{0,1},{1,2},{2,3},{3,0},{4,5},{5,6},{6,7},{7,4},{8,9},{9,10},{10,1... | collective-permute-start | bytes 387080 | tf_op jit(solution)/shard_map/ppermute | solution.py:43
  9.7 8.0 %collective-permute-start.1 = (bf16[56,1152]{1,0:T(8,128)(2,1)}, bf16[56,1152]{1,0:T(8,128)(2,1)S(1)}, u32[]{:S(2)}, u32[]{:S(2)}) collective-permute-start(bf16[56,1152]{1,0:T(8,128)(2,1)} %get-tuple-element.49.p0_ref), channel_id=1, source_target_pairs={{0,2},{1,3},{2,0},{3,1},{4,6},{5,7},{6,4},{7,5},{8,10},{9,11},{10,... | collective-permute-start | bytes 387080 | tf_op jit(solution)/shard_map/ppermute | solution.py:43
  12.1 5.5 %collective-permute-start = (bf16[56,1152]{1,0:T(8,128)(2,1)}, bf16[56,1152]{1,0:T(8,128)(2,1)S(1)}, u32[]{:S(2)}, u32[]{:S(2)}) collective-permute-start(bf16[56,1152]{1,0:T(8,128)(2,1)} %get-tuple-element.49.p0_ref), channel_id=1, source_target_pairs={{0,3},{1,0},{2,1},{3,2},{4,7},{5,4},{6,5},{7,6},{8,11},{9,8},{10,9... | collective-permute-start | bytes 387080 | tf_op jit(solution)/shard_map/ppermute | solution.py:43
  17.6 0.9 copy-start.10
  20.7 8.3 %copy-start.5 = (bf16[256,896]{1,0:T(8,128)(2,1)S(1)}, bf16[256,896]{1,0:T(8,128)(2,1)}, u32[]{:S(2)}) copy-start(bf16[256,896]{1,0:T(8,128)(2,1)} %gate_ref.1) | copy-start | bytes 1376260
  20.7 29.3 %all-to-all-start.1 = ((bf16[4,4,56,1152]{3,2,1,0:T(8,128)(2,1)}), bf16[4,4,56,1152]{3,2,1,0:T(8,128)(2,1)S(1)}, u32[]{:S(2)}, u32[]{:S(2)}) async-start(bf16[4,4,56,1152]{3,2,1,0:T(8,128)(2,1)} %broadcast_in_dim.8), calls=%async_computation.1 | async-start | bytes 4128768 | tf_op jit(solution)/shard_map/all_to_all | solution.py:35
  24.4 12.4 %collective-permute-start.5 = (bf16[4,56,1152]{2,1,0:T(8,128)(2,1)S(1)}, bf16[4,56,1152]{2,1,0:T(8,128)(2,1)S(1)}, u32[]{:S(2)}, u32[]{:S(2)}) collective-permute-start(bf16[4,56,1152]{2,1,0:T(8,128)(2,1)S(1)} %shard_map.96), channel_id=1, source_target_pairs={{0,4},{1,5},{2,6},{3,7},{4,8},{5,9},{6,10},{7,11},{8,12},{9,13},{1... | collective-permute-start | bytes 1548296 | tf_op jit(solution)/shard_map/ppermute | solution.py:43
  25.4 22.6 %collective-permute-start.4 = (bf16[4,56,1152]{2,1,0:T(8,128)(2,1)S(1)}, bf16[4,56,1152]{2,1,0:T(8,128)(2,1)}, u32[]{:S(2)}, u32[]{:S(2)}) collective-permute-start(bf16[4,56,1152]{2,1,0:T(8,128)(2,1)S(1)} %shard_map.96), channel_id=1, source_target_pairs={{0,8},{1,9},{2,10},{3,11},{4,12},{5,13},{6,14},{7,15},{8,0},{9,1},... | collective-permute-start | bytes 1548296 | tf_op jit(solution)/shard_map/ppermute | solution.py:43
  27.8 22.2 %collective-permute-start.3 = (bf16[4,56,1152]{2,1,0:T(8,128)(2,1)S(1)}, bf16[4,56,1152]{2,1,0:T(8,128)(2,1)}, u32[]{:S(2)}, u32[]{:S(2)}) collective-permute-start(bf16[4,56,1152]{2,1,0:T(8,128)(2,1)S(1)} %shard_map.96), channel_id=1, source_target_pairs={{0,12},{1,13},{2,14},{3,15},{4,0},{5,1},{6,2},{7,3},{8,4},{9,5},{1... | collective-permute-start | bytes 1548296 | tf_op jit(solution)/shard_map/ppermute | solution.py:43
  29.0 1.3 copy-start.4
  30.3 1.0 copy-start.6
  31.4 1.0 copy-start.7
  35.2 0.9 copy-start.14
  56.5 2.6 %collective-permute-start.6 = (bf16[96,256]{1,0:T(8,128)(2,1)S(1)}, bf16[96,256]{1,0:T(8,128)(2,1)S(1)}, u32[]{:S(2)}, u32[]{:S(2)}) collective-permute-start(bf16[96,256]{1,0:T(8,128)(2,1)S(1)} %get-tuple-element.64.refs_0_.refs_2_), channel_id=1, source_target_pairs={{0,16},{16,0},{32,48},{48,32},{64,80},{80,64},{96,112},{112,96},{1... | collective-permute-start | bytes 147464 | tf_op jit(solution)/shard_map/ppermute | solution.py:498
  59.2 6.2 %collective-permute-start.7 = (bf16[96,256]{1,0:T(8,128)(2,1)S(1)}, bf16[96,256]{1,0:T(8,128)(2,1)S(1)}, u32[]{:S(2)}, u32[]{:S(2)}) collective-permute-start(bf16[96,256]{1,0:T(8,128)(2,1)S(1)} %shard_map.98._.refs_0_), channel_id=1, source_target_pairs={{0,32},{16,48},{32,0},{48,16},{64,96},{80,112},{96,64},{112,80},{1... | collective-permute-start | bytes 147464 | tf_op jit(solution)/shard_map/ppermute | solution.py:566
  61.8 13.6 %copy-start.15 = (bf16[896,512]{1,0:T(8,128)(2,1)S(1)}, bf16[896,512]{1,0:T(8,128)(2,1)}, u32[]{:S(2)}) copy-start(bf16[896,512]{1,0:T(8,128)(2,1)} %copy-done.14) | copy-start | bytes 2752516
  65.3 13.2 %copy-start = (f32[256,896]{1,0:T(8,128)}, f32[256,896]{1,0:T(8,128)S(1)}, u32[]{:S(2)}) copy-start(f32[256,896]{1,0:T(8,128)S(1)} %get-tuple-element.74.m1_ref.m1_hbm) | copy-start | bytes 2752516
  65.3 13.2 %copy-start.2 = (f32[256,896]{1,0:T(8,128)}, f32[256,896]{1,0:T(8,128)S(1)}, u32[]{:S(2)}) copy-start(f32[256,896]{1,0:T(8,128)S(1)} %get-tuple-element.75.m2_ref.m2_hbm) | copy-start | bytes 2752516
  65.3 4.8 %collective-permute-start.8 = (bf16[96,256]{1,0:T(8,128)(2,1)S(1)}, bf16[96,256]{1,0:T(8,128)(2,1)S(1)}, u32[]{:S(2)}, u32[]{:S(2)}) collective-permute-start(bf16[96,256]{1,0:T(8,128)(2,1)S(1)} %shard_map.100.refs_0_), channel_id=1, source_target_pairs={{0,64},{16,80},{32,96},{48,112},{64,0},{80,16},{96,32},{112,48},{1... | collective-permute-start | bytes 147464 | tf_op jit(solution)/shard_map/ppermute | solution.py:569
  70.2 7.6 %collective-permute-start.12 = (bf16[96,256]{1,0:T(8,128)(2,1)S(1)}, bf16[96,256]{1,0:T(8,128)(2,1)S(1)}, u32[]{:S(2)}, u32[]{:S(2)}) collective-permute-start(bf16[96,256]{1,0:T(8,128)(2,1)S(1)} %shard_map.101._.refs_0_), channel_id=1, source_target_pairs={{0,128},{16,144},{32,160},{48,176},{64,192},{80,208},{96,224},{112... | collective-permute-start | bytes 147464 | tf_op jit(solution)/shard_map/ppermute | solution.py:571
  77.8 0.8 copy-start.8
  78.6 3.3 %collective-permute-start.13 = (f32[384,128]{1,0:T(8,128)S(1)}, f32[384,128]{1,0:T(8,128)S(1)}, u32[]{:S(2)}, u32[]{:S(2)}) collective-permute-start(f32[384,128]{1,0:T(8,128)S(1)} %get-tuple-element.77), channel_id=1, source_target_pairs={{0,16},{16,0},{32,48},{48,32},{64,80},{80,64},{96,112},{112,96},{1... | collective-permute-start | bytes 589832 | tf_op jit(solution)/shard_map/ppermute | solution.py:498
  82.8 16.0 %all-to-all-start.2 = ((f32[16,48,128]{2,1,0:T(8,128)}), f32[16,48,128]{2,1,0:T(8,128)S(1)}, u32[]{:S(2)}, u32[]{:S(2)}) async-start(f32[16,48,128]{2,1,0:T(8,128)} %pad_maximum_fusion), calls=%async_computation.2 | async-start | bytes 786432 | tf_op jit(solution)/shard_map/all_to_all | solution.py:576
  89.2 29.9 %collective-permute-start.9 = (bf16[224,1024]{1,0:T(8,128)(2,1)}, bf16[224,1024]{1,0:T(8,128)(2,1)}, u32[]{:S(2)}, u32[]{:S(2)}) collective-permute-start(bf16[224,1024]{1,0:T(8,128)(2,1)} %get-tuple-element.69), channel_id=1, source_target_pairs={{0,4},{1,5},{2,6},{3,7},{4,8},{5,9},{6,10},{7,11},{8,12},{9,13},{1... | collective-permute-start | bytes 1376264 | tf_op jit(solution)/shard_map/ppermute | solution.py:120
  90.6 28.5 %collective-permute-start.10 = (bf16[224,1024]{1,0:T(8,128)(2,1)}, bf16[224,1024]{1,0:T(8,128)(2,1)}, u32[]{:S(2)}, u32[]{:S(2)}) collective-permute-start(bf16[224,1024]{1,0:T(8,128)(2,1)} %get-tuple-element.70), channel_id=1, source_target_pairs={{0,12},{1,13},{2,14},{3,15},{4,0},{5,1},{6,2},{7,3},{8,4},{9,5},{1... | collective-permute-start | bytes 1376264 | tf_op jit(solution)/shard_map/ppermute | solution.py:120
  92.0 27.1 %collective-permute-start.11 = (bf16[224,1024]{1,0:T(8,128)(2,1)}, bf16[224,1024]{1,0:T(8,128)(2,1)}, u32[]{:S(2)}, u32[]{:S(2)}) collective-permute-start(bf16[224,1024]{1,0:T(8,128)(2,1)} %get-tuple-element.71), channel_id=1, source_target_pairs={{0,8},{1,9},{2,10},{3,11},{4,12},{5,13},{6,14},{7,15},{8,0},{9,1},... | collective-permute-start | bytes 1376264 | tf_op jit(solution)/shard_map/ppermute | solution.py:120
  100.0 14.1 %all-to-all-start.3 = ((f32[8,24,128]{2,1,0:T(8,128)}), f32[8,24,128]{2,1,0:T(8,128)S(1)}, u32[]{:S(2)}, u32[]{:S(2)}) async-start(f32[8,24,128]{2,1,0:T(8,128)} %broadcast_in_dim.10), calls=%async_computation.3 | async-start | bytes 196608 | tf_op jit(solution)/shard_map/all_to_all | solution.py:35
  106.5 12.7 %copy-start.11 = (f32[24,128]{1,0:T(8,128)S(1)}, f32[24,128]{1,0:T(8,128)}, u32[]{:S(2)}) copy-start(f32[24,128]{1,0:T(8,128)} %get-tuple-element.90._.gram_ref) | copy-start | bytes 36868
  110.7 25.4 %copy-start.1 = (f32[256,896]{1,0:T(8,128)S(1)}, f32[256,896]{1,0:T(8,128)}, u32[]{:S(2)}) copy-start(f32[256,896]{1,0:T(8,128)} %copy-done) | copy-start | bytes 2752516
  110.7 25.4 %copy-start.3 = (f32[256,896]{1,0:T(8,128)S(1)}, f32[256,896]{1,0:T(8,128)}, u32[]{:S(2)}) copy-start(f32[256,896]{1,0:T(8,128)} %copy-done.2) | copy-start | bytes 2752516
  114.2 0.7 copy-start.13
  115.6 15.3 %all-to-all-start.4 = ((f32[16,24,128]{2,1,0:T(8,128)}), f32[16,24,128]{2,1,0:T(8,128)S(1)}, u32[]{:S(2)}, u32[]{:S(2)}) async-start(f32[16,24,128]{2,1,0:T(8,128)} %broadcast_in_dim.11), calls=%async_computation.4 | async-start | bytes 393216 | tf_op jit(solution)/shard_map/all_to_all | solution.py:35
  119.1 1.0 copy-start.9
  120.2 15.9 %copy-start.12 = (f32[3,32,32]{2,1,0:T(8,128)S(1)}, f32[3,32,32]{2,1,0:T(8,128)}, u32[]{:S(2)}) copy-start(f32[3,32,32]{2,1,0:T(8,128)} %get-tuple-element.86.inverse_ref) | copy-start | bytes 36868
  121.7 6.1 %collective-permute-start.14 = (bf16[56,1024]{1,0:T(8,128)(2,1)S(1)}, bf16[56,1024]{1,0:T(8,128)(2,1)S(1)}, u32[]{:S(2)}, u32[]{:S(2)}) collective-permute-start(bf16[56,1024]{1,0:T(8,128)(2,1)S(1)} %get-tuple-element.80), channel_id=1, source_target_pairs={{0,1},{1,2},{2,3},{3,0},{4,5},{5,6},{6,7},{7,4},{8,9},{9,10},{10,1... | collective-permute-start | bytes 344072 | tf_op jit(solution)/shard_map/ppermute | solution.py:140
  123.0 4.8 %collective-permute-start.15 = (bf16[56,1024]{1,0:T(8,128)(2,1)S(1)}, bf16[56,1024]{1,0:T(8,128)(2,1)S(1)}, u32[]{:S(2)}, u32[]{:S(2)}) collective-permute-start(bf16[56,1024]{1,0:T(8,128)(2,1)S(1)} %get-tuple-element.81), channel_id=1, source_target_pairs={{0,3},{1,0},{2,1},{3,2},{4,7},{5,4},{6,5},{7,6},{8,11},{9,8},{10,9... | collective-permute-start | bytes 344072 | tf_op jit(solution)/shard_map/ppermute | solution.py:140
  124.4 5.7 %collective-permute-start.16 = (bf16[56,1024]{1,0:T(8,128)(2,1)S(1)}, bf16[56,1024]{1,0:T(8,128)(2,1)S(1)}, u32[]{:S(2)}, u32[]{:S(2)}) collective-permute-start(bf16[56,1024]{1,0:T(8,128)(2,1)S(1)} %get-tuple-element.82), channel_id=1, source_target_pairs={{0,2},{1,3},{2,0},{3,1},{4,6},{5,7},{6,4},{7,5},{8,10},{9,11},{10,... | collective-permute-start | bytes 344072 | tf_op jit(solution)/shard_map/ppermute | solution.py:140
  130.9 5.2 %collective-permute-start.17 = (f32[384,128]{1,0:T(8,128)S(1)}, f32[384,128]{1,0:T(8,128)S(1)}, u32[]{:S(2)}, u32[]{:S(2)}) collective-permute-start(f32[384,128]{1,0:T(8,128)S(1)} %shard_map.109.s_mine_ref), channel_id=1, source_target_pairs={{0,16},{16,0},{32,48},{48,32},{64,80},{80,64},{96,112},{112,96},{1... | collective-permute-start | bytes 589832 | tf_op jit(solution)/shard_map/ppermute | solution.py:498

commit v5 on v4

--- a/solution.py
+++ b/solution.py
@@ -44,13 +44,15 @@
     return near
 
 
-def pack_kernel(x_hbm, dy_hbm, q_ref, x_ref, dy_ref, sems):
+def pack_kernel(x_hbm, dy_hbm, q_hbm, x_ref, dy_ref, q_ref, sems):
     tokens = x_hbm.shape[1]
     copies = [pltpu.make_async_copy(x_hbm, x_ref.at[:, pl.ds(0, tokens)], sems.at[0])]
     for i in range(SIDE):
         copies.append(pltpu.make_async_copy(dy_hbm, dy_ref.at[i, :, pl.ds(0, tokens)], sems.at[1 + i]))
-    for copy in copies:
+    q_load = pltpu.make_async_copy(q_hbm, q_ref, sems.at[1 + SIDE])
+    for copy in [q_load] + copies:
         copy.start()
+    q_load.wait()
     high, low = split(q_ref[...].T)
     both = [[half[:, k * RANK : (k + 1) * RANK] for half in (high, low)] for k in range(3)]
     x_ref[:, tokens:] = jnp.concatenate(both[0] + both[1], axis=1)
@@ -71,9 +73,9 @@
             jax.ShapeDtypeStruct((rows, tokens + LANES), BF),
             jax.ShapeDtypeStruct((SIDE, rows, tokens + LANES), BF),
         ),
-        in_specs=[anywhere, anywhere, vmem],
+        in_specs=[anywhere] * 3,
         out_specs=(vmem, vmem),
-        scratch_shapes=[pltpu.SemaphoreType.DMA((1 + SIDE,))],
+        scratch_shapes=[pltpu.VMEM(q_rows.shape, F32), pltpu.SemaphoreType.DMA((2 + SIDE,))],
         compiler_params=pltpu.CompilerParams(vmem_limit_bytes=58 * MIB),
     )(x_part, dy_part, q_rows)
 
@@ -439,12 +441,10 @@
     )(gram)
 
 
-def finish_kernel(place_ref, s_mine_ref, s_other_ref, inverse_ref, p_ref, m0_hbm, m1_hbm, m2_hbm,
-                  error_hbm, q_ref, m_ref, error_ref, sems):
-    copies = [pltpu.make_async_copy(m, m_ref.at[k], sems.at[k]) for k, m in enumerate((m0_hbm, m1_hbm, m2_hbm))]
-    for copy in copies:
-        copy.start()
-    width = m_ref.shape[2]
+def finish_kernel(place_ref, s_mine_ref, s_other_ref, inverse_ref, p_ref, m0_ref, m1_ref, m2_ref,
+                  error_hbm, q_ref, error_ref, sems):
+    m_refs = (m0_ref, m1_ref, m2_ref)
+    width = m0_ref.shape[1]
 
     def rows_of(ref):
         return jnp.concatenate(
@@ -461,9 +461,8 @@
         q_new = dot3(inverse_ref[k], s[part], 1, 0)
         q_rows.append(q_new)
         p_ortho = dot3(inverse_ref[k], p_ref[part, :], 1, 0)
-        copies[k].wait()
-        error_ref[k] = (m_ref[k] - dot3(p_ortho, q_new, 0, 0)).astype(BF)
-        stores.append(pltpu.make_async_copy(error_ref.at[k], error_hbm.at[0, k], sems.at[3 + k]))
+        error_ref[k] = (m_refs[k][...] - dot3(p_ortho, q_new, 0, 0)).astype(BF)
+        stores.append(pltpu.make_async_copy(error_ref.at[k], error_hbm.at[0, k], sems.at[k]))
         stores[k].start()
     shard = q_ref.shape[1]
     at = place_ref[1] * shard
@@ -479,12 +478,11 @@
     return pl.pallas_call(
         finish_kernel,
         out_shape=(jax.ShapeDtypeStruct((1, 3, hid, width), BF), jax.ShapeDtypeStruct((ROWS, shard), F32)),
-        in_specs=[pl.BlockSpec(memory_space=pltpu.SMEM)] + [vmem] * 4 + [hbm] * 3,
+        in_specs=[pl.BlockSpec(memory_space=pltpu.SMEM)] + [vmem] * 7,
         out_specs=(hbm, vmem),
         scratch_shapes=[
-            pltpu.VMEM((3, hid, width), F32),
             pltpu.VMEM((3, hid, width), BF),
-            pltpu.SemaphoreType.DMA((6,)),
+            pltpu.SemaphoreType.DMA((3,)),
         ],
         compiler_params=pltpu.CompilerParams(vmem_limit_bytes=20 * MIB),
     )(place, s_mine, s_other, inverse, p_trans, *matrices)
@@ -498,8 +496,8 @@
     return lax.ppermute(value, "dp", CORE_PAIR)
 
 
-def z_swap(bit):
-    return [(z * 2 + c, (z ^ bit) * 2 + c) for z in range(DEPTH) for c in range(2)]
+def dp_swap(bits):
+    return [(i, i ^ bits) for i in range(2 * DEPTH)]
 
 
 def take_kernel(value_ref, _, out_ref):
@@ -521,7 +519,10 @@
     vmem = pl.BlockSpec(memory_space=pltpu.VMEM)
 
     def kernel(*refs):
-        refs[-1][...] = (sum(ref[...].astype(F32) for ref in refs[:-2]) * scale).astype(kind)
+        terms = [ref[...].astype(F32) for ref in refs[:-2]]
+        while len(terms) > 1:
+            terms = [terms[i] + terms[i + 1] for i in range(0, len(terms), 2)]
+        refs[-1][...] = (terms[0] * scale).astype(kind)
 
     return pl.pallas_call(
         kernel,
@@ -562,13 +563,12 @@
     spot = jnp.stack([y, core])
     gate_grad, up_grad, hidden, p_part, x_all = backward(spot, pieces, dy_all, weights)
     core = core.reshape(1)
-    p_pair = add((p_part, swap_core(p_part)), p_part, 1.0, BF)
-    p_next = lax.ppermute(p_pair, "dp", z_swap(1))
-    matrices, token = grad_matrices((gate_grad, up_grad, hidden), x_all, dy_all, weights, p_pair)
-    p_pair = add((p_pair, p_next), token, 1.0, BF)
-    p_pair = add((p_pair, lax.ppermute(p_pair, "dp", z_swap(2))), token, 1.0, BF)
+    near = [p_part] + [lax.ppermute(p_part, "dp", dp_swap(bits)) for bits in (1, 2, 3)]
+    matrices, token = grad_matrices((gate_grad, up_grad, hidden), x_all, dy_all, weights, p_part)
+    p_pair = add(near, token, 1.0, BF)
     blocks, token = terms(spot, w_both, gate_grad, up_grad, p_pair)
-    p_trans = add((p_pair, lax.ppermute(p_pair, "dp", z_swap(4))), token, 1.0 / n_workers)
+    others = [lax.ppermute(p_pair, "dp", dp_swap(bits)) for bits in (4, 12, 10)]
+    p_trans = add([p_pair] + others, token, 1.0 / n_workers)
     got = send_blocks(blocks)
     s_mine, s_theirs, gram = sketch(core, p_trans, matrices)
     s_pair = (s_mine + swap_core(s_theirs)).reshape(n_tensor, -1, LANES)

time: 141 us -> 136 us (0.965)
  starting transfers between devices: 62.2 us -> 59.5 us
  Pallas kernels: 29.8 us -> 28.3 us
    all_to_all x3, starting transfers between devices: 13.7 us -> 11.9 us  [spread(): lax.all_to_all(jnp.broadcast_to(value[None], (size,) + value.shape), axis...]
    ppermute x3 -> x2, starting transfers between devices: 8.07 us -> 6.6 us  [swap_core(): return lax.ppermute(value, 'dp', CORE_PAIR)]
    ppermute x3 -> x2, waiting for transfers between devices: 2.95 us -> 2.07 us  [swap_core(): return lax.ppermute(value, 'dp', CORE_PAIR)]
    ppermute x3 -> x6, starting transfers between devices: 10.9 us -> 11.6 us  [the longest x3 7.09 us: per_device(): others = [lax.ppermute(p_pair, 'dp', dp_swap(bits)) for bits in (4, 12, 10)]]
  transfers between devices with their start and end apart: 23 -> 25, of which waited for: 13 -> 12; matrix products, arithmetic and copies ran while one was open for 2% -> 2% of each run, Pallas kernels for 11% -> 11%
where the time goes in v5:
time: 136 us; the launch traced here: 135 us
  starting transfers between devices  59.5 us (44%)
  waiting for transfers between devices  34.5 us (25%)
  Pallas kernels  28.3 us (21%)
  local copies, waits for them, and re-layouts  10.4 us (8%)
    ppermute x6, waiting for transfers between devices, ring_pieces(): near[k] = lax.ppermute(value, 'tensor', ring(SIDE - k))  18.2 us
    all_to_all x3, starting transfers between devices, spread(): lax.all_to_all(jnp.broadcast_to(value[None], (size,) + value.shape), axis...  11.9 us
    ppermute x6, starting transfers between devices, ring_pieces(): near[k] = lax.ppermute(value, 'tensor', ring(SIDE - k))  9.36 us
    ppermute x3, starting transfers between devices, per_device(): others = [lax.ppermute(p_pair, 'dp', dp_swap(bits)) for bits in (4, 12, 10)]  7.09 us
    unnamed x32, local copies, waits for them, and re-layouts  6.91 us
    ppermute x2, starting transfers between devices, swap_core(): return lax.ppermute(value, 'dp', CORE_PAIR)  6.6 us
    pallas_call x1, Pallas kernels, backward(): pl.pallas_call(backward_kernel, out_shape=(grads, grads, grads, jax.Shape...  6.49 us
    all_to_all x1, starting transfers between devices, per_device(): lax.all_to_all(jnp.concatenate([s_pair, gram], axis=1), 'tensor', 0, 0, t...  6.46 us
  transfers between devices with their start and end apart: 25, of which 12 were waited for; matrix products, arithmetic and copies ran while one was open for 2% of the time, Pallas kernels for 11%

profile of v5, /device:TPU:1, one launch (start us, length us, event | category | flops | bytes accessed | tf_op | source)
XLA Modules:
  0.0 134.8 jit_solution(2607750238320344600)
XLA Ops:
  0.6 2.0 %shard_map.95 = (bf16[56,1152]{1,0:T(8,128)(2,1)}, bf16[4,56,1152]{2,1,0:T(8,128)(2,1)}) custom-call(bf16[56,1024]{1,0:T(8,128)(2,1)} %bitcast.27, bf16[56,1024]{1,0:T(8,128)(2,1)} %bitcast.28, f32[96,56]{1,0:T(8,128)} %bitcast.29), custom_call_target="tpu_custom_call" | custom-call | tf_op jit(solution)/shard_map/pallas_call | solution.py:70
  2.7 5.0 %all-to-all-start = ((bf16[4,56,1152]{2,1,0:T(8,128)(2,1)}), bf16[4,56,1152]{2,1,0:T(8,128)(2,1)S(1)}, u32[]{:S(2)}, u32[]{:S(2)}) async-start(bf16[4,56,1152]{2,1,0:T(8,128)(2,1)} %get-tuple-element.48), calls=%async_computation | async-start | bytes 1032192 | tf_op jit(solution)/shard_map/all_to_all | solution.py:108
  7.7 1.2 collective-permute-start.2
  8.9 2.5 %collective-permute-start.1 = (bf16[56,1152]{1,0:T(8,128)(2,1)}, bf16[56,1152]{1,0:T(8,128)(2,1)S(1)}, u32[]{:S(2)}, u32[]{:S(2)}) collective-permute-start(bf16[56,1152]{1,0:T(8,128)(2,1)} %get-tuple-element.49.p0_ref), channel_id=1, source_target_pairs={{0,2},{1,3},{2,0},{3,1},{4,6},{5,7},{6,4},{7,5},{8,10},{9,11},{10,... | collective-permute-start | bytes 387080 | tf_op jit(solution)/shard_map/ppermute | solution.py:43
  11.4 1.2 collective-permute-start
  12.5 0.4 collective-permute-done.2.p3_ref
  12.9 4.0 %collective-permute-done.1.p2_ref = bf16[56,1152]{1,0:T(8,128)(2,1)S(1)} collective-permute-done((bf16[56,1152]{1,0:T(8,128)(2,1)}, bf16[56,1152]{1,0:T(8,128)(2,1)S(1)}, u32[]{:S(2)}, u32[]{:S(2)}) %collective-permute-start.1) | collective-permute-done | bytes 129056 | tf_op jit(solution)/shard_map/ppermute | solution.py:43
  16.9 0.0 collective-permute-done.p1_ref
  16.9 0.0 all-to-all-done
  16.9 0.9 copy-done.10
  17.8 0.7 shard_map.96
  18.4 1.5 %broadcast_in_dim.8 = bf16[4,4,56,1152]{3,2,1,0:T(8,128)(2,1)} broadcast(bf16[4,56,1152]{2,1,0:T(8,128)(2,1)S(1)} %all-to-all-done), dimensions={1,2,3} | broadcast | bytes 2580480 | tf_op jit(solution)/shard_map/broadcast_in_dim | solution.py:36
  19.9 3.7 %all-to-all-start.1 = ((bf16[4,4,56,1152]{3,2,1,0:T(8,128)(2,1)}), bf16[4,4,56,1152]{3,2,1,0:T(8,128)(2,1)S(1)}, u32[]{:S(2)}, u32[]{:S(2)}) async-start(bf16[4,4,56,1152]{3,2,1,0:T(8,128)(2,1)} %broadcast_in_dim.8), calls=%async_computation.1 | async-start | bytes 4128768 | tf_op jit(solution)/shard_map/all_to_all | solution.py:35
  23.7 1.0 collective-permute-start.5
  24.7 2.4 %collective-permute-start.4 = (bf16[4,56,1152]{2,1,0:T(8,128)(2,1)S(1)}, bf16[4,56,1152]{2,1,0:T(8,128)(2,1)}, u32[]{:S(2)}, u32[]{:S(2)}) collective-permute-start(bf16[4,56,1152]{2,1,0:T(8,128)(2,1)S(1)} %shard_map.96), channel_id=1, source_target_pairs={{0,8},{1,9},{2,10},{3,11},{4,12},{5,13},{6,14},{7,15},{8,0},{9,1},... | collective-permute-start | bytes 1548296 | tf_op jit(solution)/shard_map/ppermute | solution.py:43
  27.0 1.2 collective-permute-start.3
  28.2 1.3 copy-done.4
  29.6 1.0 copy-done.6
  30.6 1.0 copy-done.7
  31.6 2.8 %shard_map.94 = (bf16[112,256,896]{2,1,0:T(8,128)(2,1)}, bf16[896,512]{1,0:T(8,128)(2,1)S(1)}, f32[8,128]{1,0:T(8,128)}) custom-call(bf16[256,896]{1,0:T(8,128)(2,1)S(1)} %copy-done.5, bf16[256,896]{1,0:T(8,128)(2,1)S(1)} %copy-done.6, bf16[256,896]{1,0:T(8,128)(2,1)S(1)} %copy-done.7, bf16[1,3,256,896]{3,2,1,0:T(8,128)(2,1)S(1)} %copy-done.4), custom_call_target="tpu_custom_call" | custom-call | tf_op jit(solution)/shard_map/pallas_call | solution.py:196
  34.5 0.0 copy-start.14
  34.5 0.9 copy-done.14
  35.4 0.1 pad_add_fusion.place_ref
  35.5 0.6 collective-permute-done.5
  36.0 11.2 %collective-permute-done.4 = bf16[4,56,1152]{2,1,0:T(8,128)(2,1)} collective-permute-done((bf16[4,56,1152]{2,1,0:T(8,128)(2,1)S(1)}, bf16[4,56,1152]{2,1,0:T(8,128)(2,1)}, u32[]{:S(2)}, u32[]{:S(2)}) %collective-permute-start.4) | collective-permute-done | bytes 516128 | tf_op jit(solution)/shard_map/ppermute | solution.py:43
  47.2 2.0 %collective-permute-done.3 = bf16[4,56,1152]{2,1,0:T(8,128)(2,1)} collective-permute-done((bf16[4,56,1152]{2,1,0:T(8,128)(2,1)S(1)}, bf16[4,56,1152]{2,1,0:T(8,128)(2,1)}, u32[]{:S(2)}, u32[]{:S(2)}) %collective-permute-start.3) | collective-permute-done | bytes 516128 | tf_op jit(solution)/shard_map/ppermute | solution.py:43
  49.3 6.5 %shard_map.97 = (bf16[256,1024]{1,0:T(8,128)(2,1)S(1)}, bf16[256,1024]{1,0:T(8,128)(2,1)S(1)}, bf16[256,1024]{1,0:T(8,128)(2,1)S(1)}, bf16[96,256]{1,0:T(8,128)(2,1)S(1)}, bf16[896,1152]{1,0:T(8,128)(2,1)S(1)}) custom-call(s32[2]{0:T(128)S(1)} %pad_add_fusion.place_ref, bf16[224,1152]{1,0:T(8,128)(2,1)S(1)} %bitcast.22, bf16[224,1152]{1,0:T(8,128)(2,1)} %bitcast.7.p1_ref, ...), custom_call_target="tpu_custom_call" | custom-call | flops 1409286144 | bytes 8388608 | tf_op jit(solution)/shard_map/pallas_call | solution.py:274
  55.8 4.0 %collective-permute-start.8 = (bf16[96,256]{1,0:T(8,128)(2,1)S(1)}, bf16[96,256]{1,0:T(8,128)(2,1)S(1)}, u32[]{:S(2)}, u32[]{:S(2)}) collective-permute-start(bf16[96,256]{1,0:T(8,128)(2,1)S(1)} %get-tuple-element.64._.refs_0_), channel_id=1, source_target_pairs={{0,48},{16,32},{32,16},{48,0},{64,112},{80,96},{96,80},{112,64},{1... | collective-permute-start | bytes 147464 | tf_op jit(solution)/shard_map/ppermute | solution.py:566
  59.7 0.5 collective-permute-start.6
  60.2 3.5 %shard_map.98 = (f32[256,896]{1,0:T(8,128)S(1)}, f32[256,896]{1,0:T(8,128)S(1)}, f32[256,896]{1,0:T(8,128)S(1)}, f32[8,128]{1,0:T(8,128)S(1)}) custom-call(bf16[256,1024]{1,0:T(8,128)(2,1)S(1)} %get-tuple-element.62.gate_grad_ref, bf16[256,1024]{1,0:T(8,128)(2,1)S(1)} %get-tuple-element.63.up_grad_ref, bf16[256,1024]{1,0:T(8,128)(2,1)S(1)} %get-tuple-element.65.hidden_ref, ...), custom_call_target="tpu_custom_call" | custom-call | flops 1409286144 | bytes 9437184 | tf_op jit(solution)/shard_map/pallas_call | solution.py:345
  63.8 5.9 %collective-permute-start.14 = (bf16[96,256]{1,0:T(8,128)(2,1)S(1)}, bf16[96,256]{1,0:T(8,128)(2,1)S(1)}, u32[]{:S(2)}, u32[]{:S(2)}) collective-permute-start(bf16[96,256]{1,0:T(8,128)(2,1)S(1)} %shard_map.99._.refs_0_), channel_id=1, source_target_pairs={{0,160},{16,176},{32,128},{48,144},{64,224},{80,240},{96,192},{112... | collective-permute-start | bytes 147464 | tf_op jit(solution)/shard_map/ppermute | solution.py:570
  69.7 0.3 collective-permute-start.13
  70.0 0.9 collective-permute-start.12
  70.9 2.4 %shard_map.100 = (bf16[224,1024]{1,0:T(8,128)(2,1)S(1)}, bf16[224,1024]{1,0:T(8,128)(2,1)}, bf16[224,1024]{1,0:T(8,128)(2,1)}, bf16[224,1024]{1,0:T(8,128)(2,1)}, f32[8,128]{1,0:T(8,128)S(1)}) custom-call(s32[2]{0:T(128)S(1)} %pad_add_fusion.place_ref, bf16[896,512]{1,0:T(8,128)(2,1)S(1)} %copy-done.15, ...), custom_call_target="tpu_custom_call" | custom-call | flops 939524096 | bytes 4194304 | tf_op jit(solution)/shard_map/pallas_call | solution.py:308
  73.4 1.5 %collective-permute-done.13.refs_2_ = bf16[96,256]{1,0:T(8,128)(2,1)S(1)} collective-permute-done((bf16[96,256]{1,0:T(8,128)(2,1)S(1)}, bf16[96,256]{1,0:T(8,128)(2,1)S(1)}, u32[]{:S(2)}, u32[]{:S(2)}) %collective-permute-start.13) | collective-permute-done | bytes 49184 | tf_op jit(solution)/shard_map/ppermute | solution.py:570
  74.9 0.6 shard_map.102
  75.6 2.5 %collective-permute-start.15 = (f32[384,128]{1,0:T(8,128)S(1)}, f32[384,128]{1,0:T(8,128)S(1)}, u32[]{:S(2)}, u32[]{:S(2)}) collective-permute-start(f32[384,128]{1,0:T(8,128)S(1)} %get-tuple-element.77), channel_id=1, source_target_pairs={{0,16},{16,0},{32,48},{48,32},{64,80},{80,64},{96,112},{112,96},{1... | collective-permute-start | bytes 589832 | tf_op jit(solution)/shard_map/ppermute | solution.py:496
  78.0 1.1 collective-permute-done.15
  79.2 0.8 pad_maximum_fusion
  79.9 6.5 %all-to-all-start.2 = ((f32[16,48,128]{2,1,0:T(8,128)}), f32[16,48,128]{2,1,0:T(8,128)S(1)}, u32[]{:S(2)}, u32[]{:S(2)}) async-start(f32[16,48,128]{2,1,0:T(8,128)} %pad_maximum_fusion), calls=%async_computation.2 | async-start | bytes 786432 | tf_op jit(solution)/shard_map/all_to_all | solution.py:576
  86.4 1.4 %collective-permute-start.9 = (bf16[224,1024]{1,0:T(8,128)(2,1)}, bf16[224,1024]{1,0:T(8,128)(2,1)}, u32[]{:S(2)}, u32[]{:S(2)}) collective-permute-start(bf16[224,1024]{1,0:T(8,128)(2,1)} %get-tuple-element.69), channel_id=1, source_target_pairs={{0,4},{1,5},{2,6},{3,7},{4,8},{5,9},{6,10},{7,11},{8,12},{9,13},{1... | collective-permute-start | bytes 1376264 | tf_op jit(solution)/shard_map/ppermute | solution.py:122
  87.8 1.4 %collective-permute-start.10 = (bf16[224,1024]{1,0:T(8,128)(2,1)}, bf16[224,1024]{1,0:T(8,128)(2,1)}, u32[]{:S(2)}, u32[]{:S(2)}) collective-permute-start(bf16[224,1024]{1,0:T(8,128)(2,1)} %get-tuple-element.70), channel_id=1, source_target_pairs={{0,12},{1,13},{2,14},{3,15},{4,0},{5,1},{6,2},{7,3},{8,4},{9,5},{1... | collective-permute-start | bytes 1376264 | tf_op jit(solution)/shard_map/ppermute | solution.py:122
  89.2 1.6 %collective-permute-start.11 = (bf16[224,1024]{1,0:T(8,128)(2,1)}, bf16[224,1024]{1,0:T(8,128)(2,1)}, u32[]{:S(2)}, u32[]{:S(2)}) collective-permute-start(bf16[224,1024]{1,0:T(8,128)(2,1)} %get-tuple-element.71), channel_id=1, source_target_pairs={{0,8},{1,9},{2,10},{3,11},{4,12},{5,13},{6,14},{7,15},{8,0},{9,1},... | collective-permute-start | bytes 1376264 | tf_op jit(solution)/shard_map/ppermute | solution.py:122
  90.8 5.2 %all-to-all-done.2 = f32[16,48,128]{2,1,0:T(8,128)S(1)} async-done(((f32[16,48,128]{2,1,0:T(8,128)}), f32[16,48,128]{2,1,0:T(8,128)S(1)}, u32[]{:S(2)}, u32[]{:S(2)}) %all-to-all-start.2) | async-done | bytes 393248 | tf_op jit(solution)/shard_map/all_to_all | solution.py:576
  96.0 0.6 fusion
  96.6 0.6 broadcast_in_dim.10
  97.2 4.6 %all-to-all-start.3 = ((f32[8,24,128]{2,1,0:T(8,128)}), f32[8,24,128]{2,1,0:T(8,128)S(1)}, u32[]{:S(2)}, u32[]{:S(2)}) async-start(f32[8,24,128]{2,1,0:T(8,128)} %broadcast_in_dim.10), calls=%async_computation.3 | async-start | bytes 196608 | tf_op jit(solution)/shard_map/all_to_all | solution.py:35
  101.9 4.2 %shard_map.105 = (f32[3,32,32]{2,1,0:T(8,128)}, f32[8,128]{1,0:T(8,128)}) custom-call(f32[24,128]{1,0:T(8,128)} %get-tuple-element.90._.gram_ref), custom_call_target="tpu_custom_call" | custom-call | flops 4294967296 | bytes 1048576 | tf_op jit(solution)/shard_map/pallas_call | solution.py:432
  106.1 3.5 %all-to-all-done.3.value_ref = f32[8,24,128]{2,1,0:T(8,128)S(1)} async-done(((f32[8,24,128]{2,1,0:T(8,128)}), f32[8,24,128]{2,1,0:T(8,128)S(1)}, u32[]{:S(2)}, u32[]{:S(2)}) %all-to-all-start.3) | async-done | bytes 98336 | tf_op jit(solution)/shard_map/all_to_all | solution.py:35
  109.5 0.7 copy-done.13
  110.2 0.7 broadcast_in_dim.11
  110.9 3.5 %all-to-all-start.4 = ((f32[16,24,128]{2,1,0:T(8,128)}), f32[16,24,128]{2,1,0:T(8,128)S(1)}, u32[]{:S(2)}, u32[]{:S(2)}) async-start(f32[16,24,128]{2,1,0:T(8,128)} %broadcast_in_dim.11), calls=%async_computation.4 | async-start | bytes 393216 | tf_op jit(solution)/shard_map/all_to_all | solution.py:35
  114.5 1.0 copy-done.9
  115.5 1.5 %shard_map.103 = (bf16[56,1024]{1,0:T(8,128)(2,1)S(1)}, bf16[56,1024]{1,0:T(8,128)(2,1)S(1)}, bf16[56,1024]{1,0:T(8,128)(2,1)S(1)}, bf16[56,1024]{1,0:T(8,128)(2,1)S(1)}) custom-call(s32[1]{0:T(128)} %bitcast.place_ref, bf16[4,56,1024]{2,1,0:T(8,128)(2,1)S(1)} %bitcast.25, bf16[4,56,1024]{2,1,0:T(8,128)(2,1)} %bitcast.12.g1_ref, ...), custom_call_target="tpu_custom_call" | custom-call | tf_op jit(solution)/shard_map/pallas_call | solution.py:135
  117.1 1.3 collective-permute-start.16
  118.4 1.4 %collective-permute-start.17 = (bf16[56,1024]{1,0:T(8,128)(2,1)S(1)}, bf16[56,1024]{1,0:T(8,128)(2,1)S(1)}, u32[]{:S(2)}, u32[]{:S(2)}) collective-permute-start(bf16[56,1024]{1,0:T(8,128)(2,1)S(1)} %get-tuple-element.81), channel_id=1, source_target_pairs={{0,3},{1,0},{2,1},{3,2},{4,7},{5,4},{6,5},{7,6},{8,11},{9,8},{10,9... | collective-permute-start | bytes 344072 | tf_op jit(solution)/shard_map/ppermute | solution.py:142
  119.8 1.5 %collective-permute-start.18 = (bf16[56,1024]{1,0:T(8,128)(2,1)S(1)}, bf16[56,1024]{1,0:T(8,128)(2,1)S(1)}, u32[]{:S(2)}, u32[]{:S(2)}) collective-permute-start(bf16[56,1024]{1,0:T(8,128)(2,1)S(1)} %get-tuple-element.82), channel_id=1, source_target_pairs={{0,2},{1,3},{2,0},{3,1},{4,6},{5,7},{6,4},{7,5},{8,10},{9,11},{10,... | collective-permute-start | bytes 344072 | tf_op jit(solution)/shard_map/ppermute | solution.py:142
  121.4 1.8 %collective-permute-done.16.refs_1_ = bf16[56,1024]{1,0:T(8,128)(2,1)S(1)} collective-permute-done((bf16[56,1024]{1,0:T(8,128)(2,1)S(1)}, bf16[56,1024]{1,0:T(8,128)(2,1)S(1)}, u32[]{:S(2)}, u32[]{:S(2)}) %collective-permute-start.16) | collective-permute-done | bytes 114720 | tf_op jit(solution)/shard_map/ppermute | solution.py:142
  123.2 2.3 %collective-permute-done.18.refs_3_ = bf16[56,1024]{1,0:T(8,128)(2,1)S(1)} collective-permute-done((bf16[56,1024]{1,0:T(8,128)(2,1)S(1)}, bf16[56,1024]{1,0:T(8,128)(2,1)S(1)}, u32[]{:S(2)}, u32[]{:S(2)}) %collective-permute-start.18) | collective-permute-done | bytes 114720 | tf_op jit(solution)/shard_map/ppermute | solution.py:142
  125.5 0.7 shard_map.104
  126.2 4.1 %collective-permute-start.19 = (f32[384,128]{1,0:T(8,128)S(1)}, f32[384,128]{1,0:T(8,128)S(1)}, u32[]{:S(2)}, u32[]{:S(2)}) collective-permute-start(f32[384,128]{1,0:T(8,128)S(1)} %shard_map.107.s_mine_ref), channel_id=1, source_target_pairs={{0,16},{16,0},{32,48},{48,32},{64,80},{80,64},{96,112},{112,96},{1... | collective-permute-start | bytes 589832 | tf_op jit(solution)/shard_map/ppermute | solution.py:496
  130.4 0.1 pad_add_fusion.1.place_ref
  130.4 1.0 collective-permute-done.19.s_other_ref
  131.4 3.2 %shard_map.108 = (bf16[1,3,256,896]{3,2,1,0:T(8,128)(2,1)}, f32[96,56]{1,0:T(8,128)}) custom-call(s32[2]{0:T(128)S(1)} %pad_add_fusion.1.place_ref, f32[384,128]{1,0:T(8,128)S(1)} %shard_map.107.s_mine_ref, f32[384,128]{1,0:T(8,128)S(1)} %collective-permute-done.19.s_other_ref, f32[3,32,32]{2,1,0:T(8,128)S(1)} %copy-done.12, ...), custom_call_target="tpu_custom_call" | custom-call | tf_op jit(solution)/shard_map/pallas_call | solution.py:478
  (43 shorter events, 0.2 us)
Async XLA Ops:
  2.7 14.2 %all-to-all-start = ((bf16[4,56,1152]{2,1,0:T(8,128)(2,1)}), bf16[4,56,1152]{2,1,0:T(8,128)(2,1)S(1)}, u32[]{:S(2)}, u32[]{:S(2)}) async-start(bf16[4,56,1152]{2,1,0:T(8,128)(2,1)} %get-tuple-element.48), calls=%async_computation | async-start | bytes 1032192 | tf_op jit(solution)/shard_map/all_to_all | solution.py:108
  7.7 5.2 %collective-permute-start.2 = (bf16[56,1152]{1,0:T(8,128)(2,1)}, bf16[56,1152]{1,0:T(8,128)(2,1)S(1)}, u32[]{:S(2)}, u32[]{:S(2)}) collective-permute-start(bf16[56,1152]{1,0:T(8,128)(2,1)} %get-tuple-element.49.p0_ref), channel_id=1, source_target_pairs={{0,1},{1,2},{2,3},{3,0},{4,5},{5,6},{6,7},{7,4},{8,9},{9,10},{10,1... | collective-permute-start | bytes 387080 | tf_op jit(solution)/shard_map/ppermute | solution.py:43
  8.9 8.0 %collective-permute-start.1 = (bf16[56,1152]{1,0:T(8,128)(2,1)}, bf16[56,1152]{1,0:T(8,128)(2,1)S(1)}, u32[]{:S(2)}, u32[]{:S(2)}) collective-permute-start(bf16[56,1152]{1,0:T(8,128)(2,1)} %get-tuple-element.49.p0_ref), channel_id=1, source_target_pairs={{0,2},{1,3},{2,0},{3,1},{4,6},{5,7},{6,4},{7,5},{8,10},{9,11},{10,... | collective-permute-start | bytes 387080 | tf_op jit(solution)/shard_map/ppermute | solution.py:43
  11.4 5.5 %collective-permute-start = (bf16[56,1152]{1,0:T(8,128)(2,1)}, bf16[56,1152]{1,0:T(8,128)(2,1)S(1)}, u32[]{:S(2)}, u32[]{:S(2)}) collective-permute-start(bf16[56,1152]{1,0:T(8,128)(2,1)} %get-tuple-element.49.p0_ref), channel_id=1, source_target_pairs={{0,3},{1,0},{2,1},{3,2},{4,7},{5,4},{6,5},{7,6},{8,11},{9,8},{10,9... | collective-permute-start | bytes 387080 | tf_op jit(solution)/shard_map/ppermute | solution.py:43
  16.9 0.9 copy-start.10
  19.9 8.3 %copy-start.5 = (bf16[256,896]{1,0:T(8,128)(2,1)S(1)}, bf16[256,896]{1,0:T(8,128)(2,1)}, u32[]{:S(2)}) copy-start(bf16[256,896]{1,0:T(8,128)(2,1)} %gate_ref.1) | copy-start | bytes 1376260
  19.9 29.3 %all-to-all-start.1 = ((bf16[4,4,56,1152]{3,2,1,0:T(8,128)(2,1)}), bf16[4,4,56,1152]{3,2,1,0:T(8,128)(2,1)S(1)}, u32[]{:S(2)}, u32[]{:S(2)}) async-start(bf16[4,4,56,1152]{3,2,1,0:T(8,128)(2,1)} %broadcast_in_dim.8), calls=%async_computation.1 | async-start | bytes 4128768 | tf_op jit(solution)/shard_map/all_to_all | solution.py:35
  23.7 12.4 %collective-permute-start.5 = (bf16[4,56,1152]{2,1,0:T(8,128)(2,1)S(1)}, bf16[4,56,1152]{2,1,0:T(8,128)(2,1)S(1)}, u32[]{:S(2)}, u32[]{:S(2)}) collective-permute-start(bf16[4,56,1152]{2,1,0:T(8,128)(2,1)S(1)} %shard_map.96), channel_id=1, source_target_pairs={{0,4},{1,5},{2,6},{3,7},{4,8},{5,9},{6,10},{7,11},{8,12},{9,13},{1... | collective-permute-start | bytes 1548296 | tf_op jit(solution)/shard_map/ppermute | solution.py:43
  24.7 22.6 %collective-permute-start.4 = (bf16[4,56,1152]{2,1,0:T(8,128)(2,1)S(1)}, bf16[4,56,1152]{2,1,0:T(8,128)(2,1)}, u32[]{:S(2)}, u32[]{:S(2)}) collective-permute-start(bf16[4,56,1152]{2,1,0:T(8,128)(2,1)S(1)} %shard_map.96), channel_id=1, source_target_pairs={{0,8},{1,9},{2,10},{3,11},{4,12},{5,13},{6,14},{7,15},{8,0},{9,1},... | collective-permute-start | bytes 1548296 | tf_op jit(solution)/shard_map/ppermute | solution.py:43
  27.0 22.2 %collective-permute-start.3 = (bf16[4,56,1152]{2,1,0:T(8,128)(2,1)S(1)}, bf16[4,56,1152]{2,1,0:T(8,128)(2,1)}, u32[]{:S(2)}, u32[]{:S(2)}) collective-permute-start(bf16[4,56,1152]{2,1,0:T(8,128)(2,1)S(1)} %shard_map.96), channel_id=1, source_target_pairs={{0,12},{1,13},{2,14},{3,15},{4,0},{5,1},{6,2},{7,3},{8,4},{9,5},{1... | collective-permute-start | bytes 1548296 | tf_op jit(solution)/shard_map/ppermute | solution.py:43
  28.2 1.3 copy-start.4
  29.6 1.0 copy-start.6
  30.6 1.0 copy-start.7
  34.5 0.9 copy-start.14
  55.8 8.0 %collective-permute-start.8 = (bf16[96,256]{1,0:T(8,128)(2,1)S(1)}, bf16[96,256]{1,0:T(8,128)(2,1)S(1)}, u32[]{:S(2)}, u32[]{:S(2)}) collective-permute-start(bf16[96,256]{1,0:T(8,128)(2,1)S(1)} %get-tuple-element.64._.refs_0_), channel_id=1, source_target_pairs={{0,48},{16,32},{32,16},{48,0},{64,112},{80,96},{96,80},{112,64},{1... | collective-permute-start | bytes 147464 | tf_op jit(solution)/shard_map/ppermute | solution.py:566
  59.7 4.0 %collective-permute-start.7 = (bf16[96,256]{1,0:T(8,128)(2,1)S(1)}, bf16[96,256]{1,0:T(8,128)(2,1)S(1)}, u32[]{:S(2)}, u32[]{:S(2)}) collective-permute-start(bf16[96,256]{1,0:T(8,128)(2,1)S(1)} %get-tuple-element.64._.refs_0_), channel_id=1, source_target_pairs={{0,32},{16,48},{32,0},{48,16},{64,96},{80,112},{96,64},{112,80},{1... | collective-permute-start | bytes 147464 | tf_op jit(solution)/shard_map/ppermute | solution.py:566
  59.7 4.1 %collective-permute-start.6 = (bf16[96,256]{1,0:T(8,128)(2,1)S(1)}, bf16[96,256]{1,0:T(8,128)(2,1)S(1)}, u32[]{:S(2)}, u32[]{:S(2)}) collective-permute-start(bf16[96,256]{1,0:T(8,128)(2,1)S(1)} %get-tuple-element.64._.refs_0_), channel_id=1, source_target_pairs={{0,16},{16,0},{32,48},{48,32},{64,80},{80,64},{96,112},{112,96},{1... | collective-permute-start | bytes 147464 | tf_op jit(solution)/shard_map/ppermute | solution.py:566
  60.2 10.7 %copy-start.15 = (bf16[896,512]{1,0:T(8,128)(2,1)S(1)}, bf16[896,512]{1,0:T(8,128)(2,1)}, u32[]{:S(2)}) copy-start(bf16[896,512]{1,0:T(8,128)(2,1)} %copy-done.14) | copy-start | bytes 2752516
  63.8 11.8 %copy-start = (f32[256,896]{1,0:T(8,128)}, f32[256,896]{1,0:T(8,128)S(1)}, u32[]{:S(2)}) copy-start(f32[256,896]{1,0:T(8,128)S(1)} %get-tuple-element.74.m1_ref) | copy-start | bytes 2752516
  63.8 11.8 %copy-start.2 = (f32[256,896]{1,0:T(8,128)}, f32[256,896]{1,0:T(8,128)S(1)}, u32[]{:S(2)}) copy-start(f32[256,896]{1,0:T(8,128)S(1)} %get-tuple-element.75.m2_ref) | copy-start | bytes 2752516
  63.8 9.5 %collective-permute-start.14 = (bf16[96,256]{1,0:T(8,128)(2,1)S(1)}, bf16[96,256]{1,0:T(8,128)(2,1)S(1)}, u32[]{:S(2)}, u32[]{:S(2)}) collective-permute-start(bf16[96,256]{1,0:T(8,128)(2,1)S(1)} %shard_map.99._.refs_0_), channel_id=1, source_target_pairs={{0,160},{16,176},{32,128},{48,144},{64,224},{80,240},{96,192},{112... | collective-permute-start | bytes 147464 | tf_op jit(solution)/shard_map/ppermute | solution.py:570
  69.7 5.1 %collective-permute-start.13 = (bf16[96,256]{1,0:T(8,128)(2,1)S(1)}, bf16[96,256]{1,0:T(8,128)(2,1)S(1)}, u32[]{:S(2)}, u32[]{:S(2)}) collective-permute-start(bf16[96,256]{1,0:T(8,128)(2,1)S(1)} %shard_map.99._.refs_0_), channel_id=1, source_target_pairs={{0,192},{16,208},{32,224},{48,240},{64,128},{80,144},{96,160},{112... | collective-permute-start | bytes 147464 | tf_op jit(solution)/shard_map/ppermute | solution.py:570
  70.0 4.8 %collective-permute-start.12 = (bf16[96,256]{1,0:T(8,128)(2,1)S(1)}, bf16[96,256]{1,0:T(8,128)(2,1)S(1)}, u32[]{:S(2)}, u32[]{:S(2)}) collective-permute-start(bf16[96,256]{1,0:T(8,128)(2,1)S(1)} %shard_map.99._.refs_0_), channel_id=1, source_target_pairs={{0,64},{16,80},{32,96},{48,112},{64,0},{80,16},{96,32},{112,48},{1... | collective-permute-start | bytes 147464 | tf_op jit(solution)/shard_map/ppermute | solution.py:570
  73.4 2.2 %copy-start.8 = (bf16[224,1024]{1,0:T(8,128)(2,1)}, bf16[224,1024]{1,0:T(8,128)(2,1)S(1)}, u32[]{:S(2)}) copy-start(bf16[224,1024]{1,0:T(8,128)(2,1)S(1)} %get-tuple-element.68) | copy-start | bytes 1376260
  75.6 3.6 %collective-permute-start.15 = (f32[384,128]{1,0:T(8,128)S(1)}, f32[384,128]{1,0:T(8,128)S(1)}, u32[]{:S(2)}, u32[]{:S(2)}) collective-permute-start(f32[384,128]{1,0:T(8,128)S(1)} %get-tuple-element.77), channel_id=1, source_target_pairs={{0,16},{16,0},{32,48},{48,32},{64,80},{80,64},{96,112},{112,96},{1... | collective-permute-start | bytes 589832 | tf_op jit(solution)/shard_map/ppermute | solution.py:496
  79.9 16.0 %all-to-all-start.2 = ((f32[16,48,128]{2,1,0:T(8,128)}), f32[16,48,128]{2,1,0:T(8,128)S(1)}, u32[]{:S(2)}, u32[]{:S(2)}) async-start(f32[16,48,128]{2,1,0:T(8,128)} %pad_maximum_fusion), calls=%async_computation.2 | async-start | bytes 786432 | tf_op jit(solution)/shard_map/all_to_all | solution.py:576
  86.4 28.1 %collective-permute-start.9 = (bf16[224,1024]{1,0:T(8,128)(2,1)}, bf16[224,1024]{1,0:T(8,128)(2,1)}, u32[]{:S(2)}, u32[]{:S(2)}) collective-permute-start(bf16[224,1024]{1,0:T(8,128)(2,1)} %get-tuple-element.69), channel_id=1, source_target_pairs={{0,4},{1,5},{2,6},{3,7},{4,8},{5,9},{6,10},{7,11},{8,12},{9,13},{1... | collective-permute-start | bytes 1376264 | tf_op jit(solution)/shard_map/ppermute | solution.py:122
  87.8 26.7 %collective-permute-start.10 = (bf16[224,1024]{1,0:T(8,128)(2,1)}, bf16[224,1024]{1,0:T(8,128)(2,1)}, u32[]{:S(2)}, u32[]{:S(2)}) collective-permute-start(bf16[224,1024]{1,0:T(8,128)(2,1)} %get-tuple-element.70), channel_id=1, source_target_pairs={{0,12},{1,13},{2,14},{3,15},{4,0},{5,1},{6,2},{7,3},{8,4},{9,5},{1... | collective-permute-start | bytes 1376264 | tf_op jit(solution)/shard_map/ppermute | solution.py:122
  89.2 25.3 %collective-permute-start.11 = (bf16[224,1024]{1,0:T(8,128)(2,1)}, bf16[224,1024]{1,0:T(8,128)(2,1)}, u32[]{:S(2)}, u32[]{:S(2)}) collective-permute-start(bf16[224,1024]{1,0:T(8,128)(2,1)} %get-tuple-element.71), channel_id=1, source_target_pairs={{0,8},{1,9},{2,10},{3,11},{4,12},{5,13},{6,14},{7,15},{8,0},{9,1},... | collective-permute-start | bytes 1376264 | tf_op jit(solution)/shard_map/ppermute | solution.py:122
  97.2 12.3 %all-to-all-start.3 = ((f32[8,24,128]{2,1,0:T(8,128)}), f32[8,24,128]{2,1,0:T(8,128)S(1)}, u32[]{:S(2)}, u32[]{:S(2)}) async-start(f32[8,24,128]{2,1,0:T(8,128)} %broadcast_in_dim.10), calls=%async_computation.3 | async-start | bytes 196608 | tf_op jit(solution)/shard_map/all_to_all | solution.py:35
  101.9 12.6 %copy-start.11 = (f32[24,128]{1,0:T(8,128)S(1)}, f32[24,128]{1,0:T(8,128)}, u32[]{:S(2)}) copy-start(f32[24,128]{1,0:T(8,128)} %get-tuple-element.90._.gram_ref) | copy-start | bytes 36868
  106.0 25.4 %copy-start.1 = (f32[256,896]{1,0:T(8,128)S(1)}, f32[256,896]{1,0:T(8,128)}, u32[]{:S(2)}) copy-start(f32[256,896]{1,0:T(8,128)} %copy-done) | copy-start | bytes 2752516
  106.1 25.4 %copy-start.3 = (f32[256,896]{1,0:T(8,128)S(1)}, f32[256,896]{1,0:T(8,128)}, u32[]{:S(2)}) copy-start(f32[256,896]{1,0:T(8,128)} %copy-done.2) | copy-start | bytes 2752516
  109.5 0.7 copy-start.13
  110.9 15.3 %all-to-all-start.4 = ((f32[16,24,128]{2,1,0:T(8,128)}), f32[16,24,128]{2,1,0:T(8,128)S(1)}, u32[]{:S(2)}, u32[]{:S(2)}) async-start(f32[16,24,128]{2,1,0:T(8,128)} %broadcast_in_dim.11), calls=%async_computation.4 | async-start | bytes 393216 | tf_op jit(solution)/shard_map/all_to_all | solution.py:35
  114.5 1.0 copy-start.9
  115.5 15.9 %copy-start.12 = (f32[3,32,32]{2,1,0:T(8,128)S(1)}, f32[3,32,32]{2,1,0:T(8,128)}, u32[]{:S(2)}) copy-start(f32[3,32,32]{2,1,0:T(8,128)} %get-tuple-element.86.inverse_ref) | copy-start | bytes 36868
  117.1 6.1 %collective-permute-start.16 = (bf16[56,1024]{1,0:T(8,128)(2,1)S(1)}, bf16[56,1024]{1,0:T(8,128)(2,1)S(1)}, u32[]{:S(2)}, u32[]{:S(2)}) collective-permute-start(bf16[56,1024]{1,0:T(8,128)(2,1)S(1)} %get-tuple-element.80), channel_id=1, source_target_pairs={{0,1},{1,2},{2,3},{3,0},{4,5},{5,6},{6,7},{7,4},{8,9},{9,10},{10,1... | collective-permute-start | bytes 344072 | tf_op jit(solution)/shard_map/ppermute | solution.py:142
  118.4 4.8 %collective-permute-start.17 = (bf16[56,1024]{1,0:T(8,128)(2,1)S(1)}, bf16[56,1024]{1,0:T(8,128)(2,1)S(1)}, u32[]{:S(2)}, u32[]{:S(2)}) collective-permute-start(bf16[56,1024]{1,0:T(8,128)(2,1)S(1)} %get-tuple-element.81), channel_id=1, source_target_pairs={{0,3},{1,0},{2,1},{3,2},{4,7},{5,4},{6,5},{7,6},{8,11},{9,8},{10,9... | collective-permute-start | bytes 344072 | tf_op jit(solution)/shard_map/ppermute | solution.py:142
  119.8 5.7 %collective-permute-start.18 = (bf16[56,1024]{1,0:T(8,128)(2,1)S(1)}, bf16[56,1024]{1,0:T(8,128)(2,1)S(1)}, u32[]{:S(2)}, u32[]{:S(2)}) collective-permute-start(bf16[56,1024]{1,0:T(8,128)(2,1)S(1)} %get-tuple-element.82), channel_id=1, source_target_pairs={{0,2},{1,3},{2,0},{3,1},{4,6},{5,7},{6,4},{7,5},{8,10},{9,11},{10,... | collective-permute-start | bytes 344072 | tf_op jit(solution)/shard_map/ppermute | solution.py:142
  126.2 5.2 %collective-permute-start.19 = (f32[384,128]{1,0:T(8,128)S(1)}, f32[384,128]{1,0:T(8,128)S(1)}, u32[]{:S(2)}, u32[]{:S(2)}) collective-permute-start(f32[384,128]{1,0:T(8,128)S(1)} %shard_map.107.s_mine_ref), channel_id=1, source_target_pairs={{0,16},{16,0},{32,48},{48,32},{64,80},{80,64},{96,112},{112,96},{1... | collective-permute-start | bytes 589832 | tf_op jit(solution)/shard_map/ppermute | solution.py:496

commit v6 on v5

--- a/solution.py
+++ b/solution.py
@@ -217,7 +217,7 @@
     for i, ref in enumerate((p0_ref, p1_ref, p2_ref, p3_ref)):
         at = pl.multiple_of(lax.rem(place_ref[0] + i, SIDE) * rows, 16)
         pieces.append(pltpu.make_async_copy(ref, x_ref.at[pl.ds(at, rows), :], sems.at[6 + i]))
-    for copy in [loads[2]] + pieces + loads[:2] + loads[3:]:
+    for copy in [loads[2], loads[5]] + pieces + loads[:2] + loads[3:5]:
         copy.start()
     q_dy = dy_ref[:, tokens : tokens + 2 * RANK]
     q_dy_rows = q_dy.astype(F32).T.astype(BF)
@@ -225,6 +225,13 @@
     for start in range(0, tokens, chunk):
         span = slice(start, start + chunk)
         hidden_grad_ref[:, span] = dot(w_ref[2], dy_ref[:, span], 1, 0)
+    block = rows // SIDE
+    q_plain = q_dy.astype(F32)
+    q_plain = jnp.concatenate(
+        [q_plain[(x * SIDE + y) * block : (x * SIDE + y + 1) * block] for y in range(SIDE) for x in range(SIDE)]
+    ).astype(BF)
+    loads[5].wait()
+    last_error = dot(w_ref[5], q_plain, 1, 0)
     for copy in pieces + loads[:2]:
         copy.wait()
     q_x = x_ref[:, tokens:]
@@ -249,16 +256,9 @@
             both = dot(q_both[k], right, 1, 0)
             halves = jnp.concatenate(split(both[:RANK] + both[RANK:]))
             sums[k] = sums[k] + dot(halves, left, 1, 1)
-    block = rows // SIDE
-    q_plain = q_dy.astype(F32)
-    q_plain = jnp.concatenate(
-        [q_plain[(x * SIDE + y) * block : (x * SIDE + y + 1) * block] for y in range(SIDE) for x in range(SIDE)]
-    ).astype(BF)
-    for copy in loads[3:]:
+    for copy in loads[3:5]:
         copy.wait()
-    errors = [
-        dot(w_ref[3 + k], q, 1, 0) for k, q in enumerate((q_x[:, : 2 * RANK], q_x[:, 2 * RANK :], q_plain))
-    ]
+    errors = [dot(w_ref[3 + k], q_x[:, 2 * k * RANK : 2 * (k + 1) * RANK], 1, 0) for k in range(2)] + [last_error]
     error_p = jnp.concatenate([both[:, :RANK] + both[:, RANK:] for both in errors], axis=1).T
     p = jnp.concatenate([both[:RANK] + both[RANK:] for both in sums]) + error_p
     p_out_ref[...] = p.astype(BF)
@@ -382,7 +382,11 @@
         m_high, m_low = split(m_ref[...])
         both = dot(jnp.concatenate([p_high, p_low]), m_high, 1, 0)
         term = both[:RANK] + both[RANK:] + dot(p_high, m_low, 1, 0)
-        grams.append(dot3(p_k, p_k, 1, 1))
+        grams.append(
+            lax.dot_general(
+                p_k, p_k, (((1,), (1,)), ((), ())), precision=lax.Precision.HIGHEST, preferred_element_type=F32
+            )
+        )
         rows.append(jnp.concatenate([term, jnp.zeros((RANK, LANES), F32)], axis=1))
     gram = jnp.concatenate(grams)
     gram_ref[...] = jnp.concatenate([gram[i * 24 : (i + 1) * 24] for i in range(4)], axis=1)

time: 136 us -> 136 us (level)
  no operation moved by 1% of the time
where the time goes in v6:
time: 136 us; the launch traced here: 135 us
  starting transfers between devices  59.5 us (44%)
  waiting for transfers between devices  34.5 us (25%)
  Pallas kernels  28.2 us (21%)
  local copies, waits for them, and re-layouts  10.4 us (8%)
    ppermute x6, waiting for transfers between devices, ring_pieces(): near[k] = lax.ppermute(value, 'tensor', ring(SIDE - k))  18.2 us
    all_to_all x3, starting transfers between devices, spread(): lax.all_to_all(jnp.broadcast_to(value[None], (size,) + value.shape), axis...  11.9 us
    ppermute x6, starting transfers between devices, ring_pieces(): near[k] = lax.ppermute(value, 'tensor', ring(SIDE - k))  9.36 us
    ppermute x3, starting transfers between devices, per_device(): others = [lax.ppermute(p_pair, 'dp', dp_swap(bits)) for bits in (4, 12, 10)]  7.09 us
    unnamed x32, local copies, waits for them, and re-layouts  6.92 us
    ppermute x2, starting transfers between devices, swap_core(): return lax.ppermute(value, 'dp', CORE_PAIR)  6.59 us
    all_to_all x1, starting transfers between devices, per_device(): lax.all_to_all(jnp.concatenate([s_pair, gram], axis=1), 'tensor', 0, 0, t...  6.47 us
    pallas_call x1, Pallas kernels, backward(): pl.pallas_call(backward_kernel, out_shape=(grads, grads, grads, jax.Shape...  6.38 us
  transfers between devices with their start and end apart: 25, of which 12 were waited for; matrix products, arithmetic and copies ran while one was open for 2% of the time, Pallas kernels for 11%

profile of v6, /device:TPU:1, one launch (start us, length us, event | category | flops | bytes accessed | tf_op | source)
XLA Modules:
  0.0 134.7 jit_solution(8619290038677011778)
XLA Ops:
  0.6 2.0 %shard_map.95 = (bf16[56,1152]{1,0:T(8,128)(2,1)}, bf16[4,56,1152]{2,1,0:T(8,128)(2,1)}) custom-call(bf16[56,1024]{1,0:T(8,128)(2,1)} %bitcast.27, bf16[56,1024]{1,0:T(8,128)(2,1)} %bitcast.28, f32[96,56]{1,0:T(8,128)} %bitcast.29), custom_call_target="tpu_custom_call" | custom-call | tf_op jit(solution)/shard_map/pallas_call | solution.py:70
  2.7 5.0 %all-to-all-start = ((bf16[4,56,1152]{2,1,0:T(8,128)(2,1)}), bf16[4,56,1152]{2,1,0:T(8,128)(2,1)S(1)}, u32[]{:S(2)}, u32[]{:S(2)}) async-start(bf16[4,56,1152]{2,1,0:T(8,128)(2,1)} %get-tuple-element.48), calls=%async_computation | async-start | bytes 1032192 | tf_op jit(solution)/shard_map/all_to_all | solution.py:108
  7.7 1.2 collective-permute-start.2
  8.9 2.5 %collective-permute-start.1 = (bf16[56,1152]{1,0:T(8,128)(2,1)}, bf16[56,1152]{1,0:T(8,128)(2,1)S(1)}, u32[]{:S(2)}, u32[]{:S(2)}) collective-permute-start(bf16[56,1152]{1,0:T(8,128)(2,1)} %get-tuple-element.49.p0_ref), channel_id=1, source_target_pairs={{0,2},{1,3},{2,0},{3,1},{4,6},{5,7},{6,4},{7,5},{8,10},{9,11},{10,... | collective-permute-start | bytes 387080 | tf_op jit(solution)/shard_map/ppermute | solution.py:43
  11.4 1.2 collective-permute-start
  12.5 0.4 collective-permute-done.2.p3_ref
  12.9 4.0 %collective-permute-done.1.p2_ref = bf16[56,1152]{1,0:T(8,128)(2,1)S(1)} collective-permute-done((bf16[56,1152]{1,0:T(8,128)(2,1)}, bf16[56,1152]{1,0:T(8,128)(2,1)S(1)}, u32[]{:S(2)}, u32[]{:S(2)}) %collective-permute-start.1) | collective-permute-done | bytes 129056 | tf_op jit(solution)/shard_map/ppermute | solution.py:43
  16.9 0.0 collective-permute-done.p1_ref
  16.9 0.9 copy-done.10
  17.8 0.7 shard_map.96
  18.4 1.5 %broadcast_in_dim.8 = bf16[4,4,56,1152]{3,2,1,0:T(8,128)(2,1)} broadcast(bf16[4,56,1152]{2,1,0:T(8,128)(2,1)S(1)} %all-to-all-done), dimensions={1,2,3} | broadcast | bytes 2580480 | tf_op jit(solution)/shard_map/broadcast_in_dim | solution.py:36
  19.9 3.7 %all-to-all-start.1 = ((bf16[4,4,56,1152]{3,2,1,0:T(8,128)(2,1)}), bf16[4,4,56,1152]{3,2,1,0:T(8,128)(2,1)S(1)}, u32[]{:S(2)}, u32[]{:S(2)}) async-start(bf16[4,4,56,1152]{3,2,1,0:T(8,128)(2,1)} %broadcast_in_dim.8), calls=%async_computation.1 | async-start | bytes 4128768 | tf_op jit(solution)/shard_map/all_to_all | solution.py:35
  23.7 1.0 collective-permute-start.5
  24.7 2.4 %collective-permute-start.4 = (bf16[4,56,1152]{2,1,0:T(8,128)(2,1)S(1)}, bf16[4,56,1152]{2,1,0:T(8,128)(2,1)}, u32[]{:S(2)}, u32[]{:S(2)}) collective-permute-start(bf16[4,56,1152]{2,1,0:T(8,128)(2,1)S(1)} %shard_map.96), channel_id=1, source_target_pairs={{0,8},{1,9},{2,10},{3,11},{4,12},{5,13},{6,14},{7,15},{8,0},{9,1},... | collective-permute-start | bytes 1548296 | tf_op jit(solution)/shard_map/ppermute | solution.py:43
  27.0 1.2 collective-permute-start.3
  28.2 1.3 copy-done.4
  29.6 1.0 copy-done.6
  30.6 1.0 copy-done.7
  31.6 2.8 %shard_map.94 = (bf16[112,256,896]{2,1,0:T(8,128)(2,1)}, bf16[896,512]{1,0:T(8,128)(2,1)S(1)}, f32[8,128]{1,0:T(8,128)}) custom-call(bf16[256,896]{1,0:T(8,128)(2,1)S(1)} %copy-done.5, bf16[256,896]{1,0:T(8,128)(2,1)S(1)} %copy-done.6, bf16[256,896]{1,0:T(8,128)(2,1)S(1)} %copy-done.7, bf16[1,3,256,896]{3,2,1,0:T(8,128)(2,1)S(1)} %copy-done.4), custom_call_target="tpu_custom_call" | custom-call | tf_op jit(solution)/shard_map/pallas_call | solution.py:196
  34.5 0.0 copy-start.14
  34.5 0.9 copy-done.14
  35.4 0.1 pad_add_fusion.place_ref
  35.5 0.6 collective-permute-done.5
  36.0 11.2 %collective-permute-done.4 = bf16[4,56,1152]{2,1,0:T(8,128)(2,1)} collective-permute-done((bf16[4,56,1152]{2,1,0:T(8,128)(2,1)S(1)}, bf16[4,56,1152]{2,1,0:T(8,128)(2,1)}, u32[]{:S(2)}, u32[]{:S(2)}) %collective-permute-start.4) | collective-permute-done | bytes 516128 | tf_op jit(solution)/shard_map/ppermute | solution.py:43
  47.2 2.0 %collective-permute-done.3 = bf16[4,56,1152]{2,1,0:T(8,128)(2,1)} collective-permute-done((bf16[4,56,1152]{2,1,0:T(8,128)(2,1)S(1)}, bf16[4,56,1152]{2,1,0:T(8,128)(2,1)}, u32[]{:S(2)}, u32[]{:S(2)}) %collective-permute-start.3) | collective-permute-done | bytes 516128 | tf_op jit(solution)/shard_map/ppermute | solution.py:43
  49.3 6.4 %shard_map.97 = (bf16[256,1024]{1,0:T(8,128)(2,1)S(1)}, bf16[256,1024]{1,0:T(8,128)(2,1)S(1)}, bf16[256,1024]{1,0:T(8,128)(2,1)S(1)}, bf16[96,256]{1,0:T(8,128)(2,1)S(1)}, bf16[896,1152]{1,0:T(8,128)(2,1)S(1)}) custom-call(s32[2]{0:T(128)S(1)} %pad_add_fusion.place_ref, bf16[224,1152]{1,0:T(8,128)(2,1)S(1)} %bitcast.22, bf16[224,1152]{1,0:T(8,128)(2,1)} %bitcast.7.p1_ref, ...), custom_call_target="tpu_custom_call" | custom-call | flops 1409286144 | bytes 8388608 | tf_op jit(solution)/shard_map/pallas_call | solution.py:274
  55.7 4.0 %collective-permute-start.8 = (bf16[96,256]{1,0:T(8,128)(2,1)S(1)}, bf16[96,256]{1,0:T(8,128)(2,1)S(1)}, u32[]{:S(2)}, u32[]{:S(2)}) collective-permute-start(bf16[96,256]{1,0:T(8,128)(2,1)S(1)} %get-tuple-element.64._.refs_0_), channel_id=1, source_target_pairs={{0,48},{16,32},{32,16},{48,0},{64,112},{80,96},{96,80},{112,64},{1... | collective-permute-start | bytes 147464 | tf_op jit(solution)/shard_map/ppermute | solution.py:570
  59.6 0.5 collective-permute-start.6
  60.1 3.5 %shard_map.98 = (f32[256,896]{1,0:T(8,128)S(1)}, f32[256,896]{1,0:T(8,128)S(1)}, f32[256,896]{1,0:T(8,128)S(1)}, f32[8,128]{1,0:T(8,128)S(1)}) custom-call(bf16[256,1024]{1,0:T(8,128)(2,1)S(1)} %get-tuple-element.62.gate_grad_ref, bf16[256,1024]{1,0:T(8,128)(2,1)S(1)} %get-tuple-element.63.up_grad_ref, bf16[256,1024]{1,0:T(8,128)(2,1)S(1)} %get-tuple-element.65.hidden_ref, ...), custom_call_target="tpu_custom_call" | custom-call | flops 1409286144 | bytes 9437184 | tf_op jit(solution)/shard_map/pallas_call | solution.py:345
  63.7 5.9 %collective-permute-start.14 = (bf16[96,256]{1,0:T(8,128)(2,1)S(1)}, bf16[96,256]{1,0:T(8,128)(2,1)S(1)}, u32[]{:S(2)}, u32[]{:S(2)}) collective-permute-start(bf16[96,256]{1,0:T(8,128)(2,1)S(1)} %shard_map.99._.refs_0_), channel_id=1, source_target_pairs={{0,160},{16,176},{32,128},{48,144},{64,224},{80,240},{96,192},{112... | collective-permute-start | bytes 147464 | tf_op jit(solution)/shard_map/ppermute | solution.py:574
  69.6 0.3 collective-permute-start.13
  69.9 0.9 collective-permute-start.12
  70.8 2.4 %shard_map.100 = (bf16[224,1024]{1,0:T(8,128)(2,1)S(1)}, bf16[224,1024]{1,0:T(8,128)(2,1)}, bf16[224,1024]{1,0:T(8,128)(2,1)}, bf16[224,1024]{1,0:T(8,128)(2,1)}, f32[8,128]{1,0:T(8,128)S(1)}) custom-call(s32[2]{0:T(128)S(1)} %pad_add_fusion.place_ref, bf16[896,512]{1,0:T(8,128)(2,1)S(1)} %copy-done.15, ...), custom_call_target="tpu_custom_call" | custom-call | flops 939524096 | bytes 4194304 | tf_op jit(solution)/shard_map/pallas_call | solution.py:308
  73.3 1.5 %collective-permute-done.13.refs_2_ = bf16[96,256]{1,0:T(8,128)(2,1)S(1)} collective-permute-done((bf16[96,256]{1,0:T(8,128)(2,1)S(1)}, bf16[96,256]{1,0:T(8,128)(2,1)S(1)}, u32[]{:S(2)}, u32[]{:S(2)}) %collective-permute-start.13) | collective-permute-done | bytes 49184 | tf_op jit(solution)/shard_map/ppermute | solution.py:574
  74.8 0.7 shard_map.102
  75.5 0.0 copy-done.2
  75.5 2.5 %collective-permute-start.15 = (f32[384,128]{1,0:T(8,128)S(1)}, f32[384,128]{1,0:T(8,128)S(1)}, u32[]{:S(2)}, u32[]{:S(2)}) collective-permute-start(f32[384,128]{1,0:T(8,128)S(1)} %get-tuple-element.77), channel_id=1, source_target_pairs={{0,16},{16,0},{32,48},{48,32},{64,80},{80,64},{96,112},{112,96},{1... | collective-permute-start | bytes 589832 | tf_op jit(solution)/shard_map/ppermute | solution.py:500
  77.9 1.1 collective-permute-done.15
  79.1 0.8 pad_maximum_fusion
  79.9 6.5 %all-to-all-start.2 = ((f32[16,48,128]{2,1,0:T(8,128)}), f32[16,48,128]{2,1,0:T(8,128)S(1)}, u32[]{:S(2)}, u32[]{:S(2)}) async-start(f32[16,48,128]{2,1,0:T(8,128)} %pad_maximum_fusion), calls=%async_computation.2 | async-start | bytes 786432 | tf_op jit(solution)/shard_map/all_to_all | solution.py:580
  86.3 1.4 %collective-permute-start.9 = (bf16[224,1024]{1,0:T(8,128)(2,1)}, bf16[224,1024]{1,0:T(8,128)(2,1)}, u32[]{:S(2)}, u32[]{:S(2)}) collective-permute-start(bf16[224,1024]{1,0:T(8,128)(2,1)} %get-tuple-element.69), channel_id=1, source_target_pairs={{0,4},{1,5},{2,6},{3,7},{4,8},{5,9},{6,10},{7,11},{8,12},{9,13},{1... | collective-permute-start | bytes 1376264 | tf_op jit(solution)/shard_map/ppermute | solution.py:122
  87.7 1.4 %collective-permute-start.10 = (bf16[224,1024]{1,0:T(8,128)(2,1)}, bf16[224,1024]{1,0:T(8,128)(2,1)}, u32[]{:S(2)}, u32[]{:S(2)}) collective-permute-start(bf16[224,1024]{1,0:T(8,128)(2,1)} %get-tuple-element.70), channel_id=1, source_target_pairs={{0,12},{1,13},{2,14},{3,15},{4,0},{5,1},{6,2},{7,3},{8,4},{9,5},{1... | collective-permute-start | bytes 1376264 | tf_op jit(solution)/shard_map/ppermute | solution.py:122
  89.1 1.6 %collective-permute-start.11 = (bf16[224,1024]{1,0:T(8,128)(2,1)}, bf16[224,1024]{1,0:T(8,128)(2,1)}, u32[]{:S(2)}, u32[]{:S(2)}) collective-permute-start(bf16[224,1024]{1,0:T(8,128)(2,1)} %get-tuple-element.71), channel_id=1, source_target_pairs={{0,8},{1,9},{2,10},{3,11},{4,12},{5,13},{6,14},{7,15},{8,0},{9,1},... | collective-permute-start | bytes 1376264 | tf_op jit(solution)/shard_map/ppermute | solution.py:122
  90.7 5.2 %all-to-all-done.2 = f32[16,48,128]{2,1,0:T(8,128)S(1)} async-done(((f32[16,48,128]{2,1,0:T(8,128)}), f32[16,48,128]{2,1,0:T(8,128)S(1)}, u32[]{:S(2)}, u32[]{:S(2)}) %all-to-all-start.2) | async-done | bytes 393248 | tf_op jit(solution)/shard_map/all_to_all | solution.py:580
  95.9 0.6 fusion
  96.5 0.6 broadcast_in_dim.10
  97.1 4.6 %all-to-all-start.3 = ((f32[8,24,128]{2,1,0:T(8,128)}), f32[8,24,128]{2,1,0:T(8,128)S(1)}, u32[]{:S(2)}, u32[]{:S(2)}) async-start(f32[8,24,128]{2,1,0:T(8,128)} %broadcast_in_dim.10), calls=%async_computation.3 | async-start | bytes 196608 | tf_op jit(solution)/shard_map/all_to_all | solution.py:35
  101.8 4.2 %shard_map.105 = (f32[3,32,32]{2,1,0:T(8,128)}, f32[8,128]{1,0:T(8,128)}) custom-call(f32[24,128]{1,0:T(8,128)} %get-tuple-element.90._.gram_ref), custom_call_target="tpu_custom_call" | custom-call | flops 4294967296 | bytes 1048576 | tf_op jit(solution)/shard_map/pallas_call | solution.py:436
  106.0 3.5 %all-to-all-done.3.value_ref = f32[8,24,128]{2,1,0:T(8,128)S(1)} async-done(((f32[8,24,128]{2,1,0:T(8,128)}), f32[8,24,128]{2,1,0:T(8,128)S(1)}, u32[]{:S(2)}, u32[]{:S(2)}) %all-to-all-start.3) | async-done | bytes 98336 | tf_op jit(solution)/shard_map/all_to_all | solution.py:35
  109.5 0.7 copy-done.13
  110.1 0.7 broadcast_in_dim.11
  110.8 3.5 %all-to-all-start.4 = ((f32[16,24,128]{2,1,0:T(8,128)}), f32[16,24,128]{2,1,0:T(8,128)S(1)}, u32[]{:S(2)}, u32[]{:S(2)}) async-start(f32[16,24,128]{2,1,0:T(8,128)} %broadcast_in_dim.11), calls=%async_computation.4 | async-start | bytes 393216 | tf_op jit(solution)/shard_map/all_to_all | solution.py:35
  114.4 1.0 copy-done.9
  115.4 1.5 %shard_map.103 = (bf16[56,1024]{1,0:T(8,128)(2,1)S(1)}, bf16[56,1024]{1,0:T(8,128)(2,1)S(1)}, bf16[56,1024]{1,0:T(8,128)(2,1)S(1)}, bf16[56,1024]{1,0:T(8,128)(2,1)S(1)}) custom-call(s32[1]{0:T(128)} %bitcast.place_ref, bf16[4,56,1024]{2,1,0:T(8,128)(2,1)S(1)} %bitcast.25, bf16[4,56,1024]{2,1,0:T(8,128)(2,1)} %bitcast.12.g1_ref, ...), custom_call_target="tpu_custom_call" | custom-call | tf_op jit(solution)/shard_map/pallas_call | solution.py:135
  117.0 1.3 collective-permute-start.16
  118.3 1.4 %collective-permute-start.17 = (bf16[56,1024]{1,0:T(8,128)(2,1)S(1)}, bf16[56,1024]{1,0:T(8,128)(2,1)S(1)}, u32[]{:S(2)}, u32[]{:S(2)}) collective-permute-start(bf16[56,1024]{1,0:T(8,128)(2,1)S(1)} %get-tuple-element.81), channel_id=1, source_target_pairs={{0,3},{1,0},{2,1},{3,2},{4,7},{5,4},{6,5},{7,6},{8,11},{9,8},{10,9... | collective-permute-start | bytes 344072 | tf_op jit(solution)/shard_map/ppermute | solution.py:142
  119.7 1.5 %collective-permute-start.18 = (bf16[56,1024]{1,0:T(8,128)(2,1)S(1)}, bf16[56,1024]{1,0:T(8,128)(2,1)S(1)}, u32[]{:S(2)}, u32[]{:S(2)}) collective-permute-start(bf16[56,1024]{1,0:T(8,128)(2,1)S(1)} %get-tuple-element.82), channel_id=1, source_target_pairs={{0,2},{1,3},{2,0},{3,1},{4,6},{5,7},{6,4},{7,5},{8,10},{9,11},{10,... | collective-permute-start | bytes 344072 | tf_op jit(solution)/shard_map/ppermute | solution.py:142
  121.3 1.8 %collective-permute-done.16.refs_1_ = bf16[56,1024]{1,0:T(8,128)(2,1)S(1)} collective-permute-done((bf16[56,1024]{1,0:T(8,128)(2,1)S(1)}, bf16[56,1024]{1,0:T(8,128)(2,1)S(1)}, u32[]{:S(2)}, u32[]{:S(2)}) %collective-permute-start.16) | collective-permute-done | bytes 114720 | tf_op jit(solution)/shard_map/ppermute | solution.py:142
  123.1 2.3 %collective-permute-done.18.refs_3_ = bf16[56,1024]{1,0:T(8,128)(2,1)S(1)} collective-permute-done((bf16[56,1024]{1,0:T(8,128)(2,1)S(1)}, bf16[56,1024]{1,0:T(8,128)(2,1)S(1)}, u32[]{:S(2)}, u32[]{:S(2)}) %collective-permute-start.18) | collective-permute-done | bytes 114720 | tf_op jit(solution)/shard_map/ppermute | solution.py:142
  125.4 0.7 shard_map.104
  126.2 4.1 %collective-permute-start.19 = (f32[384,128]{1,0:T(8,128)S(1)}, f32[384,128]{1,0:T(8,128)S(1)}, u32[]{:S(2)}, u32[]{:S(2)}) collective-permute-start(f32[384,128]{1,0:T(8,128)S(1)} %shard_map.107.s_mine_ref), channel_id=1, source_target_pairs={{0,16},{16,0},{32,48},{48,32},{64,80},{80,64},{96,112},{112,96},{1... | collective-permute-start | bytes 589832 | tf_op jit(solution)/shard_map/ppermute | solution.py:500
  130.3 0.1 pad_add_fusion.1.place_ref
  130.4 1.0 collective-permute-done.19.s_other_ref
  131.4 3.2 %shard_map.108 = (bf16[1,3,256,896]{3,2,1,0:T(8,128)(2,1)}, f32[96,56]{1,0:T(8,128)}) custom-call(s32[2]{0:T(128)S(1)} %pad_add_fusion.1.place_ref, f32[384,128]{1,0:T(8,128)S(1)} %shard_map.107.s_mine_ref, f32[384,128]{1,0:T(8,128)S(1)} %collective-permute-done.19.s_other_ref, f32[3,32,32]{2,1,0:T(8,128)S(1)} %copy-done.12, ...), custom_call_target="tpu_custom_call" | custom-call | tf_op jit(solution)/shard_map/pallas_call | solution.py:482
  (43 shorter events, 0.2 us)
Async XLA Ops:
  2.7 14.2 %all-to-all-start = ((bf16[4,56,1152]{2,1,0:T(8,128)(2,1)}), bf16[4,56,1152]{2,1,0:T(8,128)(2,1)S(1)}, u32[]{:S(2)}, u32[]{:S(2)}) async-start(bf16[4,56,1152]{2,1,0:T(8,128)(2,1)} %get-tuple-element.48), calls=%async_computation | async-start | bytes 1032192 | tf_op jit(solution)/shard_map/all_to_all | solution.py:108
  7.7 5.2 %collective-permute-start.2 = (bf16[56,1152]{1,0:T(8,128)(2,1)}, bf16[56,1152]{1,0:T(8,128)(2,1)S(1)}, u32[]{:S(2)}, u32[]{:S(2)}) collective-permute-start(bf16[56,1152]{1,0:T(8,128)(2,1)} %get-tuple-element.49.p0_ref), channel_id=1, source_target_pairs={{0,1},{1,2},{2,3},{3,0},{4,5},{5,6},{6,7},{7,4},{8,9},{9,10},{10,1... | collective-permute-start | bytes 387080 | tf_op jit(solution)/shard_map/ppermute | solution.py:43
  8.9 8.0 %collective-permute-start.1 = (bf16[56,1152]{1,0:T(8,128)(2,1)}, bf16[56,1152]{1,0:T(8,128)(2,1)S(1)}, u32[]{:S(2)}, u32[]{:S(2)}) collective-permute-start(bf16[56,1152]{1,0:T(8,128)(2,1)} %get-tuple-element.49.p0_ref), channel_id=1, source_target_pairs={{0,2},{1,3},{2,0},{3,1},{4,6},{5,7},{6,4},{7,5},{8,10},{9,11},{10,... | collective-permute-start | bytes 387080 | tf_op jit(solution)/shard_map/ppermute | solution.py:43
  11.4 5.5 %collective-permute-start = (bf16[56,1152]{1,0:T(8,128)(2,1)}, bf16[56,1152]{1,0:T(8,128)(2,1)S(1)}, u32[]{:S(2)}, u32[]{:S(2)}) collective-permute-start(bf16[56,1152]{1,0:T(8,128)(2,1)} %get-tuple-element.49.p0_ref), channel_id=1, source_target_pairs={{0,3},{1,0},{2,1},{3,2},{4,7},{5,4},{6,5},{7,6},{8,11},{9,8},{10,9... | collective-permute-start | bytes 387080 | tf_op jit(solution)/shard_map/ppermute | solution.py:43
  16.9 0.9 copy-start.10
  19.9 8.3 %copy-start.5 = (bf16[256,896]{1,0:T(8,128)(2,1)S(1)}, bf16[256,896]{1,0:T(8,128)(2,1)}, u32[]{:S(2)}) copy-start(bf16[256,896]{1,0:T(8,128)(2,1)} %gate_ref.1) | copy-start | bytes 1376260
  19.9 29.3 %all-to-all-start.1 = ((bf16[4,4,56,1152]{3,2,1,0:T(8,128)(2,1)}), bf16[4,4,56,1152]{3,2,1,0:T(8,128)(2,1)S(1)}, u32[]{:S(2)}, u32[]{:S(2)}) async-start(bf16[4,4,56,1152]{3,2,1,0:T(8,128)(2,1)} %broadcast_in_dim.8), calls=%async_computation.1 | async-start | bytes 4128768 | tf_op jit(solution)/shard_map/all_to_all | solution.py:35
  23.7 12.4 %collective-permute-start.5 = (bf16[4,56,1152]{2,1,0:T(8,128)(2,1)S(1)}, bf16[4,56,1152]{2,1,0:T(8,128)(2,1)S(1)}, u32[]{:S(2)}, u32[]{:S(2)}) collective-permute-start(bf16[4,56,1152]{2,1,0:T(8,128)(2,1)S(1)} %shard_map.96), channel_id=1, source_target_pairs={{0,4},{1,5},{2,6},{3,7},{4,8},{5,9},{6,10},{7,11},{8,12},{9,13},{1... | collective-permute-start | bytes 1548296 | tf_op jit(solution)/shard_map/ppermute | solution.py:43
  24.7 22.6 %collective-permute-start.4 = (bf16[4,56,1152]{2,1,0:T(8,128)(2,1)S(1)}, bf16[4,56,1152]{2,1,0:T(8,128)(2,1)}, u32[]{:S(2)}, u32[]{:S(2)}) collective-permute-start(bf16[4,56,1152]{2,1,0:T(8,128)(2,1)S(1)} %shard_map.96), channel_id=1, source_target_pairs={{0,8},{1,9},{2,10},{3,11},{4,12},{5,13},{6,14},{7,15},{8,0},{9,1},... | collective-permute-start | bytes 1548296 | tf_op jit(solution)/shard_map/ppermute | solution.py:43
  27.0 22.2 %collective-permute-start.3 = (bf16[4,56,1152]{2,1,0:T(8,128)(2,1)S(1)}, bf16[4,56,1152]{2,1,0:T(8,128)(2,1)}, u32[]{:S(2)}, u32[]{:S(2)}) collective-permute-start(bf16[4,56,1152]{2,1,0:T(8,128)(2,1)S(1)} %shard_map.96), channel_id=1, source_target_pairs={{0,12},{1,13},{2,14},{3,15},{4,0},{5,1},{6,2},{7,3},{8,4},{9,5},{1... | collective-permute-start | bytes 1548296 | tf_op jit(solution)/shard_map/ppermute | solution.py:43
  28.2 1.3 copy-start.4
  29.6 1.0 copy-start.6
  30.6 1.0 copy-start.7
  34.5 0.9 copy-start.14
  55.7 8.0 %collective-permute-start.8 = (bf16[96,256]{1,0:T(8,128)(2,1)S(1)}, bf16[96,256]{1,0:T(8,128)(2,1)S(1)}, u32[]{:S(2)}, u32[]{:S(2)}) collective-permute-start(bf16[96,256]{1,0:T(8,128)(2,1)S(1)} %get-tuple-element.64._.refs_0_), channel_id=1, source_target_pairs={{0,48},{16,32},{32,16},{48,0},{64,112},{80,96},{96,80},{112,64},{1... | collective-permute-start | bytes 147464 | tf_op jit(solution)/shard_map/ppermute | solution.py:570
  59.6 4.0 %collective-permute-start.7 = (bf16[96,256]{1,0:T(8,128)(2,1)S(1)}, bf16[96,256]{1,0:T(8,128)(2,1)S(1)}, u32[]{:S(2)}, u32[]{:S(2)}) collective-permute-start(bf16[96,256]{1,0:T(8,128)(2,1)S(1)} %get-tuple-element.64._.refs_0_), channel_id=1, source_target_pairs={{0,32},{16,48},{32,0},{48,16},{64,96},{80,112},{96,64},{112,80},{1... | collective-permute-start | bytes 147464 | tf_op jit(solution)/shard_map/ppermute | solution.py:570
  59.6 4.1 %collective-permute-start.6 = (bf16[96,256]{1,0:T(8,128)(2,1)S(1)}, bf16[96,256]{1,0:T(8,128)(2,1)S(1)}, u32[]{:S(2)}, u32[]{:S(2)}) collective-permute-start(bf16[96,256]{1,0:T(8,128)(2,1)S(1)} %get-tuple-element.64._.refs_0_), channel_id=1, source_target_pairs={{0,16},{16,0},{32,48},{48,32},{64,80},{80,64},{96,112},{112,96},{1... | collective-permute-start | bytes 147464 | tf_op jit(solution)/shard_map/ppermute | solution.py:570
  60.1 10.7 %copy-start.15 = (bf16[896,512]{1,0:T(8,128)(2,1)S(1)}, bf16[896,512]{1,0:T(8,128)(2,1)}, u32[]{:S(2)}) copy-start(bf16[896,512]{1,0:T(8,128)(2,1)} %copy-done.14) | copy-start | bytes 2752516
  63.6 11.8 %copy-start = (f32[256,896]{1,0:T(8,128)}, f32[256,896]{1,0:T(8,128)S(1)}, u32[]{:S(2)}) copy-start(f32[256,896]{1,0:T(8,128)S(1)} %get-tuple-element.74.m1_ref) | copy-start | bytes 2752516
  63.6 11.8 %copy-start.2 = (f32[256,896]{1,0:T(8,128)}, f32[256,896]{1,0:T(8,128)S(1)}, u32[]{:S(2)}) copy-start(f32[256,896]{1,0:T(8,128)S(1)} %get-tuple-element.75.m2_ref) | copy-start | bytes 2752516
  63.7 9.5 %collective-permute-start.14 = (bf16[96,256]{1,0:T(8,128)(2,1)S(1)}, bf16[96,256]{1,0:T(8,128)(2,1)S(1)}, u32[]{:S(2)}, u32[]{:S(2)}) collective-permute-start(bf16[96,256]{1,0:T(8,128)(2,1)S(1)} %shard_map.99._.refs_0_), channel_id=1, source_target_pairs={{0,160},{16,176},{32,128},{48,144},{64,224},{80,240},{96,192},{112... | collective-permute-start | bytes 147464 | tf_op jit(solution)/shard_map/ppermute | solution.py:574
  69.6 5.1 %collective-permute-start.13 = (bf16[96,256]{1,0:T(8,128)(2,1)S(1)}, bf16[96,256]{1,0:T(8,128)(2,1)S(1)}, u32[]{:S(2)}, u32[]{:S(2)}) collective-permute-start(bf16[96,256]{1,0:T(8,128)(2,1)S(1)} %shard_map.99._.refs_0_), channel_id=1, source_target_pairs={{0,192},{16,208},{32,224},{48,240},{64,128},{80,144},{96,160},{112... | collective-permute-start | bytes 147464 | tf_op jit(solution)/shard_map/ppermute | solution.py:574
  69.9 4.8 %collective-permute-start.12 = (bf16[96,256]{1,0:T(8,128)(2,1)S(1)}, bf16[96,256]{1,0:T(8,128)(2,1)S(1)}, u32[]{:S(2)}, u32[]{:S(2)}) collective-permute-start(bf16[96,256]{1,0:T(8,128)(2,1)S(1)} %shard_map.99._.refs_0_), channel_id=1, source_target_pairs={{0,64},{16,80},{32,96},{48,112},{64,0},{80,16},{96,32},{112,48},{1... | collective-permute-start | bytes 147464 | tf_op jit(solution)/shard_map/ppermute | solution.py:574
  73.3 2.2 %copy-start.8 = (bf16[224,1024]{1,0:T(8,128)(2,1)}, bf16[224,1024]{1,0:T(8,128)(2,1)S(1)}, u32[]{:S(2)}) copy-start(bf16[224,1024]{1,0:T(8,128)(2,1)S(1)} %get-tuple-element.68) | copy-start | bytes 1376260
  75.5 3.5 %collective-permute-start.15 = (f32[384,128]{1,0:T(8,128)S(1)}, f32[384,128]{1,0:T(8,128)S(1)}, u32[]{:S(2)}, u32[]{:S(2)}) collective-permute-start(f32[384,128]{1,0:T(8,128)S(1)} %get-tuple-element.77), channel_id=1, source_target_pairs={{0,16},{16,0},{32,48},{48,32},{64,80},{80,64},{96,112},{112,96},{1... | collective-permute-start | bytes 589832 | tf_op jit(solution)/shard_map/ppermute | solution.py:500
  79.9 16.0 %all-to-all-start.2 = ((f32[16,48,128]{2,1,0:T(8,128)}), f32[16,48,128]{2,1,0:T(8,128)S(1)}, u32[]{:S(2)}, u32[]{:S(2)}) async-start(f32[16,48,128]{2,1,0:T(8,128)} %pad_maximum_fusion), calls=%async_computation.2 | async-start | bytes 786432 | tf_op jit(solution)/shard_map/all_to_all | solution.py:580
  86.3 28.0 %collective-permute-start.9 = (bf16[224,1024]{1,0:T(8,128)(2,1)}, bf16[224,1024]{1,0:T(8,128)(2,1)}, u32[]{:S(2)}, u32[]{:S(2)}) collective-permute-start(bf16[224,1024]{1,0:T(8,128)(2,1)} %get-tuple-element.69), channel_id=1, source_target_pairs={{0,4},{1,5},{2,6},{3,7},{4,8},{5,9},{6,10},{7,11},{8,12},{9,13},{1... | collective-permute-start | bytes 1376264 | tf_op jit(solution)/shard_map/ppermute | solution.py:122
  87.7 26.7 %collective-permute-start.10 = (bf16[224,1024]{1,0:T(8,128)(2,1)}, bf16[224,1024]{1,0:T(8,128)(2,1)}, u32[]{:S(2)}, u32[]{:S(2)}) collective-permute-start(bf16[224,1024]{1,0:T(8,128)(2,1)} %get-tuple-element.70), channel_id=1, source_target_pairs={{0,12},{1,13},{2,14},{3,15},{4,0},{5,1},{6,2},{7,3},{8,4},{9,5},{1... | collective-permute-start | bytes 1376264 | tf_op jit(solution)/shard_map/ppermute | solution.py:122
  89.1 25.3 %collective-permute-start.11 = (bf16[224,1024]{1,0:T(8,128)(2,1)}, bf16[224,1024]{1,0:T(8,128)(2,1)}, u32[]{:S(2)}, u32[]{:S(2)}) collective-permute-start(bf16[224,1024]{1,0:T(8,128)(2,1)} %get-tuple-element.71), channel_id=1, source_target_pairs={{0,8},{1,9},{2,10},{3,11},{4,12},{5,13},{6,14},{7,15},{8,0},{9,1},... | collective-permute-start | bytes 1376264 | tf_op jit(solution)/shard_map/ppermute | solution.py:122
  97.1 12.3 %all-to-all-start.3 = ((f32[8,24,128]{2,1,0:T(8,128)}), f32[8,24,128]{2,1,0:T(8,128)S(1)}, u32[]{:S(2)}, u32[]{:S(2)}) async-start(f32[8,24,128]{2,1,0:T(8,128)} %broadcast_in_dim.10), calls=%async_computation.3 | async-start | bytes 196608 | tf_op jit(solution)/shard_map/all_to_all | solution.py:35
  101.8 12.6 %copy-start.11 = (f32[24,128]{1,0:T(8,128)S(1)}, f32[24,128]{1,0:T(8,128)}, u32[]{:S(2)}) copy-start(f32[24,128]{1,0:T(8,128)} %get-tuple-element.90._.gram_ref) | copy-start | bytes 36868
  106.0 25.4 %copy-start.1 = (f32[256,896]{1,0:T(8,128)S(1)}, f32[256,896]{1,0:T(8,128)}, u32[]{:S(2)}) copy-start(f32[256,896]{1,0:T(8,128)} %copy-done) | copy-start | bytes 2752516
  106.0 25.4 %copy-start.3 = (f32[256,896]{1,0:T(8,128)S(1)}, f32[256,896]{1,0:T(8,128)}, u32[]{:S(2)}) copy-start(f32[256,896]{1,0:T(8,128)} %copy-done.2) | copy-start | bytes 2752516
  109.5 0.7 copy-start.13
  110.8 15.3 %all-to-all-start.4 = ((f32[16,24,128]{2,1,0:T(8,128)}), f32[16,24,128]{2,1,0:T(8,128)S(1)}, u32[]{:S(2)}, u32[]{:S(2)}) async-start(f32[16,24,128]{2,1,0:T(8,128)} %broadcast_in_dim.11), calls=%async_computation.4 | async-start | bytes 393216 | tf_op jit(solution)/shard_map/all_to_all | solution.py:35
  114.4 1.0 copy-start.9
  115.4 15.9 %copy-start.12 = (f32[3,32,32]{2,1,0:T(8,128)S(1)}, f32[3,32,32]{2,1,0:T(8,128)}, u32[]{:S(2)}) copy-start(f32[3,32,32]{2,1,0:T(8,128)} %get-tuple-element.86.inverse_ref) | copy-start | bytes 36868
  117.0 6.1 %collective-permute-start.16 = (bf16[56,1024]{1,0:T(8,128)(2,1)S(1)}, bf16[56,1024]{1,0:T(8,128)(2,1)S(1)}, u32[]{:S(2)}, u32[]{:S(2)}) collective-permute-start(bf16[56,1024]{1,0:T(8,128)(2,1)S(1)} %get-tuple-element.80), channel_id=1, source_target_pairs={{0,1},{1,2},{2,3},{3,0},{4,5},{5,6},{6,7},{7,4},{8,9},{9,10},{10,1... | collective-permute-start | bytes 344072 | tf_op jit(solution)/shard_map/ppermute | solution.py:142
  118.3 4.8 %collective-permute-start.17 = (bf16[56,1024]{1,0:T(8,128)(2,1)S(1)}, bf16[56,1024]{1,0:T(8,128)(2,1)S(1)}, u32[]{:S(2)}, u32[]{:S(2)}) collective-permute-start(bf16[56,1024]{1,0:T(8,128)(2,1)S(1)} %get-tuple-element.81), channel_id=1, source_target_pairs={{0,3},{1,0},{2,1},{3,2},{4,7},{5,4},{6,5},{7,6},{8,11},{9,8},{10,9... | collective-permute-start | bytes 344072 | tf_op jit(solution)/shard_map/ppermute | solution.py:142
  119.7 5.7 %collective-permute-start.18 = (bf16[56,1024]{1,0:T(8,128)(2,1)S(1)}, bf16[56,1024]{1,0:T(8,128)(2,1)S(1)}, u32[]{:S(2)}, u32[]{:S(2)}) collective-permute-start(bf16[56,1024]{1,0:T(8,128)(2,1)S(1)} %get-tuple-element.82), channel_id=1, source_target_pairs={{0,2},{1,3},{2,0},{3,1},{4,6},{5,7},{6,4},{7,5},{8,10},{9,11},{10,... | collective-permute-start | bytes 344072 | tf_op jit(solution)/shard_map/ppermute | solution.py:142
  126.2 5.2 %collective-permute-start.19 = (f32[384,128]{1,0:T(8,128)S(1)}, f32[384,128]{1,0:T(8,128)S(1)}, u32[]{:S(2)}, u32[]{:S(2)}) collective-permute-start(f32[384,128]{1,0:T(8,128)S(1)} %shard_map.107.s_mine_ref), channel_id=1, source_target_pairs={{0,16},{16,0},{32,48},{48,32},{64,80},{80,64},{96,112},{112,96},{1... | collective-permute-start | bytes 589832 | tf_op jit(solution)/shard_map/ppermute | solution.py:500

commit v7 on v6

--- a/solution.py
+++ b/solution.py
@@ -111,11 +111,6 @@
     dy_all = spread(dy_col, "tensor", X_GROUPS, SIDE)
     far, dy_all = lax.optimization_barrier((ring_pieces(x_row, y_ring), dy_all))
     return [p.reshape(rows, -1) for p in far], dy_all.reshape(SIDE * rows, -1)
-
-
-def swap_order(value):
-    blocks = value.reshape((SIDE, SIDE, -1) + value.shape[1:])
-    return jnp.swapaxes(blocks, 0, 1).reshape(value.shape)
 
 
 def send_blocks(blocks):
@@ -324,17 +319,16 @@
         copy.start()
     tokens = hidden_ref.shape[1]
     x = x_ref[:, :tokens]
-    m0_ref[...] = dot(gate_grad_ref[...], x, 1, 1)
-    m1_ref[...] = dot(up_grad_ref[...], x, 1, 1)
     swapped = dot(hidden_ref[...], dy_ref[:, :tokens], 1, 1)
     block = swapped.shape[1] // (SIDE * SIDE)
     parts = [
         swapped[:, (x * SIDE + y) * block : (x * SIDE + y + 1) * block] for y in range(SIDE) for x in range(SIDE)
     ]
-    m2_ref[...] = jnp.concatenate(parts, axis=1)
-    for k, m_ref in enumerate((m0_ref, m1_ref, m2_ref)):
-        loads[k].wait()
-        m_ref[...] += left_ref[k].astype(F32)
+    for copy in loads:
+        copy.wait()
+    m2_ref[...] = jnp.concatenate(parts, axis=1) + left_ref[2].astype(F32)
+    m0_ref[...] = dot(gate_grad_ref[...], x, 1, 1) + left_ref[0].astype(F32)
+    m1_ref[...] = dot(up_grad_ref[...], x, 1, 1) + left_ref[1].astype(F32)
     token_ref[...] = jnp.zeros_like(token_ref)
 
 
@@ -490,10 +484,6 @@
         ],
         compiler_params=pltpu.CompilerParams(vmem_limit_bytes=20 * MIB),
     )(place, s_mine, s_other, inverse, p_trans, *matrices)
-
-
-def after(values, other):
-    return lax.optimization_barrier((values, other))[0]
 
 
 def swap_core(value):

time: 136 us -> 135 us (level)
  no operation moved by 1% of the time
where the time goes in v7:
time: 135 us; the launch traced here: 134 us
  starting transfers between devices  59.5 us (44%)
  waiting for transfers between devices  34.6 us (26%)
  Pallas kernels  27.9 us (21%)
  local copies, waits for them, and re-layouts  10.4 us (8%)
    ppermute x6, waiting for transfers between devices, ring_pieces(): near[k] = lax.ppermute(value, 'tensor', ring(SIDE - k))  18.2 us
    all_to_all x3, starting transfers between devices, spread(): lax.all_to_all(jnp.broadcast_to(value[None], (size,) + value.shape), axis...  11.9 us
    ppermute x6, starting transfers between devices, ring_pieces(): near[k] = lax.ppermute(value, 'tensor', ring(SIDE - k))  9.36 us
    ppermute x3, starting transfers between devices, per_device(): others = [lax.ppermute(p_pair, 'dp', dp_swap(bits)) for bits in (4, 12, 10)]  7.08 us
    unnamed x32, local copies, waits for them, and re-layouts  6.92 us
    ppermute x2, starting transfers between devices, swap_core(): return lax.ppermute(value, 'dp', CORE_PAIR)  6.59 us
    all_to_all x1, starting transfers between devices, per_device(): lax.all_to_all(jnp.concatenate([s_pair, gram], axis=1), 'tensor', 0, 0, t...  6.47 us
    pallas_call x1, Pallas kernels, backward(): pl.pallas_call(backward_kernel, out_shape=(grads, grads, grads, jax.Shape...  6.38 us
  transfers between devices with their start and end apart: 25, of which 12 were waited for; matrix products, arithmetic and copies ran while one was open for 2% of the time, Pallas kernels for 11%

profile of v7, /device:TPU:1, one launch (start us, length us, event | category | flops | bytes accessed | tf_op | source)
XLA Modules:
  0.0 134.4 jit_solution(18264080298305316052)
XLA Ops:
  0.6 2.0 %shard_map.95 = (bf16[56,1152]{1,0:T(8,128)(2,1)}, bf16[4,56,1152]{2,1,0:T(8,128)(2,1)}) custom-call(bf16[56,1024]{1,0:T(8,128)(2,1)} %bitcast.27, bf16[56,1024]{1,0:T(8,128)(2,1)} %bitcast.28, f32[96,56]{1,0:T(8,128)} %bitcast.29), custom_call_target="tpu_custom_call" | custom-call | tf_op jit(solution)/shard_map/pallas_call | solution.py:70
  2.7 5.0 %all-to-all-start = ((bf16[4,56,1152]{2,1,0:T(8,128)(2,1)}), bf16[4,56,1152]{2,1,0:T(8,128)(2,1)S(1)}, u32[]{:S(2)}, u32[]{:S(2)}) async-start(bf16[4,56,1152]{2,1,0:T(8,128)(2,1)} %get-tuple-element.48), calls=%async_computation | async-start | bytes 1032192 | tf_op jit(solution)/shard_map/all_to_all | solution.py:108
  7.7 1.2 collective-permute-start.2
  8.9 2.5 %collective-permute-start.1 = (bf16[56,1152]{1,0:T(8,128)(2,1)}, bf16[56,1152]{1,0:T(8,128)(2,1)S(1)}, u32[]{:S(2)}, u32[]{:S(2)}) collective-permute-start(bf16[56,1152]{1,0:T(8,128)(2,1)} %get-tuple-element.49.p0_ref), channel_id=1, source_target_pairs={{0,2},{1,3},{2,0},{3,1},{4,6},{5,7},{6,4},{7,5},{8,10},{9,11},{10,... | collective-permute-start | bytes 387080 | tf_op jit(solution)/shard_map/ppermute | solution.py:43
  11.4 1.2 collective-permute-start
  12.5 0.4 collective-permute-done.2.p3_ref
  12.9 4.0 %collective-permute-done.1.p2_ref = bf16[56,1152]{1,0:T(8,128)(2,1)S(1)} collective-permute-done((bf16[56,1152]{1,0:T(8,128)(2,1)}, bf16[56,1152]{1,0:T(8,128)(2,1)S(1)}, u32[]{:S(2)}, u32[]{:S(2)}) %collective-permute-start.1) | collective-permute-done | bytes 129056 | tf_op jit(solution)/shard_map/ppermute | solution.py:43
  16.9 0.0 collective-permute-done.p1_ref
  16.9 0.9 copy-done.10
  17.8 0.7 shard_map.96
  18.4 1.5 %broadcast_in_dim.8 = bf16[4,4,56,1152]{3,2,1,0:T(8,128)(2,1)} broadcast(bf16[4,56,1152]{2,1,0:T(8,128)(2,1)S(1)} %all-to-all-done), dimensions={1,2,3} | broadcast | bytes 2580480 | tf_op jit(solution)/shard_map/broadcast_in_dim | solution.py:36
  19.9 3.7 %all-to-all-start.1 = ((bf16[4,4,56,1152]{3,2,1,0:T(8,128)(2,1)}), bf16[4,4,56,1152]{3,2,1,0:T(8,128)(2,1)S(1)}, u32[]{:S(2)}, u32[]{:S(2)}) async-start(bf16[4,4,56,1152]{3,2,1,0:T(8,128)(2,1)} %broadcast_in_dim.8), calls=%async_computation.1 | async-start | bytes 4128768 | tf_op jit(solution)/shard_map/all_to_all | solution.py:35
  23.7 1.0 collective-permute-start.5
  24.7 2.4 %collective-permute-start.4 = (bf16[4,56,1152]{2,1,0:T(8,128)(2,1)S(1)}, bf16[4,56,1152]{2,1,0:T(8,128)(2,1)}, u32[]{:S(2)}, u32[]{:S(2)}) collective-permute-start(bf16[4,56,1152]{2,1,0:T(8,128)(2,1)S(1)} %shard_map.96), channel_id=1, source_target_pairs={{0,8},{1,9},{2,10},{3,11},{4,12},{5,13},{6,14},{7,15},{8,0},{9,1},... | collective-permute-start | bytes 1548296 | tf_op jit(solution)/shard_map/ppermute | solution.py:43
  27.0 1.2 collective-permute-start.3
  28.2 1.3 copy-done.4
  29.6 1.0 copy-done.6
  30.6 1.0 copy-done.7
  31.6 2.8 %shard_map.94 = (bf16[112,256,896]{2,1,0:T(8,128)(2,1)}, bf16[896,512]{1,0:T(8,128)(2,1)S(1)}, f32[8,128]{1,0:T(8,128)}) custom-call(bf16[256,896]{1,0:T(8,128)(2,1)S(1)} %copy-done.5, bf16[256,896]{1,0:T(8,128)(2,1)S(1)} %copy-done.6, bf16[256,896]{1,0:T(8,128)(2,1)S(1)} %copy-done.7, bf16[1,3,256,896]{3,2,1,0:T(8,128)(2,1)S(1)} %copy-done.4), custom_call_target="tpu_custom_call" | custom-call | tf_op jit(solution)/shard_map/pallas_call | solution.py:191
  34.5 0.0 copy-start.14
  34.5 0.9 copy-done.14
  35.4 0.1 pad_add_fusion.place_ref
  35.5 0.6 collective-permute-done.5
  36.0 11.2 %collective-permute-done.4 = bf16[4,56,1152]{2,1,0:T(8,128)(2,1)} collective-permute-done((bf16[4,56,1152]{2,1,0:T(8,128)(2,1)S(1)}, bf16[4,56,1152]{2,1,0:T(8,128)(2,1)}, u32[]{:S(2)}, u32[]{:S(2)}) %collective-permute-start.4) | collective-permute-done | bytes 516128 | tf_op jit(solution)/shard_map/ppermute | solution.py:43
  47.2 2.0 %collective-permute-done.3 = bf16[4,56,1152]{2,1,0:T(8,128)(2,1)} collective-permute-done((bf16[4,56,1152]{2,1,0:T(8,128)(2,1)S(1)}, bf16[4,56,1152]{2,1,0:T(8,128)(2,1)}, u32[]{:S(2)}, u32[]{:S(2)}) %collective-permute-start.3) | collective-permute-done | bytes 516128 | tf_op jit(solution)/shard_map/ppermute | solution.py:43
  49.3 6.4 %shard_map.97 = (bf16[256,1024]{1,0:T(8,128)(2,1)S(1)}, bf16[256,1024]{1,0:T(8,128)(2,1)S(1)}, bf16[256,1024]{1,0:T(8,128)(2,1)S(1)}, bf16[96,256]{1,0:T(8,128)(2,1)S(1)}, bf16[896,1152]{1,0:T(8,128)(2,1)S(1)}) custom-call(s32[2]{0:T(128)S(1)} %pad_add_fusion.place_ref, bf16[224,1152]{1,0:T(8,128)(2,1)S(1)} %bitcast.22, bf16[224,1152]{1,0:T(8,128)(2,1)} %bitcast.7.p1_ref, ...), custom_call_target="tpu_custom_call" | custom-call | flops 1409286144 | bytes 8388608 | tf_op jit(solution)/shard_map/pallas_call | solution.py:269
  55.7 4.0 %collective-permute-start.8 = (bf16[96,256]{1,0:T(8,128)(2,1)S(1)}, bf16[96,256]{1,0:T(8,128)(2,1)S(1)}, u32[]{:S(2)}, u32[]{:S(2)}) collective-permute-start(bf16[96,256]{1,0:T(8,128)(2,1)S(1)} %get-tuple-element.64._.refs_0_), channel_id=1, source_target_pairs={{0,48},{16,32},{32,16},{48,0},{64,112},{80,96},{96,80},{112,64},{1... | collective-permute-start | bytes 147464 | tf_op jit(solution)/shard_map/ppermute | solution.py:560
  59.6 0.5 collective-permute-start.6
  60.1 3.2 %shard_map.98 = (f32[256,896]{1,0:T(8,128)S(1)}, f32[256,896]{1,0:T(8,128)S(1)}, f32[256,896]{1,0:T(8,128)S(1)}, f32[8,128]{1,0:T(8,128)S(1)}) custom-call(bf16[256,1024]{1,0:T(8,128)(2,1)S(1)} %get-tuple-element.62.gate_grad_ref, bf16[256,1024]{1,0:T(8,128)(2,1)S(1)} %get-tuple-element.63.up_grad_ref, bf16[256,1024]{1,0:T(8,128)(2,1)S(1)} %get-tuple-element.65.hidden_ref, ...), custom_call_target="tpu_custom_call" | custom-call | flops 1409286144 | bytes 9437184 | tf_op jit(solution)/shard_map/pallas_call | solution.py:339
  63.4 5.9 %collective-permute-start.14 = (bf16[96,256]{1,0:T(8,128)(2,1)S(1)}, bf16[96,256]{1,0:T(8,128)(2,1)S(1)}, u32[]{:S(2)}, u32[]{:S(2)}) collective-permute-start(bf16[96,256]{1,0:T(8,128)(2,1)S(1)} %shard_map.99._.refs_0_), channel_id=1, source_target_pairs={{0,160},{16,176},{32,128},{48,144},{64,224},{80,240},{96,192},{112... | collective-permute-start | bytes 147464 | tf_op jit(solution)/shard_map/ppermute | solution.py:564
  69.3 0.3 collective-permute-start.13
  69.6 0.9 collective-permute-start.12
  70.5 2.4 %shard_map.100 = (bf16[224,1024]{1,0:T(8,128)(2,1)S(1)}, bf16[224,1024]{1,0:T(8,128)(2,1)}, bf16[224,1024]{1,0:T(8,128)(2,1)}, bf16[224,1024]{1,0:T(8,128)(2,1)}, f32[8,128]{1,0:T(8,128)S(1)}) custom-call(s32[2]{0:T(128)S(1)} %pad_add_fusion.place_ref, bf16[896,512]{1,0:T(8,128)(2,1)S(1)} %copy-done.15, ...), custom_call_target="tpu_custom_call" | custom-call | flops 939524096 | bytes 4194304 | tf_op jit(solution)/shard_map/pallas_call | solution.py:303
  72.9 1.5 %collective-permute-done.13.refs_2_ = bf16[96,256]{1,0:T(8,128)(2,1)S(1)} collective-permute-done((bf16[96,256]{1,0:T(8,128)(2,1)S(1)}, bf16[96,256]{1,0:T(8,128)(2,1)S(1)}, u32[]{:S(2)}, u32[]{:S(2)}) %collective-permute-start.13) | collective-permute-done | bytes 49184 | tf_op jit(solution)/shard_map/ppermute | solution.py:564
  74.5 0.7 shard_map.102
  75.1 0.0 copy-done.2
  75.2 2.5 %collective-permute-start.15 = (f32[384,128]{1,0:T(8,128)S(1)}, f32[384,128]{1,0:T(8,128)S(1)}, u32[]{:S(2)}, u32[]{:S(2)}) collective-permute-start(f32[384,128]{1,0:T(8,128)S(1)} %get-tuple-element.77), channel_id=1, source_target_pairs={{0,16},{16,0},{32,48},{48,32},{64,80},{80,64},{96,112},{112,96},{1... | collective-permute-start | bytes 589832 | tf_op jit(solution)/shard_map/ppermute | solution.py:490
  77.6 1.1 collective-permute-done.15
  78.8 0.8 pad_maximum_fusion
  79.5 6.5 %all-to-all-start.2 = ((f32[16,48,128]{2,1,0:T(8,128)}), f32[16,48,128]{2,1,0:T(8,128)S(1)}, u32[]{:S(2)}, u32[]{:S(2)}) async-start(f32[16,48,128]{2,1,0:T(8,128)} %pad_maximum_fusion), calls=%async_computation.2 | async-start | bytes 786432 | tf_op jit(solution)/shard_map/all_to_all | solution.py:570
  86.0 1.4 %collective-permute-start.9 = (bf16[224,1024]{1,0:T(8,128)(2,1)}, bf16[224,1024]{1,0:T(8,128)(2,1)}, u32[]{:S(2)}, u32[]{:S(2)}) collective-permute-start(bf16[224,1024]{1,0:T(8,128)(2,1)} %get-tuple-element.69), channel_id=1, source_target_pairs={{0,4},{1,5},{2,6},{3,7},{4,8},{5,9},{6,10},{7,11},{8,12},{9,13},{1... | collective-permute-start | bytes 1376264 | tf_op jit(solution)/shard_map/ppermute | solution.py:117
  87.4 1.4 %collective-permute-start.10 = (bf16[224,1024]{1,0:T(8,128)(2,1)}, bf16[224,1024]{1,0:T(8,128)(2,1)}, u32[]{:S(2)}, u32[]{:S(2)}) collective-permute-start(bf16[224,1024]{1,0:T(8,128)(2,1)} %get-tuple-element.70), channel_id=1, source_target_pairs={{0,12},{1,13},{2,14},{3,15},{4,0},{5,1},{6,2},{7,3},{8,4},{9,5},{1... | collective-permute-start | bytes 1376264 | tf_op jit(solution)/shard_map/ppermute | solution.py:117
  88.8 1.6 %collective-permute-start.11 = (bf16[224,1024]{1,0:T(8,128)(2,1)}, bf16[224,1024]{1,0:T(8,128)(2,1)}, u32[]{:S(2)}, u32[]{:S(2)}) collective-permute-start(bf16[224,1024]{1,0:T(8,128)(2,1)} %get-tuple-element.71), channel_id=1, source_target_pairs={{0,8},{1,9},{2,10},{3,11},{4,12},{5,13},{6,14},{7,15},{8,0},{9,1},... | collective-permute-start | bytes 1376264 | tf_op jit(solution)/shard_map/ppermute | solution.py:117
  90.4 5.2 %all-to-all-done.2 = f32[16,48,128]{2,1,0:T(8,128)S(1)} async-done(((f32[16,48,128]{2,1,0:T(8,128)}), f32[16,48,128]{2,1,0:T(8,128)S(1)}, u32[]{:S(2)}, u32[]{:S(2)}) %all-to-all-start.2) | async-done | bytes 393248 | tf_op jit(solution)/shard_map/all_to_all | solution.py:570
  95.6 0.6 fusion
  96.2 0.6 broadcast_in_dim.10
  96.8 4.6 %all-to-all-start.3 = ((f32[8,24,128]{2,1,0:T(8,128)}), f32[8,24,128]{2,1,0:T(8,128)S(1)}, u32[]{:S(2)}, u32[]{:S(2)}) async-start(f32[8,24,128]{2,1,0:T(8,128)} %broadcast_in_dim.10), calls=%async_computation.3 | async-start | bytes 196608 | tf_op jit(solution)/shard_map/all_to_all | solution.py:35
  101.5 4.2 %shard_map.105 = (f32[3,32,32]{2,1,0:T(8,128)}, f32[8,128]{1,0:T(8,128)}) custom-call(f32[24,128]{1,0:T(8,128)} %get-tuple-element.90._.gram_ref), custom_call_target="tpu_custom_call" | custom-call | flops 4294967296 | bytes 1048576 | tf_op jit(solution)/shard_map/pallas_call | solution.py:430
  105.7 3.5 %all-to-all-done.3.value_ref = f32[8,24,128]{2,1,0:T(8,128)S(1)} async-done(((f32[8,24,128]{2,1,0:T(8,128)}), f32[8,24,128]{2,1,0:T(8,128)S(1)}, u32[]{:S(2)}, u32[]{:S(2)}) %all-to-all-start.3) | async-done | bytes 98336 | tf_op jit(solution)/shard_map/all_to_all | solution.py:35
  109.1 0.7 copy-done.13
  109.8 0.7 broadcast_in_dim.11
  110.5 3.5 %all-to-all-start.4 = ((f32[16,24,128]{2,1,0:T(8,128)}), f32[16,24,128]{2,1,0:T(8,128)S(1)}, u32[]{:S(2)}, u32[]{:S(2)}) async-start(f32[16,24,128]{2,1,0:T(8,128)} %broadcast_in_dim.11), calls=%async_computation.4 | async-start | bytes 393216 | tf_op jit(solution)/shard_map/all_to_all | solution.py:35
  114.1 1.0 copy-done.9
  115.1 1.5 %shard_map.103 = (bf16[56,1024]{1,0:T(8,128)(2,1)S(1)}, bf16[56,1024]{1,0:T(8,128)(2,1)S(1)}, bf16[56,1024]{1,0:T(8,128)(2,1)S(1)}, bf16[56,1024]{1,0:T(8,128)(2,1)S(1)}) custom-call(s32[1]{0:T(128)} %bitcast.place_ref, bf16[4,56,1024]{2,1,0:T(8,128)(2,1)S(1)} %bitcast.25, bf16[4,56,1024]{2,1,0:T(8,128)(2,1)} %bitcast.12.g1_ref, ...), custom_call_target="tpu_custom_call" | custom-call | tf_op jit(solution)/shard_map/pallas_call | solution.py:130
  116.7 1.3 collective-permute-start.16
  118.0 1.4 %collective-permute-start.17 = (bf16[56,1024]{1,0:T(8,128)(2,1)S(1)}, bf16[56,1024]{1,0:T(8,128)(2,1)S(1)}, u32[]{:S(2)}, u32[]{:S(2)}) collective-permute-start(bf16[56,1024]{1,0:T(8,128)(2,1)S(1)} %get-tuple-element.81), channel_id=1, source_target_pairs={{0,3},{1,0},{2,1},{3,2},{4,7},{5,4},{6,5},{7,6},{8,11},{9,8},{10,9... | collective-permute-start | bytes 344072 | tf_op jit(solution)/shard_map/ppermute | solution.py:137
  119.4 1.5 %collective-permute-start.18 = (bf16[56,1024]{1,0:T(8,128)(2,1)S(1)}, bf16[56,1024]{1,0:T(8,128)(2,1)S(1)}, u32[]{:S(2)}, u32[]{:S(2)}) collective-permute-start(bf16[56,1024]{1,0:T(8,128)(2,1)S(1)} %get-tuple-element.82), channel_id=1, source_target_pairs={{0,2},{1,3},{2,0},{3,1},{4,6},{5,7},{6,4},{7,5},{8,10},{9,11},{10,... | collective-permute-start | bytes 344072 | tf_op jit(solution)/shard_map/ppermute | solution.py:137
  121.0 1.8 %collective-permute-done.16.refs_1_ = bf16[56,1024]{1,0:T(8,128)(2,1)S(1)} collective-permute-done((bf16[56,1024]{1,0:T(8,128)(2,1)S(1)}, bf16[56,1024]{1,0:T(8,128)(2,1)S(1)}, u32[]{:S(2)}, u32[]{:S(2)}) %collective-permute-start.16) | collective-permute-done | bytes 114720 | tf_op jit(solution)/shard_map/ppermute | solution.py:137
  122.8 2.3 %collective-permute-done.18.refs_3_ = bf16[56,1024]{1,0:T(8,128)(2,1)S(1)} collective-permute-done((bf16[56,1024]{1,0:T(8,128)(2,1)S(1)}, bf16[56,1024]{1,0:T(8,128)(2,1)S(1)}, u32[]{:S(2)}, u32[]{:S(2)}) %collective-permute-start.18) | collective-permute-done | bytes 114720 | tf_op jit(solution)/shard_map/ppermute | solution.py:137
  125.1 0.7 shard_map.104
  125.8 4.1 %collective-permute-start.19 = (f32[384,128]{1,0:T(8,128)S(1)}, f32[384,128]{1,0:T(8,128)S(1)}, u32[]{:S(2)}, u32[]{:S(2)}) collective-permute-start(f32[384,128]{1,0:T(8,128)S(1)} %shard_map.107.s_mine_ref), channel_id=1, source_target_pairs={{0,16},{16,0},{32,48},{48,32},{64,80},{80,64},{96,112},{112,96},{1... | collective-permute-start | bytes 589832 | tf_op jit(solution)/shard_map/ppermute | solution.py:490
  130.0 0.1 pad_add_fusion.1.place_ref
  130.0 1.0 collective-permute-done.19.s_other_ref
  131.0 3.2 %shard_map.108 = (bf16[1,3,256,896]{3,2,1,0:T(8,128)(2,1)}, f32[96,56]{1,0:T(8,128)}) custom-call(s32[2]{0:T(128)S(1)} %pad_add_fusion.1.place_ref, f32[384,128]{1,0:T(8,128)S(1)} %shard_map.107.s_mine_ref, f32[384,128]{1,0:T(8,128)S(1)} %collective-permute-done.19.s_other_ref, f32[3,32,32]{2,1,0:T(8,128)S(1)} %copy-done.12, ...), custom_call_target="tpu_custom_call" | custom-call | tf_op jit(solution)/shard_map/pallas_call | solution.py:476
  (43 shorter events, 0.2 us)
Async XLA Ops:
  2.7 14.2 %all-to-all-start = ((bf16[4,56,1152]{2,1,0:T(8,128)(2,1)}), bf16[4,56,1152]{2,1,0:T(8,128)(2,1)S(1)}, u32[]{:S(2)}, u32[]{:S(2)}) async-start(bf16[4,56,1152]{2,1,0:T(8,128)(2,1)} %get-tuple-element.48), calls=%async_computation | async-start | bytes 1032192 | tf_op jit(solution)/shard_map/all_to_all | solution.py:108
  7.7 5.2 %collective-permute-start.2 = (bf16[56,1152]{1,0:T(8,128)(2,1)}, bf16[56,1152]{1,0:T(8,128)(2,1)S(1)}, u32[]{:S(2)}, u32[]{:S(2)}) collective-permute-start(bf16[56,1152]{1,0:T(8,128)(2,1)} %get-tuple-element.49.p0_ref), channel_id=1, source_target_pairs={{0,1},{1,2},{2,3},{3,0},{4,5},{5,6},{6,7},{7,4},{8,9},{9,10},{10,1... | collective-permute-start | bytes 387080 | tf_op jit(solution)/shard_map/ppermute | solution.py:43
  8.9 8.0 %collective-permute-start.1 = (bf16[56,1152]{1,0:T(8,128)(2,1)}, bf16[56,1152]{1,0:T(8,128)(2,1)S(1)}, u32[]{:S(2)}, u32[]{:S(2)}) collective-permute-start(bf16[56,1152]{1,0:T(8,128)(2,1)} %get-tuple-element.49.p0_ref), channel_id=1, source_target_pairs={{0,2},{1,3},{2,0},{3,1},{4,6},{5,7},{6,4},{7,5},{8,10},{9,11},{10,... | collective-permute-start | bytes 387080 | tf_op jit(solution)/shard_map/ppermute | solution.py:43
  11.4 5.5 %collective-permute-start = (bf16[56,1152]{1,0:T(8,128)(2,1)}, bf16[56,1152]{1,0:T(8,128)(2,1)S(1)}, u32[]{:S(2)}, u32[]{:S(2)}) collective-permute-start(bf16[56,1152]{1,0:T(8,128)(2,1)} %get-tuple-element.49.p0_ref), channel_id=1, source_target_pairs={{0,3},{1,0},{2,1},{3,2},{4,7},{5,4},{6,5},{7,6},{8,11},{9,8},{10,9... | collective-permute-start | bytes 387080 | tf_op jit(solution)/shard_map/ppermute | solution.py:43
  16.9 0.9 copy-start.10
  19.9 8.3 %copy-start.5 = (bf16[256,896]{1,0:T(8,128)(2,1)S(1)}, bf16[256,896]{1,0:T(8,128)(2,1)}, u32[]{:S(2)}) copy-start(bf16[256,896]{1,0:T(8,128)(2,1)} %gate_ref.1) | copy-start | bytes 1376260
  19.9 29.3 %all-to-all-start.1 = ((bf16[4,4,56,1152]{3,2,1,0:T(8,128)(2,1)}), bf16[4,4,56,1152]{3,2,1,0:T(8,128)(2,1)S(1)}, u32[]{:S(2)}, u32[]{:S(2)}) async-start(bf16[4,4,56,1152]{3,2,1,0:T(8,128)(2,1)} %broadcast_in_dim.8), calls=%async_computation.1 | async-start | bytes 4128768 | tf_op jit(solution)/shard_map/all_to_all | solution.py:35
  23.7 12.4 %collective-permute-start.5 = (bf16[4,56,1152]{2,1,0:T(8,128)(2,1)S(1)}, bf16[4,56,1152]{2,1,0:T(8,128)(2,1)S(1)}, u32[]{:S(2)}, u32[]{:S(2)}) collective-permute-start(bf16[4,56,1152]{2,1,0:T(8,128)(2,1)S(1)} %shard_map.96), channel_id=1, source_target_pairs={{0,4},{1,5},{2,6},{3,7},{4,8},{5,9},{6,10},{7,11},{8,12},{9,13},{1... | collective-permute-start | bytes 1548296 | tf_op jit(solution)/shard_map/ppermute | solution.py:43
  24.7 22.6 %collective-permute-start.4 = (bf16[4,56,1152]{2,1,0:T(8,128)(2,1)S(1)}, bf16[4,56,1152]{2,1,0:T(8,128)(2,1)}, u32[]{:S(2)}, u32[]{:S(2)}) collective-permute-start(bf16[4,56,1152]{2,1,0:T(8,128)(2,1)S(1)} %shard_map.96), channel_id=1, source_target_pairs={{0,8},{1,9},{2,10},{3,11},{4,12},{5,13},{6,14},{7,15},{8,0},{9,1},... | collective-permute-start | bytes 1548296 | tf_op jit(solution)/shard_map/ppermute | solution.py:43
  27.0 22.2 %collective-permute-start.3 = (bf16[4,56,1152]{2,1,0:T(8,128)(2,1)S(1)}, bf16[4,56,1152]{2,1,0:T(8,128)(2,1)}, u32[]{:S(2)}, u32[]{:S(2)}) collective-permute-start(bf16[4,56,1152]{2,1,0:T(8,128)(2,1)S(1)} %shard_map.96), channel_id=1, source_target_pairs={{0,12},{1,13},{2,14},{3,15},{4,0},{5,1},{6,2},{7,3},{8,4},{9,5},{1... | collective-permute-start | bytes 1548296 | tf_op jit(solution)/shard_map/ppermute | solution.py:43
  28.2 1.3 copy-start.4
  29.6 1.0 copy-start.6
  30.6 1.0 copy-start.7
  34.5 0.9 copy-start.14
  55.7 7.7 %collective-permute-start.8 = (bf16[96,256]{1,0:T(8,128)(2,1)S(1)}, bf16[96,256]{1,0:T(8,128)(2,1)S(1)}, u32[]{:S(2)}, u32[]{:S(2)}) collective-permute-start(bf16[96,256]{1,0:T(8,128)(2,1)S(1)} %get-tuple-element.64._.refs_0_), channel_id=1, source_target_pairs={{0,48},{16,32},{32,16},{48,0},{64,112},{80,96},{96,80},{112,64},{1... | collective-permute-start | bytes 147464 | tf_op jit(solution)/shard_map/ppermute | solution.py:560
  59.6 3.7 %collective-permute-start.7 = (bf16[96,256]{1,0:T(8,128)(2,1)S(1)}, bf16[96,256]{1,0:T(8,128)(2,1)S(1)}, u32[]{:S(2)}, u32[]{:S(2)}) collective-permute-start(bf16[96,256]{1,0:T(8,128)(2,1)S(1)} %get-tuple-element.64._.refs_0_), channel_id=1, source_target_pairs={{0,32},{16,48},{32,0},{48,16},{64,96},{80,112},{96,64},{112,80},{1... | collective-permute-start | bytes 147464 | tf_op jit(solution)/shard_map/ppermute | solution.py:560
  59.6 3.7 %collective-permute-start.6 = (bf16[96,256]{1,0:T(8,128)(2,1)S(1)}, bf16[96,256]{1,0:T(8,128)(2,1)S(1)}, u32[]{:S(2)}, u32[]{:S(2)}) collective-permute-start(bf16[96,256]{1,0:T(8,128)(2,1)S(1)} %get-tuple-element.64._.refs_0_), channel_id=1, source_target_pairs={{0,16},{16,0},{32,48},{48,32},{64,80},{80,64},{96,112},{112,96},{1... | collective-permute-start | bytes 147464 | tf_op jit(solution)/shard_map/ppermute | solution.py:560
  60.1 10.4 %copy-start.15 = (bf16[896,512]{1,0:T(8,128)(2,1)S(1)}, bf16[896,512]{1,0:T(8,128)(2,1)}, u32[]{:S(2)}) copy-start(bf16[896,512]{1,0:T(8,128)(2,1)} %copy-done.14) | copy-start | bytes 2752516
  63.3 11.8 %copy-start = (f32[256,896]{1,0:T(8,128)}, f32[256,896]{1,0:T(8,128)S(1)}, u32[]{:S(2)}) copy-start(f32[256,896]{1,0:T(8,128)S(1)} %get-tuple-element.74.m1_ref) | copy-start | bytes 2752516
  63.3 11.8 %copy-start.2 = (f32[256,896]{1,0:T(8,128)}, f32[256,896]{1,0:T(8,128)S(1)}, u32[]{:S(2)}) copy-start(f32[256,896]{1,0:T(8,128)S(1)} %get-tuple-element.75.m2_ref) | copy-start | bytes 2752516
  63.4 9.5 %collective-permute-start.14 = (bf16[96,256]{1,0:T(8,128)(2,1)S(1)}, bf16[96,256]{1,0:T(8,128)(2,1)S(1)}, u32[]{:S(2)}, u32[]{:S(2)}) collective-permute-start(bf16[96,256]{1,0:T(8,128)(2,1)S(1)} %shard_map.99._.refs_0_), channel_id=1, source_target_pairs={{0,160},{16,176},{32,128},{48,144},{64,224},{80,240},{96,192},{112... | collective-permute-start | bytes 147464 | tf_op jit(solution)/shard_map/ppermute | solution.py:564
  69.3 5.1 %collective-permute-start.13 = (bf16[96,256]{1,0:T(8,128)(2,1)S(1)}, bf16[96,256]{1,0:T(8,128)(2,1)S(1)}, u32[]{:S(2)}, u32[]{:S(2)}) collective-permute-start(bf16[96,256]{1,0:T(8,128)(2,1)S(1)} %shard_map.99._.refs_0_), channel_id=1, source_target_pairs={{0,192},{16,208},{32,224},{48,240},{64,128},{80,144},{96,160},{112... | collective-permute-start | bytes 147464 | tf_op jit(solution)/shard_map/ppermute | solution.py:564
  69.6 4.8 %collective-permute-start.12 = (bf16[96,256]{1,0:T(8,128)(2,1)S(1)}, bf16[96,256]{1,0:T(8,128)(2,1)S(1)}, u32[]{:S(2)}, u32[]{:S(2)}) collective-permute-start(bf16[96,256]{1,0:T(8,128)(2,1)S(1)} %shard_map.99._.refs_0_), channel_id=1, source_target_pairs={{0,64},{16,80},{32,96},{48,112},{64,0},{80,16},{96,32},{112,48},{1... | collective-permute-start | bytes 147464 | tf_op jit(solution)/shard_map/ppermute | solution.py:564
  72.9 2.2 %copy-start.8 = (bf16[224,1024]{1,0:T(8,128)(2,1)}, bf16[224,1024]{1,0:T(8,128)(2,1)S(1)}, u32[]{:S(2)}) copy-start(bf16[224,1024]{1,0:T(8,128)(2,1)S(1)} %get-tuple-element.68) | copy-start | bytes 1376260
  75.2 3.5 %collective-permute-start.15 = (f32[384,128]{1,0:T(8,128)S(1)}, f32[384,128]{1,0:T(8,128)S(1)}, u32[]{:S(2)}, u32[]{:S(2)}) collective-permute-start(f32[384,128]{1,0:T(8,128)S(1)} %get-tuple-element.77), channel_id=1, source_target_pairs={{0,16},{16,0},{32,48},{48,32},{64,80},{80,64},{96,112},{112,96},{1... | collective-permute-start | bytes 589832 | tf_op jit(solution)/shard_map/ppermute | solution.py:490
  79.5 16.0 %all-to-all-start.2 = ((f32[16,48,128]{2,1,0:T(8,128)}), f32[16,48,128]{2,1,0:T(8,128)S(1)}, u32[]{:S(2)}, u32[]{:S(2)}) async-start(f32[16,48,128]{2,1,0:T(8,128)} %pad_maximum_fusion), calls=%async_computation.2 | async-start | bytes 786432 | tf_op jit(solution)/shard_map/all_to_all | solution.py:570
  86.0 28.0 %collective-permute-start.9 = (bf16[224,1024]{1,0:T(8,128)(2,1)}, bf16[224,1024]{1,0:T(8,128)(2,1)}, u32[]{:S(2)}, u32[]{:S(2)}) collective-permute-start(bf16[224,1024]{1,0:T(8,128)(2,1)} %get-tuple-element.69), channel_id=1, source_target_pairs={{0,4},{1,5},{2,6},{3,7},{4,8},{5,9},{6,10},{7,11},{8,12},{9,13},{1... | collective-permute-start | bytes 1376264 | tf_op jit(solution)/shard_map/ppermute | solution.py:117
  87.4 26.7 %collective-permute-start.10 = (bf16[224,1024]{1,0:T(8,128)(2,1)}, bf16[224,1024]{1,0:T(8,128)(2,1)}, u32[]{:S(2)}, u32[]{:S(2)}) collective-permute-start(bf16[224,1024]{1,0:T(8,128)(2,1)} %get-tuple-element.70), channel_id=1, source_target_pairs={{0,12},{1,13},{2,14},{3,15},{4,0},{5,1},{6,2},{7,3},{8,4},{9,5},{1... | collective-permute-start | bytes 1376264 | tf_op jit(solution)/shard_map/ppermute | solution.py:117
  88.8 25.3 %collective-permute-start.11 = (bf16[224,1024]{1,0:T(8,128)(2,1)}, bf16[224,1024]{1,0:T(8,128)(2,1)}, u32[]{:S(2)}, u32[]{:S(2)}) collective-permute-start(bf16[224,1024]{1,0:T(8,128)(2,1)} %get-tuple-element.71), channel_id=1, source_target_pairs={{0,8},{1,9},{2,10},{3,11},{4,12},{5,13},{6,14},{7,15},{8,0},{9,1},... | collective-permute-start | bytes 1376264 | tf_op jit(solution)/shard_map/ppermute | solution.py:117
  96.8 12.3 %all-to-all-start.3 = ((f32[8,24,128]{2,1,0:T(8,128)}), f32[8,24,128]{2,1,0:T(8,128)S(1)}, u32[]{:S(2)}, u32[]{:S(2)}) async-start(f32[8,24,128]{2,1,0:T(8,128)} %broadcast_in_dim.10), calls=%async_computation.3 | async-start | bytes 196608 | tf_op jit(solution)/shard_map/all_to_all | solution.py:35
  101.5 12.6 %copy-start.11 = (f32[24,128]{1,0:T(8,128)S(1)}, f32[24,128]{1,0:T(8,128)}, u32[]{:S(2)}) copy-start(f32[24,128]{1,0:T(8,128)} %get-tuple-element.90._.gram_ref) | copy-start | bytes 36868
  105.7 25.4 %copy-start.1 = (f32[256,896]{1,0:T(8,128)S(1)}, f32[256,896]{1,0:T(8,128)}, u32[]{:S(2)}) copy-start(f32[256,896]{1,0:T(8,128)} %copy-done) | copy-start | bytes 2752516
  105.7 25.4 %copy-start.3 = (f32[256,896]{1,0:T(8,128)S(1)}, f32[256,896]{1,0:T(8,128)}, u32[]{:S(2)}) copy-start(f32[256,896]{1,0:T(8,128)} %copy-done.2) | copy-start | bytes 2752516
  109.1 0.7 copy-start.13
  110.5 15.3 %all-to-all-start.4 = ((f32[16,24,128]{2,1,0:T(8,128)}), f32[16,24,128]{2,1,0:T(8,128)S(1)}, u32[]{:S(2)}, u32[]{:S(2)}) async-start(f32[16,24,128]{2,1,0:T(8,128)} %broadcast_in_dim.11), calls=%async_computation.4 | async-start | bytes 393216 | tf_op jit(solution)/shard_map/all_to_all | solution.py:35
  114.1 1.0 copy-start.9
  115.1 15.9 %copy-start.12 = (f32[3,32,32]{2,1,0:T(8,128)S(1)}, f32[3,32,32]{2,1,0:T(8,128)}, u32[]{:S(2)}) copy-start(f32[3,32,32]{2,1,0:T(8,128)} %get-tuple-element.86.inverse_ref) | copy-start | bytes 36868
  116.7 6.1 %collective-permute-start.16 = (bf16[56,1024]{1,0:T(8,128)(2,1)S(1)}, bf16[56,1024]{1,0:T(8,128)(2,1)S(1)}, u32[]{:S(2)}, u32[]{:S(2)}) collective-permute-start(bf16[56,1024]{1,0:T(8,128)(2,1)S(1)} %get-tuple-element.80), channel_id=1, source_target_pairs={{0,1},{1,2},{2,3},{3,0},{4,5},{5,6},{6,7},{7,4},{8,9},{9,10},{10,1... | collective-permute-start | bytes 344072 | tf_op jit(solution)/shard_map/ppermute | solution.py:137
  118.0 4.8 %collective-permute-start.17 = (bf16[56,1024]{1,0:T(8,128)(2,1)S(1)}, bf16[56,1024]{1,0:T(8,128)(2,1)S(1)}, u32[]{:S(2)}, u32[]{:S(2)}) collective-permute-start(bf16[56,1024]{1,0:T(8,128)(2,1)S(1)} %get-tuple-element.81), channel_id=1, source_target_pairs={{0,3},{1,0},{2,1},{3,2},{4,7},{5,4},{6,5},{7,6},{8,11},{9,8},{10,9... | collective-permute-start | bytes 344072 | tf_op jit(solution)/shard_map/ppermute | solution.py:137
  119.4 5.7 %collective-permute-start.18 = (bf16[56,1024]{1,0:T(8,128)(2,1)S(1)}, bf16[56,1024]{1,0:T(8,128)(2,1)S(1)}, u32[]{:S(2)}, u32[]{:S(2)}) collective-permute-start(bf16[56,1024]{1,0:T(8,128)(2,1)S(1)} %get-tuple-element.82), channel_id=1, source_target_pairs={{0,2},{1,3},{2,0},{3,1},{4,6},{5,7},{6,4},{7,5},{8,10},{9,11},{10,... | collective-permute-start | bytes 344072 | tf_op jit(solution)/shard_map/ppermute | solution.py:137
  125.8 5.2 %collective-permute-start.19 = (f32[384,128]{1,0:T(8,128)S(1)}, f32[384,128]{1,0:T(8,128)S(1)}, u32[]{:S(2)}, u32[]{:S(2)}) collective-permute-start(f32[384,128]{1,0:T(8,128)S(1)} %shard_map.107.s_mine_ref), channel_id=1, source_target_pairs={{0,16},{16,0},{32,48},{48,32},{64,80},{80,64},{96,112},{112,96},{1... | collective-permute-start | bytes 589832 | tf_op jit(solution)/shard_map/ppermute | solution.py:490

commit v8 on v7

--- a/solution.py
+++ b/solution.py
@@ -242,7 +242,7 @@
         gate_sig = jax.nn.sigmoid(gate_pre)
         gate_act = gate_pre * gate_sig
         hidden = (gate_act * up_pre).astype(BF)
-        gate_grad = (hidden_grad * up_pre * gate_sig * (1.0 + gate_pre * (1.0 - gate_sig))).astype(BF)
+        gate_grad = (hidden_grad * up_pre * gate_sig * (1.0 + gate_pre - gate_act)).astype(BF)
         up_grad = (hidden_grad * gate_act).astype(BF)
         gate_grad_ref[:, span] = gate_grad
         up_grad_ref[:, span] = up_grad

time: 135 us -> 135 us (level)
  no operation moved by 1% of the time
where the time goes in v8:
time: 135 us; the launch traced here: 134 us
  starting transfers between devices  59.5 us (44%)
  waiting for transfers between devices  34.5 us (26%)
  Pallas kernels  27.9 us (21%)
  local copies, waits for them, and re-layouts  10.4 us (8%)
    ppermute x6, waiting for transfers between devices, ring_pieces(): near[k] = lax.ppermute(value, 'tensor', ring(SIDE - k))  18.2 us
    all_to_all x3, starting transfers between devices, spread(): lax.all_to_all(jnp.broadcast_to(value[None], (size,) + value.shape), axis...  11.9 us
    ppermute x6, starting transfers between devices, ring_pieces(): near[k] = lax.ppermute(value, 'tensor', ring(SIDE - k))  9.36 us
    ppermute x3, starting transfers between devices, per_device(): others = [lax.ppermute(p_pair, 'dp', dp_swap(bits)) for bits in (4, 12, 10)]  7.07 us
    unnamed x32, local copies, waits for them, and re-layouts  6.92 us
    ppermute x2, starting transfers between devices, swap_core(): return lax.ppermute(value, 'dp', CORE_PAIR)  6.6 us
    all_to_all x1, starting transfers between devices, per_device(): lax.all_to_all(jnp.concatenate([s_pair, gram], axis=1), 'tensor', 0, 0, t...  6.47 us
    pallas_call x1, Pallas kernels, backward(): pl.pallas_call(backward_kernel, out_shape=(grads, grads, grads, jax.Shape...  6.37 us
  transfers between devices with their start and end apart: 25, of which 12 were waited for; matrix products, arithmetic and copies ran while one was open for 2% of the time, Pallas kernels for 11%

profile of v8, /device:TPU:1, one launch (start us, length us, event | category | flops | bytes accessed | tf_op | source)
XLA Modules:
  0.0 134.4 jit_solution(14583315437598088213)
XLA Ops:
  0.6 2.0 %shard_map.95 = (bf16[56,1152]{1,0:T(8,128)(2,1)}, bf16[4,56,1152]{2,1,0:T(8,128)(2,1)}) custom-call(bf16[56,1024]{1,0:T(8,128)(2,1)} %bitcast.27, bf16[56,1024]{1,0:T(8,128)(2,1)} %bitcast.28, f32[96,56]{1,0:T(8,128)} %bitcast.29), custom_call_target="tpu_custom_call" | custom-call | tf_op jit(solution)/shard_map/pallas_call | solution.py:70
  2.7 5.0 %all-to-all-start = ((bf16[4,56,1152]{2,1,0:T(8,128)(2,1)}), bf16[4,56,1152]{2,1,0:T(8,128)(2,1)S(1)}, u32[]{:S(2)}, u32[]{:S(2)}) async-start(bf16[4,56,1152]{2,1,0:T(8,128)(2,1)} %get-tuple-element.48), calls=%async_computation | async-start | bytes 1032192 | tf_op jit(solution)/shard_map/all_to_all | solution.py:108
  7.7 1.2 collective-permute-start.2
  8.9 2.5 %collective-permute-start.1 = (bf16[56,1152]{1,0:T(8,128)(2,1)}, bf16[56,1152]{1,0:T(8,128)(2,1)S(1)}, u32[]{:S(2)}, u32[]{:S(2)}) collective-permute-start(bf16[56,1152]{1,0:T(8,128)(2,1)} %get-tuple-element.49.p0_ref), channel_id=1, source_target_pairs={{0,2},{1,3},{2,0},{3,1},{4,6},{5,7},{6,4},{7,5},{8,10},{9,11},{10,... | collective-permute-start | bytes 387080 | tf_op jit(solution)/shard_map/ppermute | solution.py:43
  11.4 1.2 collective-permute-start
  12.5 0.4 collective-permute-done.2.p3_ref
  12.9 4.0 %collective-permute-done.1.p2_ref = bf16[56,1152]{1,0:T(8,128)(2,1)S(1)} collective-permute-done((bf16[56,1152]{1,0:T(8,128)(2,1)}, bf16[56,1152]{1,0:T(8,128)(2,1)S(1)}, u32[]{:S(2)}, u32[]{:S(2)}) %collective-permute-start.1) | collective-permute-done | bytes 129056 | tf_op jit(solution)/shard_map/ppermute | solution.py:43
  16.9 0.0 collective-permute-done.p1_ref
  16.9 0.9 copy-done.10
  17.8 0.7 shard_map.96
  18.4 1.5 %broadcast_in_dim.8 = bf16[4,4,56,1152]{3,2,1,0:T(8,128)(2,1)} broadcast(bf16[4,56,1152]{2,1,0:T(8,128)(2,1)S(1)} %all-to-all-done), dimensions={1,2,3} | broadcast | bytes 2580480 | tf_op jit(solution)/shard_map/broadcast_in_dim | solution.py:36
  19.9 3.7 %all-to-all-start.1 = ((bf16[4,4,56,1152]{3,2,1,0:T(8,128)(2,1)}), bf16[4,4,56,1152]{3,2,1,0:T(8,128)(2,1)S(1)}, u32[]{:S(2)}, u32[]{:S(2)}) async-start(bf16[4,4,56,1152]{3,2,1,0:T(8,128)(2,1)} %broadcast_in_dim.8), calls=%async_computation.1 | async-start | bytes 4128768 | tf_op jit(solution)/shard_map/all_to_all | solution.py:35
  23.7 1.0 collective-permute-start.5
  24.7 2.4 %collective-permute-start.4 = (bf16[4,56,1152]{2,1,0:T(8,128)(2,1)S(1)}, bf16[4,56,1152]{2,1,0:T(8,128)(2,1)}, u32[]{:S(2)}, u32[]{:S(2)}) collective-permute-start(bf16[4,56,1152]{2,1,0:T(8,128)(2,1)S(1)} %shard_map.96), channel_id=1, source_target_pairs={{0,8},{1,9},{2,10},{3,11},{4,12},{5,13},{6,14},{7,15},{8,0},{9,1},... | collective-permute-start | bytes 1548296 | tf_op jit(solution)/shard_map/ppermute | solution.py:43
  27.0 1.2 collective-permute-start.3
  28.2 1.3 copy-done.4
  29.6 1.0 copy-done.6
  30.6 1.0 copy-done.7
  31.6 2.8 %shard_map.94 = (bf16[112,256,896]{2,1,0:T(8,128)(2,1)}, bf16[896,512]{1,0:T(8,128)(2,1)S(1)}, f32[8,128]{1,0:T(8,128)}) custom-call(bf16[256,896]{1,0:T(8,128)(2,1)S(1)} %copy-done.5, bf16[256,896]{1,0:T(8,128)(2,1)S(1)} %copy-done.6, bf16[256,896]{1,0:T(8,128)(2,1)S(1)} %copy-done.7, bf16[1,3,256,896]{3,2,1,0:T(8,128)(2,1)S(1)} %copy-done.4), custom_call_target="tpu_custom_call" | custom-call | tf_op jit(solution)/shard_map/pallas_call | solution.py:191
  34.5 0.0 copy-start.14
  34.5 0.9 copy-done.14
  35.4 0.1 pad_add_fusion.place_ref
  35.5 0.6 collective-permute-done.5
  36.0 11.2 %collective-permute-done.4 = bf16[4,56,1152]{2,1,0:T(8,128)(2,1)} collective-permute-done((bf16[4,56,1152]{2,1,0:T(8,128)(2,1)S(1)}, bf16[4,56,1152]{2,1,0:T(8,128)(2,1)}, u32[]{:S(2)}, u32[]{:S(2)}) %collective-permute-start.4) | collective-permute-done | bytes 516128 | tf_op jit(solution)/shard_map/ppermute | solution.py:43
  47.2 2.0 %collective-permute-done.3 = bf16[4,56,1152]{2,1,0:T(8,128)(2,1)} collective-permute-done((bf16[4,56,1152]{2,1,0:T(8,128)(2,1)S(1)}, bf16[4,56,1152]{2,1,0:T(8,128)(2,1)}, u32[]{:S(2)}, u32[]{:S(2)}) %collective-permute-start.3) | collective-permute-done | bytes 516128 | tf_op jit(solution)/shard_map/ppermute | solution.py:43
  49.3 6.4 %shard_map.97 = (bf16[256,1024]{1,0:T(8,128)(2,1)S(1)}, bf16[256,1024]{1,0:T(8,128)(2,1)S(1)}, bf16[256,1024]{1,0:T(8,128)(2,1)S(1)}, bf16[96,256]{1,0:T(8,128)(2,1)S(1)}, bf16[896,1152]{1,0:T(8,128)(2,1)S(1)}) custom-call(s32[2]{0:T(128)S(1)} %pad_add_fusion.place_ref, bf16[224,1152]{1,0:T(8,128)(2,1)S(1)} %bitcast.22, bf16[224,1152]{1,0:T(8,128)(2,1)} %bitcast.7.p1_ref, ...), custom_call_target="tpu_custom_call" | custom-call | flops 1409286144 | bytes 8388608 | tf_op jit(solution)/shard_map/pallas_call | solution.py:269
  55.6 4.0 %collective-permute-start.8 = (bf16[96,256]{1,0:T(8,128)(2,1)S(1)}, bf16[96,256]{1,0:T(8,128)(2,1)S(1)}, u32[]{:S(2)}, u32[]{:S(2)}) collective-permute-start(bf16[96,256]{1,0:T(8,128)(2,1)S(1)} %get-tuple-element.64._.refs_0_), channel_id=1, source_target_pairs={{0,48},{16,32},{32,16},{48,0},{64,112},{80,96},{96,80},{112,64},{1... | collective-permute-start | bytes 147464 | tf_op jit(solution)/shard_map/ppermute | solution.py:560
  59.6 0.5 collective-permute-start.6
  60.1 3.2 %shard_map.98 = (f32[256,896]{1,0:T(8,128)S(1)}, f32[256,896]{1,0:T(8,128)S(1)}, f32[256,896]{1,0:T(8,128)S(1)}, f32[8,128]{1,0:T(8,128)S(1)}) custom-call(bf16[256,1024]{1,0:T(8,128)(2,1)S(1)} %get-tuple-element.62.gate_grad_ref, bf16[256,1024]{1,0:T(8,128)(2,1)S(1)} %get-tuple-element.63.up_grad_ref, bf16[256,1024]{1,0:T(8,128)(2,1)S(1)} %get-tuple-element.65.hidden_ref, ...), custom_call_target="tpu_custom_call" | custom-call | flops 1409286144 | bytes 9437184 | tf_op jit(solution)/shard_map/pallas_call | solution.py:339
  63.4 5.9 %collective-permute-start.14 = (bf16[96,256]{1,0:T(8,128)(2,1)S(1)}, bf16[96,256]{1,0:T(8,128)(2,1)S(1)}, u32[]{:S(2)}, u32[]{:S(2)}) collective-permute-start(bf16[96,256]{1,0:T(8,128)(2,1)S(1)} %shard_map.99._.refs_0_), channel_id=1, source_target_pairs={{0,160},{16,176},{32,128},{48,144},{64,224},{80,240},{96,192},{112... | collective-permute-start | bytes 147464 | tf_op jit(solution)/shard_map/ppermute | solution.py:564
  69.3 0.3 collective-permute-start.13
  69.6 0.9 collective-permute-start.12
  70.5 2.4 %shard_map.100 = (bf16[224,1024]{1,0:T(8,128)(2,1)S(1)}, bf16[224,1024]{1,0:T(8,128)(2,1)}, bf16[224,1024]{1,0:T(8,128)(2,1)}, bf16[224,1024]{1,0:T(8,128)(2,1)}, f32[8,128]{1,0:T(8,128)S(1)}) custom-call(s32[2]{0:T(128)S(1)} %pad_add_fusion.place_ref, bf16[896,512]{1,0:T(8,128)(2,1)S(1)} %copy-done.15, ...), custom_call_target="tpu_custom_call" | custom-call | flops 939524096 | bytes 4194304 | tf_op jit(solution)/shard_map/pallas_call | solution.py:303
  72.9 1.5 %collective-permute-done.13.refs_2_ = bf16[96,256]{1,0:T(8,128)(2,1)S(1)} collective-permute-done((bf16[96,256]{1,0:T(8,128)(2,1)S(1)}, bf16[96,256]{1,0:T(8,128)(2,1)S(1)}, u32[]{:S(2)}, u32[]{:S(2)}) %collective-permute-start.13) | collective-permute-done | bytes 49184 | tf_op jit(solution)/shard_map/ppermute | solution.py:564
  74.4 0.7 shard_map.102
  75.1 0.0 copy-done.2
  75.1 2.5 %collective-permute-start.15 = (f32[384,128]{1,0:T(8,128)S(1)}, f32[384,128]{1,0:T(8,128)S(1)}, u32[]{:S(2)}, u32[]{:S(2)}) collective-permute-start(f32[384,128]{1,0:T(8,128)S(1)} %get-tuple-element.77), channel_id=1, source_target_pairs={{0,16},{16,0},{32,48},{48,32},{64,80},{80,64},{96,112},{112,96},{1... | collective-permute-start | bytes 589832 | tf_op jit(solution)/shard_map/ppermute | solution.py:490
  77.6 1.1 collective-permute-done.15
  78.7 0.8 pad_maximum_fusion
  79.5 6.5 %all-to-all-start.2 = ((f32[16,48,128]{2,1,0:T(8,128)}), f32[16,48,128]{2,1,0:T(8,128)S(1)}, u32[]{:S(2)}, u32[]{:S(2)}) async-start(f32[16,48,128]{2,1,0:T(8,128)} %pad_maximum_fusion), calls=%async_computation.2 | async-start | bytes 786432 | tf_op jit(solution)/shard_map/all_to_all | solution.py:570
  86.0 1.4 %collective-permute-start.9 = (bf16[224,1024]{1,0:T(8,128)(2,1)}, bf16[224,1024]{1,0:T(8,128)(2,1)}, u32[]{:S(2)}, u32[]{:S(2)}) collective-permute-start(bf16[224,1024]{1,0:T(8,128)(2,1)} %get-tuple-element.69), channel_id=1, source_target_pairs={{0,4},{1,5},{2,6},{3,7},{4,8},{5,9},{6,10},{7,11},{8,12},{9,13},{1... | collective-permute-start | bytes 1376264 | tf_op jit(solution)/shard_map/ppermute | solution.py:117
  87.4 1.4 %collective-permute-start.10 = (bf16[224,1024]{1,0:T(8,128)(2,1)}, bf16[224,1024]{1,0:T(8,128)(2,1)}, u32[]{:S(2)}, u32[]{:S(2)}) collective-permute-start(bf16[224,1024]{1,0:T(8,128)(2,1)} %get-tuple-element.70), channel_id=1, source_target_pairs={{0,12},{1,13},{2,14},{3,15},{4,0},{5,1},{6,2},{7,3},{8,4},{9,5},{1... | collective-permute-start | bytes 1376264 | tf_op jit(solution)/shard_map/ppermute | solution.py:117
  88.8 1.6 %collective-permute-start.11 = (bf16[224,1024]{1,0:T(8,128)(2,1)}, bf16[224,1024]{1,0:T(8,128)(2,1)}, u32[]{:S(2)}, u32[]{:S(2)}) collective-permute-start(bf16[224,1024]{1,0:T(8,128)(2,1)} %get-tuple-element.71), channel_id=1, source_target_pairs={{0,8},{1,9},{2,10},{3,11},{4,12},{5,13},{6,14},{7,15},{8,0},{9,1},... | collective-permute-start | bytes 1376264 | tf_op jit(solution)/shard_map/ppermute | solution.py:117
  90.4 5.2 %all-to-all-done.2 = f32[16,48,128]{2,1,0:T(8,128)S(1)} async-done(((f32[16,48,128]{2,1,0:T(8,128)}), f32[16,48,128]{2,1,0:T(8,128)S(1)}, u32[]{:S(2)}, u32[]{:S(2)}) %all-to-all-start.2) | async-done | bytes 393248 | tf_op jit(solution)/shard_map/all_to_all | solution.py:570
  95.6 0.6 fusion
  96.2 0.6 broadcast_in_dim.10
  96.8 4.6 %all-to-all-start.3 = ((f32[8,24,128]{2,1,0:T(8,128)}), f32[8,24,128]{2,1,0:T(8,128)S(1)}, u32[]{:S(2)}, u32[]{:S(2)}) async-start(f32[8,24,128]{2,1,0:T(8,128)} %broadcast_in_dim.10), calls=%async_computation.3 | async-start | bytes 196608 | tf_op jit(solution)/shard_map/all_to_all | solution.py:35
  101.5 4.2 %shard_map.105 = (f32[3,32,32]{2,1,0:T(8,128)}, f32[8,128]{1,0:T(8,128)}) custom-call(f32[24,128]{1,0:T(8,128)} %get-tuple-element.90._.gram_ref), custom_call_target="tpu_custom_call" | custom-call | flops 4294967296 | bytes 1048576 | tf_op jit(solution)/shard_map/pallas_call | solution.py:430
  105.6 3.5 %all-to-all-done.3.value_ref = f32[8,24,128]{2,1,0:T(8,128)S(1)} async-done(((f32[8,24,128]{2,1,0:T(8,128)}), f32[8,24,128]{2,1,0:T(8,128)S(1)}, u32[]{:S(2)}, u32[]{:S(2)}) %all-to-all-start.3) | async-done | bytes 98336 | tf_op jit(solution)/shard_map/all_to_all | solution.py:35
  109.1 0.7 copy-done.13
  109.8 0.7 broadcast_in_dim.11
  110.5 3.5 %all-to-all-start.4 = ((f32[16,24,128]{2,1,0:T(8,128)}), f32[16,24,128]{2,1,0:T(8,128)S(1)}, u32[]{:S(2)}, u32[]{:S(2)}) async-start(f32[16,24,128]{2,1,0:T(8,128)} %broadcast_in_dim.11), calls=%async_computation.4 | async-start | bytes 393216 | tf_op jit(solution)/shard_map/all_to_all | solution.py:35
  114.1 1.0 copy-done.9
  115.1 1.5 %shard_map.103 = (bf16[56,1024]{1,0:T(8,128)(2,1)S(1)}, bf16[56,1024]{1,0:T(8,128)(2,1)S(1)}, bf16[56,1024]{1,0:T(8,128)(2,1)S(1)}, bf16[56,1024]{1,0:T(8,128)(2,1)S(1)}) custom-call(s32[1]{0:T(128)} %bitcast.place_ref, bf16[4,56,1024]{2,1,0:T(8,128)(2,1)S(1)} %bitcast.25, bf16[4,56,1024]{2,1,0:T(8,128)(2,1)} %bitcast.12.g1_ref, ...), custom_call_target="tpu_custom_call" | custom-call | tf_op jit(solution)/shard_map/pallas_call | solution.py:130
  116.6 1.3 collective-permute-start.16
  118.0 1.4 %collective-permute-start.17 = (bf16[56,1024]{1,0:T(8,128)(2,1)S(1)}, bf16[56,1024]{1,0:T(8,128)(2,1)S(1)}, u32[]{:S(2)}, u32[]{:S(2)}) collective-permute-start(bf16[56,1024]{1,0:T(8,128)(2,1)S(1)} %get-tuple-element.81), channel_id=1, source_target_pairs={{0,3},{1,0},{2,1},{3,2},{4,7},{5,4},{6,5},{7,6},{8,11},{9,8},{10,9... | collective-permute-start | bytes 344072 | tf_op jit(solution)/shard_map/ppermute | solution.py:137
  119.4 1.5 %collective-permute-start.18 = (bf16[56,1024]{1,0:T(8,128)(2,1)S(1)}, bf16[56,1024]{1,0:T(8,128)(2,1)S(1)}, u32[]{:S(2)}, u32[]{:S(2)}) collective-permute-start(bf16[56,1024]{1,0:T(8,128)(2,1)S(1)} %get-tuple-element.82), channel_id=1, source_target_pairs={{0,2},{1,3},{2,0},{3,1},{4,6},{5,7},{6,4},{7,5},{8,10},{9,11},{10,... | collective-permute-start | bytes 344072 | tf_op jit(solution)/shard_map/ppermute | solution.py:137
  120.9 1.8 %collective-permute-done.16.refs_1_ = bf16[56,1024]{1,0:T(8,128)(2,1)S(1)} collective-permute-done((bf16[56,1024]{1,0:T(8,128)(2,1)S(1)}, bf16[56,1024]{1,0:T(8,128)(2,1)S(1)}, u32[]{:S(2)}, u32[]{:S(2)}) %collective-permute-start.16) | collective-permute-done | bytes 114720 | tf_op jit(solution)/shard_map/ppermute | solution.py:137
  122.8 2.3 %collective-permute-done.18.refs_3_ = bf16[56,1024]{1,0:T(8,128)(2,1)S(1)} collective-permute-done((bf16[56,1024]{1,0:T(8,128)(2,1)S(1)}, bf16[56,1024]{1,0:T(8,128)(2,1)S(1)}, u32[]{:S(2)}, u32[]{:S(2)}) %collective-permute-start.18) | collective-permute-done | bytes 114720 | tf_op jit(solution)/shard_map/ppermute | solution.py:137
  125.1 0.7 shard_map.104
  125.8 4.1 %collective-permute-start.19 = (f32[384,128]{1,0:T(8,128)S(1)}, f32[384,128]{1,0:T(8,128)S(1)}, u32[]{:S(2)}, u32[]{:S(2)}) collective-permute-start(f32[384,128]{1,0:T(8,128)S(1)} %shard_map.107.s_mine_ref), channel_id=1, source_target_pairs={{0,16},{16,0},{32,48},{48,32},{64,80},{80,64},{96,112},{112,96},{1... | collective-permute-start | bytes 589832 | tf_op jit(solution)/shard_map/ppermute | solution.py:490
  130.0 0.1 pad_add_fusion.1.place_ref
  130.0 1.0 collective-permute-done.19.s_other_ref
  131.0 3.2 %shard_map.108 = (bf16[1,3,256,896]{3,2,1,0:T(8,128)(2,1)}, f32[96,56]{1,0:T(8,128)}) custom-call(s32[2]{0:T(128)S(1)} %pad_add_fusion.1.place_ref, f32[384,128]{1,0:T(8,128)S(1)} %shard_map.107.s_mine_ref, f32[384,128]{1,0:T(8,128)S(1)} %collective-permute-done.19.s_other_ref, f32[3,32,32]{2,1,0:T(8,128)S(1)} %copy-done.12, ...), custom_call_target="tpu_custom_call" | custom-call | tf_op jit(solution)/shard_map/pallas_call | solution.py:476
  (43 shorter events, 0.2 us)
Async XLA Ops:
  2.7 14.2 %all-to-all-start = ((bf16[4,56,1152]{2,1,0:T(8,128)(2,1)}), bf16[4,56,1152]{2,1,0:T(8,128)(2,1)S(1)}, u32[]{:S(2)}, u32[]{:S(2)}) async-start(bf16[4,56,1152]{2,1,0:T(8,128)(2,1)} %get-tuple-element.48), calls=%async_computation | async-start | bytes 1032192 | tf_op jit(solution)/shard_map/all_to_all | solution.py:108
  7.7 5.2 %collective-permute-start.2 = (bf16[56,1152]{1,0:T(8,128)(2,1)}, bf16[56,1152]{1,0:T(8,128)(2,1)S(1)}, u32[]{:S(2)}, u32[]{:S(2)}) collective-permute-start(bf16[56,1152]{1,0:T(8,128)(2,1)} %get-tuple-element.49.p0_ref), channel_id=1, source_target_pairs={{0,1},{1,2},{2,3},{3,0},{4,5},{5,6},{6,7},{7,4},{8,9},{9,10},{10,1... | collective-permute-start | bytes 387080 | tf_op jit(solution)/shard_map/ppermute | solution.py:43
  8.9 8.0 %collective-permute-start.1 = (bf16[56,1152]{1,0:T(8,128)(2,1)}, bf16[56,1152]{1,0:T(8,128)(2,1)S(1)}, u32[]{:S(2)}, u32[]{:S(2)}) collective-permute-start(bf16[56,1152]{1,0:T(8,128)(2,1)} %get-tuple-element.49.p0_ref), channel_id=1, source_target_pairs={{0,2},{1,3},{2,0},{3,1},{4,6},{5,7},{6,4},{7,5},{8,10},{9,11},{10,... | collective-permute-start | bytes 387080 | tf_op jit(solution)/shard_map/ppermute | solution.py:43
  11.4 5.5 %collective-permute-start = (bf16[56,1152]{1,0:T(8,128)(2,1)}, bf16[56,1152]{1,0:T(8,128)(2,1)S(1)}, u32[]{:S(2)}, u32[]{:S(2)}) collective-permute-start(bf16[56,1152]{1,0:T(8,128)(2,1)} %get-tuple-element.49.p0_ref), channel_id=1, source_target_pairs={{0,3},{1,0},{2,1},{3,2},{4,7},{5,4},{6,5},{7,6},{8,11},{9,8},{10,9... | collective-permute-start | bytes 387080 | tf_op jit(solution)/shard_map/ppermute | solution.py:43
  16.9 0.9 copy-start.10
  19.9 8.3 %copy-start.5 = (bf16[256,896]{1,0:T(8,128)(2,1)S(1)}, bf16[256,896]{1,0:T(8,128)(2,1)}, u32[]{:S(2)}) copy-start(bf16[256,896]{1,0:T(8,128)(2,1)} %gate_ref.1) | copy-start | bytes 1376260
  19.9 29.3 %all-to-all-start.1 = ((bf16[4,4,56,1152]{3,2,1,0:T(8,128)(2,1)}), bf16[4,4,56,1152]{3,2,1,0:T(8,128)(2,1)S(1)}, u32[]{:S(2)}, u32[]{:S(2)}) async-start(bf16[4,4,56,1152]{3,2,1,0:T(8,128)(2,1)} %broadcast_in_dim.8), calls=%async_computation.1 | async-start | bytes 4128768 | tf_op jit(solution)/shard_map/all_to_all | solution.py:35
  23.7 12.4 %collective-permute-start.5 = (bf16[4,56,1152]{2,1,0:T(8,128)(2,1)S(1)}, bf16[4,56,1152]{2,1,0:T(8,128)(2,1)S(1)}, u32[]{:S(2)}, u32[]{:S(2)}) collective-permute-start(bf16[4,56,1152]{2,1,0:T(8,128)(2,1)S(1)} %shard_map.96), channel_id=1, source_target_pairs={{0,4},{1,5},{2,6},{3,7},{4,8},{5,9},{6,10},{7,11},{8,12},{9,13},{1... | collective-permute-start | bytes 1548296 | tf_op jit(solution)/shard_map/ppermute | solution.py:43
  24.7 22.6 %collective-permute-start.4 = (bf16[4,56,1152]{2,1,0:T(8,128)(2,1)S(1)}, bf16[4,56,1152]{2,1,0:T(8,128)(2,1)}, u32[]{:S(2)}, u32[]{:S(2)}) collective-permute-start(bf16[4,56,1152]{2,1,0:T(8,128)(2,1)S(1)} %shard_map.96), channel_id=1, source_target_pairs={{0,8},{1,9},{2,10},{3,11},{4,12},{5,13},{6,14},{7,15},{8,0},{9,1},... | collective-permute-start | bytes 1548296 | tf_op jit(solution)/shard_map/ppermute | solution.py:43
  27.0 22.2 %collective-permute-start.3 = (bf16[4,56,1152]{2,1,0:T(8,128)(2,1)S(1)}, bf16[4,56,1152]{2,1,0:T(8,128)(2,1)}, u32[]{:S(2)}, u32[]{:S(2)}) collective-permute-start(bf16[4,56,1152]{2,1,0:T(8,128)(2,1)S(1)} %shard_map.96), channel_id=1, source_target_pairs={{0,12},{1,13},{2,14},{3,15},{4,0},{5,1},{6,2},{7,3},{8,4},{9,5},{1... | collective-permute-start | bytes 1548296 | tf_op jit(solution)/shard_map/ppermute | solution.py:43
  28.2 1.3 copy-start.4
  29.6 1.0 copy-start.6
  30.6 1.0 copy-start.7
  34.5 0.9 copy-start.14
  55.6 7.7 %collective-permute-start.8 = (bf16[96,256]{1,0:T(8,128)(2,1)S(1)}, bf16[96,256]{1,0:T(8,128)(2,1)S(1)}, u32[]{:S(2)}, u32[]{:S(2)}) collective-permute-start(bf16[96,256]{1,0:T(8,128)(2,1)S(1)} %get-tuple-element.64._.refs_0_), channel_id=1, source_target_pairs={{0,48},{16,32},{32,16},{48,0},{64,112},{80,96},{96,80},{112,64},{1... | collective-permute-start | bytes 147464 | tf_op jit(solution)/shard_map/ppermute | solution.py:560
  59.6 3.7 %collective-permute-start.7 = (bf16[96,256]{1,0:T(8,128)(2,1)S(1)}, bf16[96,256]{1,0:T(8,128)(2,1)S(1)}, u32[]{:S(2)}, u32[]{:S(2)}) collective-permute-start(bf16[96,256]{1,0:T(8,128)(2,1)S(1)} %get-tuple-element.64._.refs_0_), channel_id=1, source_target_pairs={{0,32},{16,48},{32,0},{48,16},{64,96},{80,112},{96,64},{112,80},{1... | collective-permute-start | bytes 147464 | tf_op jit(solution)/shard_map/ppermute | solution.py:560
  59.6 3.7 %collective-permute-start.6 = (bf16[96,256]{1,0:T(8,128)(2,1)S(1)}, bf16[96,256]{1,0:T(8,128)(2,1)S(1)}, u32[]{:S(2)}, u32[]{:S(2)}) collective-permute-start(bf16[96,256]{1,0:T(8,128)(2,1)S(1)} %get-tuple-element.64._.refs_0_), channel_id=1, source_target_pairs={{0,16},{16,0},{32,48},{48,32},{64,80},{80,64},{96,112},{112,96},{1... | collective-permute-start | bytes 147464 | tf_op jit(solution)/shard_map/ppermute | solution.py:560
  60.1 10.4 %copy-start.15 = (bf16[896,512]{1,0:T(8,128)(2,1)S(1)}, bf16[896,512]{1,0:T(8,128)(2,1)}, u32[]{:S(2)}) copy-start(bf16[896,512]{1,0:T(8,128)(2,1)} %copy-done.14) | copy-start | bytes 2752516
  63.3 11.8 %copy-start = (f32[256,896]{1,0:T(8,128)}, f32[256,896]{1,0:T(8,128)S(1)}, u32[]{:S(2)}) copy-start(f32[256,896]{1,0:T(8,128)S(1)} %get-tuple-element.74.m1_ref) | copy-start | bytes 2752516
  63.3 11.8 %copy-start.2 = (f32[256,896]{1,0:T(8,128)}, f32[256,896]{1,0:T(8,128)S(1)}, u32[]{:S(2)}) copy-start(f32[256,896]{1,0:T(8,128)S(1)} %get-tuple-element.75.m2_ref) | copy-start | bytes 2752516
  63.4 9.5 %collective-permute-start.14 = (bf16[96,256]{1,0:T(8,128)(2,1)S(1)}, bf16[96,256]{1,0:T(8,128)(2,1)S(1)}, u32[]{:S(2)}, u32[]{:S(2)}) collective-permute-start(bf16[96,256]{1,0:T(8,128)(2,1)S(1)} %shard_map.99._.refs_0_), channel_id=1, source_target_pairs={{0,160},{16,176},{32,128},{48,144},{64,224},{80,240},{96,192},{112... | collective-permute-start | bytes 147464 | tf_op jit(solution)/shard_map/ppermute | solution.py:564
  69.3 5.1 %collective-permute-start.13 = (bf16[96,256]{1,0:T(8,128)(2,1)S(1)}, bf16[96,256]{1,0:T(8,128)(2,1)S(1)}, u32[]{:S(2)}, u32[]{:S(2)}) collective-permute-start(bf16[96,256]{1,0:T(8,128)(2,1)S(1)} %shard_map.99._.refs_0_), channel_id=1, source_target_pairs={{0,192},{16,208},{32,224},{48,240},{64,128},{80,144},{96,160},{112... | collective-permute-start | bytes 147464 | tf_op jit(solution)/shard_map/ppermute | solution.py:564
  69.6 4.8 %collective-permute-start.12 = (bf16[96,256]{1,0:T(8,128)(2,1)S(1)}, bf16[96,256]{1,0:T(8,128)(2,1)S(1)}, u32[]{:S(2)}, u32[]{:S(2)}) collective-permute-start(bf16[96,256]{1,0:T(8,128)(2,1)S(1)} %shard_map.99._.refs_0_), channel_id=1, source_target_pairs={{0,64},{16,80},{32,96},{48,112},{64,0},{80,16},{96,32},{112,48},{1... | collective-permute-start | bytes 147464 | tf_op jit(solution)/shard_map/ppermute | solution.py:564
  72.9 2.2 %copy-start.8 = (bf16[224,1024]{1,0:T(8,128)(2,1)}, bf16[224,1024]{1,0:T(8,128)(2,1)S(1)}, u32[]{:S(2)}) copy-start(bf16[224,1024]{1,0:T(8,128)(2,1)S(1)} %get-tuple-element.68) | copy-start | bytes 1376260
  75.1 3.6 %collective-permute-start.15 = (f32[384,128]{1,0:T(8,128)S(1)}, f32[384,128]{1,0:T(8,128)S(1)}, u32[]{:S(2)}, u32[]{:S(2)}) collective-permute-start(f32[384,128]{1,0:T(8,128)S(1)} %get-tuple-element.77), channel_id=1, source_target_pairs={{0,16},{16,0},{32,48},{48,32},{64,80},{80,64},{96,112},{112,96},{1... | collective-permute-start | bytes 589832 | tf_op jit(solution)/shard_map/ppermute | solution.py:490
  79.5 16.0 %all-to-all-start.2 = ((f32[16,48,128]{2,1,0:T(8,128)}), f32[16,48,128]{2,1,0:T(8,128)S(1)}, u32[]{:S(2)}, u32[]{:S(2)}) async-start(f32[16,48,128]{2,1,0:T(8,128)} %pad_maximum_fusion), calls=%async_computation.2 | async-start | bytes 786432 | tf_op jit(solution)/shard_map/all_to_all | solution.py:570
  86.0 28.0 %collective-permute-start.9 = (bf16[224,1024]{1,0:T(8,128)(2,1)}, bf16[224,1024]{1,0:T(8,128)(2,1)}, u32[]{:S(2)}, u32[]{:S(2)}) collective-permute-start(bf16[224,1024]{1,0:T(8,128)(2,1)} %get-tuple-element.69), channel_id=1, source_target_pairs={{0,4},{1,5},{2,6},{3,7},{4,8},{5,9},{6,10},{7,11},{8,12},{9,13},{1... | collective-permute-start | bytes 1376264 | tf_op jit(solution)/shard_map/ppermute | solution.py:117
  87.4 26.7 %collective-permute-start.10 = (bf16[224,1024]{1,0:T(8,128)(2,1)}, bf16[224,1024]{1,0:T(8,128)(2,1)}, u32[]{:S(2)}, u32[]{:S(2)}) collective-permute-start(bf16[224,1024]{1,0:T(8,128)(2,1)} %get-tuple-element.70), channel_id=1, source_target_pairs={{0,12},{1,13},{2,14},{3,15},{4,0},{5,1},{6,2},{7,3},{8,4},{9,5},{1... | collective-permute-start | bytes 1376264 | tf_op jit(solution)/shard_map/ppermute | solution.py:117
  88.8 25.3 %collective-permute-start.11 = (bf16[224,1024]{1,0:T(8,128)(2,1)}, bf16[224,1024]{1,0:T(8,128)(2,1)}, u32[]{:S(2)}, u32[]{:S(2)}) collective-permute-start(bf16[224,1024]{1,0:T(8,128)(2,1)} %get-tuple-element.71), channel_id=1, source_target_pairs={{0,8},{1,9},{2,10},{3,11},{4,12},{5,13},{6,14},{7,15},{8,0},{9,1},... | collective-permute-start | bytes 1376264 | tf_op jit(solution)/shard_map/ppermute | solution.py:117
  96.8 12.3 %all-to-all-start.3 = ((f32[8,24,128]{2,1,0:T(8,128)}), f32[8,24,128]{2,1,0:T(8,128)S(1)}, u32[]{:S(2)}, u32[]{:S(2)}) async-start(f32[8,24,128]{2,1,0:T(8,128)} %broadcast_in_dim.10), calls=%async_computation.3 | async-start | bytes 196608 | tf_op jit(solution)/shard_map/all_to_all | solution.py:35
  101.5 12.6 %copy-start.11 = (f32[24,128]{1,0:T(8,128)S(1)}, f32[24,128]{1,0:T(8,128)}, u32[]{:S(2)}) copy-start(f32[24,128]{1,0:T(8,128)} %get-tuple-element.90._.gram_ref) | copy-start | bytes 36868
  105.6 25.4 %copy-start.1 = (f32[256,896]{1,0:T(8,128)S(1)}, f32[256,896]{1,0:T(8,128)}, u32[]{:S(2)}) copy-start(f32[256,896]{1,0:T(8,128)} %copy-done) | copy-start | bytes 2752516
  105.6 25.4 %copy-start.3 = (f32[256,896]{1,0:T(8,128)S(1)}, f32[256,896]{1,0:T(8,128)}, u32[]{:S(2)}) copy-start(f32[256,896]{1,0:T(8,128)} %copy-done.2) | copy-start | bytes 2752516
  109.1 0.7 copy-start.13
  110.5 15.3 %all-to-all-start.4 = ((f32[16,24,128]{2,1,0:T(8,128)}), f32[16,24,128]{2,1,0:T(8,128)S(1)}, u32[]{:S(2)}, u32[]{:S(2)}) async-start(f32[16,24,128]{2,1,0:T(8,128)} %broadcast_in_dim.11), calls=%async_computation.4 | async-start | bytes 393216 | tf_op jit(solution)/shard_map/all_to_all | solution.py:35
  114.1 1.0 copy-start.9
  115.1 15.9 %copy-start.12 = (f32[3,32,32]{2,1,0:T(8,128)S(1)}, f32[3,32,32]{2,1,0:T(8,128)}, u32[]{:S(2)}) copy-start(f32[3,32,32]{2,1,0:T(8,128)} %get-tuple-element.86.inverse_ref) | copy-start | bytes 36868
  116.6 6.1 %collective-permute-start.16 = (bf16[56,1024]{1,0:T(8,128)(2,1)S(1)}, bf16[56,1024]{1,0:T(8,128)(2,1)S(1)}, u32[]{:S(2)}, u32[]{:S(2)}) collective-permute-start(bf16[56,1024]{1,0:T(8,128)(2,1)S(1)} %get-tuple-element.80), channel_id=1, source_target_pairs={{0,1},{1,2},{2,3},{3,0},{4,5},{5,6},{6,7},{7,4},{8,9},{9,10},{10,1... | collective-permute-start | bytes 344072 | tf_op jit(solution)/shard_map/ppermute | solution.py:137
  118.0 4.8 %collective-permute-start.17 = (bf16[56,1024]{1,0:T(8,128)(2,1)S(1)}, bf16[56,1024]{1,0:T(8,128)(2,1)S(1)}, u32[]{:S(2)}, u32[]{:S(2)}) collective-permute-start(bf16[56,1024]{1,0:T(8,128)(2,1)S(1)} %get-tuple-element.81), channel_id=1, source_target_pairs={{0,3},{1,0},{2,1},{3,2},{4,7},{5,4},{6,5},{7,6},{8,11},{9,8},{10,9... | collective-permute-start | bytes 344072 | tf_op jit(solution)/shard_map/ppermute | solution.py:137
  119.4 5.7 %collective-permute-start.18 = (bf16[56,1024]{1,0:T(8,128)(2,1)S(1)}, bf16[56,1024]{1,0:T(8,128)(2,1)S(1)}, u32[]{:S(2)}, u32[]{:S(2)}) collective-permute-start(bf16[56,1024]{1,0:T(8,128)(2,1)S(1)} %get-tuple-element.82), channel_id=1, source_target_pairs={{0,2},{1,3},{2,0},{3,1},{4,6},{5,7},{6,4},{7,5},{8,10},{9,11},{10,... | collective-permute-start | bytes 344072 | tf_op jit(solution)/shard_map/ppermute | solution.py:137
  125.8 5.2 %collective-permute-start.19 = (f32[384,128]{1,0:T(8,128)S(1)}, f32[384,128]{1,0:T(8,128)S(1)}, u32[]{:S(2)}, u32[]{:S(2)}) collective-permute-start(f32[384,128]{1,0:T(8,128)S(1)} %shard_map.107.s_mine_ref), channel_id=1, source_target_pairs={{0,16},{16,0},{32,48},{48,32},{64,80},{80,64},{96,112},{112,96},{1... | collective-permute-start | bytes 589832 | tf_op jit(solution)/shard_map/ppermute | solution.py:490
